TPU v7x, 32 devices: a whole 2x2x4 slice. The times are simulated.
32 devices in a mesh: rows: 8 (over y, x, core), mlp: 4 (over z).
Axes of the slice: x: 2, y: 2, z: 4, core: 2. Of those that a mesh axis runs over, the one named last changes fastest.
Arguments:
- tokens: bfloat16 [65536, 1024], P(('rows', 'mlp')), may hold values from -6 to 6
- doc_lengths: int32 [64, 4], P(('rows', 'mlp')), may hold values from 1 to 512, 1024 in all within a row
- cotangent: bfloat16 [65536, 1024], P(('rows', 'mlp')), may hold values from -6 to 6
- norm_gain_mix: bfloat16 [1024], P(('rows', 'mlp')), may hold values from 0.5 to 1.5
- w_query: bfloat16 [1024, 512], P(('rows', 'mlp')), may hold values from -0.1875 to 0.1875
- w_key: bfloat16 [1024, 512], P(('rows', 'mlp')), may hold values from -0.1875 to 0.1875
- w_value: bfloat16 [1024, 1024], P(('rows', 'mlp')), may hold values from -0.1875 to 0.1875
- w_outgate: bfloat16 [1024, 1024], P(('rows', 'mlp')), may hold values from -0.1875 to 0.1875
- w_rank: bfloat16 [1024, 16], P(('rows', 'mlp')), may hold values from -0.1875 to 0.1875
- w_decay: bfloat16 [16, 512], replicated, may hold values from -1.5 to 1.5
- decay_bias: bfloat16 [512], replicated, may hold values from 0.5 to 5
- head_gain: bfloat16 [256], replicated, may hold values from 0.5 to 1.5
- w_output: bfloat16 [1024, 1024], P(None, ('rows', 'mlp')), may hold values from -0.375 to 0.375
- norm_gain_mlp: bfloat16 [1024], P(('rows', 'mlp')), may hold values from 0.5 to 1.5
- w_gate: bfloat16 [1024, 2816], P('rows', 'mlp'), may hold values from -0.1875 to 0.1875
- w_up: bfloat16 [1024, 2816], P('rows', 'mlp'), may hold values from -0.1875 to 0.1875
- w_down: bfloat16 [2816, 1024], P('mlp', 'rows'), may hold values from -0.21875 to 0.21875
Outputs:
- block_out: bfloat16 [65536, 1024], P(('rows', 'mlp'))
- grad_tokens: float32 [65536, 1024], P(('rows', 'mlp'))
- grad_norm_mix: float32 [1024], P(('rows', 'mlp'))
- grad_w_query: float32 [1024, 512], P(('rows', 'mlp'))
- grad_w_key: float32 [1024, 512], P(('rows', 'mlp'))
- grad_w_value: float32 [1024, 1024], P(('rows', 'mlp'))
- grad_w_outgate: float32 [1024, 1024], P(('rows', 'mlp'))
- grad_w_rank: float32 [1024, 16], P(('rows', 'mlp'))
- grad_w_decay: float32 [16, 512], replicated
- grad_decay_bias: float32 [512], replicated
- grad_head_gain: float32 [256], replicated
- grad_w_output: float32 [1024, 1024], P(None, ('rows', 'mlp'))
- grad_norm_mlp: float32 [1024], P(('rows', 'mlp'))
- grad_w_gate: float32 [1024, 2816], P('rows', 'mlp')
- grad_w_up: float32 [1024, 2816], P('rows', 'mlp')
- grad_w_down: float32 [2816, 1024], P('mlp', 'rows')
Inputs may be any that keep to these rules, and one draw needn't show every extreme that they name: `doc_lengths`: each row holds the lengths of 4 documents that fill one sequence of 1024 tokens in order; the longest is 512.
All inputs are finite; a program needn't handle non-finite values.
Results may differ from a plain program's by a relative error of at most 0.019.
Values may be sent and summed in bfloat16 or wider, within the bound.
No kernel may reach another device: no remote copies, remote signals or barrier semaphores. Data moves between devices by JAX's collectives and lax.ppermute only.
A program may use at most 448 MiB of HBM per device.

v0:
```python
import jax
import jax.numpy as jnp
from jax import lax
from jax.sharding import PartitionSpec as P

H = 4
BLOCK = 64
LEN = 1024
MB = 2
HK = 128
HV = 256
NC = 16


EPSILON = 1e-05


def rms_scale(values):
    return lax.rsqrt(jnp.mean(values * values, axis=-1, keepdims=True) + EPSILON)


def head_scale(values):
    return lax.rsqrt(jnp.maximum(jnp.mean(values * values, axis=-1, keepdims=True), 1.0))


def rounded(values):
    return lax.optimization_barrier(values.astype(jnp.bfloat16)).astype(jnp.float32)


def product(left, right):
    return jnp.dot(left, right, preferred_element_type=jnp.float32)


def product_left(left, right):
    return lax.dot_general(
        left, right, (((0,), (0,)), ((), ())), preferred_element_type=jnp.float32
    )


def product_right(left, right):
    return lax.dot_general(
        left, right, (((1,), (1,)), ((), ())), preferred_element_type=jnp.float32
    )


def norm_back(grad_norm, values, scale, gain, active=1.0):
    scaled = grad_norm * gain
    inner = jnp.mean(scaled * values, axis=-1, keepdims=True) * active
    return (scale * scaled - values * scale**3 * inner, grad_norm * values * scale)


def doc_masks(lengths, length, block_len):
    starts = jnp.cumsum(lengths, axis=-1) - lengths
    places = jnp.arange(length, dtype=jnp.int32)
    doc_ids = jnp.sum((places[None, :, None] >= starts[:, None, 1:]).astype(jnp.int32), axis=-1)
    blocks = doc_ids.reshape(lengths.shape[0], length // block_len, block_len)
    final_ids = blocks[:, :, -1]
    prior_ids = jnp.concatenate(
        [jnp.full((blocks.shape[0], 1), -1, jnp.int32), final_ids[:, :-1]], axis=1
    )
    within = jnp.arange(block_len, dtype=jnp.int32)
    causal = within[:, None] >= within[None, :]
    intra_mask = ((blocks[..., :, None] == blocks[..., None, :]) & causal).astype(jnp.float32)
    inter_mask = (blocks == prior_ids[..., None]).astype(jnp.float32)
    keep_last = (final_ids == prior_ids).astype(jnp.float32)
    reach_last = (blocks == final_ids[..., None]).astype(jnp.float32)
    return (intra_mask, inter_mask, keep_last, reach_last)


def mixer_forward(inputs, masking, weights, small_params):
    gain_mix, w_query, w_key, w_value, w_outgate, w_rank, w_output = weights
    w_decay, decay_bias, head_gain = small_params
    intra_mask, inter_mask, keep_last, reach_last = masking
    seq_count = inputs.shape[0] // LEN
    key_shape = (seq_count, NC, BLOCK, H, HK)
    val_shape = (seq_count, NC, BLOCK, H, HV)
    scale_in = rms_scale(inputs)
    normed_in = (inputs * scale_in * gain_mix.astype(jnp.float32)).astype(jnp.bfloat16)
    queries = product(normed_in, w_query).reshape(key_shape) * HK ** (-0.5)
    keys_proj = product(normed_in, w_key).reshape(key_shape)
    values = product(normed_in, w_value).astype(jnp.bfloat16).reshape(val_shape)
    gate_pre = product(normed_in, w_outgate).reshape(val_shape)
    rank_proj = product(normed_in, w_rank).astype(jnp.bfloat16)
    decay_pre = product(rank_proj, w_decay) + decay_bias.astype(jnp.float32)
    cumulative = jnp.cumsum((jax.nn.log_sigmoid(decay_pre) / 16.0).reshape(key_shape), axis=2)
    block_end = cumulative[:, :, -1:]
    grow_exp = jnp.exp(cumulative)
    shrink_exp = jnp.exp(-cumulative)
    carry_exp = jnp.exp(block_end - cumulative)
    query_scaled = queries * grow_exp
    key_scaled = keys_proj * shrink_exp
    key_decayed = keys_proj * carry_exp
    query_gated = query_scaled.astype(jnp.bfloat16)
    key_gated = key_scaled.astype(jnp.bfloat16)
    key_carry = key_decayed.astype(jnp.bfloat16)
    scores = (
        jnp.einsum("pntha,pnsha->pnhts", query_gated, key_gated, preferred_element_type=jnp.float32)
        * intra_mask[:, :, None]
    ).astype(jnp.bfloat16)
    value_kept = values * reach_last[..., None, None].astype(jnp.bfloat16)
    update = jnp.einsum(
        "pnsha,pnshb->pnhab", key_carry, value_kept, preferred_element_type=jnp.float32
    )
    keep_factor = jnp.exp(block_end[:, :, 0]) * keep_last[:, :, None, None]

    def advance(carry_state, pieces):
        factor, added_term = pieces
        return (carry_state * factor[..., None] + added_term, carry_state)

    _, before = lax.scan(
        advance,
        jnp.zeros((seq_count, H, HK, HV), jnp.float32),
        (jnp.moveaxis(keep_factor, 1, 0), jnp.moveaxis(update, 1, 0)),
    )
    before = jnp.moveaxis(before, 0, 1)
    before_low = before.astype(jnp.bfloat16)
    mixer_out = jnp.einsum("pnhts,pnshb->pnthb", scores, values, preferred_element_type=jnp.float32)
    mixer_out = (
        mixer_out
        + jnp.einsum(
            "pntha,pnhab->pnthb", query_gated, before_low, preferred_element_type=jnp.float32
        )
        * inter_mask[..., None, None]
    )
    scale_out = head_scale(mixer_out)
    normed_out = mixer_out * scale_out * head_gain.astype(jnp.float32)
    gate_act = jax.nn.silu(gate_pre)
    mixed_in = (normed_out * gate_act).reshape(inputs.shape[0], -1).astype(jnp.bfloat16)
    mixed_out = product(mixed_in, w_output)
    stored = dict(
        scale_in=scale_in,
        normed_in=normed_in,
        values=values,
        gate_pre=gate_pre,
        rank_proj=rank_proj,
        decay_pre=decay_pre,
        grow_exp=grow_exp,
        shrink_exp=shrink_exp,
        carry_exp=carry_exp,
        query_scaled=query_scaled,
        key_scaled=key_scaled,
        key_decayed=key_decayed,
        query_gated=query_gated,
        key_gated=key_gated,
        key_carry=key_carry,
        scores=scores,
        value_kept=value_kept,
        keep_factor=keep_factor,
        before=before,
        before_low=before_low,
        mixer_out=mixer_out,
        scale_out=scale_out,
        normed_out=normed_out,
        gate_act=gate_act,
        mixed_in=mixed_in,
    )
    return (mixed_out, stored)


def mixer_backward(grad_mixed, inputs, masking, weights, small_params, stored):
    gain_mix, w_query, w_key, w_value, w_outgate, w_rank, w_output = weights
    w_decay, decay_bias, head_gain = small_params
    intra_mask, inter_mask, keep_last, reach_last = masking
    row_count = inputs.shape[0]
    seq_count = row_count // LEN
    val_shape = (seq_count, NC, BLOCK, H, HV)
    grad_w_output = product_left(stored["mixed_in"], grad_mixed)
    grad_input = product_right(grad_mixed, w_output).reshape(val_shape)
    gate_pre = stored["gate_pre"]
    gate_sig = jax.nn.sigmoid(gate_pre)
    grad_gate = grad_input * stored["normed_out"] * gate_sig * (1.0 + gate_pre * (1.0 - gate_sig))
    grad_gate = grad_gate.reshape(row_count, -1).astype(jnp.bfloat16)
    unfloored = (stored["scale_out"] < 1.0).astype(jnp.float32)
    grad_out, head_terms = norm_back(
        grad_input * stored["gate_act"],
        stored["mixer_out"],
        stored["scale_out"],
        head_gain.astype(jnp.float32),
        unfloored,
    )
    grad_head_gain = jnp.sum(head_terms.reshape(-1, HV), axis=0)
    grad_out = grad_out.astype(jnp.bfloat16)
    grad_seen = grad_out * inter_mask[..., None, None].astype(jnp.bfloat16)
    values = stored["values"]
    query_gated = stored["query_gated"]
    key_carry = stored["key_carry"]
    grad_scores = (
        jnp.einsum("pnthb,pnshb->pnhts", grad_out, values, preferred_element_type=jnp.float32)
        * intra_mask[:, :, None]
    ).astype(jnp.bfloat16)
    grad_values = jnp.einsum(
        "pnhts,pnthb->pnshb", stored["scores"], grad_out, preferred_element_type=jnp.float32
    )
    grad_qgated = jnp.einsum(
        "pnhts,pnsha->pntha", grad_scores, stored["key_gated"], preferred_element_type=jnp.float32
    )
    grad_qgated = grad_qgated + jnp.einsum(
        "pnthb,pnhab->pntha", grad_seen, stored["before_low"], preferred_element_type=jnp.float32
    )
    grad_kgated = jnp.einsum(
        "pnhts,pntha->pnsha", grad_scores, query_gated, preferred_element_type=jnp.float32
    )
    grad_local = jnp.einsum(
        "pntha,pnthb->pnhab", query_gated, grad_seen, preferred_element_type=jnp.float32
    )

    def retreat(carry_grad, pieces):
        local_term, factor = pieces
        return (rounded(local_term + factor[..., None] * carry_grad), carry_grad)

    _, grad_after = lax.scan(
        retreat,
        jnp.zeros((seq_count, H, HK, HV), jnp.float32),
        (jnp.moveaxis(grad_local, 1, 0), jnp.moveaxis(stored["keep_factor"], 1, 0)),
        reverse=True,
    )
    grad_after = jnp.moveaxis(grad_after, 0, 1)
    after_low = grad_after.astype(jnp.bfloat16)
    grad_kcarry = jnp.einsum(
        "pnshb,pnhab->pnsha", stored["value_kept"], after_low, preferred_element_type=jnp.float32
    )
    grad_values = (
        grad_values
        + jnp.einsum("pnsha,pnhab->pnshb", key_carry, after_low, preferred_element_type=jnp.float32)
        * reach_last[..., None, None]
    )
    grad_end_state = jnp.sum(grad_after * stored["before"], axis=-1) * stored["keep_factor"]
    grad_cum = (
        grad_qgated * stored["query_scaled"]
        - grad_kgated * stored["key_scaled"]
        - grad_kcarry * stored["key_decayed"]
    )
    grad_end = (
        jnp.sum(grad_kcarry * stored["key_decayed"], axis=2, keepdims=True)
        + grad_end_state[:, :, None]
    )
    grad_decay = jnp.flip(jnp.cumsum(jnp.flip(grad_cum, 2), axis=2), 2) + grad_end
    grad_queries = (
        (grad_qgated * stored["grow_exp"] * HK ** (-0.5))
        .reshape(row_count, -1)
        .astype(jnp.bfloat16)
    )
    grad_keys = grad_kgated * stored["shrink_exp"] + grad_kcarry * stored["carry_exp"]
    grad_keys = grad_keys.reshape(row_count, -1).astype(jnp.bfloat16)
    grad_vals = grad_values.reshape(row_count, -1).astype(jnp.bfloat16)
    grad_pre = (
        grad_decay.reshape(row_count, -1) / 16.0 * jax.nn.sigmoid(-stored["decay_pre"])
    ).astype(jnp.bfloat16)
    grad_decay_bias = jnp.sum(grad_pre.astype(jnp.float32), axis=0)
    grad_w_decay = product_left(stored["rank_proj"], grad_pre)
    grad_rank = product_right(grad_pre, w_decay).astype(jnp.bfloat16)
    normed_in = stored["normed_in"]
    grad_normed = (
        product_right(grad_queries, w_query)
        + product_right(grad_keys, w_key)
        + product_right(grad_vals, w_value)
        + product_right(grad_gate, w_outgate)
        + product_right(grad_rank, w_rank)
    )
    grad_inputs, gain_terms = norm_back(
        grad_normed, inputs, stored["scale_in"], gain_mix.astype(jnp.float32)
    )
    big_grads = (
        jnp.sum(gain_terms, axis=0),
        product_left(normed_in, grad_queries),
        product_left(normed_in, grad_keys),
        product_left(normed_in, grad_vals),
        product_left(normed_in, grad_gate),
        product_left(normed_in, grad_rank),
        grad_w_output,
    )
    return (grad_inputs, big_grads, (grad_w_decay, grad_decay_bias, grad_head_gain))


def mlp_pass(rows_in, grad_rows, w_gate, w_up, w_down):
    gate_proj = product(rows_in, w_gate)
    up_proj = product(rows_in, w_up)
    gate_sig = jax.nn.sigmoid(gate_proj)
    hidden = (gate_proj * gate_sig * up_proj).astype(jnp.bfloat16)
    branch = product(hidden, w_down)
    grad_hidden = product_right(grad_rows, w_down)
    grad_w_down = product_left(hidden, grad_rows)
    grad_up = (grad_hidden * gate_proj * gate_sig).astype(jnp.bfloat16)
    grad_gate = (grad_hidden * up_proj * gate_sig * (1.0 + gate_proj * (1.0 - gate_sig))).astype(
        jnp.bfloat16
    )
    grad_rows_in = product_right(grad_gate, w_gate) + product_right(grad_up, w_up)
    return (
        branch,
        grad_rows_in,
        (product_left(rows_in, grad_gate), product_left(rows_in, grad_up), grad_w_down),
    )


def body(
    tokens,
    doc_lengths,
    cotangent,
    norm_gain_mix,
    w_query,
    w_key,
    w_value,
    w_outgate,
    w_rank,
    w_decay,
    decay_bias,
    head_gain,
    w_output,
    norm_gain_mlp,
    w_gate,
    w_up,
    w_down,
):
    seq_count = doc_lengths.shape[0] // MB
    rows_each = seq_count * LEN
    small_params = (w_decay, decay_bias, head_gain)
    outputs = []
    grad_list = []
    mixer_acc = None
    mlp_acc = None
    small_acc = None
    for portion in range(MB):
        mixer_weights = (
            lax.all_gather(norm_gain_mix, ("rows", "mlp"), axis=0, tiled=True),
            lax.all_gather(w_query, ("rows", "mlp"), axis=0, tiled=True),
            lax.all_gather(w_key, ("rows", "mlp"), axis=0, tiled=True),
            lax.all_gather(w_value, ("rows", "mlp"), axis=0, tiled=True),
            lax.all_gather(w_outgate, ("rows", "mlp"), axis=0, tiled=True),
            lax.all_gather(w_rank, ("rows", "mlp"), axis=0, tiled=True),
            lax.all_gather(w_output, ("rows", "mlp"), axis=1, tiled=True),
            lax.all_gather(norm_gain_mlp, ("rows", "mlp"), axis=0, tiled=True),
        )
        mlp_weights = (
            lax.all_gather(w_gate, "rows", axis=0, tiled=True),
            lax.all_gather(w_up, "rows", axis=0, tiled=True),
            lax.all_gather(w_down, "rows", axis=1, tiled=True),
        )
        first_row = portion * rows_each
        inputs = tokens[first_row : first_row + rows_each].astype(jnp.float32)
        grad_rows = cotangent[first_row : first_row + rows_each]
        masking = doc_masks(
            doc_lengths[portion * seq_count : (portion + 1) * seq_count], LEN, BLOCK
        )
        mixer_part = mixer_weights[:7]
        gain_mlp = mixer_weights[7].astype(jnp.float32)
        mixed_out, stored = mixer_forward(inputs, masking, mixer_part, small_params)
        residual = inputs + mixed_out
        scale_mid = rms_scale(residual)
        normed_mid = (residual * scale_mid * gain_mlp).astype(jnp.bfloat16)
        gathered_rows, gathered_grads = (
            lax.all_gather(normed_mid, "mlp", axis=0, tiled=True),
            lax.all_gather(grad_rows, "mlp", axis=0, tiled=True),
        )
        branch_part, grad_part, mlp_grads = mlp_pass(
            gathered_rows, gathered_grads, mlp_weights[0], mlp_weights[1], mlp_weights[2]
        )
        branch, grad_mid = (
            lax.psum_scatter(
                branch_part.astype(jnp.bfloat16), "mlp", scatter_dimension=0, tiled=True
            ).astype(jnp.float32),
            lax.psum_scatter(
                grad_part.astype(jnp.bfloat16), "mlp", scatter_dimension=0, tiled=True
            ).astype(jnp.float32),
        )
        outputs.append((residual + branch).astype(jnp.bfloat16))
        grad_mid_in, mid_terms = norm_back(grad_mid, residual, scale_mid, gain_mlp)
        grad_res = grad_rows.astype(jnp.float32) + grad_mid_in
        grad_inputs, big_grads, small_grads = mixer_backward(
            grad_res.astype(jnp.bfloat16), inputs, masking, mixer_part, small_params, stored
        )
        grad_list.append(grad_res + grad_inputs)
        big_grads = big_grads + (jnp.sum(mid_terms, axis=0),)
        if portion == 0:
            mixer_acc, mlp_acc, small_acc = (big_grads, mlp_grads, small_grads)
        else:
            mixer_acc = jax.tree.map(jnp.add, mixer_acc, big_grads)
            mlp_acc = jax.tree.map(jnp.add, mlp_acc, mlp_grads)
            small_acc = jax.tree.map(jnp.add, small_acc, small_grads)
    mixer_shards = (
        lax.psum_scatter(mixer_acc[0], ("rows", "mlp"), scatter_dimension=0, tiled=True),
        lax.psum_scatter(mixer_acc[1], ("rows", "mlp"), scatter_dimension=0, tiled=True),
        lax.psum_scatter(mixer_acc[2], ("rows", "mlp"), scatter_dimension=0, tiled=True),
        lax.psum_scatter(mixer_acc[3], ("rows", "mlp"), scatter_dimension=0, tiled=True),
        lax.psum_scatter(mixer_acc[4], ("rows", "mlp"), scatter_dimension=0, tiled=True),
        lax.psum_scatter(mixer_acc[5], ("rows", "mlp"), scatter_dimension=0, tiled=True),
        lax.psum_scatter(mixer_acc[6], ("rows", "mlp"), scatter_dimension=1, tiled=True),
        lax.psum_scatter(mixer_acc[7], ("rows", "mlp"), scatter_dimension=0, tiled=True),
    )
    mlp_shards = (
        lax.psum_scatter(mlp_acc[0], "rows", scatter_dimension=0, tiled=True),
        lax.psum_scatter(mlp_acc[1], "rows", scatter_dimension=0, tiled=True),
        lax.psum_scatter(mlp_acc[2], "rows", scatter_dimension=1, tiled=True),
    )
    small_acc = lax.psum((small_acc[0], small_acc[1], small_acc[2]), ("rows", "mlp"))
    return (
        jnp.concatenate(outputs, axis=0),
        jnp.concatenate(grad_list, axis=0),
        mixer_shards[0],
        mixer_shards[1],
        mixer_shards[2],
        mixer_shards[3],
        mixer_shards[4],
        mixer_shards[5],
        small_acc[0],
        small_acc[1],
        small_acc[2],
        mixer_shards[6],
        mixer_shards[7],
        mlp_shards[0],
        mlp_shards[1],
        mlp_shards[2],
    )


def solution(mesh):
    in_specs = (
        P(("rows", "mlp"), None),
        P(("rows", "mlp"), None),
        P(("rows", "mlp"), None),
        P(("rows", "mlp")),
        P(("rows", "mlp"), None),
        P(("rows", "mlp"), None),
        P(("rows", "mlp"), None),
        P(("rows", "mlp"), None),
        P(("rows", "mlp"), None),
        P(),
        P(),
        P(),
        P(None, ("rows", "mlp")),
        P(("rows", "mlp")),
        P("rows", "mlp"),
        P("rows", "mlp"),
        P("mlp", "rows"),
    )
    out_specs = (
        P(("rows", "mlp"), None),
        P(("rows", "mlp"), None),
        P(("rows", "mlp")),
        P(("rows", "mlp"), None),
        P(("rows", "mlp"), None),
        P(("rows", "mlp"), None),
        P(("rows", "mlp"), None),
        P(("rows", "mlp"), None),
        P(),
        P(),
        P(),
        P(None, ("rows", "mlp")),
        P(("rows", "mlp")),
        P("rows", "mlp"),
        P("rows", "mlp"),
        P("mlp", "rows"),
    )
    return jax.shard_map(body, mesh=mesh, in_specs=in_specs, out_specs=out_specs, check_vma=False)
```

profile of v0, /device:TPU:0, one launch (start us, length us, event | category | flops | bytes accessed | tf_op | source)
XLA Modules:
  0.0 2979.7 jit_solution(3565840558957283024)
XLA Ops:
  16.7 42.1 %all-reduce.5 = (bf16[1024]{0:T(1024)(128)(2,1)S(1)}, bf16[1024]{0:T(1024)(128)(2,1)S(1)}) all-reduce(bf16[1024]{0:T(1024)(128)(2,1)S(1)} %dynamic-update-slice, bf16[1024]{0:T(1024)(128)(2,1)S(1)} %dynamic-update-slice.1), channel_id=1, replica_groups=mesh['rows'=8,'mlp'=4] {'rows','mlp'}, use_global_device_ids=true, to_apply=%add | all-reduce | flops 2048 | bytes 8192
  62.6 67.1 %all-gather = bf16[32,32,16]{1,2,0:T(8,128)(2,1)S(1)} all-gather(bf16[1,32,16]{1,2,0:T(8,128)(2,1)S(1)} %bitcast.560), channel_id=1, replica_groups=mesh['rows'=8,'mlp'=4] {'rows','mlp'}, dimensions={0}, use_global_device_ids=true | all-gather | bytes 33792 | tf_op jit(solution)/shard_map/all_gather | solution.py:329
  215.4 24.8 all-gather.20.cloned.1.call-done
  275.6 33.7 %while.61 = (s32[]{:T(128)}, f32[1,4,128,256]{3,2,1,0:T(8,128)S(1)}, f32[16,1,4,128,256]{4,3,2,1,0:T(8,128)}, f32[16,1,4,128]{3,2,1,0:T(4,128)S(1)}, f32[16,1,4,128,256]{4,3,2,1,0:T(8,128)}, /*index=5*/s32[]{:T(128)}, s32[]{:T(128)}) while((s32[]{:T(128)}, f32[1,4,128,256]{3,2,1,0:T(8,128)S(1)}, ...), condition=%wide.region_14.15_spmd.clone, body=%wide.region_13.14_spmd.clone.sunk | while | flops 524291 | bytes 2627692 | solution.py:110
  326.5 33.7 %while.60 = (s32[]{:T(128)}, f32[1,4,128,256]{3,2,1,0:T(8,128)S(1)}, f32[16,1,4,128,256]{4,3,2,1,0:T(8,128)}, f32[16,1,4,128]{3,2,1,0:T(4,128)S(1)}, f32[16,1,4,128,256]{4,3,2,1,0:T(8,128)}, /*index=5*/s32[]{:T(128)}, s32[]{:T(128)}) while((s32[]{:T(128)}, f32[1,4,128,256]{3,2,1,0:T(8,128)S(1)}, f32[16,1,4,128,256]{4,3,2,1,0:T(8,128)}, ...), condition=%wide.region_5.6_spmd.clone, body=%wide.region_4.5_spmd.clone.sunk | while | flops 524291 | bytes 2627692 | solution.py:110
  392.0 142.4 %all-gather.24.cloned.1.call-done = bf16[4096,1024]{1,0:T(8,128)(2,1)} async-done(((bf16[1024,1024]{1,0:T(8,128)(2,1)}), bf16[4096,1024]{1,0:T(8,128)(2,1)}) %all-gather.24.cloned.1.call-update) | async-done | bytes 8388624 | tf_op jit(solution)/shard_map/all_gather | solution.py:351
  534.4 12.8 fusion.265
  547.2 12.6 all-gather.26.cloned.1.call-done
  559.8 12.6 fusion.264
  572.4 14.6 all-gather.30.cloned.1.call-done
  587.0 151.1 %all-gather.34.cloned.1.call-done = bf16[4096,1024]{1,0:T(8,128)(2,1)} async-done(((bf16[1024,1024]{1,0:T(8,128)(2,1)}), bf16[4096,1024]{1,0:T(8,128)(2,1)}) %all-gather.34.cloned.1.call-update) | async-done | bytes 8388624 | tf_op jit(solution)/shard_map/all_gather | solution.py:352
  738.1 22.7 multiply_convert_fusion.2
  760.8 13.6 fusion.269
  774.4 12.4 add_convert_fusion.1
  794.2 135.5 %reduce-scatter.20.cloned.1.call-done = bf16[1024,1024]{1,0:T(8,128)(2,1)} async-done(((bf16[4096,1024]{1,0:T(8,128)(2,1)}), bf16[1024,1024]{1,0:T(8,128)(2,1)}) %reduce-scatter.20.cloned.1.call-update) | async-done | bytes 2097168 | tf_op jit(solution)/shard_map/reduce_scatter | solution.py:361
  936.9 149.7 %all-gather.32.cloned.1.call-done = bf16[4096,1024]{1,0:T(8,128)(2,1)} async-done(((bf16[1024,1024]{1,0:T(8,128)(2,1)}), bf16[4096,1024]{1,0:T(8,128)(2,1)}) %all-gather.32.cloned.1.call-update) | async-done | bytes 8388624 | tf_op jit(solution)/shard_map/all_gather | solution.py:351
  1086.6 12.4 fusion.268
  1099.0 10.5 fusion.267
  1109.6 126.5 %all-gather.36.cloned.1.call-done = bf16[4096,1024]{1,0:T(8,128)(2,1)} async-done(((bf16[1024,1024]{1,0:T(8,128)(2,1)}), bf16[4096,1024]{1,0:T(8,128)(2,1)}) %all-gather.36.cloned.1.call-update) | async-done | bytes 8388624 | tf_op jit(solution)/shard_map/all_gather | solution.py:352
  1236.1 22.6 multiply_convert_fusion
  1258.6 13.3 fusion.272
  1271.9 12.7 add_convert_fusion
  1284.7 11.8 convolution_convert_fusion.1
  1296.6 11.8 convolution_convert_fusion
  1321.1 11.5 fusion.277
  1332.5 95.0 %reduce-scatter.22.cloned.1.call-done = bf16[1024,1024]{1,0:T(8,128)(2,1)} async-done(((bf16[4096,1024]{1,0:T(8,128)(2,1)}), bf16[1024,1024]{1,0:T(8,128)(2,1)}) %reduce-scatter.22.cloned.1.call-update) | async-done | bytes 2097168 | tf_op jit(solution)/shard_map/reduce_scatter | solution.py:361
  1432.3 142.7 %reduce-scatter.16.cloned.1.call-done = bf16[1024,1024]{1,0:T(8,128)(2,1)} async-done(((bf16[4096,1024]{1,0:T(8,128)(2,1)}), bf16[1024,1024]{1,0:T(8,128)(2,1)}) %reduce-scatter.16.cloned.1.call-update) | async-done | bytes 2097168 | tf_op jit(solution)/shard_map/reduce_scatter | solution.py:358
  1575.0 147.4 %reduce-scatter.18.cloned.1.call-done = bf16[1024,1024]{1,0:T(8,128)(2,1)} async-done(((bf16[4096,1024]{1,0:T(8,128)(2,1)}), bf16[1024,1024]{1,0:T(8,128)(2,1)}) %reduce-scatter.18.cloned.1.call-update) | async-done | bytes 2097168 | tf_op jit(solution)/shard_map/reduce_scatter | solution.py:358
  1722.4 12.1 fusion.10
  1759.5 16.8 fusion.66
  1814.1 45.0 %while.63 = (s32[]{:T(128)}, f32[1,4,128,256]{3,2,1,0:T(8,128)S(1)}, f32[16,1,4,128,256]{4,3,2,1,0:T(8,128)}, f32[16,1,4,128,256]{4,3,2,1,0:T(8,128)}, f32[16,1,...) while((s32[]{:T(128)}, f32[1,4,128,256]{3,2,1,0:T(8,128)S(1)}, ...), condition=%wide.region_31.32_spmd.clone, body=%wide.region_30.31_spmd.clone.sunk | while | flops 786436 | bytes 3152000 | solution.py:211
  1867.3 9.9 fusion.153
  1891.8 44.8 %while.62 = (s32[]{:T(128)}, f32[1,4,128,256]{3,2,1,0:T(8,128)S(1)}, f32[16,1,4,128,256]{4,3,2,1,0:T(8,128)}, f32[16,1,4,128,256]{4,3,2,1,0:T(8,128)}, f32[16,1,...) while((s32[]{:T(128)}, f32[1,4,128,256]{3,2,1,0:T(8,128)S(1)}, ...), condition=%wide.region_22.23_spmd.clone, body=%wide.region_21.22_spmd.clone.sunk | while | flops 786436 | bytes 3152000 | solution.py:211
  1944.8 9.6 fusion.152
  1967.2 11.8 convolution_add_fusion.4
  1979.1 10.3 fusion.278
  1989.3 11.4 convolution_add_fusion.3
  2000.8 10.4 fusion.276
  2011.3 11.5 convolution_add_fusion.5
  2109.8 9.8 fusion.24
  2120.1 42.0 %all-reduce.4 = (f32[1024]{0:T(1024)S(1)}, f32[16,512]{1,0:T(8,128)}, f32[512]{0:T(512)}, f32[256]{0:T(256)}, f32[1024]{0:T(1024)S(1)}) all-reduce(f32[1024]{0:T(1024)S(1)} %add.498, f32[16,512]{1,0:T(8,128)S(1)} %convolution_add_fusion.11, f32[512]{0:T(512)S(1)} %add.505, ...), channel_id=6, replica_groups=mesh['rows'=8,'mlp'=4] {'rows','mlp'}, use_global_device_ids=true, to_apply=%region_38.39.clone | all-reduce | flops 11008 | bytes 88064
  2180.8 16.1 reduce-scatter.36.cloned.1.call-done
  2196.9 49.1 %reduce-scatter.38.cloned.1.call-done = f32[704,128]{1,0:T(8,128)} async-done(((f32[704,1024]{1,0:T(8,128)}), f32[704,128]{1,0:T(8,128)}) %reduce-scatter.38.cloned.1.call-update) | async-done | bytes 360464 | tf_op jit(solution)/shard_map/reduce_scatter | solution.py:392
  2246.0 141.0 %reduce-scatter.24.cloned.1.call-done = f32[32,512]{1,0:T(8,128)} async-done(((f32[1024,512]{1,0:T(8,128)}), f32[32,512]{1,0:T(8,128)}) %reduce-scatter.24.cloned.1.call-update) | async-done | bytes 65552 | tf_op jit(solution)/shard_map/reduce_scatter | solution.py:381
  2387.0 138.9 %reduce-scatter.26.cloned.1.call-done = f32[32,512]{1,0:T(8,128)} async-done(((f32[1024,512]{1,0:T(8,128)}), f32[32,512]{1,0:T(8,128)}) %reduce-scatter.26.cloned.1.call-update) | async-done | bytes 65552 | tf_op jit(solution)/shard_map/reduce_scatter | solution.py:382
  2525.9 148.5 %reduce-scatter.32.cloned.1.call-done = f32[1024,32]{0,1:T(8,128)} async-done(((f32[1024,1024]{0,1:T(8,128)}), f32[1024,32]{0,1:T(8,128)}) %reduce-scatter.32.cloned.1.call-update) | async-done | bytes 131088 | tf_op jit(solution)/shard_map/reduce_scatter | solution.py:386
  2674.4 149.5 %reduce-scatter.30.cloned.1.call-done = f32[32,1024]{1,0:T(8,128)} async-done(((f32[1024,1024]{1,0:T(8,128)}), f32[32,1024]{1,0:T(8,128)}) %reduce-scatter.30.cloned.1.call-update) | async-done | bytes 131088 | tf_op jit(solution)/shard_map/reduce_scatter | solution.py:384
  2823.9 149.1 %reduce-scatter.28.cloned.1.call-done = f32[32,1024]{1,0:T(8,128)} async-done(((f32[1024,1024]{1,0:T(8,128)}), f32[32,1024]{1,0:T(8,128)}) %reduce-scatter.28.cloned.1.call-update) | async-done | bytes 131088 | tf_op jit(solution)/shard_map/reduce_scatter | solution.py:383
  (796 shorter events, 580.8 us)
Async XLA Ops:
  7.2 129.5 %copy-start = (bf16[16,512]{1,0:T(8,128)(2,1)S(1)}, bf16[16,512]{1,0:T(8,128)(2,1)}, u32[]{:S(2)}) copy-start(bf16[16,512]{1,0:T(8,128)(2,1)} %param.34) | copy-start | bytes 49156
  7.2 55.4 %copy-start.142 = (bf16[32,16]{0,1:T(8,128)(2,1)S(1)}, bf16[32,16]{0,1:T(8,128)(2,1)}, u32[]{:S(2)}) copy-start(bf16[32,16]{0,1:T(8,128)(2,1)} %param.33) | copy-start | bytes 3076
  7.2 144.7 %all-gather.18.cloned.1.call-start = ((), (), s32[]{:S(2)}) async-start(), calls=%async_computation.15 | async-start | bytes 1081344 | tf_op jit(solution)/shard_map/all_gather | solution.py:326
  7.9 151.4 %all-gather.16.cloned.1.call-start = ((), (), s32[]{:S(2)}) async-start(), calls=%async_computation.14 | async-start | bytes 1081344 | tf_op jit(solution)/shard_map/all_gather | solution.py:325
  8.7 189.9 %all-gather.14.cloned.1.call-start = ((), (), s32[]{:S(2)}) async-start(), calls=%async_computation.13 | async-start | bytes 2162688 | tf_op jit(solution)/shard_map/all_gather | solution.py:327
  9.4 230.7 %all-gather.20.cloned.1.call-start = ((), (), s32[]{:S(2)}) async-start(), calls=%async_computation.16 | async-start | bytes 2162688 | tf_op jit(solution)/shard_map/all_gather | solution.py:328
  10.0 366.4 %all-gather.22.cloned.1.call-start = ((), (), s32[]{:S(2)}) async-start(), calls=%async_computation.17 | async-start | bytes 2162688 | tf_op jit(solution)/shard_map/all_gather | solution.py:330
  10.6 381.4 %all-gather.28.cloned.1.call-start = ((), (), s32[]{:S(2)}) async-start(), calls=%async_computation.20 | async-start | bytes 1622016 | tf_op jit(solution)/shard_map/all_gather | solution.py:335
  11.2 523.2 %all-gather.24.cloned.1.call-start = ((), (), s32[]{:S(2)}) async-start(), calls=%async_computation.18 | async-start | bytes 10485760 | tf_op jit(solution)/shard_map/all_gather | solution.py:351
  14.3 352.6 %copy-start.132 = (f32[256]{0:T(256)}, f32[256]{0:T(256)S(1)}, u32[]{:S(2)}) copy-start(f32[256]{0:T(256)S(1)} %convert_element_type.500) | copy-start | bytes 3076
  15.0 122.1 %copy-start.134 = (f32[512]{0:T(512)}, f32[512]{0:T(512)S(1)}, u32[]{:S(2)}) copy-start(f32[512]{0:T(512)S(1)} %convert_element_type.487) | copy-start | bytes 6148
  58.8 193.6 %copy-start.113 = (f32[1024]{0:T(1024)}, f32[1024]{0:T(1024)S(1)}, u32[]{:S(2)}) copy-start(f32[1024]{0:T(1024)S(1)} %convert_element_type.483) | copy-start | bytes 12292
  59.4 85.6 %copy-start.136 = (f32[16]{0:T(128)}, f32[16]{0:T(128)S(1)}, u32[]{:S(2)}) copy-start(f32[16]{0:T(128)S(1)} %compare_convert_fusion.7) | copy-start | bytes 196
  59.5 90.9 %copy-start.138 = (f32[16]{0:T(128)}, f32[16]{0:T(128)S(1)}, u32[]{:S(2)}) copy-start(f32[16]{0:T(128)S(1)} %compare_convert_fusion.6) | copy-start | bytes 196
  130.6 109.5 %copy-start.115 = (f32[1024]{0:T(1024)}, f32[1024]{0:T(1024)S(1)}, u32[]{:S(2)}) copy-start(f32[1024]{0:T(1024)S(1)} %get-tuple-element.572) | copy-start | bytes 12292
  130.6 121.8 %copy-start.117 = (f32[1024]{0:T(1024)}, f32[1024]{0:T(1024)S(1)}, u32[]{:S(2)}) copy-start(f32[1024]{0:T(1024)S(1)} %get-tuple-element.610) | copy-start | bytes 12292
  134.6 130.0 %copy-start.121 = (bf16[16,64]{1,0:T(8,128)(2,1)}, bf16[16,64]{1,0:T(8,128)(2,1)S(1)}, u32[]{:S(2)}) copy-start(bf16[16,64]{1,0:T(8,128)(2,1)S(1)} %get-tuple-element.567) | copy-start | bytes 6148
  135.3 182.1 %copy-start.119 = (bf16[16,64]{1,0:T(8,128)(2,1)}, bf16[16,64]{1,0:T(8,128)(2,1)S(1)}, u32[]{:S(2)}) copy-start(bf16[16,64]{1,0:T(8,128)(2,1)S(1)} %get-tuple-element.563) | copy-start | bytes 6148
  145.0 37.1 %copy-start.34 = (f32[1,16,64,4,128]{4,1,2,3,0:T(8,128)}, f32[1,16,64,4,128]{4,1,2,3,0:T(8,128)S(1)}, u32[]{:S(2)}) copy-start(f32[1,16,64,4,128]{4,1,2,3,0:T(8,128)S(1)} %fusion.124) | copy-start | bytes 6291460
  145.0 37.0 %copy-start.95 = (f32[16,4,128]{2,0,1:T(8,128)}, f32[16,4,128]{2,0,1:T(8,128)S(1)}, u32[]{:S(2)}) copy-start(f32[16,4,128]{2,0,1:T(8,128)S(1)} %slice_bitcast_fusion.1) | copy-start | bytes 98308
  151.8 39.5 %copy-start.97 = (f32[16,4,128]{2,0,1:T(8,128)}, f32[16,4,128]{2,0,1:T(8,128)S(1)}, u32[]{:S(2)}) copy-start(f32[16,4,128]{2,0,1:T(8,128)S(1)} %slice_bitcast_fusion) | copy-start | bytes 98308
  215.4 149.6 %copy-start.7 = (bf16[16,64,4,256]{3,2,1,0:T(4,128)(2,1)}, bf16[16,64,4,256]{3,2,1,0:T(4,128)(2,1)S(1)}, u32[]{:S(2)}) copy-start(bf16[16,64,4,256]{3,2,1,0:T(4,128)(2,1)S(1)} %reshape.1382) | copy-start | bytes 6291460
  317.4 49.5 %copy-start.89 = (f32[16,64,4]{1,2,0:T(4,128)}, f32[16,64,4]{1,2,0:T(4,128)S(1)}, u32[]{:S(2)}) copy-start(f32[16,64,4]{1,2,0:T(4,128)S(1)} %fusion.222) | copy-start | bytes 49156
  385.6 174.2 %all-gather.26.cloned.1.call-start = ((), (), s32[]{:S(2)}) async-start(), calls=%async_computation.19 | async-start | bytes 1622016 | tf_op jit(solution)/shard_map/all_gather | solution.py:334
  386.4 200.7 %all-gather.30.cloned.1.call-start = ((), (), s32[]{:S(2)}) async-start(), calls=%async_computation.21 | async-start | bytes 1622016 | tf_op jit(solution)/shard_map/all_gather | solution.py:336
  387.1 351.0 %all-gather.34.cloned.1.call-start = ((), (), s32[]{:S(2)}) async-start(), calls=%async_computation.25 | async-start | bytes 10485760 | tf_op jit(solution)/shard_map/all_gather | solution.py:352
  391.9 537.7 %reduce-scatter.20.cloned.1.call-start = ((), (), s32[]{:S(2)}) async-start(), calls=%async_computation.26 | async-start | bytes 10485760 | tf_op jit(solution)/shard_map/reduce_scatter | solution.py:361
  786.8 299.8 %all-gather.32.cloned.1.call-start = ((), (), s32[]{:S(2)}) async-start(), calls=%async_computation.23 | async-start | bytes 10485760 | tf_op jit(solution)/shard_map/all_gather | solution.py:351
  936.0 150.6 %copy-start.149 = (bf16[1024,704]{0,1:T(8,128)(2,1)S(1)}, bf16[1024,704]{0,1:T(8,128)(2,1)}, u32[]{:S(2)}) copy-start(bf16[1024,704]{0,1:T(8,128)(2,1)} %all-gather.28.cloned.1.call-done) | copy-start | bytes 4325380
  936.1 300.0 %all-gather.36.cloned.1.call-start = ((), (), s32[]{:S(2)}) async-start(), calls=%async_computation.27 | async-start | bytes 10485760 | tf_op jit(solution)/shard_map/all_gather | solution.py:352
  936.8 490.7 %reduce-scatter.22.cloned.1.call-start = ((), (), s32[]{:S(2)}) async-start(), calls=%async_computation.28 | async-start | bytes 10485760 | tf_op jit(solution)/shard_map/reduce_scatter | solution.py:361
  1099.0 137.0 %copy-start.150 = (bf16[704,1024]{1,0:T(8,128)(2,1)S(1)}, bf16[704,1024]{1,0:T(8,128)(2,1)}, u32[]{:S(2)}) copy-start(bf16[704,1024]{1,0:T(8,128)(2,1)} %all-gather.30.cloned.1.call-done) | copy-start | bytes 4325380
  1284.7 290.3 %reduce-scatter.16.cloned.1.call-start = ((), (), s32[]{:S(2)}) async-start(), calls=%async_computation.22 | async-start | bytes 10485760 | tf_op jit(solution)/shard_map/reduce_scatter | solution.py:358
  1296.6 425.9 %reduce-scatter.18.cloned.1.call-start = ((), (), s32[]{:S(2)}) async-start(), calls=%async_computation.24 | async-start | bytes 10485760 | tf_op jit(solution)/shard_map/reduce_scatter | solution.py:358
  1308.5 870.9 %reduce-scatter.40.cloned.1.call-start = ((), (), s32[]{:S(2)}) async-start(), calls=%async_computation.37 | async-start | bytes 540672
  1332.5 389.9 %copy-start.129 = (f32[1024]{0:T(1024)S(1)}, f32[1024]{0:T(1024)}, u32[]{:S(2)}) copy-start(f32[1024]{0:T(1024)} %get-tuple-element.573) | copy-start | bytes 12292
  1759.4 16.9 copy-start.4
  1759.4 16.9 copy-start.6
  1967.1 213.7 %reduce-scatter.34.cloned.1.call-start = ((), (), s32[]{:S(2)}) async-start(), calls=%async_computation.34 | async-start | bytes 3244032 | tf_op jit(solution)/shard_map/reduce_scatter | solution.py:390
  1979.0 217.9 %reduce-scatter.36.cloned.1.call-start = ((), (), s32[]{:S(2)}) async-start(), calls=%async_computation.35 | async-start | bytes 3244032 | tf_op jit(solution)/shard_map/reduce_scatter | solution.py:391
  2000.8 245.3 %reduce-scatter.38.cloned.1.call-start = ((), (), s32[]{:S(2)}) async-start(), calls=%async_computation.36 | async-start | bytes 3244032 | tf_op jit(solution)/shard_map/reduce_scatter | solution.py:392
  2022.8 364.2 %reduce-scatter.24.cloned.1.call-start = ((), (), s32[]{:S(2)}) async-start(), calls=%async_computation.29 | async-start | bytes 2162688 | tf_op jit(solution)/shard_map/reduce_scatter | solution.py:381
  2030.0 495.9 %reduce-scatter.26.cloned.1.call-start = ((), (), s32[]{:S(2)}) async-start(), calls=%async_computation.30 | async-start | bytes 2162688 | tf_op jit(solution)/shard_map/reduce_scatter | solution.py:382
  2037.4 637.0 %reduce-scatter.32.cloned.1.call-start = ((), (), s32[]{:S(2)}) async-start(), calls=%async_computation.33 | async-start | bytes 4325376 | tf_op jit(solution)/shard_map/reduce_scatter | solution.py:386
  2047.0 776.9 %reduce-scatter.30.cloned.1.call-start = ((), (), s32[]{:S(2)}) async-start(), calls=%async_computation.32 | async-start | bytes 4325376 | tf_op jit(solution)/shard_map/reduce_scatter | solution.py:384
  2060.2 912.8 %reduce-scatter.28.cloned.1.call-start = ((), (), s32[]{:S(2)}) async-start(), calls=%async_computation.31 | async-start | bytes 4325376 | tf_op jit(solution)/shard_map/reduce_scatter | solution.py:383
  2109.7 53.5 %copy-start.57 = (bf16[1024,1024]{1,0:T(8,128)(2,1)S(1)}, bf16[1024,1024]{1,0:T(8,128)(2,1)}, u32[]{:S(2)}) copy-start(bf16[1024,1024]{1,0:T(8,128)(2,1)} %get-tuple-element.547) | copy-start | bytes 6291460
  2109.8 58.0 %copy-start.131 = (f32[1024]{0:T(1024)S(1)}, f32[1024]{0:T(1024)}, u32[]{:S(2)}) copy-start(f32[1024]{0:T(1024)} %get-tuple-element.611) | copy-start | bytes 12292
  (138 other events, 649.1 us)
Sparse Core Ops, SparseCore 0:
  11.0 56.6 all-gather.17
  70.7 52.6 all-gather.15
  126.4 55.5 all-gather.13
  184.8 55.3 all-gather.19
  242.9 55.3 all-gather.21
  300.0 24.1 all-gather.27
  385.7 148.6 all-gather.23
  536.2 23.5 all-gather.25
  561.7 25.2 all-gather.29
  588.4 149.6 all-gather.33
  786.9 142.6 reduce-scatter.19
  936.2 150.3 all-gather.31
  1088.2 147.8 all-gather.35
  1284.8 142.6 reduce-scatter.21
  1429.8 145.1 reduce-scatter.15
  1577.2 145.1 reduce-scatter.17
  1967.2 134.9 reduce-scatter.39
  2106.4 41.5 reduce-scatter.33
  2152.0 44.9 reduce-scatter.35
  2201.1 44.8 reduce-scatter.37
  2248.9 138.0 reduce-scatter.23
  2389.9 135.9 reduce-scatter.25
  2528.8 145.6 reduce-scatter.31
  2677.1 146.7 reduce-scatter.29
  2826.7 146.1 reduce-scatter.27
where the time goes:
time: 2990 us; the launch traced here: 2980 us
  waiting for transfers between devices  1940 us (65%)
  matrix products  457 us (15%)
  other arithmetic  245 us (8%)
  local copies, waits for them, and re-layouts  166 us (6%)
  blocking collectives  151 us (5%)
    all_gather x2, waiting for transfers between devices, body(): lax.all_gather(normed_mid, 'mlp', axis=0, tiled=True)  292 us
    reduce_scatter x2, waiting for transfers between devices, body(): lax.psum_scatter(branch_part.astype(jnp.bfloat16), 'mlp', scatter_dimensi...  290 us
    all_gather x2, waiting for transfers between devices, body(): lax.all_gather(grad_rows, 'mlp', axis=0, tiled=True)  278 us
    reduce_scatter x2, waiting for transfers between devices, body(): lax.psum_scatter(grad_part.astype(jnp.bfloat16), 'mlp', scatter_dimension...  230 us
    reduce_scatter x1, waiting for transfers between devices, body(): lax.psum_scatter(mixer_acc[4], ('rows', 'mlp'), scatter_dimension=0, tile...  149 us
    reduce_scatter x1, waiting for transfers between devices, body(): lax.psum_scatter(mixer_acc[3], ('rows', 'mlp'), scatter_dimension=0, tile...  149 us
    reduce_scatter x1, waiting for transfers between devices, body(): lax.psum_scatter(mixer_acc[6], ('rows', 'mlp'), scatter_dimension=1, tile...  149 us
    dot_general x20, matrix products, product_right(): lax.dot_general(left, right, (((1,), (1,)), ((), ())), preferred_element_...  143 us
  transfers between devices with their start and end apart: 25, of which 18 were waited for; matrix products, arithmetic and copies ran while one was open for 17% of the time, Pallas kernels for 0%

commit v1 on v0

--- a/solution.py
+++ b/solution.py
@@ -6,7 +6,6 @@
 H = 4
 BLOCK = 64
 LEN = 1024
-MB = 2
 HK = 128
 HV = 256
 NC = 16
@@ -164,7 +163,7 @@
     row_count = inputs.shape[0]
     seq_count = row_count // LEN
     val_shape = (seq_count, NC, BLOCK, H, HV)
-    grad_w_output = product_left(stored["mixed_in"], grad_mixed)
+    grad_w_output = product_left(grad_mixed, stored["mixed_in"])
     grad_input = product_right(grad_mixed, w_output).reshape(val_shape)
     gate_pre = stored["gate_pre"]
     gate_sig = jax.nn.sigmoid(gate_pre)
@@ -273,8 +272,8 @@
 
 
 def mlp_pass(rows_in, grad_rows, w_gate, w_up, w_down):
-    gate_proj = product(rows_in, w_gate)
-    up_proj = product(rows_in, w_up)
+    gate_proj = product_right(rows_in, w_gate)
+    up_proj = product_right(rows_in, w_up)
     gate_sig = jax.nn.sigmoid(gate_proj)
     hidden = (gate_proj * gate_sig * up_proj).astype(jnp.bfloat16)
     branch = product(hidden, w_down)
@@ -284,12 +283,59 @@
     grad_gate = (grad_hidden * up_proj * gate_sig * (1.0 + gate_proj * (1.0 - gate_sig))).astype(
         jnp.bfloat16
     )
-    grad_rows_in = product_right(grad_gate, w_gate) + product_right(grad_up, w_up)
+    grad_rows_in = product(grad_gate, w_gate) + product(grad_up, w_up)
     return (
         branch,
         grad_rows_in,
-        (product_left(rows_in, grad_gate), product_left(rows_in, grad_up), grad_w_down),
-    )
+        (product_left(grad_gate, rows_in), product_left(grad_up, rows_in), grad_w_down),
+    )
+
+
+def bits_of(count):
+    return count.bit_length() - 1
+
+
+def halve(grads, dim, bit, count):
+    place = (lax.axis_index("rows") >> bit) & 1
+    send = lax.dynamic_index_in_dim(grads, 1 - place, dim, keepdims=False)
+    keep = lax.dynamic_index_in_dim(grads, place, dim, keepdims=False)
+    pairs = [(i, i ^ (1 << bit)) for i in range(count)]
+    came = lax.ppermute(send.astype(jnp.bfloat16), "rows", pairs)
+    return keep.astype(jnp.float32) + came.astype(jnp.float32)
+
+
+def line_sum(grads, count):
+    me = lax.axis_index("mlp")
+    up = [(i, i + 1) for i in range(count - 1)]
+    down = [(i + 1, i) for i in range(count - 1)]
+
+    def pick(at):
+        return lax.dynamic_index_in_dim(grads, jnp.clip(at, 0, count - 1), 0, keepdims=False).astype(
+            jnp.float32
+        )
+
+    total = pick(me)
+    rising = falling = None
+    for step in range(1, count):
+        send_up = pick(me + count - step)
+        send_down = pick(me - count + step)
+        if rising is not None:
+            send_up = send_up + rising
+            send_down = send_down + falling
+        rising = lax.ppermute(send_up.astype(jnp.bfloat16), "mlp", up).astype(jnp.float32)
+        falling = lax.ppermute(send_down.astype(jnp.bfloat16), "mlp", down).astype(jnp.float32)
+    if rising is not None:
+        total = total + rising + falling
+    return total
+
+
+def reduce_rows(grads, dims, order, count):
+    dims = dict(dims)
+    for bit in order:
+        dim = dims.pop(bit)
+        grads = halve(grads, dim, bit, count)
+        dims = {b: (d - 1 if d > dim else d) for b, d in dims.items()}
+    return grads
 
 
 def body(
@@ -311,104 +357,83 @@
     w_up,
     w_down,
 ):
-    seq_count = doc_lengths.shape[0] // MB
-    rows_each = seq_count * LEN
+    rows = lax.axis_size("rows")
+    mlps = lax.axis_size("mlp")
+    nbits = bits_of(rows)
     small_params = (w_decay, decay_bias, head_gain)
-    outputs = []
-    grad_list = []
-    mixer_acc = None
-    mlp_acc = None
-    small_acc = None
-    for portion in range(MB):
-        mixer_weights = (
-            lax.all_gather(norm_gain_mix, ("rows", "mlp"), axis=0, tiled=True),
-            lax.all_gather(w_query, ("rows", "mlp"), axis=0, tiled=True),
-            lax.all_gather(w_key, ("rows", "mlp"), axis=0, tiled=True),
-            lax.all_gather(w_value, ("rows", "mlp"), axis=0, tiled=True),
-            lax.all_gather(w_outgate, ("rows", "mlp"), axis=0, tiled=True),
-            lax.all_gather(w_rank, ("rows", "mlp"), axis=0, tiled=True),
-            lax.all_gather(w_output, ("rows", "mlp"), axis=1, tiled=True),
-            lax.all_gather(norm_gain_mlp, ("rows", "mlp"), axis=0, tiled=True),
-        )
-        mlp_weights = (
-            lax.all_gather(w_gate, "rows", axis=0, tiled=True),
-            lax.all_gather(w_up, "rows", axis=0, tiled=True),
-            lax.all_gather(w_down, "rows", axis=1, tiled=True),
-        )
-        first_row = portion * rows_each
-        inputs = tokens[first_row : first_row + rows_each].astype(jnp.float32)
-        grad_rows = cotangent[first_row : first_row + rows_each]
-        masking = doc_masks(
-            doc_lengths[portion * seq_count : (portion + 1) * seq_count], LEN, BLOCK
-        )
-        mixer_part = mixer_weights[:7]
-        gain_mlp = mixer_weights[7].astype(jnp.float32)
-        mixed_out, stored = mixer_forward(inputs, masking, mixer_part, small_params)
-        residual = inputs + mixed_out
-        scale_mid = rms_scale(residual)
-        normed_mid = (residual * scale_mid * gain_mlp).astype(jnp.bfloat16)
-        gathered_rows, gathered_grads = (
-            lax.all_gather(normed_mid, "mlp", axis=0, tiled=True),
-            lax.all_gather(grad_rows, "mlp", axis=0, tiled=True),
-        )
-        branch_part, grad_part, mlp_grads = mlp_pass(
-            gathered_rows, gathered_grads, mlp_weights[0], mlp_weights[1], mlp_weights[2]
-        )
-        branch, grad_mid = (
-            lax.psum_scatter(
-                branch_part.astype(jnp.bfloat16), "mlp", scatter_dimension=0, tiled=True
-            ).astype(jnp.float32),
-            lax.psum_scatter(
-                grad_part.astype(jnp.bfloat16), "mlp", scatter_dimension=0, tiled=True
-            ).astype(jnp.float32),
-        )
-        outputs.append((residual + branch).astype(jnp.bfloat16))
-        grad_mid_in, mid_terms = norm_back(grad_mid, residual, scale_mid, gain_mlp)
-        grad_res = grad_rows.astype(jnp.float32) + grad_mid_in
-        grad_inputs, big_grads, small_grads = mixer_backward(
-            grad_res.astype(jnp.bfloat16), inputs, masking, mixer_part, small_params, stored
-        )
-        grad_list.append(grad_res + grad_inputs)
-        big_grads = big_grads + (jnp.sum(mid_terms, axis=0),)
-        if portion == 0:
-            mixer_acc, mlp_acc, small_acc = (big_grads, mlp_grads, small_grads)
-        else:
-            mixer_acc = jax.tree.map(jnp.add, mixer_acc, big_grads)
-            mlp_acc = jax.tree.map(jnp.add, mlp_acc, mlp_grads)
-            small_acc = jax.tree.map(jnp.add, small_acc, small_grads)
-    mixer_shards = (
-        lax.psum_scatter(mixer_acc[0], ("rows", "mlp"), scatter_dimension=0, tiled=True),
-        lax.psum_scatter(mixer_acc[1], ("rows", "mlp"), scatter_dimension=0, tiled=True),
-        lax.psum_scatter(mixer_acc[2], ("rows", "mlp"), scatter_dimension=0, tiled=True),
-        lax.psum_scatter(mixer_acc[3], ("rows", "mlp"), scatter_dimension=0, tiled=True),
-        lax.psum_scatter(mixer_acc[4], ("rows", "mlp"), scatter_dimension=0, tiled=True),
-        lax.psum_scatter(mixer_acc[5], ("rows", "mlp"), scatter_dimension=0, tiled=True),
-        lax.psum_scatter(mixer_acc[6], ("rows", "mlp"), scatter_dimension=1, tiled=True),
-        lax.psum_scatter(mixer_acc[7], ("rows", "mlp"), scatter_dimension=0, tiled=True),
-    )
-    mlp_shards = (
-        lax.psum_scatter(mlp_acc[0], "rows", scatter_dimension=0, tiled=True),
-        lax.psum_scatter(mlp_acc[1], "rows", scatter_dimension=0, tiled=True),
-        lax.psum_scatter(mlp_acc[2], "rows", scatter_dimension=1, tiled=True),
-    )
-    small_acc = lax.psum((small_acc[0], small_acc[1], small_acc[2]), ("rows", "mlp"))
+    shard = w_query.shape[0]
+    pad = jnp.zeros((shard, 110), jnp.bfloat16)
+    mixer_local = jnp.concatenate(
+        [
+            w_query, w_key, w_value, w_outgate, w_output.T,
+            w_rank, norm_gain_mix[:, None], norm_gain_mlp[:, None], pad,
+        ],
+        axis=1,
+    )
+    mixer_all = lax.all_gather(mixer_local, ("rows", "mlp"), axis=0, tiled=True)
+    gain_mix = mixer_all[:, 4112]
+    gain_mlp = mixer_all[:, 4113].astype(jnp.float32)
+    mixer_part = (
+        gain_mix,
+        mixer_all[:, :512],
+        mixer_all[:, 512:1024],
+        mixer_all[:, 1024:2048],
+        mixer_all[:, 2048:3072],
+        mixer_all[:, 4096:4112],
+        mixer_all[:, 3072:4096].T,
+    )
+    mlp_local = jnp.stack([w_gate.T, w_up.T, w_down])
+    mlp_all = lax.all_gather(mlp_local, ("rows", "mlp"), axis=0)
+    hid, wide = mlp_local.shape[1:]
+    mlp_all = mlp_all.reshape(rows, mlps, 3, hid, wide).transpose(2, 1, 3, 0, 4)
+    mlp_all = mlp_all.reshape(3, mlps * hid, rows * wide)
+    inputs = tokens.astype(jnp.float32)
+    masking = doc_masks(doc_lengths, LEN, BLOCK)
+    mixed_out, stored = mixer_forward(inputs, masking, mixer_part, small_params)
+    residual = inputs + mixed_out
+    scale_mid = rms_scale(residual)
+    normed_mid = (residual * scale_mid * gain_mlp).astype(jnp.bfloat16)
+    branch, grad_mid, mlp_grads = mlp_pass(normed_mid, cotangent, mlp_all[0], mlp_all[1], mlp_all[2])
+    block_out = (residual + branch).astype(jnp.bfloat16)
+    mlp_grads = jnp.stack(mlp_grads).reshape((3, mlps, hid) + (2,) * nbits + (wide,))
+    dims = {nbits - 1 - i: 3 + i for i in range(nbits)}
+    mlp_grads = reduce_rows(mlp_grads, dims, range(nbits), rows)
+    mlp_grads = line_sum(mlp_grads.transpose(1, 0, 2, 3), mlps)
+    grad_mid_in, mid_terms = norm_back(grad_mid, residual, scale_mid, gain_mlp)
+    grad_res = cotangent.astype(jnp.float32) + grad_mid_in
+    grad_inputs, big_grads, small_grads = mixer_backward(
+        grad_res.astype(jnp.bfloat16), inputs, masking, mixer_part, small_params, stored
+    )
+    grad_tokens = grad_res + grad_inputs
+    big_grads = jnp.concatenate(
+        [
+            big_grads[1], big_grads[2], big_grads[3], big_grads[4], big_grads[6],
+            big_grads[5], big_grads[0][:, None], jnp.sum(mid_terms, axis=0)[:, None],
+            jnp.zeros((rows * mlps * shard, 110), jnp.float32),
+        ],
+        axis=1,
+    )
+    big_grads = big_grads.reshape((2,) * nbits + (mlps, shard, 4224))
+    dims = {nbits - 1 - i: i for i in range(nbits)}
+    big_grads = line_sum(reduce_rows(big_grads, dims, range(nbits), rows), mlps)
+    small_acc = lax.psum(small_grads, ("rows", "mlp"))
     return (
-        jnp.concatenate(outputs, axis=0),
-        jnp.concatenate(grad_list, axis=0),
-        mixer_shards[0],
-        mixer_shards[1],
-        mixer_shards[2],
-        mixer_shards[3],
-        mixer_shards[4],
-        mixer_shards[5],
+        block_out,
+        grad_tokens,
+        big_grads[:, 4112],
+        big_grads[:, :512],
+        big_grads[:, 512:1024],
+        big_grads[:, 1024:2048],
+        big_grads[:, 2048:3072],
+        big_grads[:, 4096:4112],
         small_acc[0],
         small_acc[1],
         small_acc[2],
-        mixer_shards[6],
-        mixer_shards[7],
-        mlp_shards[0],
-        mlp_shards[1],
-        mlp_shards[2],
+        big_grads[:, 3072:4096].T,
+        big_grads[:, 4113],
+        mlp_grads[0].T,
+        mlp_grads[1].T,
+        mlp_grads[2],
     )
 
 

time: 2990 us -> 1350 us (0.45)
  waiting for transfers between devices: 1940 us -> 227 us
  local copies, waits for them, and re-layouts: 166 us -> 366 us
  blocking collectives: 151 us -> 41.1 us
  matrix products: 457 us -> 417 us
  starting transfers between devices: 2.01 us -> 39.8 us
    reduce_scatter x12 -> x0, waiting for transfers between devices: 1310 us -> none  [the longest x2 290 us: body(): lax.psum_scatter(branch_part.astype(jnp.bfloat16), 'mlp', scatter_dimensi...]
    all_gather x12 -> x2, waiting for transfers between devices: 622 us -> 59.7 us  [the longest x1 59.7 us: body(): mixer_all = lax.all_gather(mixer_local, ('rows', 'mlp'), axis=0, tiled=True)]
    ppermute x0 -> x18, waiting for transfers between devices: none -> 167 us  [the longest x6 141 us: halve(): came = lax.ppermute(send.astype(jnp.bfloat16), 'rows', pairs)]
    unnamed x2 -> x0, blocking collectives: 84.1 us -> none
    all_gather x1 -> x0, blocking collectives: 67.1 us -> none  [body(): lax.all_gather(w_rank, ('rows', 'mlp'), axis=0, tiled=True)]
    unnamed x339 -> x218, local copies, waits for them, and re-layouts: 37.1 us -> 92.4 us
    another operation x6, local copies, waits for them, and re-layouts: 23.5 us -> 74.1 us  [the longest x4 58.3 us: body(): jnp.stack(mlp_grads).reshape((3, mlps, hid) + (2,) * nbits + (wide,))]
    psum x0 -> x1, blocking collectives: none -> 41.1 us  [body(): small_acc = lax.psum(small_grads, ('rows', 'mlp'))]
  transfers between devices with their start and end apart: 25 -> 20, of which waited for: 18 -> 8; matrix products, arithmetic and copies ran while one was open for 17% -> 32% of each run, Pallas kernels for 0% -> 0%
where the time goes in v1:
time: 1350 us; the launch traced here: 1340 us
  matrix products  417 us (31%)
  local copies, waits for them, and re-layouts  366 us (27%)
  other arithmetic  231 us (17%)
  waiting for transfers between devices  227 us (17%)
  blocking collectives  41.1 us (3%)
  starting transfers between devices  39.8 us (3%)
  between operations  15.9 us (1%)
    ppermute x6, waiting for transfers between devices, halve(): came = lax.ppermute(send.astype(jnp.bfloat16), 'rows', pairs)  141 us
    dot_general x10, matrix products, product_right(): lax.dot_general(left, right, (((1,), (1,)), ((), ())), preferred_element_...  126 us
    dot_general x10, matrix products, product(): return jnp.dot(left, right, preferred_element_type=jnp.float32)  108 us
    unnamed x218, local copies, waits for them, and re-layouts  92.4 us
    dot_general x10, matrix products, product_left(): lax.dot_general(left, right, (((0,), (0,)), ((), ())), preferred_element_...  89.7 us
    all_gather x1, waiting for transfers between devices, body(): mixer_all = lax.all_gather(mixer_local, ('rows', 'mlp'), axis=0, tiled=True)  59.7 us
    another operation x4, local copies, waits for them, and re-layouts, body(): jnp.stack(mlp_grads).reshape((3, mlps, hid) + (2,) * nbits + (wide,))  58.3 us
    psum x1, blocking collectives, body(): small_acc = lax.psum(small_grads, ('rows', 'mlp'))  41.1 us
  transfers between devices with their start and end apart: 20, of which 8 were waited for; matrix products, arithmetic and copies ran while one was open for 32% of the time, Pallas kernels for 0%

profile of v1, /device:TPU:0, one launch (start us, length us, event | category | flops | bytes accessed | tf_op | source)
XLA Modules:
  0.0 1337.7 jit_solution(11857230648367102074)
XLA Ops:
  33.0 59.7 %all-gather.4.cloned.1.call-done = bf16[1024,4224]{1,0:T(8,128)(2,1)} async-done(((bf16[32,4224]{1,0:T(8,128)(2,1)}), bf16[1024,4224]{1,0:T(8,128)(2,1)}) %all-gather.4.cloned.1.call-update) | async-done | bytes 8650768 | tf_op jit(solution)/shard_map/all_gather | solution.py:373
  140.5 9.5 convolution_convert_fusion
  150.0 8.2 reshape.253
  159.2 10.8 fusion.114
  170.1 10.6 reshape.256
  205.1 8.0 broadcast.185.clone
  213.0 42.2 %while.30 = (s32[]{:T(128)}, f32[2,4,128,256]{3,2,1,0:T(8,128)S(1)}, f32[16,2,4,128,256]{4,3,2,1,0:T(8,128)}, f32[16,2,4,128]{3,2,1,0:T(4,128)S(1)}, f32[16,2,4,128,256]{4,3,2,0,1:T(8,128)}, /*index=5*/s32[]{:T(128)}, s32[]{:T(128)}) while((s32[]{:T(128)}, f32[2,4,128,256]{3,2,1,0:T(8,128)S(1)}, f32[16,2,4,128,256]{4,3,2,1,0:T(8,128)}, ...), condition=%wide.region_5.6_spmd.clone, body=%wide.region_4.5_spmd.clone.sunk | while | flops 1048579 | bytes 5255276 | solution.py:109
  255.3 13.7 %fusion.16 = (f32[2,16,64,4]{2,3,1,0:T(4,128)S(1)}, f32[2,16,4,256,64]{3,4,2,1,0:T(8,128)}) fusion(f32[2,16,4,256,64]{3,4,2,1,0:T(8,128)} %fusion.88, f32[2,16,64]{2,1,0:T(8,128)S(1)} %get-tuple-element.388, bf16[2,16,64,4,128]{4,2,3,1,0:T(8,128)(2,1)S(1)} %get-tuple-element.372, f32[16,2,4,128,256]{4,3,2,1,0:T(8,128)} %get-tuple-element.146), kind=kOutput, calls=%fused_computation.49 | convolution fusion | flops 549445632 | bytes 35692544 | tf_op jit(solution)/shard_map/pntha,pnhab->pnthb/dot_general | solution.py:119
  306.9 25.6 %copy.452 = bf16[8,4,3,704,128]{4,0,3,1,2:T(8,128)(2,1)S(1)} copy(bf16[8,4,3,704,128]{4,3,2,1,0:T(8,128)(2,1)} %bitcast.365) | data formatting | bytes 34603008 | tf_op jit(solution)/shard_map/reshape | solution.py:388
  335.9 20.0 %fusion.33 = f32[2816,2048]{0,1:T(8,128)} fusion(bf16[2048,1024]{1,0:T(8,128)(2,1)} %param.23, bf16[352,8,8,128]{3,2,1,0:T(8,128)(2,1)S(1)} %bitcast.369), kind=kOutput, calls=%fused_computation.83 | convolution fusion | flops 11811160064 | bytes 33030144 | tf_op jit(solution)/shard_map/dot_general | solution.py:40
  356.0 18.3 %fusion.43 = f32[2048,2816]{1,0:T(8,128)} fusion(bf16[2048,1024]{0,1:T(8,128)(2,1)} %multiply_convert_fusion.2, bf16[352,8,8,128]{3,2,1,0:T(8,128)(2,1)S(1)} %bitcast.371), kind=kOutput, calls=%fused_computation.93 | convolution fusion | flops 11811160064 | bytes 33030144 | tf_op jit(solution)/shard_map/dot_general | solution.py:40
  374.2 38.0 %fusion.3 = (bf16[2048,2816]{1,0:T(8,128)(2,1)}, bf16[2048,2816]{1,0:T(8,128)(2,1)}, bf16[2048,2816]{1,0:T(8,128)(2,1)}) fusion(f32[2816,2048]{0,1:T(8,128)} %fusion.33, f32[2048,2816]{1,0:T(8,128)} %fusion.43, bf16[2048,1024]{0,1:T(8,128)(2,1)} %multiply_convert_fusion.2, bf16[352,8,8,128]{3,2,1,0:T(8,128)(2,1)} %bitcast.373), kind=kOutput, calls=%fused_computation.11 | convolution fusion | flops 11903434752 | bytes 90701824 | tf_op jit(solution)/shard_map/dot_general | solution.py:40
  412.3 18.8 %fusion.37 = f32[2048,1024]{0,1:T(8,128)} fusion(bf16[2048,2816]{1,0:T(8,128)(2,1)} %get-tuple-element.355, bf16[352,8,8,128]{3,2,1,0:T(8,128)(2,1)} %bitcast.374), kind=kOutput, calls=%fused_computation.87 | convolution fusion | flops 11811160064 | bytes 25690112 | tf_op jit(solution)/shard_map/dot_general | solution.py:30
  431.1 22.3 %multiply_reduce_fusion.1 = (f32[1024]{0:T(1024)}, f32[2048]{0:T(1024)S(1)}, f32[2048,1024]{0,1:T(8,128)}) fusion(f32[2048,1024]{0,1:T(8,128)} %copy-done.12, f32[2048]{0:T(1024)S(1)} %copy-done.63, f32[1024]{0:T(1024)S(1)} %copy-done.74, f32[2048,1024]{0,1:T(8,128)} %fusion.37, bf16[2048,2816]{1,0:T(8,128)(2,1)} %get-tuple-element.354, ...), kind=kOutput, calls=%fused_computation.57 | convolution fusion | flops 11825837056 | bytes 42491904 | tf_op jit(solution)/shard_map/dot_general | solution.py:30
  460.9 8.3 fusion.109
  469.2 10.6 reshape.258
  479.8 14.4 %fusion.23 = (f32[256]{0:T(256)}, f32[2,16,64,4]{2,3,1,0:T(4,128)S(1)}, f32[2,16,64,4,256]{4,2,3,1,0:T(8,128)S(1)}, bf16[2,16,64,4,256]{4,2,3,1,0:T(8,128)(2,1)}) fusion(f32[2,16,4,256,64]{3,4,2,1,0:T(8,128)} %get-tuple-element.396, f32[2,16,64,4]{2,3,1,0:T(4,128)S(1)} %copy-done.51, f32[256]{0:T(256)S(1)} %copy-done.81, ...), kind=kLoop, calls=%fused_computation.56 | loop fusion | flops 41934592 | bytes 37816320 | tf_op jit(solution)/shard_map/reduce_sum | solution.py:180
  494.3 9.6 fusion.20
  517.7 11.2 convolution_bitcast_fusion
  536.7 53.6 %while.31 = (s32[]{:T(128)}, f32[2,4,128,256]{3,2,1,0:T(8,128)S(1)}, f32[16,2,4,128,256]{4,3,2,1,0:T(8,128)}, f32[16,2,4,128,256]{4,3,2,0,1:T(8,128)}, f32[16,2,...) while((s32[]{:T(128)}, f32[2,4,128,256]{3,2,1,0:T(8,128)S(1)}, ...), condition=%wide.region_11.12_spmd.clone, body=%wide.region_10.11_spmd.clone.sunk | while | flops 1572868 | bytes 6303872 | solution.py:210
  590.3 20.9 %multiply_reduce_fusion = (f32[16,2,4,128]{3,2,1,0:T(4,128)S(1)}, bf16[2,16,4,128,256]{4,3,2,0,1:T(8,128)(2,1)}) fusion(f32[16,2,4,128,256]{4,3,2,1,0:T(8,128)} %get-tuple-element.147, f32[16,2,4,128,256]{4,3,2,1,0:T(8,128)} %get-tuple-element.146), kind=kLoop, calls=%fused_computation.25 | loop fusion | flops 12566528 | bytes 42008576 | tf_op jit(solution)/shard_map/reduce_sum | solution.py:226
  611.2 9.8 fusion.27
  621.0 8.1 fusion.25
  629.1 17.9 %fusion.158 = f32[2816,1024]{1,0:T(8,128)} fusion(bf16[2048,2816]{1,0:T(8,128)(2,1)} %get-tuple-element.354, bf16[2048,1024]{0,1:T(8,128)(2,1)S(1)} %copy-done.43), kind=kOutput, calls=%fused_computation.268 | convolution fusion | flops 11811160064 | bytes 27262976 | tf_op jit(solution)/shard_map/dot_general | solution.py:34
  647.0 18.9 %fusion.159 = f32[2816,1024]{1,0:T(8,128)} fusion(bf16[2048,2816]{1,0:T(8,128)(2,1)} %get-tuple-element.355, bf16[2048,1024]{0,1:T(8,128)(2,1)} %multiply_convert_fusion.2), kind=kOutput, calls=%fused_computation.269 | convolution fusion | flops 11811160064 | bytes 27262976 | tf_op jit(solution)/shard_map/dot_general | solution.py:34
  670.7 12.1 fusion.69
  806.8 16.1 %fusion.15 = (f32[1024]{0:T(1024)S(1)}, f32[2048]{0:T(1024)S(1)}, f32[2048,1024]{0,1:T(8,128)}) fusion(bf16[2048,1024]{0,1:T(8,128)(2,1)S(1)} %copy-done.5, f32[2048]{0:T(1024)S(1)} %copy-done.60, f32[1024]{0:T(1024)S(1)} %copy-done.71, bf16[2048,16]{0,1:T(8,128)(2,1)S(1)} %convolution_convert_fusion.1, ...), kind=kOutput, calls=%fused_computation.43 | convolution fusion | flops 90174464 | bytes 46489600 | tf_op jit(solution)/shard_map/dot_general | solution.py:40
  823.6 10.0 fusion.60
  833.6 19.0 %concatenate.22 = f32[2,2,2,4,32,4224]{5,4,3,2,1,0:T(8,128)} concatenate(f32[2,2,2,4,32,512]{5,4,3,2,1,0:T(8,128)} %fusion.100, f32[2,2,2,4,32,512]{5,4,3,2,1,0:T(8,128)} %fusion.98, f32[2,2,2,4,32,1024]{5,4,3,2,1,0:T(8,128)} %fusion.64, f32[2,2,2,4,32,1024]{5,4,3,2,1,0:T(8,128)} %fusion.62, f32[2,2,2,4,32,1024]{5,4,3,2,1,0:T(8,128)} %fusion.60, ...), dimensions={5} | concatenate | bytes 34603008 | tf_op jit(solution)/shard_map/concatenate | solution.py:408
  859.0 15.9 %stack.28 = f32[1,4,704,2,2,2,128]{6,5,4,3,2,1,0:T(2,128)} reshape(f32[2816,1024]{1,0:T(8,128)} %fusion.158) | data formatting | bytes 23068672 | tf_op jit(solution)/shard_map/stack | solution.py:398
  874.9 10.7 copy_dynamic-update-slice_fusion.2
  885.6 15.8 %stack.29 = f32[1,4,704,2,2,2,128]{6,5,4,3,2,1,0:T(2,128)} reshape(f32[2816,1024]{1,0:T(8,128)} %fusion.159) | data formatting | bytes 23068672 | tf_op jit(solution)/shard_map/stack | solution.py:398
  901.4 18.8 %fusion.160 = f32[2816,1024]{1,0:T(8,128)} fusion(bf16[2048,2816]{1,0:T(8,128)(2,1)} %get-tuple-element.356, bf16[2048,1024]{1,0:T(8,128)(2,1)} %param.23), kind=kOutput, calls=%fused_computation.270 | convolution fusion | flops 11811160064 | bytes 27262976 | tf_op jit(solution)/shard_map/dot_general | solution.py:34
  920.2 15.9 %stack.30 = f32[1,4,704,2,2,2,128]{6,5,4,3,2,1,0:T(2,128)} reshape(f32[2816,1024]{1,0:T(8,128)} %fusion.160) | data formatting | bytes 23068672 | tf_op jit(solution)/shard_map/stack | solution.py:398
  936.1 10.7 copy_dynamic-update-slice_fusion.1
  946.8 10.7 copy_dynamic-update-slice_fusion
  957.5 9.3 fusion.6
  977.8 48.0 %collective-permute-done.1 = bf16[2,4,32,4224]{3,2,1,0:T(8,128)(2,1)} collective-permute-done((bf16[2,4,32,4224]{3,2,1,0:T(8,128)(2,1)S(1)}, bf16[2,4,32,4224]{3,2,1,0:T(8,128)(2,1)}, u32[]{:S(2)}, u32[]{:S(2)}) %collective-permute-start.1) | collective-permute-done | bytes 2162720 | tf_op jit(solution)/shard_map/ppermute | solution.py:303
  1031.1 9.1 bitcast_add_fusion.2
  1050.3 19.6 %add_convert_fusion.1 = bf16[2048,1024]{0,1:T(8,128)(2,1)} fusion(f32[2048,1024]{0,1:T(8,128)} %copy-done.12, bf16[2048,2816]{1,0:T(8,128)(2,1)} %get-tuple-element.356, bf16[352,8,8,128]{3,2,1,0:T(8,128)(2,1)} %bitcast.370), kind=kOutput, calls=%fused_computation.64 | convolution fusion | flops 11815354368 | bytes 29884416 | tf_op jit(solution)/shard_map/dot_general | solution.py:30
  1078.2 65.8 %collective-permute-done.10 = bf16[3,4,704,2,128]{4,2,0,1,3:T(8,128)(2,1)} collective-permute-done((bf16[3,4,704,2,128]{4,2,0,1,3:T(8,128)(2,1)}, bf16[3,4,704,2,128]{4,2,0,1,3:T(8,128)(2,1)}, u32[]{:S(2)}, u32[]{:S(2)}) %collective-permute-start.10) | collective-permute-done | bytes 4325408 | tf_op jit(solution)/shard_map/ppermute | solution.py:303
  1144.1 9.4 bitcast_add_fusion.3
  1159.2 11.9 fusion.12
  1178.3 27.3 %collective-permute-done.11 = bf16[3,4,704,128]{3,2,0,1:T(8,128)(2,1)} collective-permute-done((bf16[3,4,704,128]{3,2,0,1:T(8,128)(2,1)}, bf16[3,4,704,128]{3,2,0,1:T(8,128)(2,1)}, u32[]{:S(2)}, u32[]{:S(2)}) %collective-permute-start.11) | collective-permute-done | bytes 2162720 | tf_op jit(solution)/shard_map/ppermute | solution.py:303
  1225.4 9.3 copy.304
  1234.7 41.1 %all-reduce.1 = (f32[16,512]{1,0:T(8,128)}, f32[512]{0:T(512)}, f32[256]{0:T(256)}) all-reduce(f32[16,512]{1,0:T(8,128)S(1)} %fusion.157, f32[512]{0:T(512)S(1)} %copy-done.84, f32[256]{0:T(256)S(1)} %copy-done.87), channel_id=1, replica_groups=mesh['rows'=8,'mlp'=4] {'rows','mlp'}, use_global_device_ids=true, to_apply=%region_18.19 | all-reduce | flops 8960 | bytes 71680 | tf_op jit(solution)/shard_map/psum | solution.py:419
  1287.4 8.3 collective-permute-done.15
  1318.3 9.6 collective-permute-done.17
  (476 shorter events, 503.3 us)
Async XLA Ops:
  7.2 106.1 %copy-start = (bf16[16,512]{1,0:T(8,128)(2,1)S(1)}, bf16[16,512]{1,0:T(8,128)(2,1)}, u32[]{:S(2)}) copy-start(bf16[16,512]{1,0:T(8,128)(2,1)} %param.30) | copy-start | bytes 49156
  7.2 85.5 %all-gather.4.cloned.1.call-start = ((), (), s32[]{:S(2)}) async-start(), calls=%async_computation | async-start | bytes 8921088 | tf_op jit(solution)/shard_map/all_gather | solution.py:373
  11.3 295.6 %all-gather.6.cloned.1.call-start = ((), (), s32[]{:S(2)}) async-start(), calls=%async_computation.1 | async-start | bytes 17842176 | tf_op jit(solution)/shard_map/all_gather | solution.py:386
  19.8 93.4 %copy-start.85 = (f32[512]{0:T(512)}, f32[512]{0:T(512)S(1)}, u32[]{:S(2)}) copy-start(f32[512]{0:T(512)S(1)} %convert_element_type.351) | copy-start | bytes 6148
  20.4 248.7 %copy-start.80 = (f32[256]{0:T(256)}, f32[256]{0:T(256)S(1)}, u32[]{:S(2)}) copy-start(f32[256]{0:T(256)S(1)} %convert_element_type.364) | copy-start | bytes 3076
  27.3 131.0 %copy-start.82 = (f32[2,16]{1,0:T(2,128)}, f32[2,16]{1,0:T(2,128)S(1)}, u32[]{:S(2)}) copy-start(f32[2,16]{1,0:T(2,128)S(1)} %compare_convert_fusion.3) | copy-start | bytes 388
  31.0 66.3 %copy-start.59 = (f32[2048]{0:T(1024)}, f32[2048]{0:T(1024)S(1)}, u32[]{:S(2)}) copy-start(f32[2048]{0:T(1024)S(1)} %get-tuple-element.390) | copy-start | bytes 24580
  31.7 165.9 %copy-start.78 = (bf16[2,16,64]{2,1,0:T(8,128)(2,1)}, bf16[2,16,64]{2,1,0:T(8,128)(2,1)S(1)}, u32[]{:S(2)}) copy-start(bf16[2,16,64]{2,1,0:T(8,128)(2,1)S(1)} %get-tuple-element.352) | copy-start | bytes 12292
  94.1 207.5 %copy-start.73 = (f32[1024]{0:T(1024)}, f32[1024]{0:T(1024)S(1)}, u32[]{:S(2)}) copy-start(f32[1024]{0:T(1024)S(1)} %get-tuple-element.320) | copy-start | bytes 12292
  129.5 51.1 %copy-start.52 = (f32[2,16,4,128]{3,2,1,0:T(4,128)}, f32[2,16,4,128]{3,2,1,0:T(4,128)S(1)}, u32[]{:S(2)}) copy-start(f32[2,16,4,128]{3,2,1,0:T(4,128)S(1)} %copy.259) | copy-start | bytes 196612
  188.4 66.9 %copy-start.17 = (bf16[2,16,64,4,128]{4,2,3,1,0:T(8,128)(2,1)}, bf16[2,16,64,4,128]{4,2,3,1,0:T(8,128)(2,1)S(1)}, u32[]{:S(2)}) copy-start(bf16[2,16,64,4,128]{4,2,3,1,0:T(8,128)(2,1)S(1)} %get-tuple-element.372) | copy-start | bytes 6291460
  335.9 20.0 %copy-start.40 = (bf16[1,4,704,8,128]{4,3,2,1,0:T(8,128)(2,1)}, bf16[1,4,704,8,128]{4,3,2,1,0:T(8,128)(2,1)S(1)}, u32[]{:S(2)}) copy-start(bf16[1,4,704,8,128]{4,3,2,1,0:T(8,128)(2,1)S(1)} %get-tuple-element.358) | copy-start | bytes 17301508
  335.9 20.0 %copy-start.41 = (bf16[1,4,704,8,128]{4,3,2,1,0:T(8,128)(2,1)}, bf16[1,4,704,8,128]{4,3,2,1,0:T(8,128)(2,1)S(1)}, u32[]{:S(2)}) copy-start(bf16[1,4,704,8,128]{4,3,2,1,0:T(8,128)(2,1)S(1)} %get-tuple-element.360) | copy-start | bytes 17301508
  412.2 18.8 %copy-start.63 = (f32[2048]{0:T(1024)S(1)}, f32[2048]{0:T(1024)}, u32[]{:S(2)}) copy-start(f32[2048]{0:T(1024)} %copy-done.62) | copy-start | bytes 24580
  412.2 18.8 %copy-start.74 = (f32[1024]{0:T(1024)S(1)}, f32[1024]{0:T(1024)}, u32[]{:S(2)}) copy-start(f32[1024]{0:T(1024)} %copy-done.73) | copy-start | bytes 12292
  431.1 22.4 %slice-start.4 = ((s8[8388608]{0:T(1024)(128)(4,1)}), s8[4194304]{0:T(1024)(128)(4,1)S(1)}, s32[]{:S(2)}) async-start(s8[8388608]{0:T(1024)(128)(4,1)} %bitcast.353), calls=%async_computation.6 | async-start | bytes 8388608
  431.1 22.4 %slice-start.5 = ((s8[8388608]{0:T(1024)(128)(4,1)}), s8[4194304]{0:T(1024)(128)(4,1)S(1)}, s32[]{:S(2)}) async-start(s8[8388608]{0:T(1024)(128)(4,1)} %bitcast.353), calls=%async_computation.7 | async-start | bytes 8388608
  431.1 22.4 %copy-start.19 = (bf16[2048,1024]{0,1:T(8,128)(2,1)S(1)}, bf16[2048,1024]{0,1:T(8,128)(2,1)}, u32[]{:S(2)}) copy-start(bf16[2048,1024]{0,1:T(8,128)(2,1)} %copy.271) | copy-start | bytes 12582916
  431.1 22.4 %copy-start.65 = (f32[2048]{0:T(1024)S(1)}, f32[2048]{0:T(1024)}, u32[]{:S(2)}) copy-start(f32[2048]{0:T(1024)} %get-tuple-element.391) | copy-start | bytes 24580
  494.3 16.0 %slice-start = ((s8[16777216]{0:T(1024)(128)(4,1)}), s8[4194304]{0:T(1024)(128)(4,1)S(1)}, s32[]{:S(2)}) async-start(s8[16777216]{0:T(1024)(128)(4,1)} %bitcast.351), calls=%async_computation.2 | async-start | bytes 8388608
  494.3 16.0 %slice-start.1 = ((s8[16777216]{0:T(1024)(128)(4,1)}), s8[4194304]{0:T(1024)(128)(4,1)S(1)}, s32[]{:S(2)}) async-start(s8[16777216]{0:T(1024)(128)(4,1)} %bitcast.351), calls=%async_computation.3 | async-start | bytes 8388608
  590.3 20.9 %copy-start.79 = (bf16[2,16,64]{2,1,0:T(8,128)(2,1)S(1)}, bf16[2,16,64]{2,1,0:T(8,128)(2,1)}, u32[]{:S(2)}) copy-start(bf16[2,16,64]{2,1,0:T(8,128)(2,1)} %copy-done.78) | copy-start | bytes 12292
  646.9 18.9 %copy-start.3 = (f32[2,16,64,4,128]{4,1,2,3,0:T(8,128)S(1)}, f32[2,16,64,4,128]{4,1,2,3,0:T(8,128)}, u32[]{:S(2)}) copy-start(f32[2,16,64,4,128]{4,1,2,3,0:T(8,128)} %copy-done.1) | copy-start | bytes 12582916
  647.0 18.9 %copy-start.8 = (f32[2,16,64,4,128]{4,3,2,1,0:T(4,128)S(1)}, f32[2,16,64,4,128]{4,3,2,1,0:T(4,128)}, u32[]{:S(2)}) copy-start(f32[2,16,64,4,128]{4,3,2,1,0:T(4,128)} %reshape.255) | copy-start | bytes 12582916
  647.0 18.9 %copy-start.27 = (bf16[2,16,4,64,64]{4,3,2,1,0:T(8,128)(2,1)S(1)}, bf16[2,16,4,64,64]{4,3,2,1,0:T(8,128)(2,1)}, u32[]{:S(2)}) copy-start(bf16[2,16,4,64,64]{4,3,2,1,0:T(8,128)(2,1)} %multiply_convert_fusion.4) | copy-start | bytes 3145732
  647.0 18.9 %copy-start.31 = (f32[2,16,4,128,64]{3,4,2,1,0:T(8,128)S(1)}, f32[2,16,4,128,64]{3,4,2,1,0:T(8,128)}, u32[]{:S(2)}) copy-start(f32[2,16,4,128,64]{3,4,2,1,0:T(8,128)} %fusion.29) | copy-start | bytes 12582916
  806.8 16.5 %copy-start.88 = (f32[1024]{0:T(1024)S(1)}, f32[1024]{0:T(1024)}, u32[]{:S(2)}) copy-start(f32[1024]{0:T(1024)} %get-tuple-element.316) | copy-start | bytes 12292
  858.6 108.3 %collective-permute-start = (bf16[2,2,4,32,4224]{4,3,2,1,0:T(8,128)(2,1)}, bf16[2,2,4,32,4224]{4,3,2,1,0:T(8,128)(2,1)}, u32[]{:S(2)}, u32[]{:S(2)}) collective-permute-start(bf16[2,2,4,32,4224]{4,3,2,1,0:T(8,128)(2,1)} %fusion.54), channel_id=1, source_target_pairs={{0,4},{4,0},{8,12},{12,8},{16,20},{20,16},{24,28},{28,24},{1,5},{5... | collective-permute-start | bytes 12976136 | tf_op jit(solution)/shard_map/ppermute | solution.py:303
  966.8 64.2 %collective-permute-start.9 = (bf16[3,4,704,2,2,128]{5,2,0,1,3,4:T(8,128)(2,1)}, bf16[3,4,704,2,2,128]{5,2,0,1,3,4:T(8,128)(2,1)}, u32[]{:S(2)}, u32[]{:S(2)}) collective-permute-start(bf16[3,4,704,2,2,128]{5,2,0,1,3,4:T(8,128)(2,1)} %fusion.6), channel_id=1, source_target_pairs={{0,4},{4,0},{8,12},{12,8},{16,20},{20,16},{24,28},{28,24},{1,5},{5... | collective-permute-start | bytes 25952264 | tf_op jit(solution)/shard_map/ppermute | solution.py:303
  976.3 49.5 %collective-permute-start.1 = (bf16[2,4,32,4224]{3,2,1,0:T(8,128)(2,1)S(1)}, bf16[2,4,32,4224]{3,2,1,0:T(8,128)(2,1)}, u32[]{:S(2)}, u32[]{:S(2)}) collective-permute-start(bf16[2,4,32,4224]{3,2,1,0:T(8,128)(2,1)S(1)} %fusion.90), channel_id=1, source_target_pairs={{0,8},{4,12},{8,0},{12,4},{16,24},{20,28},{24,16},{28,20},{1,9},{5... | collective-permute-start | bytes 6488072 | tf_op jit(solution)/shard_map/ppermute | solution.py:303
  1029.2 40.7 %collective-permute-start.2 = (bf16[4,32,4224]{2,1,0:T(8,128)(2,1)S(1)}, bf16[4,32,4224]{2,1,0:T(8,128)(2,1)S(1)}, u32[]{:S(2)}, u32[]{:S(2)}) collective-permute-start(bf16[4,32,4224]{2,1,0:T(8,128)(2,1)S(1)} %fusion.120), channel_id=1, source_target_pairs={{0,16},{4,20},{8,24},{12,28},{16,0},{20,4},{24,8},{28,12},{1,17},{... | collective-permute-start | bytes 3244040 | tf_op jit(solution)/shard_map/ppermute | solution.py:303
  1048.9 95.2 %collective-permute-start.10 = (bf16[3,4,704,2,128]{4,2,0,1,3:T(8,128)(2,1)}, bf16[3,4,704,2,128]{4,2,0,1,3:T(8,128)(2,1)}, u32[]{:S(2)}, u32[]{:S(2)}) collective-permute-start(bf16[3,4,704,2,128]{4,2,0,1,3:T(8,128)(2,1)} %fusion.55), channel_id=1, source_target_pairs={{0,8},{4,12},{8,0},{12,4},{16,24},{20,28},{24,16},{28,20},{1,9},{5... | collective-permute-start | bytes 12976136 | tf_op jit(solution)/shard_map/ppermute | solution.py:303
  1073.8 85.3 %slice-start.6 = ((s8[8388608]{0:T(1024)(128)(4,1)}), s8[4194304]{0:T(1024)(128)(4,1)S(1)}, s32[]{:S(2)}) async-start(s8[8388608]{0:T(1024)(128)(4,1)} %bitcast.355), calls=%async_computation.8 | async-start | bytes 8388608
  1073.8 85.3 %slice-start.7 = ((s8[8388608]{0:T(1024)(128)(4,1)}), s8[4194304]{0:T(1024)(128)(4,1)S(1)}, s32[]{:S(2)}) async-start(s8[8388608]{0:T(1024)(128)(4,1)} %bitcast.355), calls=%async_computation.9 | async-start | bytes 8388608
  1073.8 98.6 %collective-permute-start.3 = (bf16[32,4224]{1,0:T(8,128)(2,1)}, bf16[32,4224]{1,0:T(8,128)(2,1)}, u32[]{:S(2)}, u32[]{:S(2)}) collective-permute-start(bf16[32,4224]{1,0:T(8,128)(2,1)} %get-tuple-element.375), channel_id=1, source_target_pairs={{0,1},{1,2},{2,3},{4,5},{5,6},{6,7},{8,9},{9,10},{10,11},{12,13},{... | collective-permute-start | bytes 811016 | tf_op jit(solution)/shard_map/ppermute | solution.py:325
  1157.7 47.9 %collective-permute-start.11 = (bf16[3,4,704,128]{3,2,0,1:T(8,128)(2,1)}, bf16[3,4,704,128]{3,2,0,1:T(8,128)(2,1)}, u32[]{:S(2)}, u32[]{:S(2)}) collective-permute-start(bf16[3,4,704,128]{3,2,0,1:T(8,128)(2,1)} %fusion.91), channel_id=1, source_target_pairs={{0,16},{4,20},{8,24},{12,28},{16,0},{20,4},{24,8},{28,12},{1,17},{... | collective-permute-start | bytes 6488072 | tf_op jit(solution)/shard_map/ppermute | solution.py:303
  1171.1 45.0 %collective-permute-start.6 = (bf16[32,4224]{1,0:T(8,128)(2,1)S(1)}, bf16[32,4224]{1,0:T(8,128)(2,1)S(1)}, u32[]{:S(2)}, u32[]{:S(2)}) collective-permute-start(bf16[32,4224]{1,0:T(8,128)(2,1)S(1)} %get-tuple-element.376), channel_id=1, source_target_pairs={{1,0},{2,1},{3,2},{5,4},{6,5},{7,6},{9,8},{10,9},{11,10},{13,12},{... | collective-permute-start | bytes 811016 | tf_op jit(solution)/shard_map/ppermute | solution.py:326
  1173.6 42.5 %copy-start.33 = (f32[4,32,4224]{2,1,0:T(8,128)S(1)}, f32[4,32,4224]{2,1,0:T(8,128)}, u32[]{:S(2)}) copy-start(f32[4,32,4224]{2,1,0:T(8,128)} %copy-done.32) | copy-start | bytes 6488068
  1173.6 42.5 %collective-permute-start.4 = (bf16[32,4224]{1,0:T(8,128)(2,1)S(1)}, bf16[32,4224]{1,0:T(8,128)(2,1)S(1)}, u32[]{:S(2)}, u32[]{:S(2)}) collective-permute-start(bf16[32,4224]{1,0:T(8,128)(2,1)S(1)} %fusion.139), channel_id=1, source_target_pairs={{0,1},{1,2},{2,3},{4,5},{5,6},{6,7},{8,9},{9,10},{10,11},{12,13},{... | collective-permute-start | bytes 811016 | tf_op jit(solution)/shard_map/ppermute | solution.py:325
  1211.9 68.0 %collective-permute-start.12 = (bf16[3,704,128]{2,1,0:T(8,128)(2,1)}, bf16[3,704,128]{2,1,0:T(8,128)(2,1)}, u32[]{:S(2)}, u32[]{:S(2)}) collective-permute-start(bf16[3,704,128]{2,1,0:T(8,128)(2,1)} %get-tuple-element.369), channel_id=1, source_target_pairs={{0,1},{1,2},{2,3},{4,5},{5,6},{6,7},{8,9},{9,10},{10,11},{12,13},{... | collective-permute-start | bytes 1622024 | tf_op jit(solution)/shard_map/ppermute | solution.py:325
  1217.0 69.0 %collective-permute-start.7 = (bf16[32,4224]{1,0:T(8,128)(2,1)}, bf16[32,4224]{1,0:T(8,128)(2,1)S(1)}, u32[]{:S(2)}, u32[]{:S(2)}) collective-permute-start(bf16[32,4224]{1,0:T(8,128)(2,1)} %get-tuple-element.374), channel_id=1, source_target_pairs={{1,0},{2,1},{3,2},{5,4},{6,5},{7,6},{9,8},{10,9},{11,10},{13,12},{... | collective-permute-start | bytes 811016 | tf_op jit(solution)/shard_map/ppermute | solution.py:326
  1275.8 24.2 %collective-permute-start.5 = (bf16[32,4224]{1,0:T(8,128)(2,1)}, bf16[32,4224]{1,0:T(8,128)(2,1)S(1)}, u32[]{:S(2)}, u32[]{:S(2)}) collective-permute-start(bf16[32,4224]{1,0:T(8,128)(2,1)} %get-tuple-element.373), channel_id=1, source_target_pairs={{0,1},{1,2},{2,3},{4,5},{5,6},{6,7},{8,9},{9,10},{10,11},{12,13},{... | collective-permute-start | bytes 811016 | tf_op jit(solution)/shard_map/ppermute | solution.py:325
  1278.6 17.1 %collective-permute-start.15 = (bf16[3,704,128]{2,1,0:T(8,128)(2,1)S(1)}, bf16[3,704,128]{2,1,0:T(8,128)(2,1)S(1)}, u32[]{:S(2)}, u32[]{:S(2)}) collective-permute-start(bf16[3,704,128]{2,1,0:T(8,128)(2,1)S(1)} %get-tuple-element.370), channel_id=1, source_target_pairs={{1,0},{2,1},{3,2},{5,4},{6,5},{7,6},{9,8},{10,9},{11,10},{13,12},{... | collective-permute-start | bytes 1622024 | tf_op jit(solution)/shard_map/ppermute | solution.py:326
  1281.4 14.7 %collective-permute-start.13 = (bf16[3,704,128]{2,1,0:T(8,128)(2,1)S(1)}, bf16[3,704,128]{2,1,0:T(8,128)(2,1)S(1)}, u32[]{:S(2)}, u32[]{:S(2)}) collective-permute-start(bf16[3,704,128]{2,1,0:T(8,128)(2,1)S(1)} %fusion.123), channel_id=1, source_target_pairs={{0,1},{1,2},{2,3},{4,5},{5,6},{6,7},{8,9},{9,10},{10,11},{12,13},{... | collective-permute-start | bytes 1622024 | tf_op jit(solution)/shard_map/ppermute | solution.py:325
  1286.1 13.9 %collective-permute-start.8 = (bf16[32,4224]{1,0:T(8,128)(2,1)S(1)}, bf16[32,4224]{1,0:T(8,128)(2,1)S(1)}, u32[]{:S(2)}, u32[]{:S(2)}) collective-permute-start(bf16[32,4224]{1,0:T(8,128)(2,1)S(1)} %fusion.138), channel_id=1, source_target_pairs={{1,0},{2,1},{3,2},{5,4},{6,5},{7,6},{9,8},{10,9},{11,10},{13,12},{... | collective-permute-start | bytes 811016 | tf_op jit(solution)/shard_map/ppermute | solution.py:326
  1298.7 14.7 %collective-permute-start.16 = (bf16[3,704,128]{2,1,0:T(8,128)(2,1)}, bf16[3,704,128]{2,1,0:T(8,128)(2,1)}, u32[]{:S(2)}, u32[]{:S(2)}) collective-permute-start(bf16[3,704,128]{2,1,0:T(8,128)(2,1)} %get-tuple-element.368), channel_id=1, source_target_pairs={{1,0},{2,1},{3,2},{5,4},{6,5},{7,6},{9,8},{10,9},{11,10},{13,12},{... | collective-permute-start | bytes 1622024 | tf_op jit(solution)/shard_map/ppermute | solution.py:326
  1300.8 17.5 %collective-permute-start.14 = (bf16[3,704,128]{2,1,0:T(8,128)(2,1)S(1)}, bf16[3,704,128]{2,1,0:T(8,128)(2,1)S(1)}, u32[]{:S(2)}, u32[]{:S(2)}) collective-permute-start(bf16[3,704,128]{2,1,0:T(8,128)(2,1)S(1)} %get-tuple-element.367), channel_id=1, source_target_pairs={{0,1},{1,2},{2,3},{4,5},{5,6},{6,7},{8,9},{9,10},{10,11},{12,13},{... | collective-permute-start | bytes 1622024 | tf_op jit(solution)/shard_map/ppermute | solution.py:325
  1314.9 13.0 collective-permute-start.17
  (75 other events, 456.2 us)
Sparse Core Ops, SparseCore 0:
  11.4 81.2 all-gather.3
  95.5 115.8 all-gather.5

commit v2 on v1

v2 whole, which is shorter than its diff:
```python
import functools

import jax
import jax.numpy as jnp
from jax import lax
from jax.experimental import pallas as pl
from jax.experimental.pallas import tpu as pltpu
from jax.sharding import PartitionSpec as P

F32 = jnp.float32
BF = jnp.bfloat16
EPS = 1e-5
LEN = 1024
BL = 64
H = 4
HK = 128
HV = 256
DK = 512
DV = 1024
CQ, CK, CV, CG, CR, CO = 0, 512, 1024, 2048, 3072, 3200
GW = 3200
SCALE = HK**-0.5
VMEM = 60 * 1024 * 1024


def nn(a,b): return lax.dot_general(a,b,(((1,),(0,)),((),())),preferred_element_type=F32)


def nt(a,b): return lax.dot_general(a,b,(((1,),(1,)),((),())),preferred_element_type=F32)


def tn(a,b): return lax.dot_general(a,b,(((0,),(0,)),((),())),preferred_element_type=F32)


def sigmoid(v): return 1.0/(1.0+jnp.exp(-v))


def softminus(x): return jnp.minimum(x,0.0)-jnp.log1p(jnp.exp(-jnp.abs(x)))


def split(x):
    hi=x.astype(BF); return hi,(x-hi.astype(F32)).astype(BF)


def doc_of(p,starts):
    out=(p>=starts[0]).astype(jnp.int32)
    for s in starts[1:]: out=out+(p>=s).astype(jnp.int32)
    return out


def tile_masks(base,T,starts):
    tc=lax.broadcasted_iota(jnp.int32,(T,1),0); tr=lax.broadcasted_iota(jnp.int32,(1,T),1)
    dc=doc_of(tc+base,starts); dr=doc_of(tr+base,starts)
    first=(tc & ~(BL-1))+base
    prior=jnp.where(first>0,doc_of(first-1,starts),-1)
    last=doc_of(first+(BL-1),starts)
    inter=(dc==prior); reach=(dc==last)
    same=(tc>>6)==(tr>>6)
    low=same&(tc>=tr)
    return inter,reach,same,low,low&(dc==dr)


def keep_of(first,starts):
    return jnp.where(first>0,(doc_of(first-1,starts)==doc_of(first+BL-1,starts)).astype(F32),0.0)


def starts_of(len_ref, seq):
    first = len_ref[seq * 4]
    second = first + len_ref[seq * 4 + 1]
    return [first, second, second + len_ref[seq * 4 + 2]]


def params(flops=0, moved=0):
    return dict(
        compiler_params=pltpu.CompilerParams(vmem_limit_bytes=VMEM),
        cost_estimate=pl.CostEstimate(flops=flops, bytes_accessed=moved, transcendentals=0),
    )


def fwd_kernel(NT,st_ref,tok_ref,w_ref,gain_ref,wdec_ref,bias_ref,hg_ref,res_ref,n_ref,q_ref,k_ref,cum_ref,dp_ref,v_ref,gp_ref,o_ref,bef_ref,mix_ref,rank_ref,state):
    T=tok_ref.shape[0]; nb=T//BL
    i=pl.program_id(0); seq=i//NT; tile=i%NT; base=tile*T
    starts=starts_of(st_ref,seq)
    inter,reach,same,low,intra=tile_masks(base,T,starts)
    @pl.when(tile==0)
    def _(): state[...]=jnp.zeros_like(state)
    x=tok_ref[...].astype(F32)
    r=lax.rsqrt(jnp.mean(x*x,axis=-1,keepdims=True)+EPS)
    n_ref[...]=(x*r*gain_ref[...]).astype(BF)
    n=n_ref[...]
    rank=nn(n,w_ref[:,CR:CR+128]).astype(BF)
    rank_ref[...]=rank
    dp=nn(rank,wdec_ref[...])+bias_ref[...]
    dp_ref[...]=dp
    dhi,dlo=split(softminus(dp)*(1.0/16.0))
    lowb=low.astype(BF)
    cum=nn(lowb,dhi)+nn(lowb,dlo)
    cum_ref[...]=cum
    q=nn(n,w_ref[:,CQ:CQ+DK])*SCALE; q_ref[...]=q
    k=nn(n,w_ref[:,CK:CK+DK]); k_ref[...]=k
    v_ref[...]=nn(n,w_ref[:,CV:CV+DV]).astype(BF)
    gp_ref[...]=nn(n,w_ref[:,CG:CG+DV]).astype(BF)
    interf=inter.astype(F32)
    ends=[cum[BL*b+BL-1:BL*b+BL,:] for b in range(nb)]
    endb=jnp.concatenate([jnp.broadcast_to(e,(BL,DK)) for e in ends],axis=0)
    qg=q*jnp.exp(cum)
    qgi=(qg*interf).astype(BF); qg=qg.astype(BF)
    kg=(k*jnp.exp(-cum)).astype(BF)
    kc=(k*jnp.exp(endb-cum)).astype(BF)
    keeps=jnp.concatenate([jnp.exp(ends[b])*keep_of(base+BL*b,starts) for b in range(nb)]+[jnp.zeros((8-nb,DK),F32)],axis=0)
    for h in range(H):
        a=slice(HK*h,HK*h+HK); c=slice(HV*h,HV*h+HV)
        v=v_ref[:,c]
        s=jnp.where(intra,nt(qg[:,a],kg[:,a]),0.0).astype(BF)
        vk=jnp.where(reach,v,jnp.zeros_like(v))
        kt=keeps[:,a].T
        o=nn(s,v)
        parts=[]
        st=state[h]
        for b in range(nb):
            t=slice(BL*b,BL*b+BL)
            sb=st.astype(BF)
            bef_ref[b,h]=sb
            parts.append(nn(qgi[t,a],sb))
            st=st*kt[:,b:b+1]+tn(kc[t,a],vk[t])
        state[h]=st
        o=o+jnp.concatenate(parts,axis=0)
        o_ref[:,c]=o
        sc=lax.rsqrt(jnp.maximum(jnp.mean(o*o,axis=-1,keepdims=True),1.0))
        gp=gp_ref[:,c].astype(F32)
        mix_ref[:,c]=(o*sc*hg_ref[...]*(gp*sigmoid(gp))).astype(BF)
    res_ref[...]=x+nt(mix_ref[...],w_ref[:,CO:CO+DV])


def fwd_call(st,tok,w,gain,wdec,bias,hg,T=256):
    n,d=tok.shape; NT=LEN//T; sd=jax.ShapeDtypeStruct
    row=lambda x: pl.BlockSpec((T,x),lambda i,s:(i,0))
    const=lambda a: pl.BlockSpec(a.shape,lambda i,s:(0,0),pipeline_mode=pl.Buffered(1))
    nb=T//BL
    outs=[(d,F32),(d,BF),(DK,F32),(DK,F32),(DK,F32),(DK,F32),(DV,BF),(DV,BF),(DV,F32),None,(DV,BF),(128,BF)]
    specs=[row(o[0]) if o else pl.BlockSpec((nb,H,HK,HV),lambda i,s:(i,0,0,0)) for o in outs]
    shapes=[sd((n,o[0]),o[1]) if o else sd((n//BL,H,HK,HV),BF) for o in outs]
    return pl.pallas_call(functools.partial(fwd_kernel,NT),
        grid_spec=pltpu.PrefetchScalarGridSpec(num_scalar_prefetch=1,grid=(n//T,),
            in_specs=[row(d),const(w),const(gain),const(wdec),const(bias),const(hg)],out_specs=specs,
            scratch_shapes=[pltpu.VMEM((H,HK,HV),F32)]),
        out_shape=shapes,name="mixer_fwd",**params(n*d*4224*2,60<<20))(st,tok,w,gain,wdec,bias,hg)


def bwd_kernel(NT,st_ref,gmix_ref,w_ref,wdec_ref,hg_ref,q_ref,k_ref,cum_ref,dp_ref,v_ref,gp_ref,o_ref,bef_ref,rank_ref,g_ref,dwd_ref,db_ref,dhg_ref,state):
    T=q_ref.shape[0]; nb=T//BL
    step=pl.program_id(0); i=pl.num_programs(0)-1-step; seq=i//NT; tile=i%NT; base=tile*T
    starts=starts_of(st_ref,seq)
    inter,reach,same,low,intra=tile_masks(base,T,starts)
    @pl.when(tile==NT-1)
    def _(): state[...]=jnp.zeros_like(state)
    @pl.when(step==0)
    def _():
        dwd_ref[...]=jnp.zeros_like(dwd_ref); db_ref[...]=jnp.zeros_like(db_ref); dhg_ref[...]=jnp.zeros_like(dhg_ref)
    cum=cum_ref[...]
    ends=[cum[BL*b+BL-1:BL*b+BL,:] for b in range(nb)]
    endb=jnp.concatenate([jnp.broadcast_to(e,(BL,DK)) for e in ends],axis=0)
    eg=jnp.exp(cum); es=jnp.exp(-cum); ec=jnp.exp(endb-cum)
    kend=jnp.concatenate([jnp.exp(ends[b])*keep_of(base+BL*b,starts) for b in range(nb)]+[jnp.zeros((8-nb,DK),F32)],axis=0)
    interb=inter.astype(F32).astype(BF); reachf=reach.astype(F32)
    tc=lax.broadcasted_iota(jnp.int32,(T,1),0); tr=lax.broadcasted_iota(jnp.int32,(1,T),1)
    upb=(same&(tc<=tr)).astype(BF); lsb=(same&(tc>tr)).astype(BF)
    hg=hg_ref[...]
    ones=jnp.ones((8,HV),BF)
    for h in range(H):
        a=slice(HK*h,HK*h+HK); c=slice(HV*h,HV*h+HV)
        gi=nn(gmix_ref[...],w_ref[:,CO+HV*h:CO+HV*h+HV])
        o=o_ref[:,c]; gp=gp_ref[:,c].astype(F32)
        ms=jnp.mean(o*o,axis=-1,keepdims=True)
        sc=lax.rsqrt(jnp.maximum(ms,1.0))
        hn0=o*sc
        s=sigmoid(gp); si=gp*s
        g_ref[:,CG+HV*h:CG+HV*h+HV]=(gi*hn0*hg*(s+si*(1.0-s))).astype(BF)
        G=gi*si
        dhg_ref[...]+=jnp.sum((G*hn0).reshape(-1,8,HV),axis=0)
        G=G*hg
        innr=jnp.mean(G*o,axis=-1,keepdims=True)*jnp.where(ms>1.0,1.0,0.0)
        go=(sc*G-o*(sc*sc*sc*innr)).astype(BF)
        goi=go*interb
        v=v_ref[:,c]
        qs=q_ref[:,a]*eg[:,a]; ks=k_ref[:,a]*es[:,a]; kd=k_ref[:,a]*ec[:,a]
        qg=qs.astype(BF); kg=ks.astype(BF); kc=kd.astype(BF)
        sco=jnp.where(intra,nt(qg,kg),0.0).astype(BF)
        gs=jnp.where(intra,nt(go,v),0.0).astype(BF)
        gv=tn(sco,go); gq=nn(gs,kg); gk=tn(gs,qg)
        kt=kend[:,a].T
        st=state[h]
        p_gv=[None]*nb; p_gq=[None]*nb; p_gkc=[None]*nb; p_end=[None]*nb
        for b in reversed(range(nb)):
            t=slice(BL*b,BL*b+BL)
            bef=bef_ref[b,h]
            sb=st.astype(BF)
            p_gv[b]=nn(kc[t],sb)
            p_gq[b]=nt(goi[t],bef)
            p_gkc[b]=nt(v[t],sb)
            m1,m2=split(st*bef.astype(F32))
            p_end[b]=(nt(ones,m1)+nt(ones,m2))[0:1]*kend[b:b+1,a]
            st=(tn(qg[t],goi[t])+kt[:,b:b+1]*st).astype(BF).astype(F32)
        state[h]=st
        cat=lambda p: jnp.concatenate(p,axis=0)
        gv=gv+cat(p_gv)*reachf
        g_ref[:,CV+HV*h:CV+HV*h+HV]=gv.astype(BF)
        gq=gq+cat(p_gq)
        gkc=cat(p_gkc)*reachf
        av1,av2=split(gq*qs-gk*ks)
        c1,c2=split(gkc*kd)
        endr=cat([jnp.broadcast_to(p,(BL,HK)) for p in p_end])
        gd=nn(upb,av1)+nn(upb,av2)+nn(lsb,c1)+nn(lsb,c2)+endr
        g_ref[:,CQ+HK*h:CQ+HK*h+HK]=(gq*eg[:,a]*SCALE).astype(BF)
        g_ref[:,CK+HK*h:CK+HK*h+HK]=(gk*es[:,a]+gkc*ec[:,a]).astype(BF)
        dp=dp_ref[:,a]
        gpre=(gd*(1.0/16.0)*(1.0/(1.0+jnp.exp(dp)))).astype(BF)
        db_ref[:,a]+=jnp.sum(gpre.astype(F32).reshape(-1,8,HK),axis=0)
        dwd_ref[:,a]+=tn(rank_ref[...],gpre)
        gr=nt(gpre,wdec_ref[:,a])
        grank=gr if h==0 else grank+gr
    g_ref[:,CR:CR+128]=grank.astype(BF)


def bwd_call(st,gmix,w,wdec,hg,q,k,cum,dp,v,gp,o,bef,rank,T=256):
    n,d=gmix.shape; NT=LEN//T; sd=jax.ShapeDtypeStruct; N1=n//T-1
    row=lambda a: pl.BlockSpec((T,a.shape[1]),lambda i,s:(N1-i,0))
    const=lambda a: pl.BlockSpec(a.shape,lambda i,s:(0,0),pipeline_mode=pl.Buffered(1))
    nb=T//BL
    acc=lambda s: pl.BlockSpec(s,lambda i,_:(0,0))
    return pl.pallas_call(functools.partial(bwd_kernel,NT),
        grid_spec=pltpu.PrefetchScalarGridSpec(num_scalar_prefetch=1,grid=(n//T,),
            in_specs=[row(gmix),const(w),const(wdec),const(hg),row(q),row(k),row(cum),row(dp),row(v),row(gp),row(o),pl.BlockSpec((nb,H,HK,HV),lambda i,s:(N1-i,0,0,0)),row(rank)],
            out_specs=[pl.BlockSpec((T,3200),lambda i,s:(N1-i,0)),acc((128,DK)),acc((8,DK)),acc((8,HV))],
            scratch_shapes=[pltpu.VMEM((H,HK,HV),F32)]),
        out_shape=[sd((n,3200),BF),sd((128,DK),F32),sd((8,DK),F32),sd((8,HV),F32)],
        name="mixer_bwd",**params(n*d*4224*3,70<<20))(st,gmix,w,wdec,hg,q,k,cum,dp,v,gp,o,bef,rank)


def dx_kernel(g_ref,w_ref,tok_ref,gain_ref,gres_ref,gt_ref,gn_ref):
    gm=nt(g_ref[...],w_ref[:,:3200])
    x=tok_ref[...].astype(F32)
    r=lax.rsqrt(jnp.mean(x*x,axis=-1,keepdims=True)+EPS)
    sc=gm*gain_ref[...]
    inner=jnp.mean(sc*x,axis=-1,keepdims=True)
    gt_ref[...]=gres_ref[...]+r*sc-x*(r*r*r*inner)
    part=jnp.sum((gm*x*r).reshape(-1,8,gm.shape[1]),axis=0)
    @pl.when(pl.program_id(0)==0)
    def _(): gn_ref[...]=part
    @pl.when(pl.program_id(0)>0)
    def _(): gn_ref[...]+=part


def dx_call(g,w,tok,gain,gres,T=256):
    n,d=tok.shape; sd=jax.ShapeDtypeStruct
    row=lambda a: pl.BlockSpec((T,a.shape[1]),lambda i:(i,0))
    const=lambda a: pl.BlockSpec(a.shape,lambda i:(0,0),pipeline_mode=pl.Buffered(1))
    return pl.pallas_call(dx_kernel,grid=(n//T,),in_specs=[row(g),const(w),row(tok),const(gain),row(gres)],
        out_specs=[row(gres),pl.BlockSpec((8,d),lambda i:(0,0))],out_shape=[sd((n,d),F32),sd((8,d),F32)],
        name="mixer_dx",**params(n*d*3200*2,40<<20))(g,w,tok,gain,gres)


def mlp_kernel(chunk, res_ref, cot_ref, gain_ref, w_hbm, bo_ref, n_ref, hid_ref, gg_ref, gu_ref, gres_ref, gmix_ref, gn_ref, w_ref, sems):
    wg_ref,wu_ref,wd_ref=w_ref.at[0],w_ref.at[1],w_ref.at[2]
    blocks,mlps,_,hid,_=w_hbm.shape
    @pl.when(pl.program_id(0)==0)
    def _():
        copies=[pltpu.make_async_copy(w_hbm.at[r,m],w_ref.at[:,pl.ds(m*hid,hid),pl.ds(r*128,128)],sems.at[r,m]) for m in range(mlps) for r in range(blocks)]
        for c in copies: c.start()
        for c in copies: c.wait()
    res=res_ref[...]
    gain=gain_ref[...]
    r=lax.rsqrt(jnp.mean(res*res,axis=-1,keepdims=True)+EPS)
    n_ref[...]=(res*r*gain).astype(BF)
    ff=wg_ref.shape[0]
    for c in range(ff//chunk):
        sl=slice(c*chunk,(c+1)*chunk)
        n=n_ref[...]
        gp=nt(n,wg_ref[sl,:]); up=nt(n,wu_ref[sl,:]); gh=nt(cot_ref[...],wd_ref[sl,:])
        s=sigmoid(gp)
        si=gp*s
        hid_ref[:,sl]=(si*up).astype(BF)
        gu_ref[:,sl]=(gh*si).astype(BF)
        gg_ref[:,sl]=(gh*up*(s+si*(1.0-s))).astype(BF)
    gm=nn(gg_ref[...],wg_ref[...])+nn(gu_ref[...],wu_ref[...])
    res=res_ref[...]
    sc=gm*gain
    inner=jnp.mean(sc*res,axis=-1,keepdims=True)
    gi=r*sc-res*(r*r*r*inner)
    gres=cot_ref[...].astype(F32)+gi
    gres_ref[...]=gres
    gmix_ref[...]=gres.astype(BF)
    part=jnp.sum((gm*res*r).reshape(-1,8,gm.shape[1]),axis=0)
    @pl.when(pl.program_id(0)==0)
    def _(): gn_ref[...]=part
    @pl.when(pl.program_id(0)>0)
    def _(): gn_ref[...]+=part
    bo_ref[...]=(res+nn(hid_ref[...],wd_ref[...])).astype(BF)


def mlp_call(res,cot,gain,w,T=256,chunk=256):
    n,d=res.shape; ff=w.shape[1]*w.shape[3]
    row=lambda w: pl.BlockSpec((T,w),lambda i:(i,0))
    const=lambda a: pl.BlockSpec(a.shape,lambda i:(0,0),pipeline_mode=pl.Buffered(1))
    sd=jax.ShapeDtypeStruct
    return pl.pallas_call(functools.partial(mlp_kernel,chunk),grid=(n//T,),
        in_specs=[row(d),row(d),const(gain),pl.BlockSpec(memory_space=pl.ANY)],
        out_specs=[row(d),row(d),row(ff),row(ff),row(ff),row(d),row(d),pl.BlockSpec((8,d),lambda i:(0,0))],
        out_shape=[sd((n,d),BF),sd((n,d),BF),sd((n,ff),BF),sd((n,ff),BF),sd((n,ff),BF),sd((n,d),F32),sd((n,d),BF),sd((8,d),F32)],
        scratch_shapes=[pltpu.VMEM((3,ff,d),BF),pltpu.SemaphoreType.DMA((w.shape[0],w.shape[1]))],
        name="mlp",**params(n*d*ff*12,90<<20))(res,cot,gain,w)


def load_half(sel_ref,x_hbm,xh,sems):
    copies=[pltpu.make_async_copy(x_hbm.at[:,pl.ds(pl.multiple_of((2*j+sel_ref[0])*128,128),128)],xh.at[:,pl.ds(128*j,128)],sems.at[j]) for j in range(4)]
    for c in copies: c.start()
    for c in copies: c.wait()


def dw_kernel(wide,sel_ref,g_ref,x_hbm,*rest):
    *recv,o_ref,xh,sems=rest
    @pl.when(pl.program_id(0)==0)
    def _(): load_half(sel_ref,x_hbm,xh,sems)
    o=tn(g_ref[...],xh[...]) if wide else tn(xh[...],g_ref[...])
    for j in range(4):
        v=o[:,128*j:128*(j+1)] if wide else o[128*j:128*(j+1),:]
        if recv: v=v+recv[0][j].astype(F32)
        o_ref[j]=v.astype(BF)


def dw_call(g,x,sel,recv=None,chunk=1408,wide=True):
    n,ff=g.shape; d=x.shape[1]
    out=pl.BlockSpec((4,chunk,128),lambda i,s:(0,i,0)) if wide else pl.BlockSpec((4,128,chunk),lambda i,s:(0,0,i))
    more=[] if recv is None else [recv]
    return pl.pallas_call(functools.partial(dw_kernel,wide),
        grid_spec=pltpu.PrefetchScalarGridSpec(num_scalar_prefetch=1,grid=(ff//chunk,),
            in_specs=[pl.BlockSpec((n,chunk),lambda i,s:(0,i)),pl.BlockSpec(memory_space=pl.ANY)]+[out]*len(more),
            out_specs=out,scratch_shapes=[pltpu.VMEM((n,d//2),BF),pltpu.SemaphoreType.DMA((4,))]),
        out_shape=jax.ShapeDtypeStruct((4,ff,128) if wide else (4,128,ff),BF),
        name="grad_w",**params(n*d*ff,n*ff*2+n*d+ff*d*2))(sel,g,x,*more)


def swap(x, axis, bit, count):
    return lax.ppermute(x, axis, [(i, i ^ (1 << bit)) for i in range(count)])


def bit_of(axis, bit):
    return (lax.axis_index(axis) >> bit) & 1


def halve(grads, dim, bit, count):
    place = bit_of("rows", bit)
    send = lax.dynamic_index_in_dim(grads, 1 - place, dim, keepdims=False)
    keep = lax.dynamic_index_in_dim(grads, place, dim, keepdims=False)
    came = swap(send.astype(BF), "rows", bit, count)
    return keep.astype(F32) + came.astype(F32)


def halve_both(grads, first, low, count):
    grads = grads.reshape((2, 2) + grads.shape[1:])
    if first == 0:
        return halve(halve(grads, 0, low + 2, count), 0, low + 1, count)
    return halve(halve(grads, 1, low + 1, count), 0, low + 2, count)


def line_sum(grads, count):
    me = lax.axis_index("mlp")
    up = [(i, i + 1) for i in range(count - 1)]
    down = [(i + 1, i) for i in range(count - 1)]

    def pick(at):
        return lax.dynamic_index_in_dim(grads, jnp.clip(at, 0, count - 1), 0, keepdims=False)

    total = pick(me)
    rising = falling = None
    for step in range(1, count):
        send_up = pick(me + count - step)
        send_down = pick(me - count + step)
        if rising is not None:
            send_up = send_up + rising
            send_down = send_down + falling
        rising = lax.ppermute(send_up.astype(BF), "mlp", up).astype(F32)
        falling = lax.ppermute(send_down.astype(BF), "mlp", down).astype(F32)
    if rising is not None:
        total = total + rising + falling
    return total


def sum_all(x, rows, mlps):
    for axis, count in (("rows", rows), ("mlp", mlps)):
        for bit in range(count.bit_length() - 1):
            x = x + swap(x, axis, bit, count)
    return x


def body(
    tokens,
    doc_lengths,
    cotangent,
    norm_gain_mix,
    w_query,
    w_key,
    w_value,
    w_outgate,
    w_rank,
    w_decay,
    decay_bias,
    head_gain,
    w_output,
    norm_gain_mlp,
    w_gate,
    w_up,
    w_down,
):
    rows = lax.axis_size("rows")
    mlps = lax.axis_size("mlp")
    low = rows.bit_length() - 4
    shard = w_query.shape[0]
    hid, wide = w_down.shape
    lens = doc_lengths.reshape(-1)
    mixer_local = jnp.concatenate(
        [
            w_query, w_key, w_value, w_outgate, w_rank,
            norm_gain_mix[:, None], norm_gain_mlp[:, None], jnp.zeros((shard, 110), BF), w_output.T,
        ],
        axis=1,
    )
    mixer_all = lax.all_gather(mixer_local, ("rows", "mlp"), axis=0, tiled=True)
    gain_mix = mixer_all[:, CR + 16].astype(F32)[None]
    gain_mlp = mixer_all[:, CR + 17].astype(F32)[None]
    mlp_local = jnp.stack([w_gate.T, w_up.T, w_down])
    mlp_all = lax.all_gather(mlp_local, ("rows", "mlp"), axis=0)
    mlp_all = mlp_all.reshape(8, rows // 8, mlps, 3, hid, wide)
    if rows > 8:
        mlp_all = mlp_all.transpose(0, 2, 3, 4, 1, 5)
    mlp_all = mlp_all.reshape(8, mlps, 3, hid, 128)
    decay_wide = jnp.concatenate([w_decay, jnp.zeros((112, DK), BF)], axis=0)
    head_row = head_gain.astype(F32)[None]
    residual, normed_in, q, k, cum, dp, v, gp, o, before, mixed, rank = fwd_call(
        lens, tokens, mixer_all, gain_mix, decay_wide, decay_bias.astype(F32)[None], head_row
    )
    block_out, normed_mid, hidden, grad_gate, grad_up, grad_res, grad_mixed, gain_mlp_part = mlp_call(
        residual, cotangent, gain_mlp, mlp_all
    )
    mine = bit_of("rows", low).astype(jnp.int32)[None]

    def grad_half(g, x, **how):
        sent = swap(dw_call(g, x, 1 - mine, **how), "rows", low, rows)
        return lambda: dw_call(g, x, mine, sent, **how)

    stacks = [grad_half(g, x) for g, x in ((grad_gate, normed_mid), (grad_up, normed_mid), (hidden, cotangent))]
    stack_out = grad_half(mixed, grad_mixed, wide=False, chunk=512)
    stacks = [s() for s in stacks]
    stack_out = stack_out()
    half = mlps * hid // 2
    parts = [
        halve_both(stacks[0], 0, low, rows),
        halve_both(stacks[1], 1, low, rows),
        jnp.concatenate(
            [halve_both(stacks[2][:, :half], 0, low, rows), halve_both(stacks[2][:, half:], 1, low, rows)], axis=0
        ),
    ]
    mlp_grads = jnp.stack([p.reshape(mlps, hid, 128) for p in parts], axis=1)
    if low:
        mlp_grads = mlp_grads.reshape((mlps, 3, hid) + (2,) * low + (wide,))
        for bit in reversed(range(low)):
            mlp_grads = halve(mlp_grads, 3, bit, rows)
    mlp_grads = line_sum(mlp_grads, mlps)

    grads, decay_part, bias_part, head_part = bwd_call(
        lens, grad_mixed, mixer_all, decay_wide, head_row, q, k, cum, dp, v, gp, o, before, rank
    )
    small = jnp.concatenate(
        [decay_part[:16].reshape(-1), bias_part.sum(0), head_part.sum(0), gain_mlp_part.sum(0)]
    )
    small = sum_all(small.reshape(-1, 256), rows, mlps).reshape(-1)
    stack_in = grad_half(grads, normed_in, wide=False, chunk=640)()
    grad_tokens, _ = dx_call(grads, mixer_all, tokens, gain_mix, grad_res)

    def finish(stack, first):
        part = halve_both(stack, first, low, rows)
        part = part.reshape((2,) * low + (mlps, shard, part.shape[-1]))
        for bit in reversed(range(low)):
            part = halve(part, 0, bit, rows)
        return line_sum(part, mlps)

    out_grads = finish(stack_out, 0)
    in_grads = jnp.concatenate(
        [finish(stack_in[:, :, :CV + 640], 0), finish(stack_in[:, :, CV + 640 :], 1)], axis=1
    )
    gain_mix_grad = jnp.sum(in_grads * mixer_local[:, :GW].astype(F32), axis=1) / norm_gain_mix.astype(F32)
    at = 16 * DK + DK + HV + (lax.axis_index("rows") * mlps + lax.axis_index("mlp")) * shard
    return (
        block_out,
        grad_tokens,
        gain_mix_grad,
        in_grads[:, CQ : CQ + DK],
        in_grads[:, CK : CK + DK],
        in_grads[:, CV : CV + DV],
        in_grads[:, CG : CG + DV],
        in_grads[:, CR : CR + 16],
        small[: 16 * DK].reshape(16, DK),
        small[16 * DK : 17 * DK],
        small[17 * DK : 17 * DK + HV],
        out_grads.T,
        lax.dynamic_slice_in_dim(small, at, shard),
        mlp_grads[0].T,
        mlp_grads[1].T,
        mlp_grads[2],
    )


def solution(mesh):
    in_specs = (
        P(("rows", "mlp"), None),
        P(("rows", "mlp"), None),
        P(("rows", "mlp"), None),
        P(("rows", "mlp")),
        P(("rows", "mlp"), None),
        P(("rows", "mlp"), None),
        P(("rows", "mlp"), None),
        P(("rows", "mlp"), None),
        P(("rows", "mlp"), None),
        P(),
        P(),
        P(),
        P(None, ("rows", "mlp")),
        P(("rows", "mlp")),
        P("rows", "mlp"),
        P("rows", "mlp"),
        P("mlp", "rows"),
    )
    out_specs = (
        P(("rows", "mlp"), None),
        P(("rows", "mlp"), None),
        P(("rows", "mlp")),
        P(("rows", "mlp"), None),
        P(("rows", "mlp"), None),
        P(("rows", "mlp"), None),
        P(("rows", "mlp"), None),
        P(("rows", "mlp"), None),
        P(),
        P(),
        P(),
        P(None, ("rows", "mlp")),
        P(("rows", "mlp")),
        P("rows", "mlp"),
        P("rows", "mlp"),
        P("mlp", "rows"),
    )
    return jax.shard_map(body, mesh=mesh, in_specs=in_specs, out_specs=out_specs, check_vma=False)
```

time: 1350 us -> 719 us (0.53)
  matrix products: 417 us -> 0 us
  Pallas kernels: 0 us -> 362 us
  local copies, waits for them, and re-layouts: 366 us -> 26.6 us
  other arithmetic: 231 us -> 18.8 us
  starting transfers between devices: 39.8 us -> 88.4 us
  blocking collectives: 41.1 us -> 0 us
  waiting for transfers between devices: 227 us -> 202 us
    dot_general x42 -> x0, matrix products: 417 us -> none  [the longest x10 126 us: product_right(): lax.dot_general(left, right, (((1,), (1,)), ((), ())), preferred_element_...]
    pallas_call x0 -> x14, Pallas kernels: none -> 362 us  [the longest x10 121 us: dw_call(): pl.pallas_call(functools.partial(dw_kernel, wide), grid_spec=pltpu.Prefet...]
    ppermute x18 -> x48, waiting for transfers between devices: 167 us -> 61.3 us  [the longest x24 38.8 us: swap(): return lax.ppermute(x, axis, [(i, i ^ 1 << bit) for i in range(count)])]
    unnamed x218 -> x40, local copies, waits for them, and re-layouts: 92.4 us -> 3.87 us
    convert_element_type x18 -> x11, local copies, waits for them, and re-layouts: 77.5 us -> 0.64 us  [the longest x7 0.4 us: halve(): came = swap(send.astype(BF), 'rows', bit, count)]
    another operation x6 -> x0, local copies, waits for them, and re-layouts: 74.1 us -> none  [the longest x4 58.3 us: body(): jnp.stack(mlp_grads).reshape((3, mlps, hid) + (2,) * nbits + (wide,))]
    reshape x6 -> x4, local copies, waits for them, and re-layouts: 65.7 us -> 1.23 us  [the longest x1 0.62 us: body(): small[:16 * DK].reshape(16, DK)]
    all_gather x1, waiting for transfers between devices: 0.01 us -> 64.3 us  [body(): mlp_all = lax.all_gather(mlp_local, ('rows', 'mlp'), axis=0)]
  transfers between devices with their start and end apart: 20 -> 50, of which waited for: 8 -> 13; matrix products, arithmetic and copies ran while one was open for 32% -> 5% of each run, Pallas kernels for 0% -> 37%
where the time goes in v2:
time: 719 us; the launch traced here: 712 us
  Pallas kernels  362 us (50%)
  waiting for transfers between devices  202 us (28%)
  starting transfers between devices  88.4 us (12%)
  local copies, waits for them, and re-layouts  26.6 us (4%)
  other arithmetic  18.8 us (3%)
  between operations  15.3 us (2%)
    pallas_call x10, Pallas kernels, dw_call(): pl.pallas_call(functools.partial(dw_kernel, wide), grid_spec=pltpu.Prefet...  121 us
    pallas_call x1, Pallas kernels, mlp_call(): pl.pallas_call(functools.partial(mlp_kernel, chunk), grid=(n // T,), in_s...  89.7 us
    all_gather x1, waiting for transfers between devices, body(): mixer_all = lax.all_gather(mixer_local, ('rows', 'mlp'), axis=0, tiled=True)  76.1 us
    pallas_call x1, Pallas kernels, bwd_call(): pl.pallas_call(functools.partial(bwd_kernel, NT), grid_spec=pltpu.Prefetc...  74.5 us
    all_gather x1, waiting for transfers between devices, body(): mlp_all = lax.all_gather(mlp_local, ('rows', 'mlp'), axis=0)  64.3 us
    ppermute x12, starting transfers between devices, line_sum(): rising = lax.ppermute(send_up.astype(BF), 'mlp', up).astype(F32)  54.6 us
    pallas_call x1, Pallas kernels, fwd_call(): pl.pallas_call(functools.partial(fwd_kernel, NT), grid_spec=pltpu.Prefetc...  52.9 us
    ppermute x24, waiting for transfers between devices, swap(): return lax.ppermute(x, axis, [(i, i ^ 1 << bit) for i in range(count)])  38.8 us
  transfers between devices with their start and end apart: 50, of which 13 were waited for; matrix products, arithmetic and copies ran while one was open for 5% of the time, Pallas kernels for 37%

profile of v2, /device:TPU:0, one launch (start us, length us, event | category | flops | bytes accessed | tf_op | source)
XLA Modules:
  0.0 712.4 jit_solution(1188557023778789134)
XLA Ops:
  9.6 1.7 concatenate.18
  11.4 2.0 pad_maximum_fusion.2
  16.6 76.1 %all-gather.4.cloned.1.call-done.w_ref = bf16[1024,4224]{1,0:T(8,128)(2,1)} async-done(((bf16[32,4224]{1,0:T(8,128)(2,1)}), bf16[1024,4224]{1,0:T(8,128)(2,1)}) %all-gather.4.cloned.1.call-update) | async-done | bytes 8650768 | tf_op jit(solution)/shard_map/all_gather | solution.py:428
  92.8 2.1 convert_reduce_fusion
  94.8 52.9 %mixer_fwd.1 = (f32[2048,1024]{1,0:T(8,128)}, bf16[2048,1024]{1,0:T(8,128)(2,1)}, f32[2048,512]{1,0:T(8,128)}, f32[2048,512]{1,0:T(8,128)}, f32[2048,512]{1,0:T(...) custom-call(s32[8]{0:T(128)} %reshape.134.st_ref, ...), custom_call_target="tpu_custom_call" | custom-call | flops 17716740096 | bytes 62914560 | tf_op jit(solution)/shard_map/mixer_fwd/pallas_call | solution.py:143
  147.8 64.3 %all-gather.6.cloned.1.call-done = bf16[96,704,128]{2,1,0:T(8,128)(2,1)} async-done(((bf16[3,704,128]{2,1,0:T(8,128)(2,1)}), bf16[96,704,128]{2,1,0:T(8,128)(2,1)}) %all-gather.6.cloned.1.call-update) | async-done | bytes 17301520 | tf_op jit(solution)/shard_map/all_gather | solution.py:432
  212.1 89.7 %mlp.1 = (bf16[2048,1024]{1,0:T(8,128)(2,1)}, bf16[2048,1024]{1,0:T(8,128)(2,1)}, bf16[2048,2816]{1,0:T(8,128)(2,1)}, bf16[2048,2816]{1,0:T(8,128)(2,1)}, bf16[2...) custom-call(f32[2048,1024]{1,0:T(8,128)} %get-tuple-element.41.res_ref, ...), custom_call_target="tpu_custom_call" | custom-call | flops 70866960384 | bytes 94371840 | tf_op jit(solution)/shard_map/mlp/pallas_call | solution.py:306
  301.7 6.7 grad_w.12
  308.8 74.5 %mixer_bwd.1 = (bf16[2048,3200]{1,0:T(8,128)(2,1)}, f32[128,512]{1,0:T(8,128)}, f32[8,512]{1,0:T(8,128)}, f32[8,256]{1,0:T(8,128)}) custom-call(s32[8]{0:T(128)} %reshape.134.st_ref, bf16[2048,1024]{1,0:T(8,128)(2,1)} %get-tuple-element.43.gmix_ref.x_hbm, bf16[1024,4224]{1,0:T(8,128)(2,1)} %all-gather.4.cloned.1.call-done.w_ref, ...), custom_call_target="tpu_custom_call" | custom-call | flops 26575110144 | bytes 73400320 | tf_op jit(solution)/shard_map/mixer_bwd/pallas_call | solution.py:231
  386.9 6.9 grad_w.13
  396.4 12.7 %grad_w.14 = bf16[4,2816,128]{2,1,0:T(8,128)(2,1)} custom-call(s32[1]{0:T(128)S(6)} %sub.12.sel_ref, bf16[2048,2816]{1,0:T(8,128)(2,1)} %get-tuple-element.62.g_ref, bf16[2048,1024]{1,0:T(8,128)(2,1)} %get-tuple-element.63.x_hbm), custom_call_target="tpu_custom_call" | custom-call | flops 5905580032 | bytes 19398656 | tf_op jit(solution)/shard_map/grad_w/pallas_call | solution.py:335
  410.1 1.5 collective-permute-start.24
  411.6 12.8 %grad_w.16 = bf16[4,2816,128]{2,1,0:T(8,128)(2,1)} custom-call(s32[1]{0:T(128)S(6)} %sub.12.sel_ref, bf16[2048,2816]{1,0:T(8,128)(2,1)} %get-tuple-element.64.g_ref, bf16[2048,1024]{1,0:T(8,128)(2,1)} %get-tuple-element.63.x_hbm), custom_call_target="tpu_custom_call" | custom-call | flops 5905580032 | bytes 19398656 | tf_op jit(solution)/shard_map/grad_w/pallas_call | solution.py:335
  425.4 2.2 collective-permute-start.25
  427.5 23.3 %mixer_dx.1 = (f32[2048,1024]{1,0:T(8,128)}, f32[8,1024]{1,0:T(8,128)}) custom-call(bf16[2048,3200]{1,0:T(8,128)(2,1)} %get-tuple-element.53.g_ref, bf16[1024,4224]{1,0:T(8,128)(2,1)} %all-gather.4.cloned.1.call-done.w_ref, bf16[2048,1024]{1,0:T(8,128)(2,1)} %tok_ref.3, f32[1,1024]{1,0:T(1,128)} %bitcast.249, f32[2048,1024]{1,0:T(8,128)} %get-tuple-element.54.gres_ref), custom_call_target="tpu_custom_call" | custom-call | flops 13421772800 | bytes 41943040 | tf_op jit(solution)/shard_map/mixer_dx/pallas_call | solution.py:258
  450.8 1.9 collective-permute-start.20
  454.0 4.5 collective-permute-start.26
  458.6 12.6 %grad_w.18 = bf16[4,2816,128]{2,1,0:T(8,128)(2,1)} custom-call(s32[1]{0:T(128)S(6)} %sub.12.sel_ref, bf16[2048,2816]{1,0:T(8,128)(2,1)} %get-tuple-element.65.g_ref, bf16[2048,1024]{1,0:T(8,128)(2,1)} %x_hbm.3), custom_call_target="tpu_custom_call" | custom-call | flops 5905580032 | bytes 19398656 | tf_op jit(solution)/shard_map/grad_w/pallas_call | solution.py:335
  472.8 13.9 %grad_w.10 = bf16[4,128,3200]{2,1,0:T(8,128)(2,1)} custom-call(s32[1]{0:T(128)S(6)} %sub.12.sel_ref, bf16[2048,3200]{1,0:T(8,128)(2,1)} %get-tuple-element.53.g_ref, bf16[2048,1024]{1,0:T(8,128)(2,1)} %get-tuple-element.56.x_hbm), custom_call_target="tpu_custom_call" | custom-call | flops 6710886400 | bytes 21757952 | tf_op jit(solution)/shard_map/grad_w/pallas_call | solution.py:335
  486.7 4.6 collective-permute-start.27
  495.0 2.5 collective-permute-done.30
  498.1 13.9 %grad_w.15 = bf16[4,2816,128]{2,1,0:T(8,128)(2,1)} custom-call(s32[1]{0:T(128)} %bitcast.11.sel_ref, bf16[2048,2816]{1,0:T(8,128)(2,1)} %get-tuple-element.62.g_ref, bf16[2048,1024]{1,0:T(8,128)(2,1)} %get-tuple-element.63.x_hbm, bf16[4,2816,128]{2,1,0:T(8,128)(2,1)} %collective-permute-done.31.rest_0_), custom_call_target="tpu_custom_call" | custom-call | flops 5905580032 | bytes 19398656 | tf_op jit(solution)/shard_map/grad_w/pallas_call | solution.py:335
  512.0 2.6 dynamic-slice_bitcast_fusion.1
  516.0 13.5 %grad_w.17 = bf16[4,2816,128]{2,1,0:T(8,128)(2,1)} custom-call(s32[1]{0:T(128)} %bitcast.11.sel_ref, bf16[2048,2816]{1,0:T(8,128)(2,1)} %get-tuple-element.64.g_ref, bf16[2048,1024]{1,0:T(8,128)(2,1)} %get-tuple-element.63.x_hbm, bf16[4,2816,128]{2,1,0:T(8,128)(2,1)} %collective-permute-done.34.rest_0_), custom_call_target="tpu_custom_call" | custom-call | flops 5905580032 | bytes 19398656 | tf_op jit(solution)/shard_map/grad_w/pallas_call | solution.py:335
  529.5 2.6 dynamic-slice_bitcast_fusion
  532.7 13.5 %grad_w.19 = bf16[4,2816,128]{2,1,0:T(8,128)(2,1)} custom-call(s32[1]{0:T(128)} %bitcast.11.sel_ref, bf16[2048,2816]{1,0:T(8,128)(2,1)} %get-tuple-element.65.g_ref, bf16[2048,1024]{1,0:T(8,128)(2,1)} %x_hbm.3, bf16[4,2816,128]{2,1,0:T(8,128)(2,1)} %collective-permute-done.37.rest_0_), custom_call_target="tpu_custom_call" | custom-call | flops 5905580032 | bytes 19398656 | tf_op jit(solution)/shard_map/grad_w/pallas_call | solution.py:335
  546.2 2.0 fusion.39
  552.1 14.6 %grad_w.11 = bf16[4,128,3200]{2,1,0:T(8,128)(2,1)} custom-call(s32[1]{0:T(128)} %bitcast.11.sel_ref, bf16[2048,3200]{1,0:T(8,128)(2,1)} %get-tuple-element.53.g_ref, bf16[2048,1024]{1,0:T(8,128)(2,1)} %get-tuple-element.56.x_hbm, bf16[4,128,3200]{2,1,0:T(8,128)(2,1)} %collective-permute-done.rest_0_), custom_call_target="tpu_custom_call" | custom-call | flops 6710886400 | bytes 21757952 | tf_op jit(solution)/shard_map/grad_w/pallas_call | solution.py:335
  566.7 1.6 slice.85
  568.2 1.5 slice.86
  573.4 8.9 %collective-permute-done.40 = bf16[2,1408,128]{2,1,0:T(8,128)(2,1)S(1)} collective-permute-done((bf16[2,1408,128]{2,1,0:T(8,128)(2,1)}, bf16[2,1408,128]{2,1,0:T(8,128)(2,1)S(1)}, u32[]{:S(2)}, u32[]{:S(2)}) %collective-permute-start.40) | collective-permute-done | bytes 720928 | tf_op jit(solution)/shard_map/ppermute | solution.py:344
  583.1 21.2 %collective-permute-done.39 = bf16[1408,128]{1,0:T(8,128)(2,1)S(1)} collective-permute-done((bf16[1408,128]{1,0:T(8,128)(2,1)S(1)}, bf16[1408,128]{1,0:T(8,128)(2,1)S(1)}, u32[]{:S(2)}, u32[]{:S(2)}) %collective-permute-start.39) | collective-permute-done | bytes 360480 | tf_op jit(solution)/shard_map/ppermute | solution.py:344
  605.0 7.3 %collective-permute-done.41 = bf16[1408,128]{1,0:T(8,128)(2,1)S(1)} collective-permute-done((bf16[1408,128]{1,0:T(8,128)(2,1)S(1)}, bf16[1408,128]{1,0:T(8,128)(2,1)S(1)}, u32[]{:S(2)}, u32[]{:S(2)}) %collective-permute-start.41) | collective-permute-done | bytes 360480 | tf_op jit(solution)/shard_map/ppermute | solution.py:344
  615.2 1.8 convert_add_fusion.1
  617.8 1.6 convert_add_fusion
  620.8 4.5 collective-permute-start.11
  627.5 4.4 collective-permute-start.12
  632.1 6.1 collective-permute-start.3
  640.9 5.2 collective-permute-start.13
  646.1 3.9 collective-permute-start.4
  650.8 4.0 collective-permute-start.42
  657.5 5.2 collective-permute-start.5
  665.2 5.0 collective-permute-start.43
  673.3 3.3 collective-permute-done.45
  677.1 1.9 fusion.3
  680.7 5.0 collective-permute-start.44
  685.7 6.8 collective-permute-done.46
  695.9 8.3 %collective-permute-done.47 = bf16[3,704,128]{2,1,0:T(8,128)(2,1)S(1)} collective-permute-done((bf16[3,704,128]{2,1,0:T(8,128)(2,1)S(1)}, bf16[3,704,128]{2,1,0:T(8,128)(2,1)S(1)}, u32[]{:S(2)}, u32[]{:S(2)}) %collective-permute-start.47) | collective-permute-done | bytes 540704 | tf_op jit(solution)/shard_map/ppermute | solution.py:383
  (193 shorter events, 57.4 us)
Async XLA Ops:
  7.3 85.5 %all-gather.4.cloned.1.call-start = ((), (), s32[]{:S(2)}) async-start(), calls=%async_computation | async-start | bytes 8921088 | tf_op jit(solution)/shard_map/all_gather | solution.py:428
  11.4 200.7 %all-gather.6.cloned.1.call-start = ((), (), s32[]{:S(2)}) async-start(), calls=%async_computation.1 | async-start | bytes 17842176 | tf_op jit(solution)/shard_map/all_gather | solution.py:432
  308.5 77.4 %collective-permute-start.22 = (bf16[4,128,1024]{2,1,0:T(8,128)(2,1)}, bf16[4,128,1024]{2,1,0:T(8,128)(2,1)S(1)}, u32[]{:S(2)}, u32[]{:S(2)}) collective-permute-start(bf16[4,128,1024]{2,1,0:T(8,128)(2,1)} %grad_w.12), channel_id=1, source_target_pairs={{0,4},{4,0},{8,12},{12,8},{16,20},{20,16},{24,28},{28,24},{1,5},{5... | collective-permute-start | bytes 3145736 | tf_op jit(solution)/shard_map/ppermute | solution.py:344
  385.5 23.7 %collective-permute-start.17 = (f32[39,256]{1,0:T(8,128)S(1)}, f32[39,256]{1,0:T(8,128)S(1)}, u32[]{:S(2)}, u32[]{:S(2)}) collective-permute-start(f32[39,256]{1,0:T(8,128)S(1)} %reshape.140), channel_id=1, source_target_pairs={{0,4},{4,0},{8,12},{12,8},{16,20},{20,16},{24,28},{28,24},{1,5},{5... | collective-permute-start | bytes 119816 | tf_op jit(solution)/shard_map/ppermute | solution.py:344
  394.9 15.0 %collective-permute-start.23 = (bf16[2,128,1024]{2,1,0:T(8,128)(2,1)S(1)}, bf16[2,128,1024]{2,1,0:T(8,128)(2,1)S(1)}, u32[]{:S(2)}, u32[]{:S(2)}) collective-permute-start(bf16[2,128,1024]{2,1,0:T(8,128)(2,1)S(1)} %dynamic-slice_bitcast_fusion.6), channel_id=1, source_target_pairs={{0,16},{4,20},{8,24},{12,28},{16,0},{20,4},{24,8},{28,12},{1,17},{... | collective-permute-start | bytes 1572872 | tf_op jit(solution)/shard_map/ppermute | solution.py:344
  409.1 89.0 %collective-permute-start.31 = (bf16[4,2816,128]{2,1,0:T(8,128)(2,1)}, bf16[4,2816,128]{2,1,0:T(8,128)(2,1)}, u32[]{:S(2)}, u32[]{:S(2)}) collective-permute-start(bf16[4,2816,128]{2,1,0:T(8,128)(2,1)} %grad_w.14), channel_id=1, source_target_pairs={{0,4},{4,0},{8,12},{12,8},{16,20},{20,16},{24,28},{28,24},{1,5},{5... | collective-permute-start | bytes 8650760 | tf_op jit(solution)/shard_map/ppermute | solution.py:344
  409.2 15.3 %collective-permute-start.18 = (f32[39,256]{1,0:T(8,128)S(1)}, f32[39,256]{1,0:T(8,128)S(1)}, u32[]{:S(2)}, u32[]{:S(2)}) collective-permute-start(f32[39,256]{1,0:T(8,128)S(1)} %add.290), channel_id=1, source_target_pairs={{0,8},{4,12},{8,0},{12,4},{16,24},{20,28},{24,16},{28,20},{1,9},{5... | collective-permute-start | bytes 119816 | tf_op jit(solution)/shard_map/ppermute | solution.py:344
  410.1 15.2 %collective-permute-start.24 = (bf16[128,1024]{1,0:T(8,128)(2,1)S(1)}, bf16[128,1024]{1,0:T(8,128)(2,1)S(1)}, u32[]{:S(2)}, u32[]{:S(2)}) collective-permute-start(bf16[128,1024]{1,0:T(8,128)(2,1)S(1)} %fusion.15), channel_id=1, source_target_pairs={{0,8},{4,12},{8,0},{12,4},{16,24},{20,28},{24,16},{28,20},{1,9},{5... | collective-permute-start | bytes 786440 | tf_op jit(solution)/shard_map/ppermute | solution.py:344
  424.5 91.5 %collective-permute-start.34 = (bf16[4,2816,128]{2,1,0:T(8,128)(2,1)}, bf16[4,2816,128]{2,1,0:T(8,128)(2,1)}, u32[]{:S(2)}, u32[]{:S(2)}) collective-permute-start(bf16[4,2816,128]{2,1,0:T(8,128)(2,1)} %grad_w.16), channel_id=1, source_target_pairs={{0,4},{4,0},{8,12},{12,8},{16,20},{20,16},{24,28},{28,24},{1,5},{5... | collective-permute-start | bytes 8650760 | tf_op jit(solution)/shard_map/ppermute | solution.py:344
  424.6 26.2 %collective-permute-start.19 = (f32[39,256]{1,0:T(8,128)S(1)}, f32[39,256]{1,0:T(8,128)S(1)}, u32[]{:S(2)}, u32[]{:S(2)}) collective-permute-start(f32[39,256]{1,0:T(8,128)S(1)} %add.291), channel_id=1, source_target_pairs={{0,16},{4,20},{8,24},{12,28},{16,0},{20,4},{24,8},{28,12},{1,17},{... | collective-permute-start | bytes 119816 | tf_op jit(solution)/shard_map/ppermute | solution.py:344
  425.4 28.6 %collective-permute-start.25 = (bf16[32,1024]{1,0:T(8,128)(2,1)S(1)}, bf16[32,1024]{1,0:T(8,128)(2,1)S(1)}, u32[]{:S(2)}, u32[]{:S(2)}) collective-permute-start(bf16[32,1024]{1,0:T(8,128)(2,1)S(1)} %get-tuple-element.135), channel_id=1, source_target_pairs={{0,1},{1,2},{2,3},{4,5},{5,6},{6,7},{8,9},{9,10},{10,11},{12,13},{... | collective-permute-start | bytes 196616 | tf_op jit(solution)/shard_map/ppermute | solution.py:382
  450.8 20.4 %collective-permute-start.20 = (f32[39,256]{1,0:T(8,128)S(1)}, f32[39,256]{1,0:T(8,128)S(1)}, u32[]{:S(2)}, u32[]{:S(2)}) collective-permute-start(f32[39,256]{1,0:T(8,128)S(1)} %add.292), channel_id=1, source_target_pairs={{0,1},{1,0},{2,3},{3,2},{4,5},{5,4},{6,7},{7,6},{8,9},{9,8},{10,11... | collective-permute-start | bytes 119816 | tf_op jit(solution)/shard_map/ppermute | solution.py:344
  452.7 18.6 %collective-permute-start.28 = (bf16[32,1024]{1,0:T(8,128)(2,1)S(1)}, bf16[32,1024]{1,0:T(8,128)(2,1)S(1)}, u32[]{:S(2)}, u32[]{:S(2)}) collective-permute-start(bf16[32,1024]{1,0:T(8,128)(2,1)S(1)} %get-tuple-element.136), channel_id=1, source_target_pairs={{1,0},{2,1},{3,2},{5,4},{6,5},{7,6},{9,8},{10,9},{11,10},{13,12},{... | collective-permute-start | bytes 196616 | tf_op jit(solution)/shard_map/ppermute | solution.py:383
  454.0 17.4 %collective-permute-start.26 = (bf16[32,1024]{1,0:T(8,128)(2,1)S(1)}, bf16[32,1024]{1,0:T(8,128)(2,1)S(1)}, u32[]{:S(2)}, u32[]{:S(2)}) collective-permute-start(bf16[32,1024]{1,0:T(8,128)(2,1)S(1)} %fusion.29), channel_id=1, source_target_pairs={{0,1},{1,2},{2,3},{4,5},{5,6},{6,7},{8,9},{9,10},{10,11},{12,13},{... | collective-permute-start | bytes 196616 | tf_op jit(solution)/shard_map/ppermute | solution.py:382
  471.2 61.5 %collective-permute-start.37 = (bf16[4,2816,128]{2,1,0:T(8,128)(2,1)}, bf16[4,2816,128]{2,1,0:T(8,128)(2,1)}, u32[]{:S(2)}, u32[]{:S(2)}) collective-permute-start(bf16[4,2816,128]{2,1,0:T(8,128)(2,1)} %grad_w.18), channel_id=1, source_target_pairs={{0,4},{4,0},{8,12},{12,8},{16,20},{20,16},{24,28},{28,24},{1,5},{5... | collective-permute-start | bytes 8650760 | tf_op jit(solution)/shard_map/ppermute | solution.py:344
  471.3 15.3 %collective-permute-start.21 = (f32[39,256]{1,0:T(8,128)S(1)}, f32[39,256]{1,0:T(8,128)S(1)}, u32[]{:S(2)}, u32[]{:S(2)}) collective-permute-start(f32[39,256]{1,0:T(8,128)S(1)} %add.293), channel_id=1, source_target_pairs={{0,2},{1,3},{2,0},{3,1},{4,6},{5,7},{6,4},{7,5},{8,10},{9,11},{10,... | collective-permute-start | bytes 119816 | tf_op jit(solution)/shard_map/ppermute | solution.py:344
  471.5 19.8 %collective-permute-start.29 = (bf16[32,1024]{1,0:T(8,128)(2,1)S(1)}, bf16[32,1024]{1,0:T(8,128)(2,1)S(1)}, u32[]{:S(2)}, u32[]{:S(2)}) collective-permute-start(bf16[32,1024]{1,0:T(8,128)(2,1)S(1)} %get-tuple-element.134), channel_id=1, source_target_pairs={{1,0},{2,1},{3,2},{5,4},{6,5},{7,6},{9,8},{10,9},{11,10},{13,12},{... | collective-permute-start | bytes 196616 | tf_op jit(solution)/shard_map/ppermute | solution.py:383
  486.7 8.3 %collective-permute-start.27 = (bf16[32,1024]{1,0:T(8,128)(2,1)S(1)}, bf16[32,1024]{1,0:T(8,128)(2,1)S(1)}, u32[]{:S(2)}, u32[]{:S(2)}) collective-permute-start(bf16[32,1024]{1,0:T(8,128)(2,1)S(1)} %get-tuple-element.133), channel_id=1, source_target_pairs={{0,1},{1,2},{2,3},{4,5},{5,6},{6,7},{8,9},{9,10},{10,11},{12,13},{... | collective-permute-start | bytes 196616 | tf_op jit(solution)/shard_map/ppermute | solution.py:382
  495.0 57.1 %collective-permute-start = (bf16[4,128,3200]{2,1,0:T(8,128)(2,1)}, bf16[4,128,3200]{2,1,0:T(8,128)(2,1)}, u32[]{:S(2)}, u32[]{:S(2)}) collective-permute-start(bf16[4,128,3200]{2,1,0:T(8,128)(2,1)} %grad_w.10), channel_id=1, source_target_pairs={{0,4},{4,0},{8,12},{12,8},{16,20},{20,16},{24,28},{28,24},{1,5},{5... | collective-permute-start | bytes 9830408 | tf_op jit(solution)/shard_map/ppermute | solution.py:344
  514.6 100.6 %collective-permute-start.32 = (bf16[2,2816,128]{2,1,0:T(8,128)(2,1)}, bf16[2,2816,128]{2,1,0:T(8,128)(2,1)}, u32[]{:S(2)}, u32[]{:S(2)}) collective-permute-start(bf16[2,2816,128]{2,1,0:T(8,128)(2,1)} %dynamic-slice_bitcast_fusion.1), channel_id=1, source_target_pairs={{0,16},{4,20},{8,24},{12,28},{16,0},{20,4},{24,8},{28,12},{1,17},{... | collective-permute-start | bytes 4325384 | tf_op jit(solution)/shard_map/ppermute | solution.py:344
  532.1 85.7 %collective-permute-start.35 = (bf16[2,2816,128]{2,1,0:T(8,128)(2,1)}, bf16[2,2816,128]{2,1,0:T(8,128)(2,1)}, u32[]{:S(2)}, u32[]{:S(2)}) collective-permute-start(bf16[2,2816,128]{2,1,0:T(8,128)(2,1)} %dynamic-slice_bitcast_fusion), channel_id=1, source_target_pairs={{0,8},{4,12},{8,0},{12,4},{16,24},{20,28},{24,16},{28,20},{1,9},{5... | collective-permute-start | bytes 4325384 | tf_op jit(solution)/shard_map/ppermute | solution.py:344
  549.1 22.2 %collective-permute-start.38 = (bf16[2,1408,128]{2,1,0:T(8,128)(2,1)}, bf16[2,1408,128]{2,1,0:T(8,128)(2,1)}, u32[]{:S(2)}, u32[]{:S(2)}) collective-permute-start(bf16[2,1408,128]{2,1,0:T(8,128)(2,1)} %dynamic-slice_bitcast_fusion.5), channel_id=1, source_target_pairs={{0,16},{4,20},{8,24},{12,28},{16,0},{20,4},{24,8},{28,12},{1,17},{... | collective-permute-start | bytes 2162696 | tf_op jit(solution)/shard_map/ppermute | solution.py:344
  551.4 30.9 %collective-permute-start.40 = (bf16[2,1408,128]{2,1,0:T(8,128)(2,1)}, bf16[2,1408,128]{2,1,0:T(8,128)(2,1)S(1)}, u32[]{:S(2)}, u32[]{:S(2)}) collective-permute-start(bf16[2,1408,128]{2,1,0:T(8,128)(2,1)} %dynamic-slice_bitcast_fusion.4), channel_id=1, source_target_pairs={{0,8},{4,12},{8,0},{12,4},{16,24},{20,28},{24,16},{28,20},{1,9},{5... | collective-permute-start | bytes 2162696 | tf_op jit(solution)/shard_map/ppermute | solution.py:344
  569.8 43.7 %collective-permute-start.1 = (bf16[2,128,1664]{2,1,0:T(8,128)(2,1)S(1)}, bf16[2,128,1664]{2,1,0:T(8,128)(2,1)S(1)}, u32[]{:S(2)}, u32[]{:S(2)}) collective-permute-start(bf16[2,128,1664]{2,1,0:T(8,128)(2,1)S(1)} %dynamic-slice_bitcast_fusion.2), channel_id=1, source_target_pairs={{0,16},{4,20},{8,24},{12,28},{16,0},{20,4},{24,8},{28,12},{1,17},{... | collective-permute-start | bytes 2555912 | tf_op jit(solution)/shard_map/ppermute | solution.py:344
  571.4 41.1 %collective-permute-start.9 = (bf16[2,128,1536]{2,1,0:T(8,128)(2,1)S(1)}, bf16[2,128,1536]{2,1,0:T(8,128)(2,1)S(1)}, u32[]{:S(2)}, u32[]{:S(2)}) collective-permute-start(bf16[2,128,1536]{2,1,0:T(8,128)(2,1)S(1)} %dynamic-slice_bitcast_fusion.3), channel_id=1, source_target_pairs={{0,8},{4,12},{8,0},{12,4},{16,24},{20,28},{24,16},{28,20},{1,9},{5... | collective-permute-start | bytes 2359304 | tf_op jit(solution)/shard_map/ppermute | solution.py:344
  582.3 22.0 %collective-permute-start.39 = (bf16[1408,128]{1,0:T(8,128)(2,1)S(1)}, bf16[1408,128]{1,0:T(8,128)(2,1)S(1)}, u32[]{:S(2)}, u32[]{:S(2)}) collective-permute-start(bf16[1408,128]{1,0:T(8,128)(2,1)S(1)} %fusion.13), channel_id=1, source_target_pairs={{0,8},{4,12},{8,0},{12,4},{16,24},{20,28},{24,16},{28,20},{1,9},{5... | collective-permute-start | bytes 1081352 | tf_op jit(solution)/shard_map/ppermute | solution.py:344
  604.3 8.0 %collective-permute-start.41 = (bf16[1408,128]{1,0:T(8,128)(2,1)S(1)}, bf16[1408,128]{1,0:T(8,128)(2,1)S(1)}, u32[]{:S(2)}, u32[]{:S(2)}) collective-permute-start(bf16[1408,128]{1,0:T(8,128)(2,1)S(1)} %fusion.14), channel_id=1, source_target_pairs={{0,16},{4,20},{8,24},{12,28},{16,0},{20,4},{24,8},{28,12},{1,17},{... | collective-permute-start | bytes 1081352 | tf_op jit(solution)/shard_map/ppermute | solution.py:344
  612.8 7.8 %collective-permute-start.10 = (bf16[128,1536]{1,0:T(8,128)(2,1)S(1)}, bf16[128,1536]{1,0:T(8,128)(2,1)S(1)}, u32[]{:S(2)}, u32[]{:S(2)}) collective-permute-start(bf16[128,1536]{1,0:T(8,128)(2,1)S(1)} %fusion.12), channel_id=1, source_target_pairs={{0,16},{4,20},{8,24},{12,28},{16,0},{20,4},{24,8},{28,12},{1,17},{... | collective-permute-start | bytes 1179656 | tf_op jit(solution)/shard_map/ppermute | solution.py:344
  613.7 18.2 %collective-permute-start.2 = (bf16[128,1664]{1,0:T(8,128)(2,1)S(1)}, bf16[128,1664]{1,0:T(8,128)(2,1)S(1)}, u32[]{:S(2)}, u32[]{:S(2)}) collective-permute-start(bf16[128,1664]{1,0:T(8,128)(2,1)S(1)} %fusion.9), channel_id=1, source_target_pairs={{0,8},{4,12},{8,0},{12,4},{16,24},{20,28},{24,16},{28,20},{1,9},{5... | collective-permute-start | bytes 1277960 | tf_op jit(solution)/shard_map/ppermute | solution.py:344
  617.1 29.0 %collective-permute-start.33 = (bf16[2816,128]{1,0:T(8,128)(2,1)S(1)}, bf16[2816,128]{1,0:T(8,128)(2,1)S(1)}, u32[]{:S(2)}, u32[]{:S(2)}) collective-permute-start(bf16[2816,128]{1,0:T(8,128)(2,1)S(1)} %fusion.5), channel_id=1, source_target_pairs={{0,8},{4,12},{8,0},{12,4},{16,24},{20,28},{24,16},{28,20},{1,9},{5... | collective-permute-start | bytes 2162696 | tf_op jit(solution)/shard_map/ppermute | solution.py:344
  625.4 24.8 %collective-permute-start.36 = (bf16[2816,128]{1,0:T(8,128)(2,1)S(1)}, bf16[2816,128]{1,0:T(8,128)(2,1)S(1)}, u32[]{:S(2)}, u32[]{:S(2)}) collective-permute-start(bf16[2816,128]{1,0:T(8,128)(2,1)S(1)} %fusion.6), channel_id=1, source_target_pairs={{0,16},{4,20},{8,24},{12,28},{16,0},{20,4},{24,8},{28,12},{1,17},{... | collective-permute-start | bytes 2162696 | tf_op jit(solution)/shard_map/ppermute | solution.py:344
  626.1 12.1 %collective-permute-start.14 = (bf16[32,1536]{1,0:T(8,128)(2,1)S(1)}, bf16[32,1536]{1,0:T(8,128)(2,1)S(1)}, u32[]{:S(2)}, u32[]{:S(2)}) collective-permute-start(bf16[32,1536]{1,0:T(8,128)(2,1)S(1)} %get-tuple-element.132), channel_id=1, source_target_pairs={{1,0},{2,1},{3,2},{5,4},{6,5},{7,6},{9,8},{10,9},{11,10},{13,12},{... | collective-permute-start | bytes 294920 | tf_op jit(solution)/shard_map/ppermute | solution.py:383
  627.5 12.0 %collective-permute-start.12 = (bf16[32,1536]{1,0:T(8,128)(2,1)S(1)}, bf16[32,1536]{1,0:T(8,128)(2,1)S(1)}, u32[]{:S(2)}, u32[]{:S(2)}) collective-permute-start(bf16[32,1536]{1,0:T(8,128)(2,1)S(1)} %fusion.23), channel_id=1, source_target_pairs={{0,1},{1,2},{2,3},{4,5},{5,6},{6,7},{8,9},{9,10},{10,11},{12,13},{... | collective-permute-start | bytes 294920 | tf_op jit(solution)/shard_map/ppermute | solution.py:382
  632.1 8.8 %collective-permute-start.3 = (bf16[32,1664]{1,0:T(8,128)(2,1)S(1)}, bf16[32,1664]{1,0:T(8,128)(2,1)S(1)}, u32[]{:S(2)}, u32[]{:S(2)}) collective-permute-start(bf16[32,1664]{1,0:T(8,128)(2,1)S(1)} %get-tuple-element.127), channel_id=1, source_target_pairs={{0,1},{1,2},{2,3},{4,5},{5,6},{6,7},{8,9},{9,10},{10,11},{12,13},{... | collective-permute-start | bytes 319496 | tf_op jit(solution)/shard_map/ppermute | solution.py:382
  638.2 17.9 %collective-permute-start.6 = (bf16[32,1664]{1,0:T(8,128)(2,1)S(1)}, bf16[32,1664]{1,0:T(8,128)(2,1)S(1)}, u32[]{:S(2)}, u32[]{:S(2)}) collective-permute-start(bf16[32,1664]{1,0:T(8,128)(2,1)S(1)} %get-tuple-element.128), channel_id=1, source_target_pairs={{1,0},{2,1},{3,2},{5,4},{6,5},{7,6},{9,8},{10,9},{11,10},{13,12},{... | collective-permute-start | bytes 319496 | tf_op jit(solution)/shard_map/ppermute | solution.py:383
  639.6 15.2 %collective-permute-start.15 = (bf16[32,1536]{1,0:T(8,128)(2,1)S(1)}, bf16[32,1536]{1,0:T(8,128)(2,1)S(1)}, u32[]{:S(2)}, u32[]{:S(2)}) collective-permute-start(bf16[32,1536]{1,0:T(8,128)(2,1)S(1)} %get-tuple-element.130), channel_id=1, source_target_pairs={{1,0},{2,1},{3,2},{5,4},{6,5},{7,6},{9,8},{10,9},{11,10},{13,12},{... | collective-permute-start | bytes 294920 | tf_op jit(solution)/shard_map/ppermute | solution.py:383
  640.9 24.3 %collective-permute-start.13 = (bf16[32,1536]{1,0:T(8,128)(2,1)S(1)}, bf16[32,1536]{1,0:T(8,128)(2,1)S(1)}, u32[]{:S(2)}, u32[]{:S(2)}) collective-permute-start(bf16[32,1536]{1,0:T(8,128)(2,1)S(1)} %get-tuple-element.129), channel_id=1, source_target_pairs={{0,1},{1,2},{2,3},{4,5},{5,6},{6,7},{8,9},{9,10},{10,11},{12,13},{... | collective-permute-start | bytes 294920 | tf_op jit(solution)/shard_map/ppermute | solution.py:382
  646.1 10.0 %collective-permute-start.4 = (bf16[32,1664]{1,0:T(8,128)(2,1)S(1)}, bf16[32,1664]{1,0:T(8,128)(2,1)S(1)}, u32[]{:S(2)}, u32[]{:S(2)}) collective-permute-start(bf16[32,1664]{1,0:T(8,128)(2,1)S(1)} %fusion.18), channel_id=1, source_target_pairs={{0,1},{1,2},{2,3},{4,5},{5,6},{6,7},{8,9},{9,10},{10,11},{12,13},{... | collective-permute-start | bytes 319496 | tf_op jit(solution)/shard_map/ppermute | solution.py:382
  650.8 12.9 %collective-permute-start.42 = (bf16[3,704,128]{2,1,0:T(8,128)(2,1)S(1)}, bf16[3,704,128]{2,1,0:T(8,128)(2,1)S(1)}, u32[]{:S(2)}, u32[]{:S(2)}) collective-permute-start(bf16[3,704,128]{2,1,0:T(8,128)(2,1)S(1)} %get-tuple-element.118), channel_id=1, source_target_pairs={{0,1},{1,2},{2,3},{4,5},{5,6},{6,7},{8,9},{9,10},{10,11},{12,13},{... | collective-permute-start | bytes 1622024 | tf_op jit(solution)/shard_map/ppermute | solution.py:382
  654.8 15.4 %collective-permute-start.16 = (bf16[32,1536]{1,0:T(8,128)(2,1)S(1)}, bf16[32,1536]{1,0:T(8,128)(2,1)S(1)}, u32[]{:S(2)}, u32[]{:S(2)}) collective-permute-start(bf16[32,1536]{1,0:T(8,128)(2,1)S(1)} %fusion.22), channel_id=1, source_target_pairs={{1,0},{2,1},{3,2},{5,4},{6,5},{7,6},{9,8},{10,9},{11,10},{13,12},{... | collective-permute-start | bytes 294920 | tf_op jit(solution)/shard_map/ppermute | solution.py:383
  656.2 14.8 %collective-permute-start.7 = (bf16[32,1664]{1,0:T(8,128)(2,1)S(1)}, bf16[32,1664]{1,0:T(8,128)(2,1)}, u32[]{:S(2)}, u32[]{:S(2)}) collective-permute-start(bf16[32,1664]{1,0:T(8,128)(2,1)S(1)} %get-tuple-element.126), channel_id=1, source_target_pairs={{1,0},{2,1},{3,2},{5,4},{6,5},{7,6},{9,8},{10,9},{11,10},{13,12},{... | collective-permute-start | bytes 319496 | tf_op jit(solution)/shard_map/ppermute | solution.py:383
  657.5 22.9 %collective-permute-start.5 = (bf16[32,1664]{1,0:T(8,128)(2,1)S(1)}, bf16[32,1664]{1,0:T(8,128)(2,1)S(1)}, u32[]{:S(2)}, u32[]{:S(2)}) collective-permute-start(bf16[32,1664]{1,0:T(8,128)(2,1)S(1)} %get-tuple-element.125), channel_id=1, source_target_pairs={{0,1},{1,2},{2,3},{4,5},{5,6},{6,7},{8,9},{9,10},{10,11},{12,13},{... | collective-permute-start | bytes 319496 | tf_op jit(solution)/shard_map/ppermute | solution.py:382
  663.8 12.8 %collective-permute-start.45 = (bf16[3,704,128]{2,1,0:T(8,128)(2,1)S(1)}, bf16[3,704,128]{2,1,0:T(8,128)(2,1)S(1)}, u32[]{:S(2)}, u32[]{:S(2)}) collective-permute-start(bf16[3,704,128]{2,1,0:T(8,128)(2,1)S(1)} %get-tuple-element.119), channel_id=1, source_target_pairs={{1,0},{2,1},{3,2},{5,4},{6,5},{7,6},{9,8},{10,9},{11,10},{13,12},{... | collective-permute-start | bytes 1622024 | tf_op jit(solution)/shard_map/ppermute | solution.py:383
  665.2 11.9 %collective-permute-start.43 = (bf16[3,704,128]{2,1,0:T(8,128)(2,1)S(1)}, bf16[3,704,128]{2,1,0:T(8,128)(2,1)S(1)}, u32[]{:S(2)}, u32[]{:S(2)}) collective-permute-start(bf16[3,704,128]{2,1,0:T(8,128)(2,1)S(1)} %fusion.2), channel_id=1, source_target_pairs={{0,1},{1,2},{2,3},{4,5},{5,6},{6,7},{8,9},{9,10},{10,11},{12,13},{... | collective-permute-start | bytes 1622024 | tf_op jit(solution)/shard_map/ppermute | solution.py:382
  671.9 8.5 %collective-permute-start.8 = (bf16[32,1664]{1,0:T(8,128)(2,1)S(1)}, bf16[32,1664]{1,0:T(8,128)(2,1)S(1)}, u32[]{:S(2)}, u32[]{:S(2)}) collective-permute-start(bf16[32,1664]{1,0:T(8,128)(2,1)S(1)} %fusion.17), channel_id=1, source_target_pairs={{1,0},{2,1},{3,2},{5,4},{6,5},{7,6},{9,8},{10,9},{11,10},{13,12},{... | collective-permute-start | bytes 319496 | tf_op jit(solution)/shard_map/ppermute | solution.py:383
  679.0 13.5 %collective-permute-start.46 = (bf16[3,704,128]{2,1,0:T(8,128)(2,1)S(1)}, bf16[3,704,128]{2,1,0:T(8,128)(2,1)S(1)}, u32[]{:S(2)}, u32[]{:S(2)}) collective-permute-start(bf16[3,704,128]{2,1,0:T(8,128)(2,1)S(1)} %get-tuple-element.117), channel_id=1, source_target_pairs={{1,0},{2,1},{3,2},{5,4},{6,5},{7,6},{9,8},{10,9},{11,10},{13,12},{... | collective-permute-start | bytes 1622024 | tf_op jit(solution)/shard_map/ppermute | solution.py:383
  680.7 15.2 %collective-permute-start.44 = (bf16[3,704,128]{2,1,0:T(8,128)(2,1)S(1)}, bf16[3,704,128]{2,1,0:T(8,128)(2,1)S(1)}, u32[]{:S(2)}, u32[]{:S(2)}) collective-permute-start(bf16[3,704,128]{2,1,0:T(8,128)(2,1)S(1)} %get-tuple-element.116), channel_id=1, source_target_pairs={{0,1},{1,2},{2,3},{4,5},{5,6},{6,7},{8,9},{9,10},{10,11},{12,13},{... | collective-permute-start | bytes 1622024 | tf_op jit(solution)/shard_map/ppermute | solution.py:382
  692.6 11.5 %collective-permute-start.47 = (bf16[3,704,128]{2,1,0:T(8,128)(2,1)S(1)}, bf16[3,704,128]{2,1,0:T(8,128)(2,1)S(1)}, u32[]{:S(2)}, u32[]{:S(2)}) collective-permute-start(bf16[3,704,128]{2,1,0:T(8,128)(2,1)S(1)} %fusion.1), channel_id=1, source_target_pairs={{1,0},{2,1},{3,2},{5,4},{6,5},{7,6},{9,8},{10,9},{11,10},{13,12},{... | collective-permute-start | bytes 1622024 | tf_op jit(solution)/shard_map/ppermute | solution.py:383
  (19 other events, 219.0 us)
Sparse Core Ops, SparseCore 0:
  11.5 81.2 all-gather.3
  96.2 115.8 all-gather.5

commit v3 on v2

v3 whole, which is shorter than its diff:
```python
import functools

import jax
import jax.numpy as jnp
from jax import lax
from jax.experimental import pallas as pl
from jax.experimental.pallas import tpu as pltpu
from jax.sharding import PartitionSpec as P

F32 = jnp.float32
BF = jnp.bfloat16
EPS = 1e-5
LEN = 1024
BL = 64
H = 4
HK = 128
HV = 256
DK = 512
DV = 1024
CQ, CK, CV, CG, CR, CO = 0, 512, 1024, 2048, 3072, 3200
GW = 3200
SCALE = HK**-0.5
VMEM = 60 * 1024 * 1024


def nn(a,b): return lax.dot_general(a,b,(((1,),(0,)),((),())),preferred_element_type=F32)


def nt(a,b): return lax.dot_general(a,b,(((1,),(1,)),((),())),preferred_element_type=F32)


def tn(a,b): return lax.dot_general(a,b,(((0,),(0,)),((),())),preferred_element_type=F32)


def sigmoid(v): return 1.0/(1.0+jnp.exp(-v))


def softminus(x): return jnp.minimum(x,0.0)-jnp.log1p(jnp.exp(-jnp.abs(x)))


def split(x):
    hi=x.astype(BF); return hi,(x-hi.astype(F32)).astype(BF)


def doc_of(p,starts):
    out=(p>=starts[0]).astype(jnp.int32)
    for s in starts[1:]: out=out+(p>=s).astype(jnp.int32)
    return out


def tile_masks(base,T,starts):
    tc=lax.broadcasted_iota(jnp.int32,(T,1),0); tr=lax.broadcasted_iota(jnp.int32,(1,T),1)
    dc=doc_of(tc+base,starts); dr=doc_of(tr+base,starts)
    first=(tc & ~(BL-1))+base
    prior=jnp.where(first>0,doc_of(first-1,starts),-1)
    last=doc_of(first+(BL-1),starts)
    inter=(dc==prior); reach=(dc==last)
    same=(tc>>6)==(tr>>6)
    low=same&(tc>=tr)
    return inter,reach,same,low,low&(dc==dr)


def keep_of(first,starts):
    return jnp.where(first>0,(doc_of(first-1,starts)==doc_of(first+BL-1,starts)).astype(F32),0.0)


def starts_of(len_ref, seq):
    first = len_ref[seq * 4]
    second = first + len_ref[seq * 4 + 1]
    return [first, second, second + len_ref[seq * 4 + 2]]


def params(flops=1):
    return dict(
        compiler_params=pltpu.CompilerParams(vmem_limit_bytes=VMEM),
        cost_estimate=pl.CostEstimate(flops=flops, bytes_accessed=1, transcendentals=0),
    )


def fwd_kernel(NT,cuts,st_ref,at_ref,tok_ref,wdec_ref,bias_ref,hg_ref,*rest):
    pieces=rest[:len(cuts)]
    n_ref,q_ref,k_ref,cum_ref,dp_ref,v_ref,gp_ref,o_ref,bef_ref,mix_ref,rank_ref,gains_ref,wout_ref,state,w_ref,sems,out_sem=rest[len(cuts):]
    T=tok_ref.shape[0]; nb=T//BL
    i=pl.program_id(0); seq=i//NT; tile=i%NT; base=tile*T
    starts=starts_of(st_ref,seq)
    inter,reach,same,low,intra=tile_masks(base,T,starts)
    @pl.when(tile==0)
    def _(): state[...]=jnp.zeros_like(state)
    save=pltpu.make_async_copy(w_ref,wout_ref,out_sem)
    @pl.when(i==0)
    def _():
        copies=[]
        for j,(block,first,width) in enumerate(cuts):
            for z in range(4):
                rows=pl.ds(pl.multiple_of(at_ref[block]*128+at_ref[8+z]*32,32),32)
                copies.append(pltpu.make_async_copy(pieces[j].at[pl.ds(32*z,32)],w_ref.at[rows,pl.ds(first,width)],sems.at[j,z]))
        for c in copies: c.start()
        for c in copies: c.wait()
        save.start()
        gains_ref[...]=w_ref[:,CR:CR+128].astype(F32).T[16:24]
    @pl.when(i==pl.num_programs(0)-1)
    def _(): save.wait()
    x=tok_ref[...].astype(F32)
    r=lax.rsqrt(jnp.mean(x*x,axis=-1,keepdims=True)+EPS)
    n_ref[...]=(x*r*gains_ref[0:1]).astype(BF)
    n=n_ref[...]
    rank=nn(n,w_ref[:,CR:CR+128]).astype(BF)
    rank_ref[...]=rank
    dp=nn(rank,wdec_ref[...])+bias_ref[...]
    dp_ref[...]=dp
    dhi,dlo=split(softminus(dp)*(1.0/16.0))
    lowb=low.astype(BF)
    cum=nn(lowb,dhi)+nn(lowb,dlo)
    cum_ref[...]=cum
    q=nn(n,w_ref[:,CQ:CQ+DK])*SCALE; q_ref[...]=q
    k=nn(n,w_ref[:,CK:CK+DK]); k_ref[...]=k
    v_ref[...]=nn(n,w_ref[:,CV:CV+DV]).astype(BF)
    gp_ref[...]=nn(n,w_ref[:,CG:CG+DV]).astype(BF)
    interf=inter.astype(F32)
    ends=[cum[BL*b+BL-1:BL*b+BL,:] for b in range(nb)]
    endb=jnp.concatenate([jnp.broadcast_to(e,(BL,DK)) for e in ends],axis=0)
    qg=q*jnp.exp(cum)
    qgi=(qg*interf).astype(BF); qg=qg.astype(BF)
    kg=(k*jnp.exp(-cum)).astype(BF)
    kc=(k*jnp.exp(endb-cum)).astype(BF)
    keeps=jnp.concatenate([jnp.exp(ends[b])*keep_of(base+BL*b,starts) for b in range(nb)]+[jnp.zeros((8-nb,DK),F32)],axis=0)
    for h in range(H):
        a=slice(HK*h,HK*h+HK); c=slice(HV*h,HV*h+HV)
        v=v_ref[:,c]
        s=jnp.where(intra,nt(qg[:,a],kg[:,a]),0.0).astype(BF)
        vk=jnp.where(reach,v,jnp.zeros_like(v))
        kt=keeps[:,a].T
        o=nn(s,v)
        parts=[]
        st=state[h]
        for b in range(nb):
            t=slice(BL*b,BL*b+BL)
            sb=st.astype(BF)
            bef_ref[b,h]=sb
            parts.append(nn(qgi[t,a],sb))
            st=st*kt[:,b:b+1]+tn(kc[t,a],vk[t])
        state[h]=st
        o=o+jnp.concatenate(parts,axis=0)
        o_ref[:,c]=o
        sc=lax.rsqrt(jnp.maximum(jnp.mean(o*o,axis=-1,keepdims=True),1.0))
        gp=gp_ref[:,c].astype(F32)
        mix_ref[:,c]=(o*sc*hg_ref[...]*(gp*sigmoid(gp))).astype(BF)


def fwd_call(st,at,tok,pieces,wdec,bias,hg,T=256):
    n,d=tok.shape; NT=LEN//T; sd=jax.ShapeDtypeStruct
    row=lambda x: pl.BlockSpec((T,x),lambda i,*s:(i,0))
    const=lambda a: pl.BlockSpec(a.shape,lambda i,*s:(0,0),pipeline_mode=pl.Buffered(1))
    hbm=pl.BlockSpec(memory_space=pl.ANY)
    nb=T//BL
    outs=[(d,BF),(DK,F32),(DK,F32),(DK,F32),(DK,F32),(DV,BF),(DV,BF),(DV,F32),None,(DV,BF),(128,BF)]
    specs=[row(o[0]) if o else pl.BlockSpec((nb,H,HK,HV),lambda i,*s:(i,0,0,0)) for o in outs]
    shapes=[sd((n,o[0]),o[1]) if o else sd((n//BL,H,HK,HV),BF) for o in outs]
    cuts=[(p[1],p[2],p[0].shape[1]) for p in pieces]
    return pl.pallas_call(functools.partial(fwd_kernel,NT,cuts),
        grid_spec=pltpu.PrefetchScalarGridSpec(num_scalar_prefetch=2,grid=(n//T,),
            in_specs=[row(d),const(wdec),const(bias),const(hg)]+[hbm]*len(pieces),out_specs=specs+[pl.BlockSpec((8,d),lambda i,*s:(0,0)),hbm],
            scratch_shapes=[pltpu.VMEM((H,HK,HV),F32),pltpu.VMEM((d,GW),BF),pltpu.SemaphoreType.DMA((len(pieces),4)),pltpu.SemaphoreType.DMA]),
        out_shape=shapes+[sd((8,d),F32),sd((d,GW),BF)],name="mixer_fwd",**params())(st,at,tok,wdec,bias,hg,*[p[0] for p in pieces])


def bwd_kernel(NT,seq,st_ref,gmix_ref,w_ref,wdec_ref,hg_ref,q_ref,k_ref,cum_ref,dp_ref,v_ref,gp_ref,o_ref,bef_ref,rank_ref,*rest):
    g_ref,dwd_ref,db_ref,dhg_ref,state=rest[-5:]
    T=q_ref.shape[0]; nb=T//BL
    step=pl.program_id(0); tile=NT-1-step; base=tile*T
    starts=starts_of(st_ref,seq)
    inter,reach,same,low,intra=tile_masks(base,T,starts)
    @pl.when(tile==NT-1)
    def _(): state[...]=jnp.zeros_like(state)
    @pl.when(step==0)
    def _():
        dwd_ref[...]=jnp.zeros_like(dwd_ref); db_ref[...]=jnp.zeros_like(db_ref); dhg_ref[...]=jnp.zeros_like(dhg_ref)
    cum=cum_ref[...]
    ends=[cum[BL*b+BL-1:BL*b+BL,:] for b in range(nb)]
    endb=jnp.concatenate([jnp.broadcast_to(e,(BL,DK)) for e in ends],axis=0)
    eg=jnp.exp(cum); es=jnp.exp(-cum); ec=jnp.exp(endb-cum)
    kend=jnp.concatenate([jnp.exp(ends[b])*keep_of(base+BL*b,starts) for b in range(nb)]+[jnp.zeros((8-nb,DK),F32)],axis=0)
    interb=inter.astype(F32).astype(BF); reachf=reach.astype(F32)
    tc=lax.broadcasted_iota(jnp.int32,(T,1),0); tr=lax.broadcasted_iota(jnp.int32,(1,T),1)
    upb=(same&(tc<=tr)).astype(BF); lsb=(same&(tc>tr)).astype(BF)
    hg=hg_ref[...]
    ones=jnp.ones((8,HV),BF)
    for h in range(H):
        a=slice(HK*h,HK*h+HK); c=slice(HV*h,HV*h+HV)
        gi=nn(gmix_ref[...],w_ref[:,HV*h:HV*h+HV])
        o=o_ref[:,c]; gp=gp_ref[:,c].astype(F32)
        ms=jnp.mean(o*o,axis=-1,keepdims=True)
        sc=lax.rsqrt(jnp.maximum(ms,1.0))
        hn0=o*sc
        s=sigmoid(gp); si=gp*s
        g_ref[:,CG+HV*h:CG+HV*h+HV]=(gi*hn0*hg*(s+si*(1.0-s))).astype(BF)
        G=gi*si
        dhg_ref[...]+=jnp.sum((G*hn0).reshape(-1,8,HV),axis=0)
        G=G*hg
        innr=jnp.mean(G*o,axis=-1,keepdims=True)*jnp.where(ms>1.0,1.0,0.0)
        go=(sc*G-o*(sc*sc*sc*innr)).astype(BF)
        goi=go*interb
        v=v_ref[:,c]
        qs=q_ref[:,a]*eg[:,a]; ks=k_ref[:,a]*es[:,a]; kd=k_ref[:,a]*ec[:,a]
        qg=qs.astype(BF); kg=ks.astype(BF); kc=kd.astype(BF)
        sco=jnp.where(intra,nt(qg,kg),0.0).astype(BF)
        gs=jnp.where(intra,nt(go,v),0.0).astype(BF)
        gv=tn(sco,go); gq=nn(gs,kg); gk=tn(gs,qg)
        kt=kend[:,a].T
        st=state[h]
        p_gv=[None]*nb; p_gq=[None]*nb; p_gkc=[None]*nb; p_end=[None]*nb
        for b in reversed(range(nb)):
            t=slice(BL*b,BL*b+BL)
            bef=bef_ref[b,h]
            sb=st.astype(BF)
            p_gv[b]=nn(kc[t],sb)
            p_gq[b]=nt(goi[t],bef)
            p_gkc[b]=nt(v[t],sb)
            m1,m2=split(st*bef.astype(F32))
            p_end[b]=(nt(ones,m1)+nt(ones,m2))[0:1]*kend[b:b+1,a]
            st=(tn(qg[t],goi[t])+kt[:,b:b+1]*st).astype(BF).astype(F32)
        state[h]=st
        cat=lambda p: jnp.concatenate(p,axis=0)
        gv=gv+cat(p_gv)*reachf
        g_ref[:,CV+HV*h:CV+HV*h+HV]=gv.astype(BF)
        gq=gq+cat(p_gq)
        gkc=cat(p_gkc)*reachf
        av1,av2=split(gq*qs-gk*ks)
        c1,c2=split(gkc*kd)
        endr=cat([jnp.broadcast_to(p,(BL,HK)) for p in p_end])
        gd=nn(upb,av1)+nn(upb,av2)+nn(lsb,c1)+nn(lsb,c2)+endr
        g_ref[:,CQ+HK*h:CQ+HK*h+HK]=(gq*eg[:,a]*SCALE).astype(BF)
        g_ref[:,CK+HK*h:CK+HK*h+HK]=(gk*es[:,a]+gkc*ec[:,a]).astype(BF)
        dp=dp_ref[:,a]
        gpre=(gd*(1.0/16.0)*(1.0/(1.0+jnp.exp(dp)))).astype(BF)
        db_ref[:,a]+=jnp.sum(gpre.astype(F32).reshape(-1,8,HK),axis=0)
        dwd_ref[:,a]+=tn(rank_ref[...],gpre)
        gr=nt(gpre,wdec_ref[:,a])
        grank=gr if h==0 else grank+gr
    g_ref[:,CR:CR+128]=grank.astype(BF)


def bwd_call(seq,before_g,deps,st,gmix,w,wdec,hg,q,k,cum,dp,v,gp,o,bef,rank,T=256):
    n,d=gmix.shape; NT=LEN//T; sd=jax.ShapeDtypeStruct; top=seq*NT+NT-1
    row=lambda a: pl.BlockSpec((T,a.shape[1]),lambda i,s:(top-i,0))
    const=lambda a: pl.BlockSpec(a.shape,lambda i,s:(0,0),pipeline_mode=pl.Buffered(1))
    hbm=pl.BlockSpec(memory_space=pl.ANY)
    nb=T//BL
    acc=lambda s: pl.BlockSpec(s,lambda i,_:(0,0))
    more=list(deps)+([before_g] if before_g is not None else [])
    return pl.pallas_call(functools.partial(bwd_kernel,NT,seq),
        grid_spec=pltpu.PrefetchScalarGridSpec(num_scalar_prefetch=1,grid=(NT,),
            in_specs=[row(gmix),const(w),const(wdec),const(hg),row(q),row(k),row(cum),row(dp),row(v),row(gp),row(o),pl.BlockSpec((nb,H,HK,HV),lambda i,s:(top-i,0,0,0)),row(rank)]+[hbm]*len(more),
            out_specs=[pl.BlockSpec((T,GW),lambda i,s:(top-i,0)),acc((128,DK)),acc((8,DK)),acc((8,HV))],
            scratch_shapes=[pltpu.VMEM((H,HK,HV),F32)]),
        input_output_aliases={} if before_g is None else {13+len(more):0},
        out_shape=[sd((n,GW),BF),sd((128,DK),F32),sd((8,DK),F32),sd((8,HV),F32)],
        name="mixer_bwd",**params())(st,gmix,w,wdec,hg,q,k,cum,dp,v,gp,o,bef,rank,*more)


def dx_kernel(g_ref,w_ref,tok_ref,gain_ref,gres_ref,*rest):
    gt_ref=rest[-1]
    gm=nt(g_ref[...],w_ref[...])
    x=tok_ref[...].astype(F32)
    r=lax.rsqrt(jnp.mean(x*x,axis=-1,keepdims=True)+EPS)
    sc=gm*gain_ref[...]
    inner=jnp.mean(sc*x,axis=-1,keepdims=True)
    gt_ref[...]=gres_ref[...]+r*sc-x*(r*r*r*inner)


def dx_call(part,parts,begun,g,w,tok,gain,gres,deps,T=256):
    n,d=tok.shape; sd=jax.ShapeDtypeStruct; steps=n//T//parts; first=part*steps
    row=lambda a: pl.BlockSpec((T,a.shape[1]),lambda i:(first+i,0))
    const=lambda a: pl.BlockSpec(a.shape,lambda i:(0,0),pipeline_mode=pl.Buffered(1))
    hbm=pl.BlockSpec(memory_space=pl.ANY)
    more=list(deps)+([] if begun is None else [begun])
    return pl.pallas_call(dx_kernel,grid=(steps,),in_specs=[row(g),const(w),row(tok),const(gain),row(gres)]+[hbm]*len(more),
        out_specs=row(gres),out_shape=sd((n,d),F32),input_output_aliases={} if begun is None else {4+len(more):0},
        name="mixer_dx",**params(5*10**10))(g,w,tok,gain,gres,*more)


def load_w(w_hbm,w_ref,sems,stacks):
    blocks,mlps,_,_=w_hbm.shape
    hid=w_ref.shape[1]//mlps
    copies=[pltpu.make_async_copy(w_hbm.at[r,m,pl.ds(s*hid,hid)],w_ref.at[i,pl.ds(m*hid,hid),pl.ds(r*128,128)],sems.at[i,r,m]) for i,s in enumerate(stacks) for m in range(mlps) for r in range(blocks)]
    for c in copies: c.start()
    for c in copies: c.wait()


def mlp_kernel(chunk,tok_ref,mix_ref,cot_ref,gain_ref,wo_ref,w_hbm,res_ref,n_ref,hid_ref,gg_ref,gu_ref,gres_ref,gmix_ref,gn_ref,w_ref,sems):
    @pl.when(pl.program_id(0)==0)
    def _(): load_w(w_hbm,w_ref,sems,(0,1,2))
    wg_ref,wu_ref,wd_ref=w_ref.at[0],w_ref.at[1],w_ref.at[2]
    res=tok_ref[...].astype(F32)+nt(mix_ref[...],wo_ref[...])
    res_ref[...]=res
    gain=gain_ref[...]
    r=lax.rsqrt(jnp.mean(res*res,axis=-1,keepdims=True)+EPS)
    n_ref[...]=(res*r*gain).astype(BF)
    ff=wg_ref.shape[0]
    for c in range(ff//chunk):
        sl=slice(c*chunk,(c+1)*chunk)
        n=n_ref[...]
        gp=nt(n,wg_ref[sl,:]); up=nt(n,wu_ref[sl,:]); gh=nt(cot_ref[...],wd_ref[sl,:])
        s=sigmoid(gp)
        si=gp*s
        hid_ref[:,sl]=(si*up).astype(BF)
        gu_ref[:,sl]=(gh*si).astype(BF)
        gg_ref[:,sl]=(gh*up*(s+si*(1.0-s))).astype(BF)
    gm=nn(gg_ref[...],wg_ref[...])+nn(gu_ref[...],wu_ref[...])
    res=res_ref[...]
    sc=gm*gain
    inner=jnp.mean(sc*res,axis=-1,keepdims=True)
    gi=r*sc-res*(r*r*r*inner)
    gres=cot_ref[...].astype(F32)+gi
    gres_ref[...]=gres
    gmix_ref[...]=gres.astype(BF)
    part=jnp.sum((gm*res*r).reshape(-1,8,gm.shape[1]),axis=0)
    @pl.when(pl.program_id(0)==0)
    def _(): gn_ref[...]=part
    @pl.when(pl.program_id(0)>0)
    def _(): gn_ref[...]+=part


def mlp_call(tok,mix,cot,gain,wo,w,ff,T=256,chunk=256):
    n,d=tok.shape
    row=lambda w: pl.BlockSpec((T,w),lambda i:(i,0))
    const=lambda a: pl.BlockSpec(a.shape,lambda i:(0,0),pipeline_mode=pl.Buffered(1))
    sd=jax.ShapeDtypeStruct
    return pl.pallas_call(functools.partial(mlp_kernel,chunk),grid=(n//T,),
        in_specs=[row(d),row(d),row(d),const(gain),const(wo),pl.BlockSpec(memory_space=pl.ANY)],
        out_specs=[row(d),row(d),row(ff),row(ff),row(ff),row(d),row(d),pl.BlockSpec((8,d),lambda i:(0,0))],
        out_shape=[sd((n,d),F32),sd((n,d),BF),sd((n,ff),BF),sd((n,ff),BF),sd((n,ff),BF),sd((n,d),F32),sd((n,d),BF),sd((8,d),F32)],
        scratch_shapes=[pltpu.VMEM((3,ff,d),BF),pltpu.SemaphoreType.DMA((3,)+w.shape[:2])],
        name="mlp",**params())(tok,mix,cot,gain,wo,w)


def down_kernel(res_ref,hid_ref,w_hbm,*rest):
    o_ref,w_ref,sems=rest[-3:]
    @pl.when(pl.program_id(0)==0)
    def _(): load_w(w_hbm,w_ref,sems,(2,))
    o_ref[...]=(res_ref[...]+nn(hid_ref[...],w_ref[0])).astype(BF)


def down_call(part,parts,begun,res,hid,w,deps,T=256):
    n,d=res.shape; ff=hid.shape[1]; steps=n//T//parts; first=part*steps
    row=lambda w: pl.BlockSpec((T,w),lambda i:(first+i,0))
    hbm=pl.BlockSpec(memory_space=pl.ANY)
    more=list(deps)+([] if begun is None else [begun])
    return pl.pallas_call(down_kernel,grid=(steps,),in_specs=[row(d),row(ff),hbm]+[hbm]*len(more),out_specs=row(d),
        out_shape=jax.ShapeDtypeStruct((n,d),BF),input_output_aliases={} if begun is None else {2+len(more):0},
        scratch_shapes=[pltpu.VMEM((1,ff,d),BF),pltpu.SemaphoreType.DMA((1,)+w.shape[:2])],
        name="mlp_down",**params())(res,hid,w,*more)


def dw_kernel(count,wide,sel_ref,*rest):
    g_refs=rest[:count]; x_hbm=rest[count]
    outs=rest[-2*count-2:-2]; xp,sems=rest[-2:]
    i=pl.program_id(0); steps=pl.num_programs(0)//count
    @pl.when(i==0)
    def _():
        copies=[]
        for p in range(2):
            for j in range(4):
                at=pl.multiple_of((2*j+(1-sel_ref[0] if p==0 else sel_ref[0]))*128,128)
                copies.append(pltpu.make_async_copy(x_hbm.at[:,pl.ds(at,128)],xp.at[:,pl.ds(512*p+128*j,128)],sems.at[p,j]))
        for c in copies: c.start()
        for c in copies: c.wait()
    for s in range(count):
        @pl.when(i//steps==s)
        def _():
            o=tn(g_refs[s][...],xp[...]) if wide else tn(xp[...],g_refs[s][...])
            for p in range(2):
                for j in range(4):
                    b=slice(512*p+128*j,512*p+128*j+128)
                    outs[2*s+p][j]=(o[:,b] if wide else o[b,:]).astype(BF)


def dw_call(gs,x,sel,deps,chunk,wide=True):
    n,ff=gs[0].shape; d=x.shape[1]; steps=ff//chunk; count=len(gs)
    hbm=pl.BlockSpec(memory_space=pl.ANY)
    spot=lambda i,s: jnp.clip(i-s*steps,0,steps-1)
    def out(s):
        return pl.BlockSpec((4,chunk,128),lambda i,_:(0,spot(i,s),0)) if wide else pl.BlockSpec((4,128,chunk),lambda i,_:(0,0,spot(i,s)))
    def inp(s):
        return pl.BlockSpec((n,chunk),lambda i,_:(0,spot(i,s)))
    return pl.pallas_call(functools.partial(dw_kernel,count,wide),
        grid_spec=pltpu.PrefetchScalarGridSpec(num_scalar_prefetch=1,grid=(steps*count,),
            in_specs=[inp(s) for s in range(count)]+[hbm]*(1+len(deps)),
            out_specs=[out(s) for s in range(count) for _ in range(2)],
            scratch_shapes=[pltpu.VMEM((n,d),BF),pltpu.SemaphoreType.DMA((2,4))]),
        out_shape=[jax.ShapeDtypeStruct((4,ff,128) if wide else (4,128,ff),BF)]*(2*count),
        name="grad_w",**params(10**11 if wide else 1))(sel,*gs,x,*deps)


def plane_kernel(count,at_ref,*rest):
    ins,outs=rest[:2*count],rest[-4:]
    for j in range(4):
        row=0
        for t in range(count):
            keep,came=ins[2*t],ins[2*t+1]
            rows=keep.shape[1]
            outs[j][0,row:row+rows]=(keep[at_ref[j]].astype(F32)+came[at_ref[j]].astype(F32)).astype(BF)
            row+=rows


def plane_call(pairs,at,deps,steps=8):
    each=[p[0].shape[1]//steps for p in pairs]
    return pl.pallas_call(functools.partial(plane_kernel,len(pairs)),
        grid_spec=pltpu.PrefetchScalarGridSpec(num_scalar_prefetch=1,grid=(steps,),
            in_specs=[pl.BlockSpec((4,r,128),lambda i,_:(0,i,0)) for r in each for _ in range(2)]+[pl.BlockSpec(memory_space=pl.ANY)]*len(deps),
            out_specs=[pl.BlockSpec((1,sum(each),128),lambda i,_:(i,0,0))]*4),
        out_shape=[jax.ShapeDtypeStruct((steps,sum(each),128),BF)]*4,name="plane",**params())(at,*[x for p in pairs for x in p],*deps)


def line_kernel(at_ref,*rest):
    ins=rest[:4]
    scr,turned=rest[-2:]; outs=rest[-6:-2]
    steps,rows,_=ins[0].shape
    main=rows-128
    for i in range(steps):
        v=functools.reduce(jnp.add,[x[i].astype(F32) for x in ins])
        scr[i]=v[:main].astype(BF)
        turned[i]=v[main:].T.astype(BF)
    each=steps//4
    for k in range(4):
        for e in range(each):
            outs[k][e*main:(e+1)*main]=scr[at_ref[k]*each+e]
        at=pl.multiple_of(at_ref[k]*32,32)
        for i in range(steps):
            outs[k][each*main+32*i:each*main+32*(i+1)]=turned[i,pl.ds(at,32)]


def line_call(parts,at,deps):
    steps,rows,_=parts[0].shape
    out=steps//4*(rows-128)+steps*32
    full=pl.BlockSpec(parts[0].shape,lambda i,_:(0,0,0))
    return pl.pallas_call(line_kernel,
        grid_spec=pltpu.PrefetchScalarGridSpec(num_scalar_prefetch=1,grid=(1,),
            in_specs=[full]*4+[pl.BlockSpec(memory_space=pl.ANY)]*len(deps),
            out_specs=[pl.BlockSpec((out,128),lambda i,_:(0,0))]*4,
            scratch_shapes=[pltpu.VMEM((steps,rows-128,128),BF),pltpu.VMEM((steps,128,128),BF)]),
        out_shape=[jax.ShapeDtypeStruct((out,128),BF)]*4,name="line",**params())(at,*parts,*deps)


def spread_kernel(sizes,count,at_ref,*rest):
    outs=rest[-count:]
    for j in range(count):
        first=k=0
        for stacks,parts in sizes:
            for t in range(stacks):
                v=rest[k][t,at_ref[j]].astype(F32)
                for p in range(1,parts): v=v+rest[k+p][t,at_ref[j]].astype(F32)
                outs[j][first+t]=v.astype(BF)
            first+=stacks; k+=parts


def spread(groups,at,axis,chunk,deps):
    _,count,rows,cols=groups[0][0].shape
    size=[rows,cols]; size[axis]=chunk
    place=(lambda i: (i,0)) if axis==0 else (lambda i: (0,i))
    stacks=sum(g[0].shape[0] for g in groups)
    return pl.pallas_call(functools.partial(spread_kernel,[(g[0].shape[0],len(g)) for g in groups],count),
        grid_spec=pltpu.PrefetchScalarGridSpec(num_scalar_prefetch=1,grid=((rows,cols)[axis]//chunk,),
            in_specs=[pl.BlockSpec((g[0].shape[0],count,*size),lambda i,_:(0,0,*place(i))) for g in groups for p in g]+[pl.BlockSpec(memory_space=pl.ANY)]*len(deps),
            out_specs=[pl.BlockSpec((stacks,*size),lambda i,_:(0,*place(i)))]*count),
        out_shape=[jax.ShapeDtypeStruct((stacks,rows,cols),BF)]*count,name="spread",**params())(at,*[p for g in groups for p in g],*deps)


def sum_kernel(count,*refs):
    refs[-1][...]=functools.reduce(jnp.add,[r[...].astype(F32) for r in refs[:count]])


def sum_call(parts,deps):
    full=pl.BlockSpec(parts[0].shape,lambda i:(0,)*parts[0].ndim)
    return pl.pallas_call(functools.partial(sum_kernel,len(parts)),grid=(1,),
        in_specs=[full]*len(parts)+[pl.BlockSpec(memory_space=pl.ANY)]*len(deps),out_specs=full,
        out_shape=jax.ShapeDtypeStruct(parts[0].shape,F32),name="sum_parts",**params())(*parts,*deps)


def rows_kernel(x_ref,*rest):
    rest[-1][...]=jnp.sum(x_ref[...],axis=0)


def rows_call(x,deps):
    return pl.pallas_call(rows_kernel,grid=(1,),
        in_specs=[pl.BlockSpec(x.shape,lambda i:(0,0,0))]+[pl.BlockSpec(memory_space=pl.ANY)]*len(deps),
        out_specs=pl.BlockSpec(x.shape[1:],lambda i:(0,0)),
        out_shape=jax.ShapeDtypeStruct(x.shape[1:],F32),name="sum_rows",**params())(x,*deps)


def swap(x, axis, bit, count):
    return lax.ppermute(x, axis, [(i, i ^ (1 << bit)) for i in range(count)])


def bit_of(axis, bit):
    return (lax.axis_index(axis) >> bit) & 1


def halve(x, dim, bit, count):
    place = bit_of("rows", bit)
    send = lax.dynamic_index_in_dim(x, 1 - place, dim, keepdims=False)
    keep = lax.dynamic_index_in_dim(x, place, dim, keepdims=False)
    return keep.astype(F32) + swap(send.astype(BF), "rows", bit, count).astype(F32)


def total(parts):
    return functools.reduce(jnp.add, [p.astype(F32) for p in parts])


def send_blocks(blocks, low, count):
    return [blocks[0]] + [
        lax.ppermute(blocks[j], "rows", [(i, i ^ (j << (low + 1))) for i in range(count)]) for j in range(1, 4)
    ]


def send_line(blocks, count):
    return [blocks[0]] + [
        lax.ppermute(blocks[j], "mlp", [(i, (i + j) % count) for i in range(count)]) for j in range(1, count)
    ]


def gather_pieces(x, low, mlps):
    half = x.shape[1] // 256 * 128
    line = [x] + [lax.ppermute(x, "mlp", [(i, (i + step) % mlps) for i in range(mlps)]) for step in range(1, mlps)]
    pieces = []
    for first, cols, bits in ((0, slice(0, half), (1, 2)), (half, slice(half, None), (2, 1))):
        held = [(jnp.concatenate([p[:, cols] for p in line], axis=0), 0)]
        for bit in bits + (0,):
            held = held + [(swap(p, "rows", bit, 8), at ^ (1 << bit)) for p, at in held]
        pieces += [(p, at, first) for p, at in held]
    return pieces


def body(
    tokens,
    doc_lengths,
    cotangent,
    norm_gain_mix,
    w_query,
    w_key,
    w_value,
    w_outgate,
    w_rank,
    w_decay,
    decay_bias,
    head_gain,
    w_output,
    norm_gain_mlp,
    w_gate,
    w_up,
    w_down,
):
    rows = lax.axis_size("rows")
    mlps = lax.axis_size("mlp")
    low = rows.bit_length() - 4
    shard = w_query.shape[0]
    hid, wide = w_down.shape
    lens = doc_lengths.reshape(-1)
    mixer_local = jnp.concatenate(
        [
            w_query, w_key, w_value, w_outgate, w_rank,
            norm_gain_mix[:, None], norm_gain_mlp[:, None], jnp.zeros((shard, 110), BF),
        ],
        axis=1,
    )
    mlp_local = jnp.concatenate([w_gate.T, w_up.T, w_down], axis=0)
    here = lax.axis_index("rows")
    if low == 0:
        local = [mlp_local, w_output.T.reshape(shard, 8, 128).transpose(1, 0, 2).reshape(8 * shard, 128)]
        mlp_all = lax.all_gather(jnp.concatenate(local, axis=0), ("rows", "mlp"), axis=0)
        w_out = mlp_all[:, 3 * hid :].reshape(rows * mlps, 8, shard, 128).transpose(0, 2, 1, 3).reshape(-1, DV)
        mlp_all = mlp_all.reshape(rows, mlps, 3 * hid + 8 * shard, 128)
        pieces = gather_pieces(mixer_local, low, mlps)
        at = jnp.concatenate([jnp.arange(8) ^ here, (lax.axis_index("mlp") - jnp.arange(mlps)) % mlps])
    else:
        mlp_all = lax.all_gather(mlp_local, ("rows", "mlp"), axis=0)
        mlp_all = mlp_all.reshape(8, rows // 8, mlps, 3 * hid, wide).transpose(0, 2, 3, 1, 4)
        mlp_all = mlp_all.reshape(8, mlps, 3 * hid, 128)
        w_out = lax.all_gather(w_output.T, ("rows", "mlp"), axis=0, tiled=True)
        whole = lax.all_gather(mixer_local, ("rows", "mlp"), axis=0, tiled=True)
        pieces = [(whole[128 * b : 128 * b + 128], b, 0) for b in range(8)]
        at = jnp.concatenate([jnp.arange(8), jnp.arange(4)])
    decay_wide = jnp.concatenate([w_decay, jnp.zeros((112, DK), BF)], axis=0)
    head_row = head_gain.astype(F32)[None]
    normed_in, q, k, cum, dp, v, gp, o, before, mixed, rank, gains, w_in = fwd_call(
        lens, at.astype(jnp.int32), tokens, pieces, decay_wide, decay_bias.astype(F32)[None], head_row
    )
    gain_mix, gain_mlp = gains[:1], gains[1:2]
    residual, normed_mid, hidden, grad_gate, grad_up, grad_res, grad_mixed, gain_mlp_part = mlp_call(
        tokens, mixed, cotangent, gain_mlp, w_out, mlp_all, mlps * hid
    )
    mine = bit_of("rows", low).astype(jnp.int32)[None]

    def with_other_core(send, keep):
        return [keep, swap(send, "rows", low, rows)]

    def within(parts, dim):
        if not low:
            return parts
        x = total(parts)
        x = x.reshape(x.shape[:dim] + (2,) * low + (x.shape[dim] >> low,) + x.shape[dim + 1 :])
        for bit in reversed(range(low)):
            x = halve(x, dim, bit, rows)
        return [x.astype(BF)]

    in_plane = ((here >> (low + 1)) ^ jnp.arange(4)).astype(jnp.int32)
    in_line = ((lax.axis_index("mlp") + jnp.arange(mlps)) % mlps).astype(jnp.int32)
    down_send, down_keep = dw_call([hidden], cotangent, mine, [normed_mid], 1408)
    down = with_other_core(down_send, down_keep)
    gate_send, gate_keep, up_send, up_keep = dw_call([grad_gate, grad_up], normed_mid, mine, [down_keep], 1408)
    gate = with_other_core(gate_send, gate_keep)
    up = with_other_core(up_send, up_keep)
    out_send, out_keep = dw_call([mixed], grad_mixed, mine, [gate_keep, down[1]], 512)
    out = with_other_core(out_send, out_keep)
    blocks = plane_call([gate, up, down, out], in_plane, [])
    common = (lens, grad_mixed, w_out, decay_wide, head_row, q, k, cum, dp, v, gp, o, before, rank)
    grads, small, deps = None, None, list(blocks)
    for seq in reversed(range(doc_lengths.shape[0])):
        grads, *sums = bwd_call(seq, grads, deps, *common)
        small = sums if small is None else [a + b for a, b in zip(small, sums)]
        deps = []
    in_send, in_keep = dw_call([grads], normed_in, mine, [], 640, wide=False)
    inner = with_other_core(in_send, in_keep)
    small = jnp.concatenate(
        [small[0][:16].reshape(-1), small[1].sum(0), small[2].sum(0), gain_mlp_part.sum(0)]
    )
    small = lax.all_gather(small.reshape(-1, 256), ("rows", "mlp"), axis=0)
    blocks = send_blocks(blocks, low, rows)
    if low:
        blocks = total(blocks)
        main = blocks[:, :-128].reshape(8, 3, -1, 128).transpose(1, 0, 2, 3).reshape(3, mlps, hid, 128)
        main = within([main], 3)[0]
        out = within([blocks[:, -128:].reshape(-1, 128)], 1)[0].reshape(DV, mlps, shard)
        main = send_line([jnp.take(main, in_line[j], axis=1) for j in range(mlps)], mlps)
        out = send_line([jnp.take(out, in_line[j], axis=1) for j in range(mlps)], mlps)
        deps = [in_keep]
    else:
        blocks = line_call(blocks, in_line, [in_keep])
        main = send_line(blocks, mlps)
        deps = list(blocks)
    grad_tokens = dx_call(0, 2, None, grads, w_in, tokens, gain_mix, grad_res, deps)
    blocks = spread([[p[None] for p in inner]], in_plane, 1, 640, [grad_tokens])
    grad_tokens = dx_call(1, 2, grad_tokens, grads, w_in, tokens, gain_mix, grad_res, list(blocks))
    block_out = down_call(0, 2, None, residual, hidden, mlp_all, [grad_tokens])
    block_out = down_call(1, 2, block_out, residual, hidden, mlp_all, [])
    blocks = within(send_blocks(blocks, low, rows), 1)
    blocks = [b.reshape(1, mlps, shard, GW) for b in blocks]
    if low:
        in_grads = send_line([jnp.take(blocks[0], in_line[j], axis=1).astype(BF) for j in range(mlps)], mlps)
    else:
        in_grads = send_line(spread([blocks], in_line, 1, 640, [block_out]), mlps)
    small = rows_call(small, [in_grads[0], block_out]).reshape(-1)
    if low:
        mlp_grads, out_grads = total(main), total(out)
    else:
        main = sum_call(main, [small])
        mlp_grads = main[: 3 * hid].reshape(2, 3, hid // 2, 128).transpose(1, 0, 2, 3).reshape(3, hid, 128)
        out_grads = main[3 * hid :].reshape(8, shard, 128).transpose(0, 2, 1).reshape(DV, shard)
    in_grads = total(in_grads)[0]
    gain_mix_grad = jnp.sum(in_grads * mixer_local.astype(F32), axis=1) / norm_gain_mix.astype(F32)
    at = 16 * DK + DK + HV + (here * mlps + lax.axis_index("mlp")) * shard
    return (
        block_out,
        grad_tokens,
        gain_mix_grad,
        in_grads[:, CQ : CQ + DK],
        in_grads[:, CK : CK + DK],
        in_grads[:, CV : CV + DV],
        in_grads[:, CG : CG + DV],
        in_grads[:, CR : CR + 16],
        small[: 16 * DK].reshape(16, DK),
        small[16 * DK : 17 * DK],
        small[17 * DK : 17 * DK + HV],
        out_grads,
        lax.dynamic_slice_in_dim(small, at, shard),
        mlp_grads[0].T,
        mlp_grads[1].T,
        mlp_grads[2],
    )


def solution(mesh):
    in_specs = (
        P(("rows", "mlp"), None),
        P(("rows", "mlp"), None),
        P(("rows", "mlp"), None),
        P(("rows", "mlp")),
        P(("rows", "mlp"), None),
        P(("rows", "mlp"), None),
        P(("rows", "mlp"), None),
        P(("rows", "mlp"), None),
        P(("rows", "mlp"), None),
        P(),
        P(),
        P(),
        P(None, ("rows", "mlp")),
        P(("rows", "mlp")),
        P("rows", "mlp"),
        P("rows", "mlp"),
        P("mlp", "rows"),
    )
    out_specs = (
        P(("rows", "mlp"), None),
        P(("rows", "mlp"), None),
        P(("rows", "mlp")),
        P(("rows", "mlp"), None),
        P(("rows", "mlp"), None),
        P(("rows", "mlp"), None),
        P(("rows", "mlp"), None),
        P(("rows", "mlp"), None),
        P(),
        P(),
        P(),
        P(None, ("rows", "mlp")),
        P(("rows", "mlp")),
        P("rows", "mlp"),
        P("rows", "mlp"),
        P("mlp", "rows"),
    )
    return jax.shard_map(body, mesh=mesh, in_specs=in_specs, out_specs=out_specs, check_vma=False)
```

time: 719 us -> 615 us (0.86)
  waiting for transfers between devices: 202 us -> 126 us
  starting transfers between devices: 88.4 us -> 31.1 us
  Pallas kernels: 362 us -> 395 us
  other arithmetic: 18.8 us -> 6.41 us
    all_gather x2, waiting for transfers between devices: 140 us -> 29.5 us  [the longest x1 15.2 us: body(): lax.all_gather(jnp.concatenate(local, axis=0), ('rows', 'mlp'), axis=0)]
    ppermute x24 -> x15, starting transfers between devices: 70.3 us -> 21.6 us  [the longest x6 8.38 us: send_line(): lax.ppermute(blocks[j], 'mlp', [(i, (i + j) % count) for i in range(count)])]
    pallas_call x13 -> x17, Pallas kernels: 272 us -> 308 us  [the longest x4 88.1 us: dw_call(): pl.pallas_call(functools.partial(dw_kernel, count, wide), grid_spec=pltpu...]
    ppermute x24 -> x15, waiting for transfers between devices: 22.5 us -> 53.5 us  [the longest x3 26.2 us: gather_pieces(): lax.ppermute(x, 'mlp', [(i, (i + step) % mlps) for i in range(mlps)])]
    unnamed x40 -> x84, local copies, waits for them, and re-layouts: 3.87 us -> 13.4 us
    squeeze x8 -> x0, local copies, waits for them, and re-layouts: 9.24 us -> none  [the longest x7 8.24 us: halve(): send = lax.dynamic_index_in_dim(grads, 1 - place, dim, keepdims=False)]
    ppermute x24 -> x19, starting transfers between devices: 18 us -> 9.44 us  [swap(): return lax.ppermute(x, axis, [(i, i ^ 1 << bit) for i in range(count)])]
    ppermute x24 -> x19, waiting for transfers between devices: 38.8 us -> 43.4 us  [swap(): return lax.ppermute(x, axis, [(i, i ^ 1 << bit) for i in range(count)])]
  transfers between devices with their start and end apart: 50 -> 36, of which waited for: 13 -> 13; matrix products, arithmetic and copies ran while one was open for 5% -> 3% of each run, Pallas kernels for 37% -> 44%
where the time goes in v3:
time: 615 us; the launch traced here: 606 us
  Pallas kernels  395 us (64%)
  waiting for transfers between devices  126 us (20%)
  local copies, waits for them, and re-layouts  31.7 us (5%)
  starting transfers between devices  31.1 us (5%)
  between operations  15 us (2%)
  other arithmetic  6.41 us (1%)
    pallas_call x4, Pallas kernels, dw_call(): pl.pallas_call(functools.partial(dw_kernel, count, wide), grid_spec=pltpu...  88.1 us
    pallas_call x1, Pallas kernels, mlp_call(): pl.pallas_call(functools.partial(mlp_kernel, chunk), grid=(n // T,), in_s...  86.6 us
    pallas_call x2, Pallas kernels, bwd_call(): pl.pallas_call(functools.partial(bwd_kernel, NT, seq), grid_spec=pltpu.Pr...  78.6 us
    pallas_call x1, Pallas kernels, fwd_call(): pl.pallas_call(functools.partial(fwd_kernel, NT, cuts), grid_spec=pltpu.P...  51.1 us
    ppermute x19, waiting for transfers between devices, swap(): return lax.ppermute(x, axis, [(i, i ^ 1 << bit) for i in range(count)])  43.4 us
    pallas_call x2, Pallas kernels, dx_call(): pl.pallas_call(dx_kernel, grid=(steps,), in_specs=[row(g), const(w), row(...  28 us
    ppermute x3, waiting for transfers between devices, gather_pieces(): lax.ppermute(x, 'mlp', [(i, (i + step) % mlps) for i in range(mlps)])  26.2 us
    pallas_call x2, Pallas kernels, down_call(): pl.pallas_call(down_kernel, grid=(steps,), in_specs=[row(d), row(ff), hbm...  24.9 us
  transfers between devices with their start and end apart: 36, of which 13 were waited for; matrix products, arithmetic and copies ran while one was open for 3% of the time, Pallas kernels for 44%

profile of v3, /device:TPU:0, one launch (start us, length us, event | category | flops | bytes accessed | tf_op | source)
XLA Modules:
  0.0 605.6 jit_solution(14211335326752175370)
XLA Ops:
  8.0 2.0 pad_maximum_fusion
  13.4 5.1 collective-permute-start.2
  20.5 4.1 collective-permute-done.2
  24.6 22.1 %collective-permute-done.1 = bf16[32,3200]{1,0:T(8,128)(2,1)S(1)} collective-permute-done((bf16[32,3200]{1,0:T(8,128)(2,1)S(1)}, bf16[32,3200]{1,0:T(8,128)(2,1)S(1)}, u32[]{:S(2)}, u32[]{:S(2)}) %collective-permute-start.1) | collective-permute-done | bytes 204832 | tf_op jit(solution)/shard_map/ppermute | solution.py:524
  46.8 1.6 collective-permute-start.10
  49.1 1.5 collective-permute-start.3
  51.2 10.3 %collective-permute-done.10.rest_9_ = bf16[128,1664]{1,0:T(8,128)(2,1)S(1)} collective-permute-done((bf16[128,1664]{1,0:T(8,128)(2,1)S(1)}, bf16[128,1664]{1,0:T(8,128)(2,1)S(1)}, u32[]{:S(2)}, u32[]{:S(2)}) %collective-permute-start.10) | collective-permute-done | bytes 426016 | tf_op jit(solution)/shard_map/ppermute | solution.py:492
  62.8 9.3 %collective-permute-done.4.rest_2_ = bf16[128,1536]{1,0:T(8,128)(2,1)S(1)} collective-permute-done((bf16[128,1536]{1,0:T(8,128)(2,1)S(1)}, bf16[128,1536]{1,0:T(8,128)(2,1)S(1)}, u32[]{:S(2)}, u32[]{:S(2)}) %collective-permute-start.4) | collective-permute-done | bytes 393248 | tf_op jit(solution)/shard_map/ppermute | solution.py:492
  72.1 1.6 collective-permute-start.5
  73.7 9.7 %collective-permute-done.11.rest_10_ = bf16[128,1664]{1,0:T(8,128)(2,1)S(1)} collective-permute-done((bf16[128,1664]{1,0:T(8,128)(2,1)S(1)}, bf16[128,1664]{1,0:T(8,128)(2,1)S(1)}, u32[]{:S(2)}, u32[]{:S(2)}) %collective-permute-start.11) | collective-permute-done | bytes 426016 | tf_op jit(solution)/shard_map/ppermute | solution.py:492
  83.9 12.0 %collective-permute-done.12.rest_11_ = bf16[128,1664]{1,0:T(8,128)(2,1)S(1)} collective-permute-done((bf16[128,1664]{1,0:T(8,128)(2,1)S(1)}, bf16[128,1664]{1,0:T(8,128)(2,1)S(1)}, u32[]{:S(2)}, u32[]{:S(2)}) %collective-permute-start.12) | collective-permute-done | bytes 426016 | tf_op jit(solution)/shard_map/ppermute | solution.py:492
  101.2 51.1 %mixer_fwd.1 = (bf16[2048,1024]{1,0:T(8,128)(2,1)}, f32[2048,512]{1,0:T(8,128)}, f32[2048,512]{1,0:T(8,128)}, f32[2048,512]{1,0:T(8,128)}, f32[2048,512]{1,0:T(8...) custom-call(s32[8]{0:T(128)} %reshape.91.st_ref, ...), custom_call_target="tpu_custom_call" | custom-call | flops 1 | bytes 1 | tf_op jit(solution)/shard_map/mixer_fwd/pallas_call | solution.py:160
  152.3 1.4 fusion.9
  153.7 15.2 %all-gather.6.cloned.1.call-done = bf16[75776,128]{1,0:T(8,128)(2,1)} async-done(((bf16[2368,128]{1,0:T(8,128)(2,1)}), bf16[75776,128]{1,0:T(8,128)(2,1)}) %all-gather.6.cloned.1.call-update) | async-done | bytes 19398672 | tf_op jit(solution)/shard_map/all_gather | solution.py:570
  168.9 1.7 slice.121
  171.7 1.9 copy.73
  173.6 86.6 %mlp.1 = (f32[2048,1024]{1,0:T(8,128)}, bf16[2048,1024]{1,0:T(8,128)(2,1)}, bf16[2048,2816]{1,0:T(8,128)(2,1)}, bf16[2048,2816]{1,0:T(8,128)(2,1)}, bf16[2048,28...) custom-call(bf16[2048,1024]{1,0:T(8,128)(2,1)} %tok_ref.7, ...), custom_call_target="tpu_custom_call" | custom-call | flops 1 | bytes 1 | tf_op jit(solution)/shard_map/mlp/pallas_call | solution.py:329
  260.2 19.8 %grad_w.4 = (bf16[4,2816,128]{2,1,0:T(8,128)(2,1)}, bf16[4,2816,128]{2,1,0:T(8,128)(2,1)}) custom-call(s32[1]{0:T(128)} %bitcast.13.sel_ref, bf16[2048,2816]{1,0:T(8,128)(2,1)} %get-tuple-element.74.rest_0_.hid_ref, bf16[2048,1024]{1,0:T(8,128)(2,1)} %rest_1_.1, bf16[2048,1024]{1,0:T(8,128)(2,1)} %get-tuple-element.87.rest_2_), custom_call_target="tpu_custom_call" | custom-call | flops 99999997952 | bytes 1 | tf_op jit(solution)/shard_map/grad_w/pallas_call | solution.py:386
  280.3 35.4 %grad_w.5 = (bf16[4,2816,128]{2,1,0:T(8,128)(2,1)}, bf16[4,2816,128]{2,1,0:T(8,128)(2,1)}, bf16[4,2816,128]{2,1,0:T(8,128)(2,1)}, bf16[4,2816,128]{2,1,0:T(8,128)(2,1)}) custom-call(s32[1]{0:T(128)} %bitcast.13.sel_ref, bf16[2048,2816]{1,0:T(8,128)(2,1)} %get-tuple-element.85.rest_0_, bf16[2048,2816]{1,0:T(8,128)(2,1)} %get-tuple-element.86.rest_1_, ...), custom_call_target="tpu_custom_call" | custom-call | flops 99999997952 | bytes 1 | tf_op jit(solution)/shard_map/grad_w/pallas_call | solution.py:386
  316.3 1.6 copy-done.3
  317.9 9.8 %grad_w.6 = (bf16[4,1024,128]{2,1,0:T(8,128)(2,1)}, bf16[4,1024,128]{2,1,0:T(8,128)(2,1)}) custom-call(s32[1]{0:T(128)} %bitcast.13.sel_ref, bf16[2048,1024]{1,0:T(8,128)(2,1)} %get-tuple-element.71.mix_ref.rest_0_, bf16[2048,1024]{1,0:T(8,128)(2,1)} %get-tuple-element.75.rest_1_.gmix_ref, bf16[4,2816,128]{2,1,0:T(8,128)(2,1)} %get-tuple-element.89.rest_2_.rest_0_, ...), custom_call_target="tpu_custom_call" | custom-call | flops 99999997952 | bytes 1 | tf_op jit(solution)/shard_map/grad_w/pallas_call | solution.py:386
  328.6 2.1 collective-permute-done.20.rest_7_
  331.6 12.6 %plane.1 = (bf16[8,1184,128]{2,1,0:T(8,128)(2,1)}, bf16[8,1184,128]{2,1,0:T(8,128)(2,1)}, bf16[8,1184,128]{2,1,0:T(8,128)(2,1)}, bf16[8,1184,128]{2,1,0:T(8,128)(2,1)}) custom-call(s32[4]{0:T(128)} %iota_xor_fusion.at_ref, bf16[4,2816,128]{2,1,0:T(8,128)(2,1)} %get-tuple-element.89.rest_2_.rest_0_, bf16[4,2816,128]{2,1,0:T(8,128)(2,1)} %collective-permute-done.17.rest_1_, ...), custom_call_target="tpu_custom_call" | custom-call | flops 1 | bytes 1 | tf_op jit(solution)/shard_map/plane/pallas_call | solution.py:408
  344.2 1.5 collective-permute-start.22
  346.3 1.5 collective-permute-start.24
  348.3 39.4 %mixer_bwd.2 = (bf16[2048,3200]{1,0:T(8,128)(2,1)}, f32[128,512]{1,0:T(8,128)}, f32[8,512]{1,0:T(8,128)}, f32[8,256]{1,0:T(8,128)}) custom-call(s32[8]{0:T(128)} %reshape.91.st_ref, bf16[2048,1024]{1,0:T(8,128)(2,1)} %get-tuple-element.75.rest_1_.gmix_ref, bf16[1024,1024]{1,0:T(8,128)(2,1)} %bitcast.64, bf16[128,512]{1,0:T(8,128)(2,1)} %concatenate.28.wdec_ref, ...), custom_call_target="tpu_custom_call" | custom-call | flops 1 | bytes 1 | tf_op jit(solution)/shard_map/mixer_bwd/pallas_call | solution.py:251
  387.7 39.2 %mixer_bwd.3 = (bf16[2048,3200]{1,0:T(8,128)(2,1)}, f32[128,512]{1,0:T(8,128)}, f32[8,512]{1,0:T(8,128)}, f32[8,256]{1,0:T(8,128)}) custom-call(s32[8]{0:T(128)} %reshape.91.st_ref, bf16[2048,1024]{1,0:T(8,128)(2,1)} %get-tuple-element.75.rest_1_.gmix_ref, bf16[1024,1024]{1,0:T(8,128)(2,1)} %bitcast.65, ...), custom_call_target="tpu_custom_call", output_to_operand_aliasing={{0}: (14, {})} | custom-call | flops 1 | bytes 1 | tf_op jit(solution)/shard_map/mixer_bwd/pallas_call | solution.py:251
  426.9 23.1 %grad_w.7 = (bf16[4,128,3200]{2,1,0:T(8,128)(2,1)}, bf16[4,128,3200]{2,1,0:T(8,128)(2,1)}) custom-call(s32[1]{0:T(128)} %bitcast.13.sel_ref, bf16[2048,3200]{1,0:T(8,128)(2,1)} %get-tuple-element.101.rest_0_.g_ref, bf16[2048,1024]{1,0:T(8,128)(2,1)} %get-tuple-element.104.rest_1_), custom_call_target="tpu_custom_call" | custom-call | flops 1 | bytes 1 | tf_op jit(solution)/shard_map/grad_w/pallas_call | solution.py:386
  450.1 2.4 collective-permute-done.23.rest_2_
  452.5 8.2 %line.1 = (bf16[2368,128]{1,0:T(8,128)(2,1)}, bf16[2368,128]{1,0:T(8,128)(2,1)}, bf16[2368,128]{1,0:T(8,128)(2,1)}, bf16[2368,128]{1,0:T(8,128)(2,1)}) custom-call(s32[4]{0:T(128)} %and_select_fusion.at_ref, bf16[8,1184,128]{2,1,0:T(8,128)(2,1)} %get-tuple-element.96.rest_0_, bf16[8,1184,128]{2,1,0:T(8,128)(2,1)} %collective-permute-done.22.rest_1_, ...), custom_call_target="tpu_custom_call" | custom-call | flops 1 | bytes 1 | tf_op jit(solution)/shard_map/line/pallas_call | solution.py:437
  460.7 14.3 %mixer_dx.2.rest_2_.rest_4_ = f32[2048,1024]{1,0:T(8,128)} custom-call(bf16[2048,3200]{1,0:T(8,128)(2,1)} %get-tuple-element.101.rest_0_.g_ref, bf16[1024,3200]{1,0:T(8,128)(2,1)} %get-tuple-element.102.w_ref, bf16[2048,1024]{1,0:T(8,128)(2,1)} %tok_ref.7, f32[1,1024]{1,0:T(1,128)} %get-tuple-element.183.gain_ref, f32[2048,1024]{1,0:T(8,128)} %get-tuple-element.103.gres_ref, ...), custom_call_target="tpu_custom_call" | custom-call | flops 49999998976 | bytes 1 | tf_op jit(solution)/shard_map/mixer_dx/pallas_call | solution.py:277
  475.0 1.7 copy-done.2
  476.8 7.0 %spread.2 = (bf16[1,128,3200]{2,1,0:T(8,128)(2,1)}, bf16[1,128,3200]{2,1,0:T(8,128)(2,1)}, bf16[1,128,3200]{2,1,0:T(8,128)(2,1)}, bf16[1,128,3200]{2,1,0:T(8,128)(2,1)}) custom-call(s32[4]{0:T(128)} %iota_xor_fusion.at_ref, bf16[1,4,128,3200]{3,2,1,0:T(8,128)(2,1)} %bitcast.66, bf16[1,4,128,3200]{3,2,1,0:T(8,128)(2,1)} %bitcast.70, ...), custom_call_target="tpu_custom_call" | custom-call | flops 1 | bytes 1 | tf_op jit(solution)/shard_map/spread/pallas_call | solution.py:462
  486.1 1.9 collective-permute-start.32
  487.9 2.4 collective-permute-start.33
  490.4 1.5 collective-permute-start.26
  491.8 11.8 %collective-permute-done.25 = bf16[1,128,3200]{2,1,0:T(8,128)(2,1)S(1)} collective-permute-done((bf16[1,128,3200]{2,1,0:T(8,128)(2,1)}, bf16[1,128,3200]{2,1,0:T(8,128)(2,1)S(1)}, u32[]{:S(2)}, u32[]{:S(2)}) %collective-permute-start.25) | collective-permute-done | bytes 819232 | tf_op jit(solution)/shard_map/ppermute | solution.py:512
  505.1 13.6 %mixer_dx.3.rest_0_ = f32[2048,1024]{1,0:T(8,128)} custom-call(bf16[2048,3200]{1,0:T(8,128)(2,1)} %get-tuple-element.101.rest_0_.g_ref, bf16[1024,3200]{1,0:T(8,128)(2,1)} %get-tuple-element.102.w_ref, bf16[2048,1024]{1,0:T(8,128)(2,1)} %tok_ref.7, f32[1,1024]{1,0:T(1,128)} %get-tuple-element.183.gain_ref, ...), custom_call_target="tpu_custom_call", output_to_operand_aliasing={{}: (9, {})} | custom-call | flops 49999998976 | bytes 1 | tf_op jit(solution)/shard_map/mixer_dx/pallas_call | solution.py:277
  518.7 12.4 %mlp_down.2.rest_0_ = bf16[2048,1024]{1,0:T(8,128)(2,1)} custom-call(f32[2048,1024]{1,0:T(8,128)} %get-tuple-element.73.res_ref, bf16[2048,2816]{1,0:T(8,128)(2,1)} %get-tuple-element.74.rest_0_.hid_ref, bf16[8,4,2368,128]{3,2,1,0:T(8,128)(2,1)} %bitcast.61, f32[2048,1024]{1,0:T(8,128)} %mixer_dx.3.rest_0_), custom_call_target="tpu_custom_call" | custom-call | flops 1 | bytes 1 | tf_op jit(solution)/shard_map/mlp_down/pallas_call | solution.py:349
  531.1 12.5 %mlp_down.3.rest_4_.rest_1_ = bf16[2048,1024]{1,0:T(8,128)(2,1)} custom-call(f32[2048,1024]{1,0:T(8,128)} %get-tuple-element.73.res_ref, bf16[2048,2816]{1,0:T(8,128)(2,1)} %get-tuple-element.74.rest_0_.hid_ref, bf16[8,4,2368,128]{3,2,1,0:T(8,128)(2,1)} %bitcast.62, bf16[2048,1024]{1,0:T(8,128)(2,1)} %mlp_down.2.rest_0_), custom_call_target="tpu_custom_call", output_to_operand_aliasing={{}: (3, {})} | custom-call | flops 1 | bytes 1 | tf_op jit(solution)/shard_map/mlp_down/pallas_call | solution.py:349
  544.8 5.1 spread.3
  549.9 14.3 %all-gather.4.cloned.1.call-done.x_ref = f32[32,39,256]{2,1,0:T(8,128)} async-done(((f32[1,39,256]{2,1,0:T(8,128)}), f32[32,39,256]{2,1,0:T(8,128)}) %all-gather.4.cloned.1.call-update) | async-done | bytes 1277968 | tf_op jit(solution)/shard_map/all_gather | solution.py:627
  564.2 2.0 sum_rows.1
  567.5 1.5 reshape.103.refs_4_
  570.5 2.9 sum_parts.1
  578.1 2.3 collective-permute-start.29
  582.5 4.9 collective-permute-done.28
  587.4 8.1 %collective-permute-done.29 = bf16[1,32,3200]{2,1,0:T(8,128)(2,1)S(1)} collective-permute-done((bf16[1,32,3200]{2,1,0:T(8,128)(2,1)S(1)}, bf16[1,32,3200]{2,1,0:T(8,128)(2,1)S(1)}, u32[]{:S(2)}, u32[]{:S(2)}) %collective-permute-start.29) | collective-permute-done | bytes 204832 | tf_op jit(solution)/shard_map/ppermute | solution.py:518
  (178 shorter events, 36.7 us)
Async XLA Ops:
  7.2 41.2 %copy-start.14 = (bf16[32,1024]{1,0:T(8,128)(2,1)S(1)}, bf16[32,1024]{1,0:T(8,128)(2,1)}, u32[]{:S(2)}) copy-start(bf16[32,1024]{1,0:T(8,128)(2,1)} %param.23) | copy-start | bytes 196612
  7.2 41.2 %copy-start.24 = (bf16[32,512]{1,0:T(8,128)(2,1)S(1)}, bf16[32,512]{1,0:T(8,128)(2,1)}, u32[]{:S(2)}) copy-start(bf16[32,512]{1,0:T(8,128)(2,1)} %param.22) | copy-start | bytes 98308
  7.2 41.2 %copy-start.25 = (bf16[32,512]{1,0:T(8,128)(2,1)S(1)}, bf16[32,512]{1,0:T(8,128)(2,1)}, u32[]{:S(2)}) copy-start(bf16[32,512]{1,0:T(8,128)(2,1)} %param.21) | copy-start | bytes 98308
  7.2 90.0 %copy-start.37 = (s32[2,4]{1,0:T(2,128)S(1)}, s32[2,4]{1,0:T(2,128)}, u32[]{:S(2)}) copy-start(s32[2,4]{1,0:T(2,128)} %param.18) | copy-start | bytes 100
  7.2 90.6 %copy-start.38 = (bf16[256]{0:T(256)(128)(2,1)S(1)}, bf16[256]{0:T(256)(128)(2,1)}, u32[]{:S(2)}) copy-start(bf16[256]{0:T(256)(128)(2,1)} %param.28) | copy-start | bytes 1540
  7.3 91.1 %copy-start.32 = (bf16[512]{0:T(512)(128)(2,1)S(1)}, bf16[512]{0:T(512)(128)(2,1)}, u32[]{:S(2)}) copy-start(bf16[512]{0:T(512)(128)(2,1)} %param.27) | copy-start | bytes 3076
  7.3 91.7 %copy-start.27 = (bf16[16,512]{1,0:T(8,128)(2,1)S(1)}, bf16[16,512]{1,0:T(8,128)(2,1)}, u32[]{:S(2)}) copy-start(bf16[16,512]{1,0:T(8,128)(2,1)} %param.26) | copy-start | bytes 49156
  7.3 161.7 %all-gather.6.cloned.1.call-start = ((), (), s32[]{:S(2)}) async-start(), calls=%async_computation.1 | async-start | bytes 20004864 | tf_op jit(solution)/shard_map/all_gather | solution.py:570
  10.0 554.2 %all-gather.4.cloned.1.call-start = ((), (), s32[]{:S(2)}) async-start(), calls=%async_computation | async-start | bytes 1351680 | tf_op jit(solution)/shard_map/all_gather | solution.py:627
  13.4 33.4 %copy-start.7 = (bf16[32,3200]{1,0:T(8,128)(2,1)}, bf16[32,3200]{1,0:T(8,128)(2,1)S(1)}, u32[]{:S(2)}) copy-start(bf16[32,3200]{1,0:T(8,128)(2,1)S(1)} %concatenate.30) | copy-start | bytes 614404
  13.4 11.2 %collective-permute-start.2 = (bf16[32,3200]{1,0:T(8,128)(2,1)S(1)}, bf16[32,3200]{1,0:T(8,128)(2,1)S(1)}, u32[]{:S(2)}, u32[]{:S(2)}) collective-permute-start(bf16[32,3200]{1,0:T(8,128)(2,1)S(1)} %concatenate.30), channel_id=1, source_target_pairs={{0,3},{1,0},{2,1},{3,2},{4,7},{5,4},{6,5},{7,6},{8,11},{9,8},{10,9... | collective-permute-start | bytes 614408 | tf_op jit(solution)/shard_map/ppermute | solution.py:524
  18.5 28.2 %collective-permute-start.1 = (bf16[32,3200]{1,0:T(8,128)(2,1)S(1)}, bf16[32,3200]{1,0:T(8,128)(2,1)S(1)}, u32[]{:S(2)}, u32[]{:S(2)}) collective-permute-start(bf16[32,3200]{1,0:T(8,128)(2,1)S(1)} %concatenate.30), channel_id=1, source_target_pairs={{0,2},{1,3},{2,0},{3,1},{4,6},{5,7},{6,4},{7,5},{8,10},{9,11},{10,... | collective-permute-start | bytes 614408 | tf_op jit(solution)/shard_map/ppermute | solution.py:524
  18.5 28.2 %collective-permute-start = (bf16[32,3200]{1,0:T(8,128)(2,1)S(1)}, bf16[32,3200]{1,0:T(8,128)(2,1)S(1)}, u32[]{:S(2)}, u32[]{:S(2)}) collective-permute-start(bf16[32,3200]{1,0:T(8,128)(2,1)S(1)} %concatenate.30), channel_id=1, source_target_pairs={{0,1},{1,2},{2,3},{3,0},{4,5},{5,6},{6,7},{7,4},{8,9},{9,10},{10,1... | collective-permute-start | bytes 614408 | tf_op jit(solution)/shard_map/ppermute | solution.py:524
  46.8 53.5 %copy-start.4 = (bf16[128,1664]{1,0:T(8,128)(2,1)}, bf16[128,1664]{1,0:T(8,128)(2,1)S(1)}, u32[]{:S(2)}) copy-start(bf16[128,1664]{1,0:T(8,128)(2,1)S(1)} %pad_maximum_fusion.1.rest_8_) | copy-start | bytes 1277956
  46.8 14.7 %collective-permute-start.10 = (bf16[128,1664]{1,0:T(8,128)(2,1)S(1)}, bf16[128,1664]{1,0:T(8,128)(2,1)S(1)}, u32[]{:S(2)}, u32[]{:S(2)}) collective-permute-start(bf16[128,1664]{1,0:T(8,128)(2,1)S(1)} %pad_maximum_fusion.1.rest_8_), channel_id=1, source_target_pairs={{0,16},{4,20},{8,24},{12,28},{16,0},{20,4},{24,8},{28,12},{1,17},{... | collective-permute-start | bytes 1277960 | tf_op jit(solution)/shard_map/ppermute | solution.py:492
  48.5 51.8 %copy-start.5 = (bf16[128,1536]{1,0:T(8,128)(2,1)}, bf16[128,1536]{1,0:T(8,128)(2,1)S(1)}, u32[]{:S(2)}) copy-start(bf16[128,1536]{1,0:T(8,128)(2,1)S(1)} %fusion.2.rest_0_) | copy-start | bytes 1179652
  48.5 2.7 collective-permute-start.6
  48.6 23.5 %collective-permute-start.4 = (bf16[128,1536]{1,0:T(8,128)(2,1)S(1)}, bf16[128,1536]{1,0:T(8,128)(2,1)S(1)}, u32[]{:S(2)}, u32[]{:S(2)}) collective-permute-start(bf16[128,1536]{1,0:T(8,128)(2,1)S(1)} %fusion.2.rest_0_), channel_id=1, source_target_pairs={{0,16},{4,20},{8,24},{12,28},{16,0},{20,4},{24,8},{28,12},{1,17},{... | collective-permute-start | bytes 1179656 | tf_op jit(solution)/shard_map/ppermute | solution.py:492
  49.1 23.0 %collective-permute-start.3 = (bf16[128,1536]{1,0:T(8,128)(2,1)S(1)}, bf16[128,1536]{1,0:T(8,128)(2,1)}, u32[]{:S(2)}, u32[]{:S(2)}) collective-permute-start(bf16[128,1536]{1,0:T(8,128)(2,1)S(1)} %fusion.2.rest_0_), channel_id=1, source_target_pairs={{0,8},{4,12},{8,0},{12,4},{16,24},{20,28},{24,16},{28,20},{1,9},{5... | collective-permute-start | bytes 1179656 | tf_op jit(solution)/shard_map/ppermute | solution.py:492
  50.6 32.7 %collective-permute-start.11 = (bf16[128,1664]{1,0:T(8,128)(2,1)S(1)}, bf16[128,1664]{1,0:T(8,128)(2,1)S(1)}, u32[]{:S(2)}, u32[]{:S(2)}) collective-permute-start(bf16[128,1664]{1,0:T(8,128)(2,1)S(1)} %pad_maximum_fusion.1.rest_8_), channel_id=1, source_target_pairs={{0,8},{4,12},{8,0},{12,4},{16,24},{20,28},{24,16},{28,20},{1,9},{5... | collective-permute-start | bytes 1277960 | tf_op jit(solution)/shard_map/ppermute | solution.py:492
  51.2 44.7 %copy-start.21 = (bf16[128,1536]{1,0:T(8,128)(2,1)}, bf16[128,1536]{1,0:T(8,128)(2,1)S(1)}, u32[]{:S(2)}) copy-start(bf16[128,1536]{1,0:T(8,128)(2,1)S(1)} %collective-permute-done.6.rest_4_) | copy-start | bytes 1179652
  51.2 32.2 %collective-permute-start.13 = (bf16[128,1664]{1,0:T(8,128)(2,1)S(1)}, bf16[128,1664]{1,0:T(8,128)(2,1)S(1)}, u32[]{:S(2)}, u32[]{:S(2)}) collective-permute-start(bf16[128,1664]{1,0:T(8,128)(2,1)S(1)} %pad_maximum_fusion.1.rest_8_), channel_id=1, source_target_pairs={{0,4},{4,0},{8,12},{12,8},{16,20},{20,16},{24,28},{28,24},{1,5},{5... | collective-permute-start | bytes 1277960 | tf_op jit(solution)/shard_map/ppermute | solution.py:492
  61.5 38.8 %copy-start.15 = (bf16[128,1664]{1,0:T(8,128)(2,1)}, bf16[128,1664]{1,0:T(8,128)(2,1)S(1)}, u32[]{:S(2)}) copy-start(bf16[128,1664]{1,0:T(8,128)(2,1)S(1)} %collective-permute-done.10.rest_9_) | copy-start | bytes 1277956
  61.5 34.4 %collective-permute-start.12 = (bf16[128,1664]{1,0:T(8,128)(2,1)S(1)}, bf16[128,1664]{1,0:T(8,128)(2,1)S(1)}, u32[]{:S(2)}, u32[]{:S(2)}) collective-permute-start(bf16[128,1664]{1,0:T(8,128)(2,1)S(1)} %collective-permute-done.10.rest_9_), channel_id=1, source_target_pairs={{0,8},{4,12},{8,0},{12,4},{16,24},{20,28},{24,16},{28,20},{1,9},{5... | collective-permute-start | bytes 1277960 | tf_op jit(solution)/shard_map/ppermute | solution.py:492
  72.1 23.8 %collective-permute-start.8 = (bf16[128,1536]{1,0:T(8,128)(2,1)S(1)}, bf16[128,1536]{1,0:T(8,128)(2,1)S(1)}, u32[]{:S(2)}, u32[]{:S(2)}) collective-permute-start(bf16[128,1536]{1,0:T(8,128)(2,1)S(1)} %collective-permute-done.4.rest_2_), channel_id=1, source_target_pairs={{0,4},{4,0},{8,12},{12,8},{16,20},{20,16},{24,28},{28,24},{1,5},{5... | collective-permute-start | bytes 1179656 | tf_op jit(solution)/shard_map/ppermute | solution.py:492
  72.1 25.1 %collective-permute-start.5 = (bf16[128,1536]{1,0:T(8,128)(2,1)}, bf16[128,1536]{1,0:T(8,128)(2,1)}, u32[]{:S(2)}, u32[]{:S(2)}) collective-permute-start(bf16[128,1536]{1,0:T(8,128)(2,1)} %collective-permute-done.3.rest_1_), channel_id=1, source_target_pairs={{0,16},{4,20},{8,24},{12,28},{16,0},{20,4},{24,8},{28,12},{1,17},{... | collective-permute-start | bytes 1179656 | tf_op jit(solution)/shard_map/ppermute | solution.py:492
  83.4 16.9 %collective-permute-start.15 = (bf16[128,1664]{1,0:T(8,128)(2,1)S(1)}, bf16[128,1664]{1,0:T(8,128)(2,1)S(1)}, u32[]{:S(2)}, u32[]{:S(2)}) collective-permute-start(bf16[128,1664]{1,0:T(8,128)(2,1)S(1)} %collective-permute-done.11.rest_10_), channel_id=1, source_target_pairs={{0,4},{4,0},{8,12},{12,8},{16,20},{20,16},{24,28},{28,24},{1,5},{5... | collective-permute-start | bytes 1277960 | tf_op jit(solution)/shard_map/ppermute | solution.py:492
  83.4 16.9 %collective-permute-start.14 = (bf16[128,1664]{1,0:T(8,128)(2,1)S(1)}, bf16[128,1664]{1,0:T(8,128)(2,1)S(1)}, u32[]{:S(2)}, u32[]{:S(2)}) collective-permute-start(bf16[128,1664]{1,0:T(8,128)(2,1)S(1)} %collective-permute-done.10.rest_9_), channel_id=1, source_target_pairs={{0,4},{4,0},{8,12},{12,8},{16,20},{20,16},{24,28},{28,24},{1,5},{5... | collective-permute-start | bytes 1277960 | tf_op jit(solution)/shard_map/ppermute | solution.py:492
  95.9 4.4 collective-permute-start.16
  96.7 3.5 collective-permute-start.7
  97.2 3.1 collective-permute-start.9
  280.0 36.3 %collective-permute-start.19 = (bf16[4,2816,128]{2,1,0:T(8,128)(2,1)}, bf16[4,2816,128]{2,1,0:T(8,128)(2,1)S(1)}, u32[]{:S(2)}, u32[]{:S(2)}) collective-permute-start(bf16[4,2816,128]{2,1,0:T(8,128)(2,1)} %get-tuple-element.93), channel_id=1, source_target_pairs={{0,4},{4,0},{8,12},{12,8},{16,20},{20,16},{24,28},{28,24},{1,5},{5... | collective-permute-start | bytes 8650760 | tf_op jit(solution)/shard_map/ppermute | solution.py:492
  315.7 12.8 %collective-permute-start.17 = (bf16[4,2816,128]{2,1,0:T(8,128)(2,1)}, bf16[4,2816,128]{2,1,0:T(8,128)(2,1)}, u32[]{:S(2)}, u32[]{:S(2)}) collective-permute-start(bf16[4,2816,128]{2,1,0:T(8,128)(2,1)} %get-tuple-element.90), channel_id=1, source_target_pairs={{0,4},{4,0},{8,12},{12,8},{16,20},{20,16},{24,28},{28,24},{1,5},{5... | collective-permute-start | bytes 8650760 | tf_op jit(solution)/shard_map/ppermute | solution.py:492
  316.0 12.5 %collective-permute-start.18 = (bf16[4,2816,128]{2,1,0:T(8,128)(2,1)}, bf16[4,2816,128]{2,1,0:T(8,128)(2,1)}, u32[]{:S(2)}, u32[]{:S(2)}) collective-permute-start(bf16[4,2816,128]{2,1,0:T(8,128)(2,1)} %get-tuple-element.92), channel_id=1, source_target_pairs={{0,4},{4,0},{8,12},{12,8},{16,20},{20,16},{24,28},{28,24},{1,5},{5... | collective-permute-start | bytes 8650760 | tf_op jit(solution)/shard_map/ppermute | solution.py:492
  327.7 2.9 collective-permute-start.20
  344.2 105.9 %collective-permute-start.22 = (bf16[8,1184,128]{2,1,0:T(8,128)(2,1)}, bf16[8,1184,128]{2,1,0:T(8,128)(2,1)}, u32[]{:S(2)}, u32[]{:S(2)}) collective-permute-start(bf16[8,1184,128]{2,1,0:T(8,128)(2,1)} %get-tuple-element.97.rest_1_), channel_id=1, source_target_pairs={{0,8},{4,12},{8,0},{12,4},{16,24},{20,28},{24,16},{28,20},{1,9},{5... | collective-permute-start | bytes 7274504 | tf_op jit(solution)/shard_map/ppermute | solution.py:512
  345.7 106.8 %collective-permute-start.23 = (bf16[8,1184,128]{2,1,0:T(8,128)(2,1)}, bf16[8,1184,128]{2,1,0:T(8,128)(2,1)}, u32[]{:S(2)}, u32[]{:S(2)}) collective-permute-start(bf16[8,1184,128]{2,1,0:T(8,128)(2,1)} %get-tuple-element.98.rest_2_), channel_id=1, source_target_pairs={{0,16},{4,20},{8,24},{12,28},{16,0},{20,4},{24,8},{28,12},{1,17},{... | collective-permute-start | bytes 7274504 | tf_op jit(solution)/shard_map/ppermute | solution.py:512
  346.3 106.2 %collective-permute-start.24 = (bf16[8,1184,128]{2,1,0:T(8,128)(2,1)}, bf16[8,1184,128]{2,1,0:T(8,128)(2,1)}, u32[]{:S(2)}, u32[]{:S(2)}) collective-permute-start(bf16[8,1184,128]{2,1,0:T(8,128)(2,1)} %get-tuple-element.99.rest_3_), channel_id=1, source_target_pairs={{0,24},{4,28},{8,16},{12,20},{16,8},{20,12},{24,0},{28,4},{1,25},{... | collective-permute-start | bytes 7274504 | tf_op jit(solution)/shard_map/ppermute | solution.py:512
  450.0 25.1 %collective-permute-start.21 = (bf16[4,128,3200]{2,1,0:T(8,128)(2,1)}, bf16[4,128,3200]{2,1,0:T(8,128)(2,1)S(1)}, u32[]{:S(2)}, u32[]{:S(2)}) collective-permute-start(bf16[4,128,3200]{2,1,0:T(8,128)(2,1)} %get-tuple-element.106), channel_id=1, source_target_pairs={{0,4},{4,0},{8,12},{12,8},{16,20},{20,16},{24,28},{28,24},{1,5},{5... | collective-permute-start | bytes 9830408 | tf_op jit(solution)/shard_map/ppermute | solution.py:492
  483.7 19.9 %collective-permute-start.25 = (bf16[1,128,3200]{2,1,0:T(8,128)(2,1)}, bf16[1,128,3200]{2,1,0:T(8,128)(2,1)S(1)}, u32[]{:S(2)}, u32[]{:S(2)}) collective-permute-start(bf16[1,128,3200]{2,1,0:T(8,128)(2,1)} %get-tuple-element.112.rest_1_), channel_id=1, source_target_pairs={{0,8},{4,12},{8,0},{12,4},{16,24},{20,28},{24,16},{28,20},{1,9},{5... | collective-permute-start | bytes 2457608 | tf_op jit(solution)/shard_map/ppermute | solution.py:512
  485.9 83.7 %collective-permute-start.31 = (bf16[2368,128]{1,0:T(8,128)(2,1)}, bf16[2368,128]{1,0:T(8,128)(2,1)S(1)}, u32[]{:S(2)}, u32[]{:S(2)}) collective-permute-start(bf16[2368,128]{1,0:T(8,128)(2,1)} %get-tuple-element.108.rest_1_), channel_id=1, source_target_pairs={{0,1},{1,2},{2,3},{3,0},{4,5},{5,6},{6,7},{7,4},{8,9},{9,10},{10,1... | collective-permute-start | bytes 1818632 | tf_op jit(solution)/shard_map/ppermute | solution.py:518
  486.1 83.6 %collective-permute-start.32 = (bf16[2368,128]{1,0:T(8,128)(2,1)}, bf16[2368,128]{1,0:T(8,128)(2,1)}, u32[]{:S(2)}, u32[]{:S(2)}) collective-permute-start(bf16[2368,128]{1,0:T(8,128)(2,1)} %get-tuple-element.109.rest_2_), channel_id=1, source_target_pairs={{0,2},{1,3},{2,0},{3,1},{4,6},{5,7},{6,4},{7,5},{8,10},{9,11},{10,... | collective-permute-start | bytes 1818632 | tf_op jit(solution)/shard_map/ppermute | solution.py:518
  487.9 81.7 %collective-permute-start.33 = (bf16[2368,128]{1,0:T(8,128)(2,1)}, bf16[2368,128]{1,0:T(8,128)(2,1)}, u32[]{:S(2)}, u32[]{:S(2)}) collective-permute-start(bf16[2368,128]{1,0:T(8,128)(2,1)} %get-tuple-element.110.rest_3_), channel_id=1, source_target_pairs={{0,3},{1,0},{2,1},{3,2},{4,7},{5,4},{6,5},{7,6},{8,11},{9,8},{10,9... | collective-permute-start | bytes 1818632 | tf_op jit(solution)/shard_map/ppermute | solution.py:518
  490.4 53.2 %collective-permute-start.26 = (bf16[1,128,3200]{2,1,0:T(8,128)(2,1)}, bf16[1,128,3200]{2,1,0:T(8,128)(2,1)S(1)}, u32[]{:S(2)}, u32[]{:S(2)}) collective-permute-start(bf16[1,128,3200]{2,1,0:T(8,128)(2,1)} %get-tuple-element.113.rest_2_), channel_id=1, source_target_pairs={{0,16},{4,20},{8,24},{12,28},{16,0},{20,4},{24,8},{28,12},{1,17},{... | collective-permute-start | bytes 2457608 | tf_op jit(solution)/shard_map/ppermute | solution.py:512
  503.6 40.0 %collective-permute-start.27 = (bf16[1,128,3200]{2,1,0:T(8,128)(2,1)}, bf16[1,128,3200]{2,1,0:T(8,128)(2,1)S(1)}, u32[]{:S(2)}, u32[]{:S(2)}) collective-permute-start(bf16[1,128,3200]{2,1,0:T(8,128)(2,1)} %get-tuple-element.114.rest_3_), channel_id=1, source_target_pairs={{0,24},{4,28},{8,16},{12,20},{16,8},{20,12},{24,0},{28,4},{1,25},{... | collective-permute-start | bytes 2457608 | tf_op jit(solution)/shard_map/ppermute | solution.py:512
  577.6 9.8 %collective-permute-start.28 = (bf16[1,32,3200]{2,1,0:T(8,128)(2,1)S(1)}, bf16[1,32,3200]{2,1,0:T(8,128)(2,1)S(1)}, u32[]{:S(2)}, u32[]{:S(2)}) collective-permute-start(bf16[1,32,3200]{2,1,0:T(8,128)(2,1)S(1)} %copy-done.36), channel_id=1, source_target_pairs={{0,1},{1,2},{2,3},{3,0},{4,5},{5,6},{6,7},{7,4},{8,9},{9,10},{10,1... | collective-permute-start | bytes 614408 | tf_op jit(solution)/shard_map/ppermute | solution.py:518
  578.1 17.4 %collective-permute-start.29 = (bf16[1,32,3200]{2,1,0:T(8,128)(2,1)S(1)}, bf16[1,32,3200]{2,1,0:T(8,128)(2,1)S(1)}, u32[]{:S(2)}, u32[]{:S(2)}) collective-permute-start(bf16[1,32,3200]{2,1,0:T(8,128)(2,1)S(1)} %copy-done.35), channel_id=1, source_target_pairs={{0,2},{1,3},{2,0},{3,1},{4,6},{5,7},{6,4},{7,5},{8,10},{9,11},{10,... | collective-permute-start | bytes 614408 | tf_op jit(solution)/shard_map/ppermute | solution.py:518
  580.5 15.1 %collective-permute-start.30 = (bf16[1,32,3200]{2,1,0:T(8,128)(2,1)S(1)}, bf16[1,32,3200]{2,1,0:T(8,128)(2,1)S(1)}, u32[]{:S(2)}, u32[]{:S(2)}) collective-permute-start(bf16[1,32,3200]{2,1,0:T(8,128)(2,1)S(1)} %copy-done.34), channel_id=1, source_target_pairs={{0,3},{1,0},{2,1},{3,2},{4,7},{5,4},{6,5},{7,6},{8,11},{9,8},{10,9... | collective-permute-start | bytes 614408 | tf_op jit(solution)/shard_map/ppermute | solution.py:518
  (29 other events, 273.4 us)
Sparse Core Ops, SparseCore 0:
  10.9 157.9 all-gather.5
  486.0 78.0 all-gather.3

commit v4 on v3

--- a/solution.py
+++ b/solution.py
@@ -276,7 +276,7 @@
     more=list(deps)+([] if begun is None else [begun])
     return pl.pallas_call(dx_kernel,grid=(steps,),in_specs=[row(g),const(w),row(tok),const(gain),row(gres)]+[hbm]*len(more),
         out_specs=row(gres),out_shape=sd((n,d),F32),input_output_aliases={} if begun is None else {4+len(more):0},
-        name="mixer_dx",**params(5*10**10))(g,w,tok,gain,gres,*more)
+        name="mixer_dx",**params())(g,w,tok,gain,gres,*more)
 
 
 def load_w(w_hbm,w_ref,sems,stacks):
@@ -399,7 +399,7 @@
         for t in range(count):
             keep,came=ins[2*t],ins[2*t+1]
             rows=keep.shape[1]
-            outs[j][0,row:row+rows]=(keep[at_ref[j]].astype(F32)+came[at_ref[j]].astype(F32)).astype(BF)
+            outs[j][0,row:row+rows]=keep[at_ref[j]]+came[at_ref[j]]
             row+=rows
 
 
@@ -412,34 +412,44 @@
         out_shape=[jax.ShapeDtypeStruct((steps,sum(each),128),BF)]*4,name="plane",**params())(at,*[x for p in pairs for x in p],*deps)
 
 
-def line_kernel(at_ref,*rest):
-    ins=rest[:4]
-    scr,turned=rest[-2:]; outs=rest[-6:-2]
+def line_kernel(*refs):
+    ins=refs[:4]
+    out,scr,turned=refs[-3:]
     steps,rows,_=ins[0].shape
     main=rows-128
     for i in range(steps):
         v=functools.reduce(jnp.add,[x[i].astype(F32) for x in ins])
         scr[i]=v[:main].astype(BF)
         turned[i]=v[main:].T.astype(BF)
-    each=steps//4
+    each=steps//4; size=each*main+32*steps
     for k in range(4):
         for e in range(each):
-            outs[k][e*main:(e+1)*main]=scr[at_ref[k]*each+e]
-        at=pl.multiple_of(at_ref[k]*32,32)
+            out[k*size+e*main:k*size+(e+1)*main]=scr[k*each+e]
         for i in range(steps):
-            outs[k][each*main+32*i:each*main+32*(i+1)]=turned[i,pl.ds(at,32)]
-
-
-def line_call(parts,at,deps):
+            at=k*size+each*main+32*i
+            out[at:at+32]=turned[i,32*k:32*k+32]
+
+
+def line_call(parts,deps):
     steps,rows,_=parts[0].shape
-    out=steps//4*(rows-128)+steps*32
-    full=pl.BlockSpec(parts[0].shape,lambda i,_:(0,0,0))
-    return pl.pallas_call(line_kernel,
-        grid_spec=pltpu.PrefetchScalarGridSpec(num_scalar_prefetch=1,grid=(1,),
-            in_specs=[full]*4+[pl.BlockSpec(memory_space=pl.ANY)]*len(deps),
-            out_specs=[pl.BlockSpec((out,128),lambda i,_:(0,0))]*4,
-            scratch_shapes=[pltpu.VMEM((steps,rows-128,128),BF),pltpu.VMEM((steps,128,128),BF)]),
-        out_shape=[jax.ShapeDtypeStruct((out,128),BF)]*4,name="line",**params())(at,*parts,*deps)
+    shape=(4*(steps//4*(rows-128)+steps*32),128)
+    full=pl.BlockSpec(parts[0].shape,lambda i:(0,0,0))
+    return pl.pallas_call(line_kernel,grid=(1,),
+        in_specs=[full]*4+[pl.BlockSpec(memory_space=pl.ANY)]*len(deps),out_specs=pl.BlockSpec(shape,lambda i:(0,0)),
+        scratch_shapes=[pltpu.VMEM((steps,rows-128,128),BF),pltpu.VMEM((steps,128,128),BF)],
+        out_shape=jax.ShapeDtypeStruct(shape,BF),name="line",**params(5*10**10))(*parts,*deps)
+
+
+def stack_kernel(count,*refs):
+    refs[-1][...]=functools.reduce(jnp.add,[r[...].astype(F32) for r in refs[:count]]).astype(BF)
+
+
+def stack_call(parts,chunk,deps):
+    rows,cols=parts[0].shape
+    spec=pl.BlockSpec((rows,chunk),lambda i:(0,i))
+    return pl.pallas_call(functools.partial(stack_kernel,len(parts)),grid=(cols//chunk,),
+        in_specs=[spec]*len(parts)+[pl.BlockSpec(memory_space=pl.ANY)]*len(deps),out_specs=spec,
+        out_shape=jax.ShapeDtypeStruct((rows,cols),BF),name="stack",**params())(*parts,*deps)
 
 
 def spread_kernel(sizes,count,at_ref,*rest):
@@ -466,19 +476,8 @@
         out_shape=[jax.ShapeDtypeStruct((stacks,rows,cols),BF)]*count,name="spread",**params())(at,*[p for g in groups for p in g],*deps)
 
 
-def sum_kernel(count,*refs):
-    refs[-1][...]=functools.reduce(jnp.add,[r[...].astype(F32) for r in refs[:count]])
-
-
-def sum_call(parts,deps):
-    full=pl.BlockSpec(parts[0].shape,lambda i:(0,)*parts[0].ndim)
-    return pl.pallas_call(functools.partial(sum_kernel,len(parts)),grid=(1,),
-        in_specs=[full]*len(parts)+[pl.BlockSpec(memory_space=pl.ANY)]*len(deps),out_specs=full,
-        out_shape=jax.ShapeDtypeStruct(parts[0].shape,F32),name="sum_parts",**params())(*parts,*deps)
-
-
 def rows_kernel(x_ref,*rest):
-    rest[-1][...]=jnp.sum(x_ref[...],axis=0)
+    rest[-1][...]=jnp.sum(x_ref[...].astype(F32),axis=0)
 
 
 def rows_call(x,deps):
@@ -635,28 +634,26 @@
         out = send_line([jnp.take(out, in_line[j], axis=1) for j in range(mlps)], mlps)
         deps = [in_keep]
     else:
-        blocks = line_call(blocks, in_line, [in_keep])
-        main = send_line(blocks, mlps)
-        deps = list(blocks)
-    grad_tokens = dx_call(0, 2, None, grads, w_in, tokens, gain_mix, grad_res, deps)
-    blocks = spread([[p[None] for p in inner]], in_plane, 1, 640, [grad_tokens])
-    grad_tokens = dx_call(1, 2, grad_tokens, grads, w_in, tokens, gain_mix, grad_res, list(blocks))
+        blocks = line_call(blocks, [in_keep])
+        main = lax.psum_scatter(blocks, "mlp", scatter_dimension=0, tiled=True)
+        deps = [blocks]
+    blocks = spread([[p[None] for p in inner]], in_plane, 1, 640, deps)
+    grad_tokens = dx_call(0, 2, None, grads, w_in, tokens, gain_mix, grad_res, list(blocks))
+    grad_tokens = dx_call(1, 2, grad_tokens, grads, w_in, tokens, gain_mix, grad_res, [])
     block_out = down_call(0, 2, None, residual, hidden, mlp_all, [grad_tokens])
-    block_out = down_call(1, 2, block_out, residual, hidden, mlp_all, [])
+    small = rows_call(small, [block_out])
     blocks = within(send_blocks(blocks, low, rows), 1)
-    blocks = [b.reshape(1, mlps, shard, GW) for b in blocks]
-    if low:
-        in_grads = send_line([jnp.take(blocks[0], in_line[j], axis=1).astype(BF) for j in range(mlps)], mlps)
-    else:
-        in_grads = send_line(spread([blocks], in_line, 1, 640, [block_out]), mlps)
-    small = rows_call(small, [in_grads[0], block_out]).reshape(-1)
+    blocks = stack_call([b.reshape(-1, GW) for b in blocks], 640, [block_out]).reshape(mlps, shard, GW)
+    in_grads = lax.all_to_all(blocks, "mlp", 0, 0, tiled=True)
+    block_out = down_call(1, 2, block_out, residual, hidden, mlp_all, [small, blocks])
+    small = small.reshape(-1)
+    in_grads = total([in_grads[j] for j in range(mlps)])
     if low:
         mlp_grads, out_grads = total(main), total(out)
     else:
-        main = sum_call(main, [small])
+        main = main.astype(F32)
         mlp_grads = main[: 3 * hid].reshape(2, 3, hid // 2, 128).transpose(1, 0, 2, 3).reshape(3, hid, 128)
         out_grads = main[3 * hid :].reshape(8, shard, 128).transpose(0, 2, 1).reshape(DV, shard)
-    in_grads = total(in_grads)[0]
     gain_mix_grad = jnp.sum(in_grads * mixer_local.astype(F32), axis=1) / norm_gain_mix.astype(F32)
     at = 16 * DK + DK + HV + (here * mlps + lax.axis_index("mlp")) * shard
     return (

time: 615 us -> 583 us (0.948)
  waiting for transfers between devices: 126 us -> 104 us
    all_to_all x0 -> x1, waiting for transfers between devices: none -> 19.1 us  [body(): in_grads = lax.all_to_all(blocks, 'mlp', 0, 0, tiled=True)]
    all_gather x1, waiting for transfers between devices: 14.3 us -> 0.02 us  [body(): small = lax.all_gather(small.reshape(-1, 256), ('rows', 'mlp'), axis=0)]
    ppermute x6, waiting for transfers between devices: 14.2 us -> 0.02 us  [send_blocks(): lax.ppermute(blocks[j], 'rows', [(i, i ^ j << low + 1) for i in range(cou...]
    ppermute x6 -> x0, waiting for transfers between devices: 13 us -> none  [send_line(): lax.ppermute(blocks[j], 'mlp', [(i, (i + j) % count) for i in range(count)])]
    ppermute x6 -> x0, starting transfers between devices: 8.38 us -> none  [send_line(): lax.ppermute(blocks[j], 'mlp', [(i, (i + j) % count) for i in range(count)])]
    unnamed x84 -> x70, local copies, waits for them, and re-layouts: 13.4 us -> 12.7 us
  transfers between devices with their start and end apart: 36 -> 32, of which waited for: 13 -> 9; matrix products, arithmetic and copies ran while one was open for 3% -> 4% of each run, Pallas kernels for 44% -> 47%
where the time goes in v4:
time: 583 us; the launch traced here: 575 us
  Pallas kernels  391 us (67%)
  waiting for transfers between devices  104 us (18%)
  local copies, waits for them, and re-layouts  31.3 us (5%)
  starting transfers between devices  26.2 us (4%)
  between operations  14.6 us (3%)
  other arithmetic  7.31 us (1%)
    pallas_call x4, Pallas kernels, dw_call(): pl.pallas_call(functools.partial(dw_kernel, count, wide), grid_spec=pltpu...  88.3 us
    pallas_call x1, Pallas kernels, mlp_call(): pl.pallas_call(functools.partial(mlp_kernel, chunk), grid=(n // T,), in_s...  86.5 us
    pallas_call x2, Pallas kernels, bwd_call(): pl.pallas_call(functools.partial(bwd_kernel, NT, seq), grid_spec=pltpu.Pr...  78.6 us
    pallas_call x1, Pallas kernels, fwd_call(): pl.pallas_call(functools.partial(fwd_kernel, NT, cuts), grid_spec=pltpu.P...  51 us
    ppermute x19, waiting for transfers between devices, swap(): return lax.ppermute(x, axis, [(i, i ^ 1 << bit) for i in range(count)])  43.4 us
    pallas_call x2, Pallas kernels, dx_call(): pl.pallas_call(dx_kernel, grid=(steps,), in_specs=[row(g), const(w), row(...  27.8 us
    ppermute x3, waiting for transfers between devices, gather_pieces(): lax.ppermute(x, 'mlp', [(i, (i + step) % mlps) for i in range(mlps)])  26.2 us
    pallas_call x2, Pallas kernels, down_call(): pl.pallas_call(down_kernel, grid=(steps,), in_specs=[row(d), row(ff), hbm...  25.1 us
  transfers between devices with their start and end apart: 32, of which 9 were waited for; matrix products, arithmetic and copies ran while one was open for 4% of the time, Pallas kernels for 47%

profile of v4, /device:TPU:0, one launch (start us, length us, event | category | flops | bytes accessed | tf_op | source)
XLA Modules:
  0.0 574.9 jit_solution(14628216867788646352)
XLA Ops:
  8.0 2.0 pad_maximum_fusion
  12.4 1.0 concatenate.30
  13.4 5.1 collective-permute-start.2
  18.5 1.0 collective-permute-start
  20.5 4.2 collective-permute-done.2
  24.6 22.1 %collective-permute-done.1 = bf16[32,3200]{1,0:T(8,128)(2,1)S(1)} collective-permute-done((bf16[32,3200]{1,0:T(8,128)(2,1)S(1)}, bf16[32,3200]{1,0:T(8,128)(2,1)S(1)}, u32[]{:S(2)}, u32[]{:S(2)}) %collective-permute-start.1) | collective-permute-done | bytes 204832 | tf_op jit(solution)/shard_map/ppermute | solution.py:523
  46.8 1.6 collective-permute-start.10
  49.2 1.5 collective-permute-start.3
  51.2 10.3 %collective-permute-done.10.rest_9_ = bf16[128,1664]{1,0:T(8,128)(2,1)S(1)} collective-permute-done((bf16[128,1664]{1,0:T(8,128)(2,1)S(1)}, bf16[128,1664]{1,0:T(8,128)(2,1)S(1)}, u32[]{:S(2)}, u32[]{:S(2)}) %collective-permute-start.10) | collective-permute-done | bytes 426016 | tf_op jit(solution)/shard_map/ppermute | solution.py:491
  61.5 1.3 collective-permute-start.12
  62.8 9.3 %collective-permute-done.4.rest_2_ = bf16[128,1536]{1,0:T(8,128)(2,1)S(1)} collective-permute-done((bf16[128,1536]{1,0:T(8,128)(2,1)S(1)}, bf16[128,1536]{1,0:T(8,128)(2,1)S(1)}, u32[]{:S(2)}, u32[]{:S(2)}) %collective-permute-start.4) | collective-permute-done | bytes 393248 | tf_op jit(solution)/shard_map/ppermute | solution.py:491
  72.1 1.6 collective-permute-start.5
  73.7 9.7 %collective-permute-done.11.rest_10_ = bf16[128,1664]{1,0:T(8,128)(2,1)S(1)} collective-permute-done((bf16[128,1664]{1,0:T(8,128)(2,1)S(1)}, bf16[128,1664]{1,0:T(8,128)(2,1)S(1)}, u32[]{:S(2)}, u32[]{:S(2)}) %collective-permute-start.11) | collective-permute-done | bytes 426016 | tf_op jit(solution)/shard_map/ppermute | solution.py:491
  83.9 12.0 %collective-permute-done.12.rest_11_ = bf16[128,1664]{1,0:T(8,128)(2,1)S(1)} collective-permute-done((bf16[128,1664]{1,0:T(8,128)(2,1)S(1)}, bf16[128,1664]{1,0:T(8,128)(2,1)S(1)}, u32[]{:S(2)}, u32[]{:S(2)}) %collective-permute-start.12) | collective-permute-done | bytes 426016 | tf_op jit(solution)/shard_map/ppermute | solution.py:491
  101.2 51.0 %mixer_fwd.1 = (bf16[2048,1024]{1,0:T(8,128)(2,1)}, f32[2048,512]{1,0:T(8,128)}, f32[2048,512]{1,0:T(8,128)}, f32[2048,512]{1,0:T(8,128)}, f32[2048,512]{1,0:T(8...) custom-call(s32[8]{0:T(128)} %reshape.101.st_ref, ...), custom_call_target="tpu_custom_call" | custom-call | flops 1 | bytes 1 | tf_op jit(solution)/shard_map/mixer_fwd/pallas_call | solution.py:160
  152.2 1.4 fusion.8
  153.7 15.3 %all-gather.6.cloned.1.call-done = bf16[75776,128]{1,0:T(8,128)(2,1)} async-done(((bf16[2368,128]{1,0:T(8,128)(2,1)}), bf16[75776,128]{1,0:T(8,128)(2,1)}) %all-gather.6.cloned.1.call-update) | async-done | bytes 19398672 | tf_op jit(solution)/shard_map/all_gather | solution.py:569
  168.9 1.7 slice.137
  170.7 1.0 copy.62
  171.7 1.9 copy.73
  173.6 86.5 %mlp.1 = (f32[2048,1024]{1,0:T(8,128)}, bf16[2048,1024]{1,0:T(8,128)(2,1)}, bf16[2048,2816]{1,0:T(8,128)(2,1)}, bf16[2048,2816]{1,0:T(8,128)(2,1)}, bf16[2048,28...) custom-call(bf16[2048,1024]{1,0:T(8,128)(2,1)} %tok_ref.7, ...), custom_call_target="tpu_custom_call" | custom-call | flops 1 | bytes 1 | tf_op jit(solution)/shard_map/mlp/pallas_call | solution.py:329
  260.2 19.8 %grad_w.4 = (bf16[4,2816,128]{2,1,0:T(8,128)(2,1)}, bf16[4,2816,128]{2,1,0:T(8,128)(2,1)}) custom-call(s32[1]{0:T(128)} %bitcast.13.sel_ref, bf16[2048,2816]{1,0:T(8,128)(2,1)} %get-tuple-element.66.rest_0_.hid_ref, bf16[2048,1024]{1,0:T(8,128)(2,1)} %rest_1_.1, bf16[2048,1024]{1,0:T(8,128)(2,1)} %get-tuple-element.79.rest_2_), custom_call_target="tpu_custom_call" | custom-call | flops 99999997952 | bytes 1 | tf_op jit(solution)/shard_map/grad_w/pallas_call | solution.py:386
  280.3 35.4 %grad_w.5 = (bf16[4,2816,128]{2,1,0:T(8,128)(2,1)}, bf16[4,2816,128]{2,1,0:T(8,128)(2,1)}, bf16[4,2816,128]{2,1,0:T(8,128)(2,1)}, bf16[4,2816,128]{2,1,0:T(8,128)(2,1)}) custom-call(s32[1]{0:T(128)} %bitcast.13.sel_ref, bf16[2048,2816]{1,0:T(8,128)(2,1)} %get-tuple-element.77.rest_0_, bf16[2048,2816]{1,0:T(8,128)(2,1)} %get-tuple-element.78.rest_1_, ...), custom_call_target="tpu_custom_call" | custom-call | flops 99999997952 | bytes 1 | tf_op jit(solution)/shard_map/grad_w/pallas_call | solution.py:386
  316.3 1.6 copy-done.3
  317.9 9.8 %grad_w.6 = (bf16[4,1024,128]{2,1,0:T(8,128)(2,1)}, bf16[4,1024,128]{2,1,0:T(8,128)(2,1)}) custom-call(s32[1]{0:T(128)} %bitcast.13.sel_ref, bf16[2048,1024]{1,0:T(8,128)(2,1)} %get-tuple-element.63.mix_ref.rest_0_, bf16[2048,1024]{1,0:T(8,128)(2,1)} %get-tuple-element.67.rest_1_.gmix_ref, bf16[4,2816,128]{2,1,0:T(8,128)(2,1)} %get-tuple-element.81.rest_2_.rest_0_, ...), custom_call_target="tpu_custom_call" | custom-call | flops 99999997952 | bytes 1 | tf_op jit(solution)/shard_map/grad_w/pallas_call | solution.py:386
  328.6 2.1 collective-permute-done.20.rest_7_
  331.6 12.9 %plane.1 = (bf16[8,1184,128]{2,1,0:T(8,128)(2,1)}, bf16[8,1184,128]{2,1,0:T(8,128)(2,1)}, bf16[8,1184,128]{2,1,0:T(8,128)(2,1)}, bf16[8,1184,128]{2,1,0:T(8,128)(2,1)}) custom-call(s32[4]{0:T(128)} %iota_xor_fusion.at_ref, bf16[4,2816,128]{2,1,0:T(8,128)(2,1)} %get-tuple-element.81.rest_2_.rest_0_, bf16[4,2816,128]{2,1,0:T(8,128)(2,1)} %collective-permute-done.17.rest_1_, ...), custom_call_target="tpu_custom_call" | custom-call | flops 1 | bytes 1 | tf_op jit(solution)/shard_map/plane/pallas_call | solution.py:408
  344.6 1.5 collective-permute-start.22
  346.7 1.4 collective-permute-start.24
  348.1 39.4 %mixer_bwd.2 = (bf16[2048,3200]{1,0:T(8,128)(2,1)}, f32[128,512]{1,0:T(8,128)}, f32[8,512]{1,0:T(8,128)}, f32[8,256]{1,0:T(8,128)}) custom-call(s32[8]{0:T(128)} %reshape.101.st_ref, bf16[2048,1024]{1,0:T(8,128)(2,1)} %get-tuple-element.67.rest_1_.gmix_ref, bf16[1024,1024]{1,0:T(8,128)(2,1)} %bitcast.65, bf16[128,512]{1,0:T(8,128)(2,1)} %concatenate.28.wdec_ref, ...), custom_call_target="tpu_custom_call" | custom-call | flops 1 | bytes 1 | tf_op jit(solution)/shard_map/mixer_bwd/pallas_call | solution.py:251
  387.5 39.2 %mixer_bwd.3 = (bf16[2048,3200]{1,0:T(8,128)(2,1)}, f32[128,512]{1,0:T(8,128)}, f32[8,512]{1,0:T(8,128)}, f32[8,256]{1,0:T(8,128)}) custom-call(s32[8]{0:T(128)} %reshape.101.st_ref, bf16[2048,1024]{1,0:T(8,128)(2,1)} %get-tuple-element.67.rest_1_.gmix_ref, bf16[1024,1024]{1,0:T(8,128)(2,1)} %bitcast.66, ...), custom_call_target="tpu_custom_call", output_to_operand_aliasing={{0}: (14, {})} | custom-call | flops 1 | bytes 1 | tf_op jit(solution)/shard_map/mixer_bwd/pallas_call | solution.py:251
  429.8 23.2 %grad_w.7 = (bf16[4,128,3200]{2,1,0:T(8,128)(2,1)}, bf16[4,128,3200]{2,1,0:T(8,128)(2,1)}) custom-call(s32[1]{0:T(128)} %bitcast.13.sel_ref, bf16[2048,3200]{1,0:T(8,128)(2,1)} %get-tuple-element.100.rest_0_.g_ref, bf16[2048,1024]{1,0:T(8,128)(2,1)} %get-tuple-element.103.rest_1_), custom_call_target="tpu_custom_call" | custom-call | flops 1 | bytes 1 | tf_op jit(solution)/shard_map/grad_w/pallas_call | solution.py:386
  453.1 7.5 %line.1.rest_2_ = bf16[9472,128]{1,0:T(8,128)(2,1)} custom-call(bf16[8,1184,128]{2,1,0:T(8,128)(2,1)} %get-tuple-element.88.rest_0_.refs_0_, bf16[8,1184,128]{2,1,0:T(8,128)(2,1)} %collective-permute-done.22.refs_1_, bf16[8,1184,128]{2,1,0:T(8,128)(2,1)} %collective-permute-done.23.refs_2_, bf16[8,1184,128]{2,1,0:T(8,128)(2,1)} %collective-permute-done.24.refs_3_, ...), custom_call_target="tpu_custom_call" | custom-call | flops 49999998976 | bytes 1 | tf_op jit(solution)/shard_map/line/pallas_call | solution.py:437
  460.7 1.7 copy-done.2
  462.4 6.8 %spread.1 = (bf16[1,128,3200]{2,1,0:T(8,128)(2,1)}, bf16[1,128,3200]{2,1,0:T(8,128)(2,1)}, bf16[1,128,3200]{2,1,0:T(8,128)(2,1)}, bf16[1,128,3200]{2,1,0:T(8,128)(2,1)}) custom-call(s32[4]{0:T(128)} %iota_xor_fusion.at_ref, bf16[1,4,128,3200]{3,2,1,0:T(8,128)(2,1)} %bitcast.72, bf16[1,4,128,3200]{3,2,1,0:T(8,128)(2,1)} %bitcast.73, ...), custom_call_target="tpu_custom_call" | custom-call | flops 1 | bytes 1 | tf_op jit(solution)/shard_map/spread/pallas_call | solution.py:472
  469.2 1.5 collective-permute-start.25
  471.3 1.4 collective-permute-start.27
  472.7 14.2 %mixer_dx.2.rest_0_ = f32[2048,1024]{1,0:T(8,128)} custom-call(bf16[2048,3200]{1,0:T(8,128)(2,1)} %get-tuple-element.100.rest_0_.g_ref, bf16[1024,3200]{1,0:T(8,128)(2,1)} %get-tuple-element.101.w_ref, bf16[2048,1024]{1,0:T(8,128)(2,1)} %tok_ref.7, f32[1,1024]{1,0:T(1,128)} %get-tuple-element.167.gain_ref, f32[2048,1024]{1,0:T(8,128)} %get-tuple-element.102.gres_ref, ...), custom_call_target="tpu_custom_call" | custom-call | flops 1 | bytes 1 | tf_op jit(solution)/shard_map/mixer_dx/pallas_call | solution.py:277
  486.8 13.7 %mixer_dx.3.rest_0_ = f32[2048,1024]{1,0:T(8,128)} custom-call(bf16[2048,3200]{1,0:T(8,128)(2,1)} %get-tuple-element.100.rest_0_.g_ref, bf16[1024,3200]{1,0:T(8,128)(2,1)} %get-tuple-element.101.w_ref, bf16[2048,1024]{1,0:T(8,128)(2,1)} %tok_ref.7, f32[1,1024]{1,0:T(1,128)} %get-tuple-element.167.gain_ref, ...), custom_call_target="tpu_custom_call", output_to_operand_aliasing={{}: (5, {})} | custom-call | flops 1 | bytes 1 | tf_op jit(solution)/shard_map/mixer_dx/pallas_call | solution.py:277
  500.5 12.7 %mlp_down.2.rest_0_.refs_4_.rest_2_ = bf16[2048,1024]{1,0:T(8,128)(2,1)} custom-call(f32[2048,1024]{1,0:T(8,128)} %get-tuple-element.65.res_ref, bf16[2048,2816]{1,0:T(8,128)(2,1)} %get-tuple-element.66.rest_0_.hid_ref, bf16[8,4,2368,128]{3,2,1,0:T(8,128)(2,1)} %bitcast.62, f32[2048,1024]{1,0:T(8,128)} %mixer_dx.3.rest_0_), custom_call_target="tpu_custom_call" | custom-call | flops 1 | bytes 1 | tf_op jit(solution)/shard_map/mlp_down/pallas_call | solution.py:349
  514.7 4.5 stack.1
  519.2 3.5 all-to-all-start
  522.7 2.0 sum_rows.1.rest_0_
  524.8 1.3 slice.151
  530.1 12.5 %mlp_down.3 = bf16[2048,1024]{1,0:T(8,128)(2,1)} custom-call(f32[2048,1024]{1,0:T(8,128)} %get-tuple-element.65.res_ref, bf16[2048,2816]{1,0:T(8,128)(2,1)} %get-tuple-element.66.rest_0_.hid_ref, bf16[8,4,2368,128]{3,2,1,0:T(8,128)(2,1)} %bitcast.63, f32[39,256]{1,0:T(8,128)} %sum_rows.1.rest_0_, ...), custom_call_target="tpu_custom_call", output_to_operand_aliasing={{}: (5, {})} | custom-call | flops 1 | bytes 1 | tf_op jit(solution)/shard_map/mlp_down/pallas_call | solution.py:349
  542.5 19.1 %all-to-all-done = bf16[4,32,3200]{2,1,0:T(8,128)(2,1)S(1)} async-done(((bf16[4,32,3200]{2,1,0:T(8,128)(2,1)}), bf16[4,32,3200]{2,1,0:T(8,128)(2,1)S(1)}, u32[]{:S(2)}, u32[]{:S(2)}) %all-to-all-start) | async-done | bytes 819232 | tf_op jit(solution)/shard_map/all_to_all | solution.py:647
  566.0 1.1 slice.153
  567.1 1.0 fusion.5
  (153 shorter events, 27.9 us)
Async XLA Ops:
  7.2 41.2 %copy-start.12 = (bf16[32,1024]{1,0:T(8,128)(2,1)S(1)}, bf16[32,1024]{1,0:T(8,128)(2,1)}, u32[]{:S(2)}) copy-start(bf16[32,1024]{1,0:T(8,128)(2,1)} %param.23) | copy-start | bytes 196612
  7.2 41.2 %copy-start.22 = (bf16[32,512]{1,0:T(8,128)(2,1)S(1)}, bf16[32,512]{1,0:T(8,128)(2,1)}, u32[]{:S(2)}) copy-start(bf16[32,512]{1,0:T(8,128)(2,1)} %param.22) | copy-start | bytes 98308
  7.2 41.2 %copy-start.23 = (bf16[32,512]{1,0:T(8,128)(2,1)S(1)}, bf16[32,512]{1,0:T(8,128)(2,1)}, u32[]{:S(2)}) copy-start(bf16[32,512]{1,0:T(8,128)(2,1)} %param.21) | copy-start | bytes 98308
  7.2 90.0 %copy-start.30 = (s32[2,4]{1,0:T(2,128)S(1)}, s32[2,4]{1,0:T(2,128)}, u32[]{:S(2)}) copy-start(s32[2,4]{1,0:T(2,128)} %param.18) | copy-start | bytes 100
  7.2 90.6 %copy-start.31 = (bf16[256]{0:T(256)(128)(2,1)S(1)}, bf16[256]{0:T(256)(128)(2,1)}, u32[]{:S(2)}) copy-start(bf16[256]{0:T(256)(128)(2,1)} %param.28) | copy-start | bytes 1540
  7.3 91.1 %copy-start.28 = (bf16[512]{0:T(512)(128)(2,1)S(1)}, bf16[512]{0:T(512)(128)(2,1)}, u32[]{:S(2)}) copy-start(bf16[512]{0:T(512)(128)(2,1)} %param.27) | copy-start | bytes 3076
  7.3 91.7 %copy-start.25 = (bf16[16,512]{1,0:T(8,128)(2,1)S(1)}, bf16[16,512]{1,0:T(8,128)(2,1)}, u32[]{:S(2)}) copy-start(bf16[16,512]{1,0:T(8,128)(2,1)} %param.26) | copy-start | bytes 49156
  7.3 161.7 %all-gather.6.cloned.1.call-start = ((), (), s32[]{:S(2)}) async-start(), calls=%async_computation.4 | async-start | bytes 20004864 | tf_op jit(solution)/shard_map/all_gather | solution.py:569
  10.0 512.7 %all-gather.4.cloned.1.call-start = ((), (), s32[]{:S(2)}) async-start(), calls=%async_computation.2 | async-start | bytes 1351680 | tf_op jit(solution)/shard_map/all_gather | solution.py:626
  13.4 33.4 %copy-start.7 = (bf16[32,3200]{1,0:T(8,128)(2,1)}, bf16[32,3200]{1,0:T(8,128)(2,1)S(1)}, u32[]{:S(2)}) copy-start(bf16[32,3200]{1,0:T(8,128)(2,1)S(1)} %concatenate.30) | copy-start | bytes 614404
  13.4 11.2 %collective-permute-start.2 = (bf16[32,3200]{1,0:T(8,128)(2,1)S(1)}, bf16[32,3200]{1,0:T(8,128)(2,1)S(1)}, u32[]{:S(2)}, u32[]{:S(2)}) collective-permute-start(bf16[32,3200]{1,0:T(8,128)(2,1)S(1)} %concatenate.30), channel_id=1, source_target_pairs={{0,3},{1,0},{2,1},{3,2},{4,7},{5,4},{6,5},{7,6},{8,11},{9,8},{10,9... | collective-permute-start | bytes 614408 | tf_op jit(solution)/shard_map/ppermute | solution.py:523
  18.5 28.2 %collective-permute-start.1 = (bf16[32,3200]{1,0:T(8,128)(2,1)S(1)}, bf16[32,3200]{1,0:T(8,128)(2,1)S(1)}, u32[]{:S(2)}, u32[]{:S(2)}) collective-permute-start(bf16[32,3200]{1,0:T(8,128)(2,1)S(1)} %concatenate.30), channel_id=1, source_target_pairs={{0,2},{1,3},{2,0},{3,1},{4,6},{5,7},{6,4},{7,5},{8,10},{9,11},{10,... | collective-permute-start | bytes 614408 | tf_op jit(solution)/shard_map/ppermute | solution.py:523
  18.5 28.2 %collective-permute-start = (bf16[32,3200]{1,0:T(8,128)(2,1)S(1)}, bf16[32,3200]{1,0:T(8,128)(2,1)S(1)}, u32[]{:S(2)}, u32[]{:S(2)}) collective-permute-start(bf16[32,3200]{1,0:T(8,128)(2,1)S(1)} %concatenate.30), channel_id=1, source_target_pairs={{0,1},{1,2},{2,3},{3,0},{4,5},{5,6},{6,7},{7,4},{8,9},{9,10},{10,1... | collective-permute-start | bytes 614408 | tf_op jit(solution)/shard_map/ppermute | solution.py:523
  46.8 53.5 %copy-start.4 = (bf16[128,1664]{1,0:T(8,128)(2,1)}, bf16[128,1664]{1,0:T(8,128)(2,1)S(1)}, u32[]{:S(2)}) copy-start(bf16[128,1664]{1,0:T(8,128)(2,1)S(1)} %pad_maximum_fusion.1.rest_8_) | copy-start | bytes 1277956
  46.8 14.7 %collective-permute-start.10 = (bf16[128,1664]{1,0:T(8,128)(2,1)S(1)}, bf16[128,1664]{1,0:T(8,128)(2,1)S(1)}, u32[]{:S(2)}, u32[]{:S(2)}) collective-permute-start(bf16[128,1664]{1,0:T(8,128)(2,1)S(1)} %pad_maximum_fusion.1.rest_8_), channel_id=1, source_target_pairs={{0,16},{4,20},{8,24},{12,28},{16,0},{20,4},{24,8},{28,12},{1,17},{... | collective-permute-start | bytes 1277960 | tf_op jit(solution)/shard_map/ppermute | solution.py:491
  48.5 51.8 %copy-start.5 = (bf16[128,1536]{1,0:T(8,128)(2,1)}, bf16[128,1536]{1,0:T(8,128)(2,1)S(1)}, u32[]{:S(2)}) copy-start(bf16[128,1536]{1,0:T(8,128)(2,1)S(1)} %fusion.2.rest_0_) | copy-start | bytes 1179652
  48.5 2.7 collective-permute-start.6
  48.6 23.5 %collective-permute-start.4 = (bf16[128,1536]{1,0:T(8,128)(2,1)S(1)}, bf16[128,1536]{1,0:T(8,128)(2,1)S(1)}, u32[]{:S(2)}, u32[]{:S(2)}) collective-permute-start(bf16[128,1536]{1,0:T(8,128)(2,1)S(1)} %fusion.2.rest_0_), channel_id=1, source_target_pairs={{0,16},{4,20},{8,24},{12,28},{16,0},{20,4},{24,8},{28,12},{1,17},{... | collective-permute-start | bytes 1179656 | tf_op jit(solution)/shard_map/ppermute | solution.py:491
  49.2 23.0 %collective-permute-start.3 = (bf16[128,1536]{1,0:T(8,128)(2,1)S(1)}, bf16[128,1536]{1,0:T(8,128)(2,1)}, u32[]{:S(2)}, u32[]{:S(2)}) collective-permute-start(bf16[128,1536]{1,0:T(8,128)(2,1)S(1)} %fusion.2.rest_0_), channel_id=1, source_target_pairs={{0,8},{4,12},{8,0},{12,4},{16,24},{20,28},{24,16},{28,20},{1,9},{5... | collective-permute-start | bytes 1179656 | tf_op jit(solution)/shard_map/ppermute | solution.py:491
  50.6 32.7 %collective-permute-start.11 = (bf16[128,1664]{1,0:T(8,128)(2,1)S(1)}, bf16[128,1664]{1,0:T(8,128)(2,1)S(1)}, u32[]{:S(2)}, u32[]{:S(2)}) collective-permute-start(bf16[128,1664]{1,0:T(8,128)(2,1)S(1)} %pad_maximum_fusion.1.rest_8_), channel_id=1, source_target_pairs={{0,8},{4,12},{8,0},{12,4},{16,24},{20,28},{24,16},{28,20},{1,9},{5... | collective-permute-start | bytes 1277960 | tf_op jit(solution)/shard_map/ppermute | solution.py:491
  51.2 44.7 %copy-start.19 = (bf16[128,1536]{1,0:T(8,128)(2,1)}, bf16[128,1536]{1,0:T(8,128)(2,1)S(1)}, u32[]{:S(2)}) copy-start(bf16[128,1536]{1,0:T(8,128)(2,1)S(1)} %collective-permute-done.6.rest_4_) | copy-start | bytes 1179652
  51.2 32.2 %collective-permute-start.13 = (bf16[128,1664]{1,0:T(8,128)(2,1)S(1)}, bf16[128,1664]{1,0:T(8,128)(2,1)S(1)}, u32[]{:S(2)}, u32[]{:S(2)}) collective-permute-start(bf16[128,1664]{1,0:T(8,128)(2,1)S(1)} %pad_maximum_fusion.1.rest_8_), channel_id=1, source_target_pairs={{0,4},{4,0},{8,12},{12,8},{16,20},{20,16},{24,28},{28,24},{1,5},{5... | collective-permute-start | bytes 1277960 | tf_op jit(solution)/shard_map/ppermute | solution.py:491
  61.5 38.8 %copy-start.13 = (bf16[128,1664]{1,0:T(8,128)(2,1)}, bf16[128,1664]{1,0:T(8,128)(2,1)S(1)}, u32[]{:S(2)}) copy-start(bf16[128,1664]{1,0:T(8,128)(2,1)S(1)} %collective-permute-done.10.rest_9_) | copy-start | bytes 1277956
  61.5 34.4 %collective-permute-start.12 = (bf16[128,1664]{1,0:T(8,128)(2,1)S(1)}, bf16[128,1664]{1,0:T(8,128)(2,1)S(1)}, u32[]{:S(2)}, u32[]{:S(2)}) collective-permute-start(bf16[128,1664]{1,0:T(8,128)(2,1)S(1)} %collective-permute-done.10.rest_9_), channel_id=1, source_target_pairs={{0,8},{4,12},{8,0},{12,4},{16,24},{20,28},{24,16},{28,20},{1,9},{5... | collective-permute-start | bytes 1277960 | tf_op jit(solution)/shard_map/ppermute | solution.py:491
  72.1 23.8 %collective-permute-start.8 = (bf16[128,1536]{1,0:T(8,128)(2,1)S(1)}, bf16[128,1536]{1,0:T(8,128)(2,1)S(1)}, u32[]{:S(2)}, u32[]{:S(2)}) collective-permute-start(bf16[128,1536]{1,0:T(8,128)(2,1)S(1)} %collective-permute-done.4.rest_2_), channel_id=1, source_target_pairs={{0,4},{4,0},{8,12},{12,8},{16,20},{20,16},{24,28},{28,24},{1,5},{5... | collective-permute-start | bytes 1179656 | tf_op jit(solution)/shard_map/ppermute | solution.py:491
  72.1 25.1 %collective-permute-start.5 = (bf16[128,1536]{1,0:T(8,128)(2,1)}, bf16[128,1536]{1,0:T(8,128)(2,1)}, u32[]{:S(2)}, u32[]{:S(2)}) collective-permute-start(bf16[128,1536]{1,0:T(8,128)(2,1)} %collective-permute-done.3.rest_1_), channel_id=1, source_target_pairs={{0,16},{4,20},{8,24},{12,28},{16,0},{20,4},{24,8},{28,12},{1,17},{... | collective-permute-start | bytes 1179656 | tf_op jit(solution)/shard_map/ppermute | solution.py:491
  83.4 16.9 %collective-permute-start.15 = (bf16[128,1664]{1,0:T(8,128)(2,1)S(1)}, bf16[128,1664]{1,0:T(8,128)(2,1)S(1)}, u32[]{:S(2)}, u32[]{:S(2)}) collective-permute-start(bf16[128,1664]{1,0:T(8,128)(2,1)S(1)} %collective-permute-done.11.rest_10_), channel_id=1, source_target_pairs={{0,4},{4,0},{8,12},{12,8},{16,20},{20,16},{24,28},{28,24},{1,5},{5... | collective-permute-start | bytes 1277960 | tf_op jit(solution)/shard_map/ppermute | solution.py:491
  83.4 16.9 %collective-permute-start.14 = (bf16[128,1664]{1,0:T(8,128)(2,1)S(1)}, bf16[128,1664]{1,0:T(8,128)(2,1)S(1)}, u32[]{:S(2)}, u32[]{:S(2)}) collective-permute-start(bf16[128,1664]{1,0:T(8,128)(2,1)S(1)} %collective-permute-done.10.rest_9_), channel_id=1, source_target_pairs={{0,4},{4,0},{8,12},{12,8},{16,20},{20,16},{24,28},{28,24},{1,5},{5... | collective-permute-start | bytes 1277960 | tf_op jit(solution)/shard_map/ppermute | solution.py:491
  95.9 4.4 collective-permute-start.16
  96.7 3.5 collective-permute-start.7
  97.2 3.1 collective-permute-start.9
  280.0 36.3 %collective-permute-start.19 = (bf16[4,2816,128]{2,1,0:T(8,128)(2,1)}, bf16[4,2816,128]{2,1,0:T(8,128)(2,1)S(1)}, u32[]{:S(2)}, u32[]{:S(2)}) collective-permute-start(bf16[4,2816,128]{2,1,0:T(8,128)(2,1)} %get-tuple-element.85), channel_id=1, source_target_pairs={{0,4},{4,0},{8,12},{12,8},{16,20},{20,16},{24,28},{28,24},{1,5},{5... | collective-permute-start | bytes 8650760 | tf_op jit(solution)/shard_map/ppermute | solution.py:491
  315.7 12.8 %collective-permute-start.17 = (bf16[4,2816,128]{2,1,0:T(8,128)(2,1)}, bf16[4,2816,128]{2,1,0:T(8,128)(2,1)}, u32[]{:S(2)}, u32[]{:S(2)}) collective-permute-start(bf16[4,2816,128]{2,1,0:T(8,128)(2,1)} %get-tuple-element.82), channel_id=1, source_target_pairs={{0,4},{4,0},{8,12},{12,8},{16,20},{20,16},{24,28},{28,24},{1,5},{5... | collective-permute-start | bytes 8650760 | tf_op jit(solution)/shard_map/ppermute | solution.py:491
  316.0 12.5 %collective-permute-start.18 = (bf16[4,2816,128]{2,1,0:T(8,128)(2,1)}, bf16[4,2816,128]{2,1,0:T(8,128)(2,1)}, u32[]{:S(2)}, u32[]{:S(2)}) collective-permute-start(bf16[4,2816,128]{2,1,0:T(8,128)(2,1)} %get-tuple-element.84), channel_id=1, source_target_pairs={{0,4},{4,0},{8,12},{12,8},{16,20},{20,16},{24,28},{28,24},{1,5},{5... | collective-permute-start | bytes 8650760 | tf_op jit(solution)/shard_map/ppermute | solution.py:491
  327.7 2.9 collective-permute-start.20
  344.6 108.5 %collective-permute-start.22 = (bf16[8,1184,128]{2,1,0:T(8,128)(2,1)}, bf16[8,1184,128]{2,1,0:T(8,128)(2,1)}, u32[]{:S(2)}, u32[]{:S(2)}) collective-permute-start(bf16[8,1184,128]{2,1,0:T(8,128)(2,1)} %get-tuple-element.89.rest_1_), channel_id=1, source_target_pairs={{0,8},{4,12},{8,0},{12,4},{16,24},{20,28},{24,16},{28,20},{1,9},{5... | collective-permute-start | bytes 7274504 | tf_op jit(solution)/shard_map/ppermute | solution.py:511
  346.1 107.0 %collective-permute-start.23 = (bf16[8,1184,128]{2,1,0:T(8,128)(2,1)}, bf16[8,1184,128]{2,1,0:T(8,128)(2,1)}, u32[]{:S(2)}, u32[]{:S(2)}) collective-permute-start(bf16[8,1184,128]{2,1,0:T(8,128)(2,1)} %get-tuple-element.90.rest_2_), channel_id=1, source_target_pairs={{0,16},{4,20},{8,24},{12,28},{16,0},{20,4},{24,8},{28,12},{1,17},{... | collective-permute-start | bytes 7274504 | tf_op jit(solution)/shard_map/ppermute | solution.py:511
  346.7 106.4 %collective-permute-start.24 = (bf16[8,1184,128]{2,1,0:T(8,128)(2,1)}, bf16[8,1184,128]{2,1,0:T(8,128)(2,1)}, u32[]{:S(2)}, u32[]{:S(2)}) collective-permute-start(bf16[8,1184,128]{2,1,0:T(8,128)(2,1)} %get-tuple-element.91.rest_3_), channel_id=1, source_target_pairs={{0,24},{4,28},{8,16},{12,20},{16,8},{20,12},{24,0},{28,4},{1,25},{... | collective-permute-start | bytes 7274504 | tf_op jit(solution)/shard_map/ppermute | solution.py:511
  387.5 40.0 %copy-start.27 = (f32[8,256]{1,0:T(8,128)S(1)}, f32[8,256]{1,0:T(8,128)}, u32[]{:S(2)}) copy-start(f32[8,256]{1,0:T(8,128)} %get-tuple-element.97) | copy-start | bytes 24580
  387.5 40.8 %copy-start.26 = (f32[8,512]{1,0:T(8,128)S(1)}, f32[8,512]{1,0:T(8,128)}, u32[]{:S(2)}) copy-start(f32[8,512]{1,0:T(8,128)} %get-tuple-element.95) | copy-start | bytes 49156
  429.7 134.8 %reduce-scatter.2.cloned.1.call-start = ((), (), s32[]{:S(2)}) async-start(), calls=%async_computation.3 | async-start | bytes 3031040 | tf_op jit(solution)/shard_map/reduce_scatter | solution.py:638
  453.0 7.7 %collective-permute-start.21 = (bf16[4,128,3200]{2,1,0:T(8,128)(2,1)}, bf16[4,128,3200]{2,1,0:T(8,128)(2,1)S(1)}, u32[]{:S(2)}, u32[]{:S(2)}) collective-permute-start(bf16[4,128,3200]{2,1,0:T(8,128)(2,1)} %get-tuple-element.105), channel_id=1, source_target_pairs={{0,4},{4,0},{8,12},{12,8},{16,20},{20,16},{24,28},{28,24},{1,5},{5... | collective-permute-start | bytes 9830408 | tf_op jit(solution)/shard_map/ppermute | solution.py:491
  469.2 44.0 %collective-permute-start.25 = (bf16[1,128,3200]{2,1,0:T(8,128)(2,1)}, bf16[1,128,3200]{2,1,0:T(8,128)(2,1)S(1)}, u32[]{:S(2)}, u32[]{:S(2)}) collective-permute-start(bf16[1,128,3200]{2,1,0:T(8,128)(2,1)} %get-tuple-element.107.rest_1_), channel_id=1, source_target_pairs={{0,8},{4,12},{8,0},{12,4},{16,24},{20,28},{24,16},{28,20},{1,9},{5... | collective-permute-start | bytes 2457608 | tf_op jit(solution)/shard_map/ppermute | solution.py:511
  470.7 42.6 %collective-permute-start.26 = (bf16[1,128,3200]{2,1,0:T(8,128)(2,1)}, bf16[1,128,3200]{2,1,0:T(8,128)(2,1)S(1)}, u32[]{:S(2)}, u32[]{:S(2)}) collective-permute-start(bf16[1,128,3200]{2,1,0:T(8,128)(2,1)} %get-tuple-element.108.rest_2_), channel_id=1, source_target_pairs={{0,16},{4,20},{8,24},{12,28},{16,0},{20,4},{24,8},{28,12},{1,17},{... | collective-permute-start | bytes 2457608 | tf_op jit(solution)/shard_map/ppermute | solution.py:511
  471.3 42.0 %collective-permute-start.27 = (bf16[1,128,3200]{2,1,0:T(8,128)(2,1)}, bf16[1,128,3200]{2,1,0:T(8,128)(2,1)S(1)}, u32[]{:S(2)}, u32[]{:S(2)}) collective-permute-start(bf16[1,128,3200]{2,1,0:T(8,128)(2,1)} %get-tuple-element.109.rest_3_), channel_id=1, source_target_pairs={{0,24},{4,28},{8,16},{12,20},{16,8},{20,12},{24,0},{28,4},{1,25},{... | collective-permute-start | bytes 2457608 | tf_op jit(solution)/shard_map/ppermute | solution.py:511
  519.2 42.4 %all-to-all-start = ((bf16[4,32,3200]{2,1,0:T(8,128)(2,1)}), bf16[4,32,3200]{2,1,0:T(8,128)(2,1)S(1)}, u32[]{:S(2)}, u32[]{:S(2)}) async-start(bf16[4,32,3200]{2,1,0:T(8,128)(2,1)} %bitcast.69), calls=%async_computation | async-start | bytes 1638400 | tf_op jit(solution)/shard_map/all_to_all | solution.py:647
  530.1 32.5 %copy-start.29 = (bf16[32]{0:T(256)(128)(2,1)S(1)}, bf16[32]{0:T(256)(128)(2,1)}, u32[]{:S(2)}) copy-start(bf16[32]{0:T(256)(128)(2,1)} %param.20) | copy-start | bytes 196
  530.1 38.1 %copy-start.1 = (bf16[1024,32]{0,1:T(8,128)(2,1)S(1)}, bf16[1024,32]{0,1:T(8,128)(2,1)}, u32[]{:S(2)}) copy-start(bf16[1024,32]{0,1:T(8,128)(2,1)} %param.29) | copy-start | bytes 196612
  (16 other events, 121.3 us)
Sparse Core Ops, SparseCore 0:
  10.9 157.9 all-gather.5
  429.8 65.0 all-gather.3
  497.2 61.0 reduce-scatter.1

commit v5 on v4

--- a/solution.py
+++ b/solution.py
@@ -79,14 +79,14 @@
 
 def fwd_kernel(NT,cuts,st_ref,at_ref,tok_ref,wdec_ref,bias_ref,hg_ref,*rest):
     pieces=rest[:len(cuts)]
-    n_ref,q_ref,k_ref,cum_ref,dp_ref,v_ref,gp_ref,o_ref,bef_ref,mix_ref,rank_ref,gains_ref,wout_ref,state,w_ref,sems,out_sem=rest[len(cuts):]
+    n_ref,q_ref,k_ref,cum_ref,dp_ref,v_ref,gp_ref,o_ref,bef_ref,mix_ref,rank_ref,gains_ref,win_ref,wout_ref,state,w_ref,sems,save_sems=rest[len(cuts):]
     T=tok_ref.shape[0]; nb=T//BL
     i=pl.program_id(0); seq=i//NT; tile=i%NT; base=tile*T
     starts=starts_of(st_ref,seq)
     inter,reach,same,low,intra=tile_masks(base,T,starts)
     @pl.when(tile==0)
     def _(): state[...]=jnp.zeros_like(state)
-    save=pltpu.make_async_copy(w_ref,wout_ref,out_sem)
+    saves=[pltpu.make_async_copy(w_ref.at[:,pl.ds(0,GW)],win_ref,save_sems.at[0]),pltpu.make_async_copy(w_ref.at[:,pl.ds(GW,DV)],wout_ref,save_sems.at[1])]
     @pl.when(i==0)
     def _():
         copies=[]
@@ -96,10 +96,11 @@
                 copies.append(pltpu.make_async_copy(pieces[j].at[pl.ds(32*z,32)],w_ref.at[rows,pl.ds(first,width)],sems.at[j,z]))
         for c in copies: c.start()
         for c in copies: c.wait()
-        save.start()
+        for c in saves: c.start()
         gains_ref[...]=w_ref[:,CR:CR+128].astype(F32).T[16:24]
     @pl.when(i==pl.num_programs(0)-1)
-    def _(): save.wait()
+    def _():
+        for c in saves: c.wait()
     x=tok_ref[...].astype(F32)
     r=lax.rsqrt(jnp.mean(x*x,axis=-1,keepdims=True)+EPS)
     n_ref[...]=(x*r*gains_ref[0:1]).astype(BF)
@@ -108,39 +109,43 @@
     rank_ref[...]=rank
     dp=nn(rank,wdec_ref[...])+bias_ref[...]
     dp_ref[...]=dp
+    q_ref[...]=nn(n_ref[...],w_ref[:,CQ:CQ+DK])*SCALE
+    k_ref[...]=nn(n_ref[...],w_ref[:,CK:CK+DK])
     dhi,dlo=split(softminus(dp)*(1.0/16.0))
     lowb=low.astype(BF)
     cum=nn(lowb,dhi)+nn(lowb,dlo)
     cum_ref[...]=cum
-    q=nn(n,w_ref[:,CQ:CQ+DK])*SCALE; q_ref[...]=q
-    k=nn(n,w_ref[:,CK:CK+DK]); k_ref[...]=k
-    v_ref[...]=nn(n,w_ref[:,CV:CV+DV]).astype(BF)
-    gp_ref[...]=nn(n,w_ref[:,CG:CG+DV]).astype(BF)
+    heads=range(H)
+    sa=[slice(HK*h,HK*h+HK) for h in heads]; sv=[slice(HV*h,HV*h+HV) for h in heads]
+    blocks=[slice(BL*b,BL*b+BL) for b in range(nb)]
+    for h in heads: v_ref[:,sv[h]]=nn(n_ref[...],w_ref[:,CV+HV*h:CV+HV*h+HV]).astype(BF)
     interf=inter.astype(F32)
     ends=[cum[BL*b+BL-1:BL*b+BL,:] for b in range(nb)]
     endb=jnp.concatenate([jnp.broadcast_to(e,(BL,DK)) for e in ends],axis=0)
-    qg=q*jnp.exp(cum)
-    qgi=(qg*interf).astype(BF); qg=qg.astype(BF)
-    kg=(k*jnp.exp(-cum)).astype(BF)
-    kc=(k*jnp.exp(endb-cum)).astype(BF)
     keeps=jnp.concatenate([jnp.exp(ends[b])*keep_of(base+BL*b,starts) for b in range(nb)]+[jnp.zeros((8-nb,DK),F32)],axis=0)
-    for h in range(H):
-        a=slice(HK*h,HK*h+HK); c=slice(HV*h,HV*h+HV)
-        v=v_ref[:,c]
-        s=jnp.where(intra,nt(qg[:,a],kg[:,a]),0.0).astype(BF)
-        vk=jnp.where(reach,v,jnp.zeros_like(v))
-        kt=keeps[:,a].T
-        o=nn(s,v)
-        parts=[]
-        st=state[h]
-        for b in range(nb):
-            t=slice(BL*b,BL*b+BL)
-            sb=st.astype(BF)
+    qgi=[None]*H; kc=[None]*H; s=[None]*H
+    for h in heads:
+        a=sa[h]; c=cum[:,a]
+        qf=q_ref[:,a]*jnp.exp(c); kf=k_ref[:,a]
+        qgi[h]=(qf*interf).astype(BF)
+        kc[h]=(kf*jnp.exp(endb[:,a]-c)).astype(BF)
+        s[h]=jnp.where(intra,nt(qf.astype(BF),(kf*jnp.exp(-c)).astype(BF)),0.0).astype(BF)
+    for h in heads: gp_ref[:,sv[h]]=nn(n_ref[...],w_ref[:,CG+HV*h:CG+HV*h+HV]).astype(BF)
+    vk=[jnp.where(reach,v_ref[:,sv[h]],jnp.zeros((T,HV),BF)) for h in heads]
+    upd=[[tn(kc[h][t],vk[h][t]) for t in blocks] for h in heads]
+    kt=[keeps[:,sa[h]].T for h in heads]
+    cur=[state[h] for h in heads]
+    parts=[[None]*nb for h in heads]
+    for b in range(nb):
+        for h in heads:
+            sb=cur[h].astype(BF)
             bef_ref[b,h]=sb
-            parts.append(nn(qgi[t,a],sb))
-            st=st*kt[:,b:b+1]+tn(kc[t,a],vk[t])
-        state[h]=st
-        o=o+jnp.concatenate(parts,axis=0)
+            parts[h][b]=nn(qgi[h][blocks[b]],sb)
+            cur[h]=cur[h]*kt[h][:,b:b+1]+upd[h][b]
+    for h in heads: state[h]=cur[h]
+    for h in heads:
+        c=sv[h]
+        o=nn(s[h],v_ref[:,c])+jnp.concatenate(parts[h],axis=0)
         o_ref[:,c]=o
         sc=lax.rsqrt(jnp.maximum(jnp.mean(o*o,axis=-1,keepdims=True),1.0))
         gp=gp_ref[:,c].astype(F32)
@@ -159,9 +164,9 @@
     cuts=[(p[1],p[2],p[0].shape[1]) for p in pieces]
     return pl.pallas_call(functools.partial(fwd_kernel,NT,cuts),
         grid_spec=pltpu.PrefetchScalarGridSpec(num_scalar_prefetch=2,grid=(n//T,),
-            in_specs=[row(d),const(wdec),const(bias),const(hg)]+[hbm]*len(pieces),out_specs=specs+[pl.BlockSpec((8,d),lambda i,*s:(0,0)),hbm],
-            scratch_shapes=[pltpu.VMEM((H,HK,HV),F32),pltpu.VMEM((d,GW),BF),pltpu.SemaphoreType.DMA((len(pieces),4)),pltpu.SemaphoreType.DMA]),
-        out_shape=shapes+[sd((8,d),F32),sd((d,GW),BF)],name="mixer_fwd",**params())(st,at,tok,wdec,bias,hg,*[p[0] for p in pieces])
+            in_specs=[row(d),const(wdec),const(bias),const(hg)]+[hbm]*len(pieces),out_specs=specs+[pl.BlockSpec((8,d),lambda i,*s:(0,0)),hbm,hbm],
+            scratch_shapes=[pltpu.VMEM((H,HK,HV),F32),pltpu.VMEM((d,GW+DV),BF),pltpu.SemaphoreType.DMA((len(pieces),4)),pltpu.SemaphoreType.DMA((2,))]),
+        out_shape=shapes+[sd((8,d),F32),sd((d,GW),BF),sd((d,DV),BF)],name="mixer_fwd",**params())(st,at,tok,wdec,bias,hg,*[p[0] for p in pieces])
 
 
 def bwd_kernel(NT,seq,st_ref,gmix_ref,w_ref,wdec_ref,hg_ref,q_ref,k_ref,cum_ref,dp_ref,v_ref,gp_ref,o_ref,bef_ref,rank_ref,*rest):
@@ -185,9 +190,15 @@
     upb=(same&(tc<=tr)).astype(BF); lsb=(same&(tc>tr)).astype(BF)
     hg=hg_ref[...]
     ones=jnp.ones((8,HV),BF)
-    for h in range(H):
-        a=slice(HK*h,HK*h+HK); c=slice(HV*h,HV*h+HV)
-        gi=nn(gmix_ref[...],w_ref[:,HV*h:HV*h+HV])
+    heads=range(H)
+    sa=[slice(HK*h,HK*h+HK) for h in heads]; sc_=[slice(HV*h,HV*h+HV) for h in heads]
+    go=[None]*H; goi=[None]*H
+    qs=[q_ref[:,sa[h]]*eg[:,sa[h]] for h in heads]; ks=[k_ref[:,sa[h]]*es[:,sa[h]] for h in heads]; kd=[k_ref[:,sa[h]]*ec[:,sa[h]] for h in heads]
+    qg=[x.astype(BF) for x in qs]; kg=[x.astype(BF) for x in ks]; kc=[x.astype(BF) for x in kd]
+    sco=[jnp.where(intra,nt(qg[h],kg[h]),0.0).astype(BF) for h in heads]
+    for h in heads:
+        c=sc_[h]
+        gi=nn(gmix_ref[...],w_ref[:,c])
         o=o_ref[:,c]; gp=gp_ref[:,c].astype(F32)
         ms=jnp.mean(o*o,axis=-1,keepdims=True)
         sc=lax.rsqrt(jnp.maximum(ms,1.0))
@@ -198,36 +209,36 @@
         dhg_ref[...]+=jnp.sum((G*hn0).reshape(-1,8,HV),axis=0)
         G=G*hg
         innr=jnp.mean(G*o,axis=-1,keepdims=True)*jnp.where(ms>1.0,1.0,0.0)
-        go=(sc*G-o*(sc*sc*sc*innr)).astype(BF)
-        goi=go*interb
-        v=v_ref[:,c]
-        qs=q_ref[:,a]*eg[:,a]; ks=k_ref[:,a]*es[:,a]; kd=k_ref[:,a]*ec[:,a]
-        qg=qs.astype(BF); kg=ks.astype(BF); kc=kd.astype(BF)
-        sco=jnp.where(intra,nt(qg,kg),0.0).astype(BF)
-        gs=jnp.where(intra,nt(go,v),0.0).astype(BF)
-        gv=tn(sco,go); gq=nn(gs,kg); gk=tn(gs,qg)
-        kt=kend[:,a].T
-        st=state[h]
-        p_gv=[None]*nb; p_gq=[None]*nb; p_gkc=[None]*nb; p_end=[None]*nb
-        for b in reversed(range(nb)):
-            t=slice(BL*b,BL*b+BL)
-            bef=bef_ref[b,h]
-            sb=st.astype(BF)
-            p_gv[b]=nn(kc[t],sb)
-            p_gq[b]=nt(goi[t],bef)
-            p_gkc[b]=nt(v[t],sb)
-            m1,m2=split(st*bef.astype(F32))
-            p_end[b]=(nt(ones,m1)+nt(ones,m2))[0:1]*kend[b:b+1,a]
-            st=(tn(qg[t],goi[t])+kt[:,b:b+1]*st).astype(BF).astype(F32)
-        state[h]=st
-        cat=lambda p: jnp.concatenate(p,axis=0)
-        gv=gv+cat(p_gv)*reachf
+        go[h]=(sc*G-o*(sc*sc*sc*innr)).astype(BF)
+        goi[h]=go[h]*interb
+    gs=[jnp.where(intra,nt(go[h],v_ref[:,sc_[h]]),0.0).astype(BF) for h in heads]
+    loc=[[tn(qg[h][BL*b:BL*b+BL],goi[h][BL*b:BL*b+BL]) for b in range(nb)] for h in heads]
+    kt=[kend[:,sa[h]].T for h in heads]
+    sbs=[[None]*nb for h in heads]
+    p_end=[[None]*nb for h in heads]
+    for b in reversed(range(nb)):
+        for h in heads:
+            st=state[h] if b==nb-1 else cur[h]
+            sbs[h][b]=st.astype(BF)
+            m1,m2=split(st*bef_ref[b,h].astype(F32))
+            p_end[h][b]=(nt(ones,m1)+nt(ones,m2))[0:1]*kend[b:b+1,sa[h]]
+            st=(loc[h][b]+kt[h][:,b:b+1]*st).astype(BF).astype(F32)
+            if b==nb-1:
+                if h==0: cur=[None]*H
+            cur[h]=st
+    for h in heads: state[h]=cur[h]
+    cat=lambda p: jnp.concatenate(p,axis=0)
+    for h in heads:
+        a=sa[h]; c=sc_[h]; v=v_ref[:,c]
+        tt=[slice(BL*b,BL*b+BL) for b in range(nb)]
+        gv=tn(sco[h],go[h])+cat([nn(kc[h][tt[b]],sbs[h][b]) for b in range(nb)])*reachf
         g_ref[:,CV+HV*h:CV+HV*h+HV]=gv.astype(BF)
-        gq=gq+cat(p_gq)
-        gkc=cat(p_gkc)*reachf
-        av1,av2=split(gq*qs-gk*ks)
-        c1,c2=split(gkc*kd)
-        endr=cat([jnp.broadcast_to(p,(BL,HK)) for p in p_end])
+        gq=nn(gs[h],kg[h])+cat([nt(goi[h][tt[b]],bef_ref[b,h]) for b in range(nb)])
+        gk=tn(gs[h],qg[h])
+        gkc=cat([nt(v[tt[b]],sbs[h][b]) for b in range(nb)])*reachf
+        av1,av2=split(gq*qs[h]-gk*ks[h])
+        c1,c2=split(gkc*kd[h])
+        endr=cat([jnp.broadcast_to(p,(BL,HK)) for p in p_end[h]])
         gd=nn(upb,av1)+nn(upb,av2)+nn(lsb,c1)+nn(lsb,c2)+endr
         g_ref[:,CQ+HK*h:CQ+HK*h+HK]=(gq*eg[:,a]*SCALE).astype(BF)
         g_ref[:,CK+HK*h:CK+HK*h+HK]=(gk*es[:,a]+gkc*ec[:,a]).astype(BF)
@@ -238,6 +249,7 @@
         gr=nt(gpre,wdec_ref[:,a])
         grank=gr if h==0 else grank+gr
     g_ref[:,CR:CR+128]=grank.astype(BF)
+    g_ref[:,GW:]=jnp.zeros((T,128),BF)
 
 
 def bwd_call(seq,before_g,deps,st,gmix,w,wdec,hg,q,k,cum,dp,v,gp,o,bef,rank,T=256):
@@ -251,16 +263,16 @@
     return pl.pallas_call(functools.partial(bwd_kernel,NT,seq),
         grid_spec=pltpu.PrefetchScalarGridSpec(num_scalar_prefetch=1,grid=(NT,),
             in_specs=[row(gmix),const(w),const(wdec),const(hg),row(q),row(k),row(cum),row(dp),row(v),row(gp),row(o),pl.BlockSpec((nb,H,HK,HV),lambda i,s:(top-i,0,0,0)),row(rank)]+[hbm]*len(more),
-            out_specs=[pl.BlockSpec((T,GW),lambda i,s:(top-i,0)),acc((128,DK)),acc((8,DK)),acc((8,HV))],
+            out_specs=[pl.BlockSpec((T,GW+128),lambda i,s:(top-i,0)),acc((128,DK)),acc((8,DK)),acc((8,HV))],
             scratch_shapes=[pltpu.VMEM((H,HK,HV),F32)]),
         input_output_aliases={} if before_g is None else {13+len(more):0},
-        out_shape=[sd((n,GW),BF),sd((128,DK),F32),sd((8,DK),F32),sd((8,HV),F32)],
+        out_shape=[sd((n,GW+128),BF),sd((128,DK),F32),sd((8,DK),F32),sd((8,HV),F32)],
         name="mixer_bwd",**params())(st,gmix,w,wdec,hg,q,k,cum,dp,v,gp,o,bef,rank,*more)
 
 
 def dx_kernel(g_ref,w_ref,tok_ref,gain_ref,gres_ref,*rest):
     gt_ref=rest[-1]
-    gm=nt(g_ref[...],w_ref[...])
+    gm=nt(g_ref[:,:GW],w_ref[...])
     x=tok_ref[...].astype(F32)
     r=lax.rsqrt(jnp.mean(x*x,axis=-1,keepdims=True)+EPS)
     sc=gm*gain_ref[...]
@@ -268,7 +280,7 @@
     gt_ref[...]=gres_ref[...]+r*sc-x*(r*r*r*inner)
 
 
-def dx_call(part,parts,begun,g,w,tok,gain,gres,deps,T=256):
+def dx_call(part,parts,begun,g,w,tok,gain,gres,deps,flops=1,T=256):
     n,d=tok.shape; sd=jax.ShapeDtypeStruct; steps=n//T//parts; first=part*steps
     row=lambda a: pl.BlockSpec((T,a.shape[1]),lambda i:(first+i,0))
     const=lambda a: pl.BlockSpec(a.shape,lambda i:(0,0),pipeline_mode=pl.Buffered(1))
@@ -276,7 +288,7 @@
     more=list(deps)+([] if begun is None else [begun])
     return pl.pallas_call(dx_kernel,grid=(steps,),in_specs=[row(g),const(w),row(tok),const(gain),row(gres)]+[hbm]*len(more),
         out_specs=row(gres),out_shape=sd((n,d),F32),input_output_aliases={} if begun is None else {4+len(more):0},
-        name="mixer_dx",**params())(g,w,tok,gain,gres,*more)
+        name="mixer_dx",**params(flops))(g,w,tok,gain,gres,*more)
 
 
 def load_w(w_hbm,w_ref,sems,stacks):
@@ -352,7 +364,7 @@
         name="mlp_down",**params())(res,hid,w,*more)
 
 
-def dw_kernel(count,wide,sel_ref,*rest):
+def dw_kernel(count,wide,extra,sel_ref,*rest):
     g_refs=rest[:count]; x_hbm=rest[count]
     outs=rest[-2*count-2:-2]; xp,sems=rest[-2:]
     i=pl.program_id(0); steps=pl.num_programs(0)//count
@@ -373,23 +385,30 @@
                 for j in range(4):
                     b=slice(512*p+128*j,512*p+128*j+128)
                     outs[2*s+p][j]=(o[:,b] if wide else o[b,:]).astype(BF)
-
-
-def dw_call(gs,x,sel,deps,chunk,wide=True):
-    n,ff=gs[0].shape; d=x.shape[1]; steps=ff//chunk; count=len(gs)
+    if extra:
+        @pl.when(i==pl.num_programs(0)-1)
+        def _():
+            for p in range(2):
+                for j in range(4): outs[p][j,:,-128:]=rest[count+1][...]
+
+
+def dw_call(gs,x,sel,deps,chunk,wide=True,extra=None):
+    n,ff=gs[0].shape
+    d=x.shape[1]; steps=ff//chunk; count=len(gs)
     hbm=pl.BlockSpec(memory_space=pl.ANY)
     spot=lambda i,s: jnp.clip(i-s*steps,0,steps-1)
     def out(s):
         return pl.BlockSpec((4,chunk,128),lambda i,_:(0,spot(i,s),0)) if wide else pl.BlockSpec((4,128,chunk),lambda i,_:(0,0,spot(i,s)))
+    more=[] if extra is None else [pl.BlockSpec((128,128),lambda i,_:(0,0))]
     def inp(s):
         return pl.BlockSpec((n,chunk),lambda i,_:(0,spot(i,s)))
-    return pl.pallas_call(functools.partial(dw_kernel,count,wide),
+    return pl.pallas_call(functools.partial(dw_kernel,count,wide,extra is not None),
         grid_spec=pltpu.PrefetchScalarGridSpec(num_scalar_prefetch=1,grid=(steps*count,),
-            in_specs=[inp(s) for s in range(count)]+[hbm]*(1+len(deps)),
+            in_specs=[inp(s) for s in range(count)]+[hbm]+more+[hbm]*len(deps),
             out_specs=[out(s) for s in range(count) for _ in range(2)],
             scratch_shapes=[pltpu.VMEM((n,d),BF),pltpu.SemaphoreType.DMA((2,4))]),
         out_shape=[jax.ShapeDtypeStruct((4,ff,128) if wide else (4,128,ff),BF)]*(2*count),
-        name="grad_w",**params(10**11 if wide else 1))(sel,*gs,x,*deps)
+        name="grad_w",**params(10**11 if wide else 1))(sel,*gs,x,*([] if extra is None else [extra]),*deps)
 
 
 def plane_kernel(count,at_ref,*rest):
@@ -437,19 +456,23 @@
     return pl.pallas_call(line_kernel,grid=(1,),
         in_specs=[full]*4+[pl.BlockSpec(memory_space=pl.ANY)]*len(deps),out_specs=pl.BlockSpec(shape,lambda i:(0,0)),
         scratch_shapes=[pltpu.VMEM((steps,rows-128,128),BF),pltpu.VMEM((steps,128,128),BF)],
-        out_shape=jax.ShapeDtypeStruct(shape,BF),name="line",**params(5*10**10))(*parts,*deps)
-
-
-def stack_kernel(count,*refs):
-    refs[-1][...]=functools.reduce(jnp.add,[r[...].astype(F32) for r in refs[:count]]).astype(BF)
-
-
-def stack_call(parts,chunk,deps):
-    rows,cols=parts[0].shape
-    spec=pl.BlockSpec((rows,chunk),lambda i:(0,i))
-    return pl.pallas_call(functools.partial(stack_kernel,len(parts)),grid=(cols//chunk,),
-        in_specs=[spec]*len(parts)+[pl.BlockSpec(memory_space=pl.ANY)]*len(deps),out_specs=spec,
-        out_shape=jax.ShapeDtypeStruct((rows,cols),BF),name="stack",**params())(*parts,*deps)
+        out_shape=jax.ShapeDtypeStruct(shape,BF),name="line",**params())(*parts,*deps)
+
+
+def stack_kernel(*refs):
+    out=refs[-1]
+    v=functools.reduce(jnp.add,[r[...].astype(F32) for r in refs[:4]]).astype(BF)
+    out[:,:GW]=v[:,:GW]
+    for m in range(4):
+        for j in range(4): out[32*m:32*m+32,GW+128*j:GW+128*j+128]=v[32*j:32*j+32,GW:]
+
+
+def stack_call(parts,deps):
+    shape=(128,GW+512)
+    spec=pl.BlockSpec(parts[0].shape,lambda i:(0,0))
+    return pl.pallas_call(stack_kernel,grid=(1,),
+        in_specs=[spec]*4+[pl.BlockSpec(memory_space=pl.ANY)]*len(deps),out_specs=pl.BlockSpec(shape,lambda i:(0,0)),
+        out_shape=jax.ShapeDtypeStruct(shape,BF),name="stack",**params())(*parts,*deps)
 
 
 def spread_kernel(sizes,count,at_ref,*rest):
@@ -474,17 +497,6 @@
             in_specs=[pl.BlockSpec((g[0].shape[0],count,*size),lambda i,_:(0,0,*place(i))) for g in groups for p in g]+[pl.BlockSpec(memory_space=pl.ANY)]*len(deps),
             out_specs=[pl.BlockSpec((stacks,*size),lambda i,_:(0,*place(i)))]*count),
         out_shape=[jax.ShapeDtypeStruct((stacks,rows,cols),BF)]*count,name="spread",**params())(at,*[p for g in groups for p in g],*deps)
-
-
-def rows_kernel(x_ref,*rest):
-    rest[-1][...]=jnp.sum(x_ref[...].astype(F32),axis=0)
-
-
-def rows_call(x,deps):
-    return pl.pallas_call(rows_kernel,grid=(1,),
-        in_specs=[pl.BlockSpec(x.shape,lambda i:(0,0,0))]+[pl.BlockSpec(memory_space=pl.ANY)]*len(deps),
-        out_specs=pl.BlockSpec(x.shape[1:],lambda i:(0,0)),
-        out_shape=jax.ShapeDtypeStruct(x.shape[1:],F32),name="sum_rows",**params())(x,*deps)
 
 
 def swap(x, axis, bit, count):
@@ -558,30 +570,26 @@
     mixer_local = jnp.concatenate(
         [
             w_query, w_key, w_value, w_outgate, w_rank,
-            norm_gain_mix[:, None], norm_gain_mlp[:, None], jnp.zeros((shard, 110), BF),
+            norm_gain_mix[:, None], norm_gain_mlp[:, None], jnp.zeros((shard, 110), BF), w_output.T,
         ],
         axis=1,
     )
     mlp_local = jnp.concatenate([w_gate.T, w_up.T, w_down], axis=0)
     here = lax.axis_index("rows")
     if low == 0:
-        local = [mlp_local, w_output.T.reshape(shard, 8, 128).transpose(1, 0, 2).reshape(8 * shard, 128)]
-        mlp_all = lax.all_gather(jnp.concatenate(local, axis=0), ("rows", "mlp"), axis=0)
-        w_out = mlp_all[:, 3 * hid :].reshape(rows * mlps, 8, shard, 128).transpose(0, 2, 1, 3).reshape(-1, DV)
-        mlp_all = mlp_all.reshape(rows, mlps, 3 * hid + 8 * shard, 128)
+        mlp_all = lax.all_gather(mlp_local, ("rows", "mlp"), axis=0).reshape(rows, mlps, 3 * hid, 128)
         pieces = gather_pieces(mixer_local, low, mlps)
         at = jnp.concatenate([jnp.arange(8) ^ here, (lax.axis_index("mlp") - jnp.arange(mlps)) % mlps])
     else:
         mlp_all = lax.all_gather(mlp_local, ("rows", "mlp"), axis=0)
         mlp_all = mlp_all.reshape(8, rows // 8, mlps, 3 * hid, wide).transpose(0, 2, 3, 1, 4)
         mlp_all = mlp_all.reshape(8, mlps, 3 * hid, 128)
-        w_out = lax.all_gather(w_output.T, ("rows", "mlp"), axis=0, tiled=True)
         whole = lax.all_gather(mixer_local, ("rows", "mlp"), axis=0, tiled=True)
         pieces = [(whole[128 * b : 128 * b + 128], b, 0) for b in range(8)]
         at = jnp.concatenate([jnp.arange(8), jnp.arange(4)])
     decay_wide = jnp.concatenate([w_decay, jnp.zeros((112, DK), BF)], axis=0)
     head_row = head_gain.astype(F32)[None]
-    normed_in, q, k, cum, dp, v, gp, o, before, mixed, rank, gains, w_in = fwd_call(
+    normed_in, q, k, cum, dp, v, gp, o, before, mixed, rank, gains, w_in, w_out = fwd_call(
         lens, at.astype(jnp.int32), tokens, pieces, decay_wide, decay_bias.astype(F32)[None], head_row
     )
     gain_mix, gain_mlp = gains[:1], gains[1:2]
@@ -618,12 +626,17 @@
         grads, *sums = bwd_call(seq, grads, deps, *common)
         small = sums if small is None else [a + b for a, b in zip(small, sums)]
         deps = []
-    in_send, in_keep = dw_call([grads], normed_in, mine, [], 640, wide=False)
-    inner = with_other_core(in_send, in_keep)
     small = jnp.concatenate(
         [small[0][:16].reshape(-1), small[1].sum(0), small[2].sum(0), gain_mlp_part.sum(0)]
     )
-    small = lax.all_gather(small.reshape(-1, 256), ("rows", "mlp"), axis=0)
+    count = small.shape[0]
+    if low:
+        small_sum = lax.all_gather(small.reshape(-1, 256), ("rows", "mlp"), axis=0).sum(0).reshape(-1)
+    small = jnp.concatenate([small, jnp.zeros((128 * 128 - count,), F32)]).reshape(128, 128).astype(BF)
+    in_send, in_keep = dw_call([grads], normed_in, mine, [], 1664, wide=False, extra=small)
+    inner = with_other_core(in_send, in_keep)
+    grad_tokens = dx_call(0, 2, None, grads, w_in, tokens, gain_mix, grad_res, [in_keep], 5 * 10**10)
+    inner = spread([[p[None] for p in inner]], in_plane, 1, 1664, [grad_tokens])
     blocks = send_blocks(blocks, low, rows)
     if low:
         blocks = total(blocks)
@@ -632,29 +645,34 @@
         out = within([blocks[:, -128:].reshape(-1, 128)], 1)[0].reshape(DV, mlps, shard)
         main = send_line([jnp.take(main, in_line[j], axis=1) for j in range(mlps)], mlps)
         out = send_line([jnp.take(out, in_line[j], axis=1) for j in range(mlps)], mlps)
-        deps = [in_keep]
+        deps = list(inner)
     else:
-        blocks = line_call(blocks, [in_keep])
+        blocks = line_call(blocks, list(inner))
         main = lax.psum_scatter(blocks, "mlp", scatter_dimension=0, tiled=True)
         deps = [blocks]
-    blocks = spread([[p[None] for p in inner]], in_plane, 1, 640, deps)
-    grad_tokens = dx_call(0, 2, None, grads, w_in, tokens, gain_mix, grad_res, list(blocks))
-    grad_tokens = dx_call(1, 2, grad_tokens, grads, w_in, tokens, gain_mix, grad_res, [])
+    blocks = inner
+    grad_tokens = dx_call(1, 2, grad_tokens, grads, w_in, tokens, gain_mix, grad_res, deps)
     block_out = down_call(0, 2, None, residual, hidden, mlp_all, [grad_tokens])
-    small = rows_call(small, [block_out])
     blocks = within(send_blocks(blocks, low, rows), 1)
-    blocks = stack_call([b.reshape(-1, GW) for b in blocks], 640, [block_out]).reshape(mlps, shard, GW)
+    if low:
+        blocks = total([b[0] for b in blocks]).astype(BF).reshape(mlps, shard, GW + 128)
+    else:
+        blocks = stack_call([b[0] for b in blocks], [block_out]).reshape(mlps, shard, GW + 512)
     in_grads = lax.all_to_all(blocks, "mlp", 0, 0, tiled=True)
-    block_out = down_call(1, 2, block_out, residual, hidden, mlp_all, [small, blocks])
-    small = small.reshape(-1)
+    block_out = down_call(1, 2, block_out, residual, hidden, mlp_all, [blocks])
     in_grads = total([in_grads[j] for j in range(mlps)])
+    if low:
+        small = small_sum
+    else:
+        small = in_grads[:, GW:].reshape(shard, 4, 128).transpose(1, 0, 2).reshape(-1)[:count]
+    in_grads = in_grads[:, :GW]
     if low:
         mlp_grads, out_grads = total(main), total(out)
     else:
         main = main.astype(F32)
         mlp_grads = main[: 3 * hid].reshape(2, 3, hid // 2, 128).transpose(1, 0, 2, 3).reshape(3, hid, 128)
         out_grads = main[3 * hid :].reshape(8, shard, 128).transpose(0, 2, 1).reshape(DV, shard)
-    gain_mix_grad = jnp.sum(in_grads * mixer_local.astype(F32), axis=1) / norm_gain_mix.astype(F32)
+    gain_mix_grad = jnp.sum(in_grads * mixer_local[:, :GW].astype(F32), axis=1) / norm_gain_mix.astype(F32)
     at = 16 * DK + DK + HV + (here * mlps + lax.axis_index("mlp")) * shard
     return (
         block_out,

time: 583 us -> 545 us (0.935)
  Pallas kernels: 391 us -> 358 us
  local copies, waits for them, and re-layouts: 31.3 us -> 23.1 us
    pallas_call x2, Pallas kernels: 78.6 us -> 58.2 us  [bwd_call(): pl.pallas_call(functools.partial(bwd_kernel, NT, seq), grid_spec=pltpu.Pr...]
    ppermute x6, waiting for transfers between devices: 0.02 us -> 10.6 us  [send_blocks(): lax.ppermute(blocks[j], 'rows', [(i, i ^ j << low + 1) for i in range(cou...]
    pallas_call x1, Pallas kernels: 51 us -> 42.1 us  [fwd_call(): pl.pallas_call(functools.partial(fwd_kernel, NT, cuts), grid_spec=pltpu.P...]
    all_to_all x1, waiting for transfers between devices: 19.1 us -> 10.6 us  [body(): in_grads = lax.all_to_all(blocks, 'mlp', 0, 0, tiled=True)]
    unnamed x70 -> x88, local copies, waits for them, and re-layouts: 12.7 us -> 9.75 us
    pallas_call x6 -> x5, Pallas kernels: 94.9 us -> 92.6 us  [the longest x4 89.2 us: dw_call(): pl.pallas_call(functools.partial(dw_kernel, count, wide, extra is not Non...]
    all_gather x2 -> x1, waiting for transfers between devices: 15.3 us -> 14 us  [body(): lax.all_gather(mlp_local, ('rows', 'mlp'), axis=0)]
  transfers between devices with their start and end apart: 32 -> 31, of which waited for: 9 -> 10; matrix products, arithmetic and copies ran while one was open for 4% -> 3% of each run, Pallas kernels for 47% -> 43%
where the time goes in v5:
time: 545 us; the launch traced here: 539 us
  Pallas kernels  358 us (66%)
  waiting for transfers between devices  107 us (20%)
  starting transfers between devices  28.4 us (5%)
  local copies, waits for them, and re-layouts  23.1 us (4%)
  between operations  14.9 us (3%)
  other arithmetic  7.34 us (1%)
    pallas_call x4, Pallas kernels, dw_call(): pl.pallas_call(functools.partial(dw_kernel, count, wide, extra is not Non...  89.2 us
    pallas_call x1, Pallas kernels, mlp_call(): pl.pallas_call(functools.partial(mlp_kernel, chunk), grid=(n // T,), in_s...  86.5 us
    pallas_call x2, Pallas kernels, bwd_call(): pl.pallas_call(functools.partial(bwd_kernel, NT, seq), grid_spec=pltpu.Pr...  58.2 us
    ppermute x19, waiting for transfers between devices, swap(): return lax.ppermute(x, axis, [(i, i ^ 1 << bit) for i in range(count)])  47.8 us
    pallas_call x1, Pallas kernels, fwd_call(): pl.pallas_call(functools.partial(fwd_kernel, NT, cuts), grid_spec=pltpu.P...  42.1 us
    pallas_call x2, Pallas kernels, dx_call(): pl.pallas_call(dx_kernel, grid=(steps,), in_specs=[row(g), const(w), row(...  27.8 us
    pallas_call x2, Pallas kernels, down_call(): pl.pallas_call(down_kernel, grid=(steps,), in_specs=[row(d), row(ff), hbm...  25.1 us
    ppermute x3, waiting for transfers between devices, gather_pieces(): lax.ppermute(x, 'mlp', [(i, (i + step) % mlps) for i in range(mlps)])  24 us
  transfers between devices with their start and end apart: 31, of which 10 were waited for; matrix products, arithmetic and copies ran while one was open for 3% of the time, Pallas kernels for 43%

profile of v5, /device:TPU:0, one launch (start us, length us, event | category | flops | bytes accessed | tf_op | source)
XLA Modules:
  0.0 538.7 jit_solution(17260590290957351088)
XLA Ops:
  7.3 1.9 pad_maximum_fusion.1
  11.6 1.0 concatenate.34
  12.6 3.1 collective-permute-start
  15.7 2.6 collective-permute-start.1
  18.3 1.3 collective-permute-start.2
  19.6 1.0 concatenate.36
  20.6 4.6 collective-permute-done
  25.2 19.4 %collective-permute-done.1 = bf16[32,4224]{1,0:T(8,128)(2,1)S(1)} collective-permute-done((bf16[32,4224]{1,0:T(8,128)(2,1)S(1)}, bf16[32,4224]{1,0:T(8,128)(2,1)S(1)}, u32[]{:S(2)}, u32[]{:S(2)}) %collective-permute-start.1) | collective-permute-done | bytes 270368 | tf_op jit(solution)/shard_map/ppermute | solution.py:535
  44.8 1.8 collective-permute-start.10
  46.7 1.6 collective-permute-start.3
  49.1 14.4 %collective-permute-done.3.rest_1_ = bf16[128,2048]{1,0:T(8,128)(2,1)S(1)} collective-permute-done((bf16[128,2048]{1,0:T(8,128)(2,1)S(1)}, bf16[128,2048]{1,0:T(8,128)(2,1)S(1)}, u32[]{:S(2)}, u32[]{:S(2)}) %collective-permute-start.3) | collective-permute-done | bytes 524320 | tf_op jit(solution)/shard_map/ppermute | solution.py:503
  63.5 2.6 collective-permute-start.12
  66.1 12.3 %collective-permute-done.4.rest_2_ = bf16[128,2048]{1,0:T(8,128)(2,1)} collective-permute-done((bf16[128,2048]{1,0:T(8,128)(2,1)S(1)}, bf16[128,2048]{1,0:T(8,128)(2,1)}, u32[]{:S(2)}, u32[]{:S(2)}) %collective-permute-start.4) | collective-permute-done | bytes 524320 | tf_op jit(solution)/shard_map/ppermute | solution.py:503
  78.3 1.5 collective-permute-start.5
  79.9 7.5 %collective-permute-done.11.rest_10_ = bf16[128,2176]{1,0:T(8,128)(2,1)S(1)} collective-permute-done((bf16[128,2176]{1,0:T(8,128)(2,1)S(1)}, bf16[128,2176]{1,0:T(8,128)(2,1)S(1)}, u32[]{:S(2)}, u32[]{:S(2)}) %collective-permute-start.11) | collective-permute-done | bytes 557088 | tf_op jit(solution)/shard_map/ppermute | solution.py:503
  87.9 11.5 %collective-permute-done.12.rest_11_ = bf16[128,2176]{1,0:T(8,128)(2,1)S(1)} collective-permute-done((bf16[128,2176]{1,0:T(8,128)(2,1)S(1)}, bf16[128,2176]{1,0:T(8,128)(2,1)S(1)}, u32[]{:S(2)}, u32[]{:S(2)}) %collective-permute-start.12) | collective-permute-done | bytes 557088 | tf_op jit(solution)/shard_map/ppermute | solution.py:503
  103.8 42.1 %mixer_fwd.1 = (bf16[2048,1024]{1,0:T(8,128)(2,1)}, f32[2048,512]{1,0:T(8,128)}, f32[2048,512]{1,0:T(8,128)}, f32[2048,512]{1,0:T(8,128)}, f32[2048,512]{1,0:T(8...) custom-call(s32[8]{0:T(128)} %reshape.80.st_ref, ...), custom_call_target="tpu_custom_call" | custom-call | flops 1 | bytes 1 | tf_op jit(solution)/shard_map/mixer_fwd/pallas_call | solution.py:165
  145.9 1.4 fusion.7
  147.3 14.0 %all-gather.3.cloned.1.call-done = bf16[67584,128]{1,0:T(8,128)(2,1)} async-done(((bf16[2112,128]{1,0:T(8,128)(2,1)}), bf16[67584,128]{1,0:T(8,128)(2,1)}) %all-gather.3.cloned.1.call-update) | async-done | bytes 17301520 | tf_op jit(solution)/shard_map/all_gather | solution.py:580
  161.3 86.5 %mlp.1 = (f32[2048,1024]{1,0:T(8,128)}, bf16[2048,1024]{1,0:T(8,128)(2,1)}, bf16[2048,2816]{1,0:T(8,128)(2,1)}, bf16[2048,2816]{1,0:T(8,128)(2,1)}, bf16[2048,28...) custom-call(bf16[2048,1024]{1,0:T(8,128)(2,1)} %tok_ref.7, ...), custom_call_target="tpu_custom_call" | custom-call | flops 1 | bytes 1 | tf_op jit(solution)/shard_map/mlp/pallas_call | solution.py:341
  247.8 19.8 %grad_w.4 = (bf16[4,2816,128]{2,1,0:T(8,128)(2,1)}, bf16[4,2816,128]{2,1,0:T(8,128)(2,1)}) custom-call(s32[1]{0:T(128)} %bitcast.8.sel_ref, bf16[2048,2816]{1,0:T(8,128)(2,1)} %get-tuple-element.68.rest_0_.hid_ref, bf16[2048,1024]{1,0:T(8,128)(2,1)} %rest_1_.1, bf16[2048,1024]{1,0:T(8,128)(2,1)} %get-tuple-element.81.rest_2_), custom_call_target="tpu_custom_call" | custom-call | flops 99999997952 | bytes 1 | tf_op jit(solution)/shard_map/grad_w/pallas_call | solution.py:405
  268.0 35.4 %grad_w.5 = (bf16[4,2816,128]{2,1,0:T(8,128)(2,1)}, bf16[4,2816,128]{2,1,0:T(8,128)(2,1)}, bf16[4,2816,128]{2,1,0:T(8,128)(2,1)}, bf16[4,2816,128]{2,1,0:T(8,128)(2,1)}) custom-call(s32[1]{0:T(128)} %bitcast.8.sel_ref, bf16[2048,2816]{1,0:T(8,128)(2,1)} %get-tuple-element.79.rest_0_, bf16[2048,2816]{1,0:T(8,128)(2,1)} %get-tuple-element.80.rest_1_, ...), custom_call_target="tpu_custom_call" | custom-call | flops 99999997952 | bytes 1 | tf_op jit(solution)/shard_map/grad_w/pallas_call | solution.py:405
  304.0 1.6 copy-done.1
  305.5 9.9 %grad_w.6 = (bf16[4,1024,128]{2,1,0:T(8,128)(2,1)}, bf16[4,1024,128]{2,1,0:T(8,128)(2,1)}) custom-call(s32[1]{0:T(128)} %bitcast.8.sel_ref, bf16[2048,1024]{1,0:T(8,128)(2,1)} %get-tuple-element.64.mix_ref.rest_0_, bf16[2048,1024]{1,0:T(8,128)(2,1)} %get-tuple-element.69.rest_1_.gmix_ref, bf16[4,2816,128]{2,1,0:T(8,128)(2,1)} %get-tuple-element.83.rest_2_.rest_0_, ...), custom_call_target="tpu_custom_call" | custom-call | flops 99999997952 | bytes 1 | tf_op jit(solution)/shard_map/grad_w/pallas_call | solution.py:405
  316.3 2.1 collective-permute-done.20.rest_7_
  318.4 1.0 copy-done.4
  319.4 12.8 %plane.1 = (bf16[8,1184,128]{2,1,0:T(8,128)(2,1)}, bf16[8,1184,128]{2,1,0:T(8,128)(2,1)}, bf16[8,1184,128]{2,1,0:T(8,128)(2,1)}, bf16[8,1184,128]{2,1,0:T(8,128)(2,1)}) custom-call(s32[4]{0:T(128)} %iota_xor_fusion.at_ref, bf16[4,2816,128]{2,1,0:T(8,128)(2,1)} %get-tuple-element.83.rest_2_.rest_0_, bf16[4,2816,128]{2,1,0:T(8,128)(2,1)} %collective-permute-done.17.rest_1_, ...), custom_call_target="tpu_custom_call" | custom-call | flops 1 | bytes 1 | tf_op jit(solution)/shard_map/plane/pallas_call | solution.py:427
  332.2 1.5 collective-permute-start.25
  334.3 1.5 collective-permute-start.27
  335.8 29.2 %mixer_bwd.2 = (bf16[2048,3328]{1,0:T(8,128)(2,1)}, f32[128,512]{1,0:T(8,128)}, f32[8,512]{1,0:T(8,128)}, f32[8,256]{1,0:T(8,128)}) custom-call(s32[8]{0:T(128)} %reshape.80.st_ref, bf16[2048,1024]{1,0:T(8,128)(2,1)} %get-tuple-element.69.rest_1_.gmix_ref, bf16[1024,1024]{1,0:T(8,128)(2,1)} %get-tuple-element.66.wo_ref.w_ref, ...), custom_call_target="tpu_custom_call" | custom-call | flops 1 | bytes 1 | tf_op jit(solution)/shard_map/mixer_bwd/pallas_call | solution.py:263
  364.9 29.0 %mixer_bwd.3 = (bf16[2048,3328]{1,0:T(8,128)(2,1)}, f32[128,512]{1,0:T(8,128)}, f32[8,512]{1,0:T(8,128)}, f32[8,256]{1,0:T(8,128)}) custom-call(s32[8]{0:T(128)} %reshape.80.st_ref, bf16[2048,1024]{1,0:T(8,128)(2,1)} %get-tuple-element.69.rest_1_.gmix_ref, bf16[1024,1024]{1,0:T(8,128)(2,1)} %get-tuple-element.66.wo_ref.w_ref, ...), custom_call_target="tpu_custom_call", output_to_operand_aliasing={{0}: (14, {})} | custom-call | flops 1 | bytes 1 | tf_op jit(solution)/shard_map/mixer_bwd/pallas_call | solution.py:263
  397.8 24.1 %grad_w.7 = (bf16[4,128,3328]{2,1,0:T(8,128)(2,1)}, bf16[4,128,3328]{2,1,0:T(8,128)(2,1)}) custom-call(s32[1]{0:T(128)} %bitcast.8.sel_ref, bf16[2048,3328]{1,0:T(8,128)(2,1)} %get-tuple-element.95.rest_0_.g_ref, bf16[2048,1024]{1,0:T(8,128)(2,1)} %get-tuple-element.96.rest_1_, bf16[128,128]{1,0:T(8,128)(2,1)} %bitcast.75), custom_call_target="tpu_custom_call" | custom-call | flops 1 | bytes 1 | tf_op jit(solution)/shard_map/grad_w/pallas_call | solution.py:405
  422.0 13.7 %mixer_dx.2.rest_2_.rest_1_ = f32[2048,1024]{1,0:T(8,128)} custom-call(bf16[2048,3328]{1,0:T(8,128)(2,1)} %get-tuple-element.95.rest_0_.g_ref, bf16[1024,3200]{1,0:T(8,128)(2,1)} %get-tuple-element.106.w_ref, bf16[2048,1024]{1,0:T(8,128)(2,1)} %tok_ref.7, f32[1,1024]{1,0:T(1,128)} %get-tuple-element.154.gain_ref, f32[2048,1024]{1,0:T(8,128)} %get-tuple-element.107.gres_ref, ...), custom_call_target="tpu_custom_call" | custom-call | flops 49999998976 | bytes 1 | tf_op jit(solution)/shard_map/mixer_dx/pallas_call | solution.py:289
  435.7 1.7 copy-done
  437.4 5.2 spread.1
  442.7 7.7 %line.1.rest_0_ = bf16[9472,128]{1,0:T(8,128)(2,1)} custom-call(bf16[8,1184,128]{2,1,0:T(8,128)(2,1)} %get-tuple-element.90.rest_0_.refs_0_, bf16[8,1184,128]{2,1,0:T(8,128)(2,1)} %collective-permute-done.25.refs_1_, bf16[8,1184,128]{2,1,0:T(8,128)(2,1)} %collective-permute-done.26.refs_2_, bf16[8,1184,128]{2,1,0:T(8,128)(2,1)} %collective-permute-done.27.refs_3_, ...), custom_call_target="tpu_custom_call" | custom-call | flops 1 | bytes 1 | tf_op jit(solution)/shard_map/line/pallas_call | solution.py:456
  450.3 1.5 collective-permute-start.22
  452.4 1.5 collective-permute-start.24
  453.9 14.1 %mixer_dx.3.rest_0_ = f32[2048,1024]{1,0:T(8,128)} custom-call(bf16[2048,3328]{1,0:T(8,128)(2,1)} %get-tuple-element.95.rest_0_.g_ref, bf16[1024,3200]{1,0:T(8,128)(2,1)} %get-tuple-element.106.w_ref, bf16[2048,1024]{1,0:T(8,128)(2,1)} %tok_ref.7, f32[1,1024]{1,0:T(1,128)} %get-tuple-element.154.gain_ref, ...), custom_call_target="tpu_custom_call", output_to_operand_aliasing={{}: (6, {})} | custom-call | flops 1 | bytes 1 | tf_op jit(solution)/shard_map/mixer_dx/pallas_call | solution.py:289
  468.0 12.7 %mlp_down.2.refs_4_.rest_1_ = bf16[2048,1024]{1,0:T(8,128)(2,1)} custom-call(f32[2048,1024]{1,0:T(8,128)} %get-tuple-element.67.res_ref, bf16[2048,2816]{1,0:T(8,128)(2,1)} %get-tuple-element.68.rest_0_.hid_ref, bf16[8,4,2112,128]{3,2,1,0:T(8,128)(2,1)} %bitcast.51, f32[2048,1024]{1,0:T(8,128)} %mixer_dx.3.rest_0_), custom_call_target="tpu_custom_call" | custom-call | flops 1 | bytes 1 | tf_op jit(solution)/shard_map/mlp_down/pallas_call | solution.py:361
  480.7 10.6 %collective-permute-done.23 = bf16[1,128,3328]{2,1,0:T(8,128)(2,1)S(1)} collective-permute-done((bf16[1,128,3328]{2,1,0:T(8,128)(2,1)}, bf16[1,128,3328]{2,1,0:T(8,128)(2,1)S(1)}, u32[]{:S(2)}, u32[]{:S(2)}) %collective-permute-start.23) | collective-permute-done | bytes 852000 | tf_op jit(solution)/shard_map/ppermute | solution.py:523
  491.4 0.9 copy-done.6
  492.6 3.4 stack.1
  496.0 3.5 all-to-all-start
  499.7 12.4 %mlp_down.3 = bf16[2048,1024]{1,0:T(8,128)(2,1)} custom-call(f32[2048,1024]{1,0:T(8,128)} %get-tuple-element.67.res_ref, bf16[2048,2816]{1,0:T(8,128)(2,1)} %get-tuple-element.68.rest_0_.hid_ref, bf16[8,4,2112,128]{3,2,1,0:T(8,128)(2,1)} %bitcast.52, bf16[4,32,3712]{2,1,0:T(8,128)(2,1)} %bitcast.54, ...), custom_call_target="tpu_custom_call", output_to_operand_aliasing={{}: (4, {})} | custom-call | flops 1 | bytes 1 | tf_op jit(solution)/shard_map/mlp_down/pallas_call | solution.py:361
  512.2 10.6 %all-to-all-done = bf16[4,32,3712]{2,1,0:T(8,128)(2,1)S(1)} async-done(((bf16[4,32,3712]{2,1,0:T(8,128)(2,1)}), bf16[4,32,3712]{2,1,0:T(8,128)(2,1)S(1)}, u32[]{:S(2)}, u32[]{:S(2)}) %all-to-all-start) | async-done | bytes 950304 | tf_op jit(solution)/shard_map/all_to_all | solution.py:661
  528.0 1.1 slice.163
  529.1 1.0 fusion.5
  (166 shorter events, 22.4 us)
Async XLA Ops:
  7.2 39.4 %copy-start.19 = (bf16[32,512]{1,0:T(8,128)(2,1)S(1)}, bf16[32,512]{1,0:T(8,128)(2,1)}, u32[]{:S(2)}) copy-start(bf16[32,512]{1,0:T(8,128)(2,1)} %param.21) | copy-start | bytes 98308
  7.2 39.4 %copy-start.21 = (bf16[32,512]{1,0:T(8,128)(2,1)S(1)}, bf16[32,512]{1,0:T(8,128)(2,1)}, u32[]{:S(2)}) copy-start(bf16[32,512]{1,0:T(8,128)(2,1)} %param.22) | copy-start | bytes 98308
  7.2 39.4 %copy-start.9 = (bf16[32,1024]{1,0:T(8,128)(2,1)S(1)}, bf16[32,1024]{1,0:T(8,128)(2,1)}, u32[]{:S(2)}) copy-start(bf16[32,1024]{1,0:T(8,128)(2,1)} %param.23) | copy-start | bytes 196612
  7.2 154.1 %all-gather.3.cloned.1.call-start = ((), (), s32[]{:S(2)}) async-start(), calls=%async_computation.3 | async-start | bytes 17842176 | tf_op jit(solution)/shard_map/all_gather | solution.py:580
  9.2 91.5 %copy-start.33 = (bf16[16,512]{1,0:T(8,128)(2,1)S(1)}, bf16[16,512]{1,0:T(8,128)(2,1)}, u32[]{:S(2)}) copy-start(bf16[16,512]{1,0:T(8,128)(2,1)} %param.26) | copy-start | bytes 49156
  9.2 92.2 %copy-start.39 = (bf16[256]{0:T(256)(128)(2,1)S(1)}, bf16[256]{0:T(256)(128)(2,1)}, u32[]{:S(2)}) copy-start(bf16[256]{0:T(256)(128)(2,1)} %param.28) | copy-start | bytes 1540
  9.2 92.7 %copy-start.38 = (s32[2,4]{1,0:T(2,128)S(1)}, s32[2,4]{1,0:T(2,128)}, u32[]{:S(2)}) copy-start(s32[2,4]{1,0:T(2,128)} %param.18) | copy-start | bytes 100
  9.2 93.3 %copy-start.36 = (bf16[512]{0:T(512)(128)(2,1)S(1)}, bf16[512]{0:T(512)(128)(2,1)}, u32[]{:S(2)}) copy-start(bf16[512]{0:T(512)(128)(2,1)} %param.27) | copy-start | bytes 3076
  9.2 518.8 %reduce-scatter.2.cloned.1.call-start = ((), (), s32[]{:S(2)}) async-start(), calls=%async_computation.2 | async-start | bytes 3031040 | tf_op jit(solution)/shard_map/reduce_scatter | solution.py:651
  10.1 34.6 %copy-start.23 = (bf16[32,16]{1,0:T(8,128)(2,1)}, bf16[32,16]{1,0:T(8,128)(2,1)S(1)}, u32[]{:S(2)}) copy-start(bf16[32,16]{1,0:T(8,128)(2,1)S(1)} %copy.48) | copy-start | bytes 3076
  10.8 33.8 %copy-start.25 = (bf16[32,1]{1,0:T(8,128)(2,1)}, bf16[32,1]{1,0:T(8,128)(2,1)S(1)}, u32[]{:S(2)}) copy-start(bf16[32,1]{1,0:T(8,128)(2,1)S(1)} %copy.49) | copy-start | bytes 196
  11.6 33.1 %copy-start.27 = (bf16[32,1]{1,0:T(8,128)(2,1)}, bf16[32,1]{1,0:T(8,128)(2,1)S(1)}, u32[]{:S(2)}) copy-start(bf16[32,1]{1,0:T(8,128)(2,1)S(1)} %copy.50) | copy-start | bytes 196
  11.6 33.1 %copy-start.29 = (bf16[32,110]{1,0:T(8,128)(2,1)}, bf16[32,110]{1,0:T(8,128)(2,1)S(1)}, u32[]{:S(2)}) copy-start(bf16[32,110]{1,0:T(8,128)(2,1)S(1)} %broadcast_in_dim.38) | copy-start | bytes 21124
  12.6 12.5 %collective-permute-start = (bf16[32,4224]{1,0:T(8,128)(2,1)S(1)}, bf16[32,4224]{1,0:T(8,128)(2,1)S(1)}, u32[]{:S(2)}, u32[]{:S(2)}) collective-permute-start(bf16[32,4224]{1,0:T(8,128)(2,1)S(1)} %concatenate.34), channel_id=1, source_target_pairs={{0,1},{1,2},{2,3},{3,0},{4,5},{5,6},{6,7},{7,4},{8,9},{9,10},{10,1... | collective-permute-start | bytes 811016 | tf_op jit(solution)/shard_map/ppermute | solution.py:535
  15.7 28.9 %collective-permute-start.1 = (bf16[32,4224]{1,0:T(8,128)(2,1)S(1)}, bf16[32,4224]{1,0:T(8,128)(2,1)S(1)}, u32[]{:S(2)}, u32[]{:S(2)}) collective-permute-start(bf16[32,4224]{1,0:T(8,128)(2,1)S(1)} %concatenate.34), channel_id=1, source_target_pairs={{0,2},{1,3},{2,0},{3,1},{4,6},{5,7},{6,4},{7,5},{8,10},{9,11},{10,... | collective-permute-start | bytes 811016 | tf_op jit(solution)/shard_map/ppermute | solution.py:535
  18.3 26.4 %collective-permute-start.2 = (bf16[32,4224]{1,0:T(8,128)(2,1)S(1)}, bf16[32,4224]{1,0:T(8,128)(2,1)S(1)}, u32[]{:S(2)}, u32[]{:S(2)}) collective-permute-start(bf16[32,4224]{1,0:T(8,128)(2,1)S(1)} %concatenate.34), channel_id=1, source_target_pairs={{0,3},{1,0},{2,1},{3,2},{4,7},{5,4},{6,5},{7,6},{8,11},{9,8},{10,9... | collective-permute-start | bytes 811016 | tf_op jit(solution)/shard_map/ppermute | solution.py:535
  44.8 59.0 %copy-start.2 = (bf16[128,2176]{1,0:T(8,128)(2,1)}, bf16[128,2176]{1,0:T(8,128)(2,1)S(1)}, u32[]{:S(2)}) copy-start(bf16[128,2176]{1,0:T(8,128)(2,1)S(1)} %pad_maximum_fusion.rest_8_) | copy-start | bytes 1671172
  44.8 18.7 %collective-permute-start.10 = (bf16[128,2176]{1,0:T(8,128)(2,1)S(1)}, bf16[128,2176]{1,0:T(8,128)(2,1)S(1)}, u32[]{:S(2)}, u32[]{:S(2)}) collective-permute-start(bf16[128,2176]{1,0:T(8,128)(2,1)S(1)} %pad_maximum_fusion.rest_8_), channel_id=1, source_target_pairs={{0,16},{4,20},{8,24},{12,28},{16,0},{20,4},{24,8},{28,12},{1,17},{... | collective-permute-start | bytes 1671176 | tf_op jit(solution)/shard_map/ppermute | solution.py:503
  46.7 57.0 %copy-start.3 = (bf16[128,2048]{1,0:T(8,128)(2,1)}, bf16[128,2048]{1,0:T(8,128)(2,1)S(1)}, u32[]{:S(2)}) copy-start(bf16[128,2048]{1,0:T(8,128)(2,1)S(1)} %pad_maximum_fusion.2.rest_0_) | copy-start | bytes 1572868
  46.7 16.8 %collective-permute-start.3 = (bf16[128,2048]{1,0:T(8,128)(2,1)S(1)}, bf16[128,2048]{1,0:T(8,128)(2,1)S(1)}, u32[]{:S(2)}, u32[]{:S(2)}) collective-permute-start(bf16[128,2048]{1,0:T(8,128)(2,1)S(1)} %pad_maximum_fusion.2.rest_0_), channel_id=1, source_target_pairs={{0,8},{4,12},{8,0},{12,4},{16,24},{20,28},{24,16},{28,20},{1,9},{5... | collective-permute-start | bytes 1572872 | tf_op jit(solution)/shard_map/ppermute | solution.py:503
  48.3 30.0 %collective-permute-start.4 = (bf16[128,2048]{1,0:T(8,128)(2,1)S(1)}, bf16[128,2048]{1,0:T(8,128)(2,1)}, u32[]{:S(2)}, u32[]{:S(2)}) collective-permute-start(bf16[128,2048]{1,0:T(8,128)(2,1)S(1)} %pad_maximum_fusion.2.rest_0_), channel_id=1, source_target_pairs={{0,16},{4,20},{8,24},{12,28},{16,0},{20,4},{24,8},{28,12},{1,17},{... | collective-permute-start | bytes 1572872 | tf_op jit(solution)/shard_map/ppermute | solution.py:503
  48.8 31.1 %collective-permute-start.6 = (bf16[128,2048]{1,0:T(8,128)(2,1)S(1)}, bf16[128,2048]{1,0:T(8,128)(2,1)S(1)}, u32[]{:S(2)}, u32[]{:S(2)}) collective-permute-start(bf16[128,2048]{1,0:T(8,128)(2,1)S(1)} %pad_maximum_fusion.2.rest_0_), channel_id=1, source_target_pairs={{0,4},{4,0},{8,12},{12,8},{16,20},{20,16},{24,28},{28,24},{1,5},{5... | collective-permute-start | bytes 1572872 | tf_op jit(solution)/shard_map/ppermute | solution.py:503
  48.8 38.6 %collective-permute-start.11 = (bf16[128,2176]{1,0:T(8,128)(2,1)S(1)}, bf16[128,2176]{1,0:T(8,128)(2,1)S(1)}, u32[]{:S(2)}, u32[]{:S(2)}) collective-permute-start(bf16[128,2176]{1,0:T(8,128)(2,1)S(1)} %pad_maximum_fusion.rest_8_), channel_id=1, source_target_pairs={{0,8},{4,12},{8,0},{12,4},{16,24},{20,28},{24,16},{28,20},{1,9},{5... | collective-permute-start | bytes 1671176 | tf_op jit(solution)/shard_map/ppermute | solution.py:503
  63.5 35.9 %copy-start.16 = (bf16[128,2048]{1,0:T(8,128)(2,1)}, bf16[128,2048]{1,0:T(8,128)(2,1)S(1)}, u32[]{:S(2)}) copy-start(bf16[128,2048]{1,0:T(8,128)(2,1)S(1)} %collective-permute-done.3.rest_1_) | copy-start | bytes 1572868
  63.5 23.9 %collective-permute-start.13 = (bf16[128,2176]{1,0:T(8,128)(2,1)S(1)}, bf16[128,2176]{1,0:T(8,128)(2,1)S(1)}, u32[]{:S(2)}, u32[]{:S(2)}) collective-permute-start(bf16[128,2176]{1,0:T(8,128)(2,1)S(1)} %pad_maximum_fusion.rest_8_), channel_id=1, source_target_pairs={{0,4},{4,0},{8,12},{12,8},{16,20},{20,16},{24,28},{28,24},{1,5},{5... | collective-permute-start | bytes 1671176 | tf_op jit(solution)/shard_map/ppermute | solution.py:503
  63.5 40.2 %copy-start.12 = (bf16[128,2176]{1,0:T(8,128)(2,1)}, bf16[128,2176]{1,0:T(8,128)(2,1)S(1)}, u32[]{:S(2)}) copy-start(bf16[128,2176]{1,0:T(8,128)(2,1)S(1)} %collective-permute-done.10.rest_9_) | copy-start | bytes 1671172
  63.5 35.9 %collective-permute-start.12 = (bf16[128,2176]{1,0:T(8,128)(2,1)S(1)}, bf16[128,2176]{1,0:T(8,128)(2,1)S(1)}, u32[]{:S(2)}, u32[]{:S(2)}) collective-permute-start(bf16[128,2176]{1,0:T(8,128)(2,1)S(1)} %collective-permute-done.10.rest_9_), channel_id=1, source_target_pairs={{0,8},{4,12},{8,0},{12,4},{16,24},{20,28},{24,16},{28,20},{1,9},{5... | collective-permute-start | bytes 1671176 | tf_op jit(solution)/shard_map/ppermute | solution.py:503
  78.3 21.0 %collective-permute-start.5 = (bf16[128,2048]{1,0:T(8,128)(2,1)S(1)}, bf16[128,2048]{1,0:T(8,128)(2,1)}, u32[]{:S(2)}, u32[]{:S(2)}) collective-permute-start(bf16[128,2048]{1,0:T(8,128)(2,1)S(1)} %collective-permute-done.3.rest_1_), channel_id=1, source_target_pairs={{0,16},{4,20},{8,24},{12,28},{16,0},{20,4},{24,8},{28,12},{1,17},{... | collective-permute-start | bytes 1572872 | tf_op jit(solution)/shard_map/ppermute | solution.py:503
  79.9 20.0 %collective-permute-start.7 = (bf16[128,2048]{1,0:T(8,128)(2,1)S(1)}, bf16[128,2048]{1,0:T(8,128)(2,1)S(1)}, u32[]{:S(2)}, u32[]{:S(2)}) collective-permute-start(bf16[128,2048]{1,0:T(8,128)(2,1)S(1)} %collective-permute-done.3.rest_1_), channel_id=1, source_target_pairs={{0,4},{4,0},{8,12},{12,8},{16,20},{20,16},{24,28},{28,24},{1,5},{5... | collective-permute-start | bytes 1572872 | tf_op jit(solution)/shard_map/ppermute | solution.py:503
  87.4 16.3 %collective-permute-start.14 = (bf16[128,2176]{1,0:T(8,128)(2,1)S(1)}, bf16[128,2176]{1,0:T(8,128)(2,1)}, u32[]{:S(2)}, u32[]{:S(2)}) collective-permute-start(bf16[128,2176]{1,0:T(8,128)(2,1)S(1)} %collective-permute-done.10.rest_9_), channel_id=1, source_target_pairs={{0,4},{4,0},{8,12},{12,8},{16,20},{20,16},{24,28},{28,24},{1,5},{5... | collective-permute-start | bytes 1671176 | tf_op jit(solution)/shard_map/ppermute | solution.py:503
  87.4 16.3 %collective-permute-start.15 = (bf16[128,2176]{1,0:T(8,128)(2,1)S(1)}, bf16[128,2176]{1,0:T(8,128)(2,1)}, u32[]{:S(2)}, u32[]{:S(2)}) collective-permute-start(bf16[128,2176]{1,0:T(8,128)(2,1)S(1)} %collective-permute-done.11.rest_10_), channel_id=1, source_target_pairs={{0,4},{4,0},{8,12},{12,8},{16,20},{20,16},{24,28},{28,24},{1,5},{5... | collective-permute-start | bytes 1671176 | tf_op jit(solution)/shard_map/ppermute | solution.py:503
  99.4 4.4 collective-permute-start.16
  99.4 4.3 collective-permute-start.8
  99.9 3.8 collective-permute-start.9
  267.6 36.3 %collective-permute-start.19 = (bf16[4,2816,128]{2,1,0:T(8,128)(2,1)}, bf16[4,2816,128]{2,1,0:T(8,128)(2,1)S(1)}, u32[]{:S(2)}, u32[]{:S(2)}) collective-permute-start(bf16[4,2816,128]{2,1,0:T(8,128)(2,1)} %get-tuple-element.87), channel_id=1, source_target_pairs={{0,4},{4,0},{8,12},{12,8},{16,20},{20,16},{24,28},{28,24},{1,5},{5... | collective-permute-start | bytes 8650760 | tf_op jit(solution)/shard_map/ppermute | solution.py:503
  303.4 12.9 %collective-permute-start.17 = (bf16[4,2816,128]{2,1,0:T(8,128)(2,1)}, bf16[4,2816,128]{2,1,0:T(8,128)(2,1)}, u32[]{:S(2)}, u32[]{:S(2)}) collective-permute-start(bf16[4,2816,128]{2,1,0:T(8,128)(2,1)} %get-tuple-element.84), channel_id=1, source_target_pairs={{0,4},{4,0},{8,12},{12,8},{16,20},{20,16},{24,28},{28,24},{1,5},{5... | collective-permute-start | bytes 8650760 | tf_op jit(solution)/shard_map/ppermute | solution.py:503
  303.7 12.6 %collective-permute-start.18 = (bf16[4,2816,128]{2,1,0:T(8,128)(2,1)}, bf16[4,2816,128]{2,1,0:T(8,128)(2,1)}, u32[]{:S(2)}, u32[]{:S(2)}) collective-permute-start(bf16[4,2816,128]{2,1,0:T(8,128)(2,1)} %get-tuple-element.86), channel_id=1, source_target_pairs={{0,4},{4,0},{8,12},{12,8},{16,20},{20,16},{24,28},{28,24},{1,5},{5... | collective-permute-start | bytes 8650760 | tf_op jit(solution)/shard_map/ppermute | solution.py:503
  315.4 2.9 collective-permute-start.20
  332.2 110.4 %collective-permute-start.25 = (bf16[8,1184,128]{2,1,0:T(8,128)(2,1)}, bf16[8,1184,128]{2,1,0:T(8,128)(2,1)}, u32[]{:S(2)}, u32[]{:S(2)}) collective-permute-start(bf16[8,1184,128]{2,1,0:T(8,128)(2,1)} %get-tuple-element.91.rest_1_), channel_id=1, source_target_pairs={{0,8},{4,12},{8,0},{12,4},{16,24},{20,28},{24,16},{28,20},{1,9},{5... | collective-permute-start | bytes 7274504 | tf_op jit(solution)/shard_map/ppermute | solution.py:523
  333.7 109.0 %collective-permute-start.26 = (bf16[8,1184,128]{2,1,0:T(8,128)(2,1)}, bf16[8,1184,128]{2,1,0:T(8,128)(2,1)}, u32[]{:S(2)}, u32[]{:S(2)}) collective-permute-start(bf16[8,1184,128]{2,1,0:T(8,128)(2,1)} %get-tuple-element.92.rest_2_), channel_id=1, source_target_pairs={{0,16},{4,20},{8,24},{12,28},{16,0},{20,4},{24,8},{28,12},{1,17},{... | collective-permute-start | bytes 7274504 | tf_op jit(solution)/shard_map/ppermute | solution.py:523
  334.3 108.4 %collective-permute-start.27 = (bf16[8,1184,128]{2,1,0:T(8,128)(2,1)}, bf16[8,1184,128]{2,1,0:T(8,128)(2,1)}, u32[]{:S(2)}, u32[]{:S(2)}) collective-permute-start(bf16[8,1184,128]{2,1,0:T(8,128)(2,1)} %get-tuple-element.93.rest_3_), channel_id=1, source_target_pairs={{0,24},{4,28},{8,16},{12,20},{16,8},{20,12},{24,0},{28,4},{1,25},{... | collective-permute-start | bytes 7274504 | tf_op jit(solution)/shard_map/ppermute | solution.py:523
  364.9 29.8 %copy-start.35 = (f32[8,256]{1,0:T(8,128)S(1)}, f32[8,256]{1,0:T(8,128)}, u32[]{:S(2)}) copy-start(f32[8,256]{1,0:T(8,128)} %get-tuple-element.101) | copy-start | bytes 24580
  364.9 30.6 %copy-start.34 = (f32[8,512]{1,0:T(8,128)S(1)}, f32[8,512]{1,0:T(8,128)}, u32[]{:S(2)}) copy-start(f32[8,512]{1,0:T(8,128)} %get-tuple-element.99) | copy-start | bytes 49156
  421.9 13.8 %collective-permute-start.21 = (bf16[4,128,3328]{2,1,0:T(8,128)(2,1)}, bf16[4,128,3328]{2,1,0:T(8,128)(2,1)S(1)}, u32[]{:S(2)}, u32[]{:S(2)}) collective-permute-start(bf16[4,128,3328]{2,1,0:T(8,128)(2,1)} %get-tuple-element.105), channel_id=1, source_target_pairs={{0,4},{4,0},{8,12},{12,8},{16,20},{20,16},{24,28},{28,24},{1,5},{5... | collective-permute-start | bytes 10223624 | tf_op jit(solution)/shard_map/ppermute | solution.py:503
  450.3 30.4 %collective-permute-start.22 = (bf16[1,128,3328]{2,1,0:T(8,128)(2,1)}, bf16[1,128,3328]{2,1,0:T(8,128)(2,1)S(1)}, u32[]{:S(2)}, u32[]{:S(2)}) collective-permute-start(bf16[1,128,3328]{2,1,0:T(8,128)(2,1)} %get-tuple-element.109.refs_5_), channel_id=1, source_target_pairs={{0,8},{4,12},{8,0},{12,4},{16,24},{20,28},{24,16},{28,20},{1,9},{5... | collective-permute-start | bytes 2555912 | tf_op jit(solution)/shard_map/ppermute | solution.py:523
  451.8 39.5 %collective-permute-start.23 = (bf16[1,128,3328]{2,1,0:T(8,128)(2,1)}, bf16[1,128,3328]{2,1,0:T(8,128)(2,1)S(1)}, u32[]{:S(2)}, u32[]{:S(2)}) collective-permute-start(bf16[1,128,3328]{2,1,0:T(8,128)(2,1)} %get-tuple-element.110.refs_6_), channel_id=1, source_target_pairs={{0,16},{4,20},{8,24},{12,28},{16,0},{20,4},{24,8},{28,12},{1,17},{... | collective-permute-start | bytes 2555912 | tf_op jit(solution)/shard_map/ppermute | solution.py:523
  452.4 38.9 %collective-permute-start.24 = (bf16[1,128,3328]{2,1,0:T(8,128)(2,1)S(1)}, bf16[1,128,3328]{2,1,0:T(8,128)(2,1)S(1)}, u32[]{:S(2)}, u32[]{:S(2)}) collective-permute-start(bf16[1,128,3328]{2,1,0:T(8,128)(2,1)S(1)} %copy-done.8), channel_id=1, source_target_pairs={{0,24},{4,28},{8,16},{12,20},{16,8},{20,12},{24,0},{28,4},{1,25},{... | collective-permute-start | bytes 2555912 | tf_op jit(solution)/shard_map/ppermute | solution.py:523
  496.0 26.7 %all-to-all-start = ((bf16[4,32,3712]{2,1,0:T(8,128)(2,1)}), bf16[4,32,3712]{2,1,0:T(8,128)(2,1)S(1)}, u32[]{:S(2)}, u32[]{:S(2)}) async-start(bf16[4,32,3712]{2,1,0:T(8,128)(2,1)} %bitcast.53), calls=%async_computation | async-start | bytes 1900544 | tf_op jit(solution)/shard_map/all_to_all | solution.py:661
  (23 other events, 179.1 us)
Sparse Core Ops, SparseCore 0:
  10.9 150.4 all-gather.2
  450.5 47.3 reduce-scatter.1

commit v6 on v5

--- a/solution.py
+++ b/solution.py
@@ -364,6 +364,17 @@
         name="mlp_down",**params())(res,hid,w,*more)
 
 
+def small_block(refs):
+    *parts,gain=refs
+    v=[functools.reduce(jnp.add,[p[...] for p in parts[t::3]]) for t in range(3)]+[gain[...]]
+    rows=[v[0][:16,128*j:128*j+128] for j in range(4)]
+    for x in v[1:]:
+        x=jnp.sum(x,axis=0,keepdims=True)
+        rows+=[x[:,128*j:128*j+128] for j in range(x.shape[1]//128)]
+    rows.append(jnp.zeros((128-64-4-2-8,128),F32))
+    return jnp.concatenate(rows,axis=0).astype(BF)
+
+
 def dw_kernel(count,wide,extra,sel_ref,*rest):
     g_refs=rest[:count]; x_hbm=rest[count]
     outs=rest[-2*count-2:-2]; xp,sems=rest[-2:]
@@ -389,26 +400,26 @@
         @pl.when(i==pl.num_programs(0)-1)
         def _():
             for p in range(2):
-                for j in range(4): outs[p][j,:,-128:]=rest[count+1][...]
-
-
-def dw_call(gs,x,sel,deps,chunk,wide=True,extra=None):
+                for j in range(4): outs[p][j,:,-128:]=small_block(rest[count+1:count+1+extra])
+
+
+def dw_call(gs,x,sel,deps,chunk,wide=True,extra=()):
     n,ff=gs[0].shape
     d=x.shape[1]; steps=ff//chunk; count=len(gs)
     hbm=pl.BlockSpec(memory_space=pl.ANY)
     spot=lambda i,s: jnp.clip(i-s*steps,0,steps-1)
     def out(s):
         return pl.BlockSpec((4,chunk,128),lambda i,_:(0,spot(i,s),0)) if wide else pl.BlockSpec((4,128,chunk),lambda i,_:(0,0,spot(i,s)))
-    more=[] if extra is None else [pl.BlockSpec((128,128),lambda i,_:(0,0))]
+    more=[pl.BlockSpec(e.shape,lambda i,_:(0,0)) for e in extra]
     def inp(s):
         return pl.BlockSpec((n,chunk),lambda i,_:(0,spot(i,s)))
-    return pl.pallas_call(functools.partial(dw_kernel,count,wide,extra is not None),
+    return pl.pallas_call(functools.partial(dw_kernel,count,wide,len(extra)),
         grid_spec=pltpu.PrefetchScalarGridSpec(num_scalar_prefetch=1,grid=(steps*count,),
             in_specs=[inp(s) for s in range(count)]+[hbm]+more+[hbm]*len(deps),
             out_specs=[out(s) for s in range(count) for _ in range(2)],
             scratch_shapes=[pltpu.VMEM((n,d),BF),pltpu.SemaphoreType.DMA((2,4))]),
         out_shape=[jax.ShapeDtypeStruct((4,ff,128) if wide else (4,128,ff),BF)]*(2*count),
-        name="grad_w",**params(10**11 if wide else 1))(sel,*gs,x,*([] if extra is None else [extra]),*deps)
+        name="grad_w",**params(10**11 if wide else 1))(sel,*gs,x,*extra,*deps)
 
 
 def plane_kernel(count,at_ref,*rest):
@@ -621,19 +632,19 @@
     out = with_other_core(out_send, out_keep)
     blocks = plane_call([gate, up, down, out], in_plane, [])
     common = (lens, grad_mixed, w_out, decay_wide, head_row, q, k, cum, dp, v, gp, o, before, rank)
-    grads, small, deps = None, None, list(blocks)
+    grads, small, deps = None, [], list(blocks)
     for seq in reversed(range(doc_lengths.shape[0])):
         grads, *sums = bwd_call(seq, grads, deps, *common)
-        small = sums if small is None else [a + b for a, b in zip(small, sums)]
+        small += sums
         deps = []
-    small = jnp.concatenate(
-        [small[0][:16].reshape(-1), small[1].sum(0), small[2].sum(0), gain_mlp_part.sum(0)]
-    )
-    count = small.shape[0]
+    in_send, in_keep = dw_call([grads], normed_in, mine, [], 1664, wide=False, extra=small + [gain_mlp_part])
     if low:
-        small_sum = lax.all_gather(small.reshape(-1, 256), ("rows", "mlp"), axis=0).sum(0).reshape(-1)
-    small = jnp.concatenate([small, jnp.zeros((128 * 128 - count,), F32)]).reshape(128, 128).astype(BF)
-    in_send, in_keep = dw_call([grads], normed_in, mine, [], 1664, wide=False, extra=small)
+        small = [total(small[t::3]) for t in range(3)]
+        small = jnp.concatenate(
+            [small[0][:16].reshape(16, 4, 128).transpose(1, 0, 2).reshape(-1)]
+            + [p.sum(0) for p in (small[1], small[2], gain_mlp_part)]
+        ).reshape(-1, 128)
+        small = lax.all_gather(small, ("rows", "mlp"), axis=0).sum(0)
     inner = with_other_core(in_send, in_keep)
     grad_tokens = dx_call(0, 2, None, grads, w_in, tokens, gain_mix, grad_res, [in_keep], 5 * 10**10)
     inner = spread([[p[None] for p in inner]], in_plane, 1, 1664, [grad_tokens])
@@ -661,10 +672,8 @@
     in_grads = lax.all_to_all(blocks, "mlp", 0, 0, tiled=True)
     block_out = down_call(1, 2, block_out, residual, hidden, mlp_all, [blocks])
     in_grads = total([in_grads[j] for j in range(mlps)])
-    if low:
-        small = small_sum
-    else:
-        small = in_grads[:, GW:].reshape(shard, 4, 128).transpose(1, 0, 2).reshape(-1)[:count]
+    if not low:
+        small = in_grads[:, GW:].reshape(shard, 4, 128).transpose(1, 0, 2).reshape(128, 128)
     in_grads = in_grads[:, :GW]
     if low:
         mlp_grads, out_grads = total(main), total(out)
@@ -673,7 +682,7 @@
         mlp_grads = main[: 3 * hid].reshape(2, 3, hid // 2, 128).transpose(1, 0, 2, 3).reshape(3, hid, 128)
         out_grads = main[3 * hid :].reshape(8, shard, 128).transpose(0, 2, 1).reshape(DV, shard)
     gain_mix_grad = jnp.sum(in_grads * mixer_local[:, :GW].astype(F32), axis=1) / norm_gain_mix.astype(F32)
-    at = 16 * DK + DK + HV + (here * mlps + lax.axis_index("mlp")) * shard
+    at = (here * mlps + lax.axis_index("mlp")) * shard
     return (
         block_out,
         grad_tokens,
@@ -683,11 +692,11 @@
         in_grads[:, CV : CV + DV],
         in_grads[:, CG : CG + DV],
         in_grads[:, CR : CR + 16],
-        small[: 16 * DK].reshape(16, DK),
-        small[16 * DK : 17 * DK],
-        small[17 * DK : 17 * DK + HV],
+        small[:64].reshape(4, 16, 128).transpose(1, 0, 2).reshape(16, DK),
+        small[64:68].reshape(-1),
+        small[68:70].reshape(-1),
         out_grads,
-        lax.dynamic_slice_in_dim(small, at, shard),
+        lax.dynamic_slice_in_dim(small[70:78].reshape(-1), at, shard),
         mlp_grads[0].T,
         mlp_grads[1].T,
         mlp_grads[2],

time: 545 us -> 541 us (level)
  transfers between devices with their start and end apart: 31 -> 31, of which waited for: 10 -> 11; matrix products, arithmetic and copies ran while one was open for 3% -> 3% of each run, Pallas kernels for 43% -> 43%
where the time goes in v6:
time: 541 us; the launch traced here: 535 us
  Pallas kernels  358 us (66%)
  waiting for transfers between devices  107 us (20%)
  starting transfers between devices  28.4 us (5%)
  local copies, waits for them, and re-layouts  21.5 us (4%)
  between operations  14.9 us (3%)
    pallas_call x4, Pallas kernels, dw_call(): pl.pallas_call(functools.partial(dw_kernel, count, wide, len(extra)), gri...  89.5 us
    pallas_call x1, Pallas kernels, mlp_call(): pl.pallas_call(functools.partial(mlp_kernel, chunk), grid=(n // T,), in_s...  86.5 us
    pallas_call x2, Pallas kernels, bwd_call(): pl.pallas_call(functools.partial(bwd_kernel, NT, seq), grid_spec=pltpu.Pr...  58.2 us
    ppermute x19, waiting for transfers between devices, swap(): return lax.ppermute(x, axis, [(i, i ^ 1 << bit) for i in range(count)])  47.8 us
    pallas_call x1, Pallas kernels, fwd_call(): pl.pallas_call(functools.partial(fwd_kernel, NT, cuts), grid_spec=pltpu.P...  42.1 us
    pallas_call x2, Pallas kernels, dx_call(): pl.pallas_call(dx_kernel, grid=(steps,), in_specs=[row(g), const(w), row(...  27.8 us
    pallas_call x2, Pallas kernels, down_call(): pl.pallas_call(down_kernel, grid=(steps,), in_specs=[row(d), row(ff), hbm...  25.1 us
    ppermute x3, waiting for transfers between devices, gather_pieces(): lax.ppermute(x, 'mlp', [(i, (i + step) % mlps) for i in range(mlps)])  24 us
  transfers between devices with their start and end apart: 31, of which 11 were waited for; matrix products, arithmetic and copies ran while one was open for 3% of the time, Pallas kernels for 43%

profile of v6, /device:TPU:0, one launch (start us, length us, event | category | flops | bytes accessed | tf_op | source)
XLA Modules:
  0.0 534.9 jit_solution(13312982882120360377)
XLA Ops:
  7.3 1.9 pad_maximum_fusion.1
  11.6 1.0 concatenate.30
  12.6 3.1 collective-permute-start
  15.7 2.6 collective-permute-start.1
  18.3 1.3 collective-permute-start.2
  19.6 1.0 concatenate.32
  20.6 4.6 collective-permute-done
  25.2 19.4 %collective-permute-done.1 = bf16[32,4224]{1,0:T(8,128)(2,1)S(1)} collective-permute-done((bf16[32,4224]{1,0:T(8,128)(2,1)S(1)}, bf16[32,4224]{1,0:T(8,128)(2,1)S(1)}, u32[]{:S(2)}, u32[]{:S(2)}) %collective-permute-start.1) | collective-permute-done | bytes 270368 | tf_op jit(solution)/shard_map/ppermute | solution.py:546
  44.8 1.8 collective-permute-start.10
  46.7 1.6 collective-permute-start.3
  49.1 14.4 %collective-permute-done.3.rest_1_ = bf16[128,2048]{1,0:T(8,128)(2,1)S(1)} collective-permute-done((bf16[128,2048]{1,0:T(8,128)(2,1)S(1)}, bf16[128,2048]{1,0:T(8,128)(2,1)S(1)}, u32[]{:S(2)}, u32[]{:S(2)}) %collective-permute-start.3) | collective-permute-done | bytes 524320 | tf_op jit(solution)/shard_map/ppermute | solution.py:514
  63.5 2.6 collective-permute-start.12
  66.1 12.3 %collective-permute-done.4.rest_2_ = bf16[128,2048]{1,0:T(8,128)(2,1)} collective-permute-done((bf16[128,2048]{1,0:T(8,128)(2,1)S(1)}, bf16[128,2048]{1,0:T(8,128)(2,1)}, u32[]{:S(2)}, u32[]{:S(2)}) %collective-permute-start.4) | collective-permute-done | bytes 524320 | tf_op jit(solution)/shard_map/ppermute | solution.py:514
  78.4 1.5 collective-permute-start.5
  79.9 7.5 %collective-permute-done.11.rest_10_ = bf16[128,2176]{1,0:T(8,128)(2,1)S(1)} collective-permute-done((bf16[128,2176]{1,0:T(8,128)(2,1)S(1)}, bf16[128,2176]{1,0:T(8,128)(2,1)S(1)}, u32[]{:S(2)}, u32[]{:S(2)}) %collective-permute-start.11) | collective-permute-done | bytes 557088 | tf_op jit(solution)/shard_map/ppermute | solution.py:514
  87.9 11.5 %collective-permute-done.12.rest_11_ = bf16[128,2176]{1,0:T(8,128)(2,1)S(1)} collective-permute-done((bf16[128,2176]{1,0:T(8,128)(2,1)S(1)}, bf16[128,2176]{1,0:T(8,128)(2,1)S(1)}, u32[]{:S(2)}, u32[]{:S(2)}) %collective-permute-start.12) | collective-permute-done | bytes 557088 | tf_op jit(solution)/shard_map/ppermute | solution.py:514
  103.8 42.1 %mixer_fwd.1 = (bf16[2048,1024]{1,0:T(8,128)(2,1)}, f32[2048,512]{1,0:T(8,128)}, f32[2048,512]{1,0:T(8,128)}, f32[2048,512]{1,0:T(8,128)}, f32[2048,512]{1,0:T(8...) custom-call(s32[8]{0:T(128)} %reshape.87.st_ref, ...), custom_call_target="tpu_custom_call" | custom-call | flops 1 | bytes 1 | tf_op jit(solution)/shard_map/mixer_fwd/pallas_call | solution.py:165
  145.9 1.4 fusion.5
  147.3 14.0 %all-gather.3.cloned.1.call-done = bf16[67584,128]{1,0:T(8,128)(2,1)} async-done(((bf16[2112,128]{1,0:T(8,128)(2,1)}), bf16[67584,128]{1,0:T(8,128)(2,1)}) %all-gather.3.cloned.1.call-update) | async-done | bytes 17301520 | tf_op jit(solution)/shard_map/all_gather | solution.py:591
  161.3 86.5 %mlp.1 = (f32[2048,1024]{1,0:T(8,128)}, bf16[2048,1024]{1,0:T(8,128)(2,1)}, bf16[2048,2816]{1,0:T(8,128)(2,1)}, bf16[2048,2816]{1,0:T(8,128)(2,1)}, bf16[2048,28...) custom-call(bf16[2048,1024]{1,0:T(8,128)(2,1)} %tok_ref.7, ...), custom_call_target="tpu_custom_call" | custom-call | flops 1 | bytes 1 | tf_op jit(solution)/shard_map/mlp/pallas_call | solution.py:341
  247.9 19.8 %grad_w.4 = (bf16[4,2816,128]{2,1,0:T(8,128)(2,1)}, bf16[4,2816,128]{2,1,0:T(8,128)(2,1)}) custom-call(s32[1]{0:T(128)} %bitcast.8.sel_ref, bf16[2048,2816]{1,0:T(8,128)(2,1)} %get-tuple-element.68.rest_0_.hid_ref, bf16[2048,1024]{1,0:T(8,128)(2,1)} %rest_1_.1, bf16[2048,1024]{1,0:T(8,128)(2,1)} %get-tuple-element.81.rest_2_), custom_call_target="tpu_custom_call" | custom-call | flops 99999997952 | bytes 1 | tf_op jit(solution)/shard_map/grad_w/pallas_call | solution.py:416
  268.0 35.4 %grad_w.5 = (bf16[4,2816,128]{2,1,0:T(8,128)(2,1)}, bf16[4,2816,128]{2,1,0:T(8,128)(2,1)}, bf16[4,2816,128]{2,1,0:T(8,128)(2,1)}, bf16[4,2816,128]{2,1,0:T(8,128)(2,1)}) custom-call(s32[1]{0:T(128)} %bitcast.8.sel_ref, bf16[2048,2816]{1,0:T(8,128)(2,1)} %get-tuple-element.79.rest_0_, bf16[2048,2816]{1,0:T(8,128)(2,1)} %get-tuple-element.80.rest_1_, ...), custom_call_target="tpu_custom_call" | custom-call | flops 99999997952 | bytes 1 | tf_op jit(solution)/shard_map/grad_w/pallas_call | solution.py:416
  304.0 1.6 copy-done.1
  305.6 9.9 %grad_w.6 = (bf16[4,1024,128]{2,1,0:T(8,128)(2,1)}, bf16[4,1024,128]{2,1,0:T(8,128)(2,1)}) custom-call(s32[1]{0:T(128)} %bitcast.8.sel_ref, bf16[2048,1024]{1,0:T(8,128)(2,1)} %get-tuple-element.64.mix_ref.rest_0_, bf16[2048,1024]{1,0:T(8,128)(2,1)} %get-tuple-element.69.rest_1_.gmix_ref, bf16[4,2816,128]{2,1,0:T(8,128)(2,1)} %get-tuple-element.83.rest_2_.rest_0_, ...), custom_call_target="tpu_custom_call" | custom-call | flops 99999997952 | bytes 1 | tf_op jit(solution)/shard_map/grad_w/pallas_call | solution.py:416
  316.3 2.1 collective-permute-done.20.rest_7_
  318.4 1.0 copy-done.4
  319.5 12.8 %plane.1 = (bf16[8,1184,128]{2,1,0:T(8,128)(2,1)}, bf16[8,1184,128]{2,1,0:T(8,128)(2,1)}, bf16[8,1184,128]{2,1,0:T(8,128)(2,1)}, bf16[8,1184,128]{2,1,0:T(8,128)(2,1)}) custom-call(s32[4]{0:T(128)} %iota_xor_fusion.at_ref, bf16[4,2816,128]{2,1,0:T(8,128)(2,1)} %get-tuple-element.83.rest_2_.rest_0_, bf16[4,2816,128]{2,1,0:T(8,128)(2,1)} %collective-permute-done.17.rest_1_, ...), custom_call_target="tpu_custom_call" | custom-call | flops 1 | bytes 1 | tf_op jit(solution)/shard_map/plane/pallas_call | solution.py:438
  332.3 1.5 collective-permute-start.25
  334.4 1.5 collective-permute-start.27
  335.8 29.2 %mixer_bwd.2 = (bf16[2048,3328]{1,0:T(8,128)(2,1)}, f32[128,512]{1,0:T(8,128)}, f32[8,512]{1,0:T(8,128)}, f32[8,256]{1,0:T(8,128)}) custom-call(s32[8]{0:T(128)} %reshape.87.st_ref, bf16[2048,1024]{1,0:T(8,128)(2,1)} %get-tuple-element.69.rest_1_.gmix_ref, bf16[1024,1024]{1,0:T(8,128)(2,1)} %get-tuple-element.66.wo_ref.w_ref, ...), custom_call_target="tpu_custom_call" | custom-call | flops 1 | bytes 1 | tf_op jit(solution)/shard_map/mixer_bwd/pallas_call | solution.py:263
  365.0 29.1 %mixer_bwd.3 = (bf16[2048,3328]{1,0:T(8,128)(2,1)}, f32[128,512]{1,0:T(8,128)}, f32[8,512]{1,0:T(8,128)}, f32[8,256]{1,0:T(8,128)}) custom-call(s32[8]{0:T(128)} %reshape.87.st_ref, bf16[2048,1024]{1,0:T(8,128)(2,1)} %get-tuple-element.69.rest_1_.gmix_ref, bf16[1024,1024]{1,0:T(8,128)(2,1)} %get-tuple-element.66.wo_ref.w_ref, ...), custom_call_target="tpu_custom_call", output_to_operand_aliasing={{0}: (14, {})} | custom-call | flops 1 | bytes 1 | tf_op jit(solution)/shard_map/mixer_bwd/pallas_call | solution.py:263
  394.1 24.4 %grad_w.7 = (bf16[4,128,3328]{2,1,0:T(8,128)(2,1)}, bf16[4,128,3328]{2,1,0:T(8,128)(2,1)}) custom-call(s32[1]{0:T(128)} %bitcast.8.sel_ref, bf16[2048,3328]{1,0:T(8,128)(2,1)} %get-tuple-element.95.rest_0_.g_ref, bf16[2048,1024]{1,0:T(8,128)(2,1)} %get-tuple-element.96.rest_1_, f32[128,512]{1,0:T(8,128)} %get-tuple-element.97.rest_2_, ...), custom_call_target="tpu_custom_call" | custom-call | flops 1 | bytes 1 | tf_op jit(solution)/shard_map/grad_w/pallas_call | solution.py:416
  418.5 13.7 %mixer_dx.2.rest_2_.rest_1_ = f32[2048,1024]{1,0:T(8,128)} custom-call(bf16[2048,3328]{1,0:T(8,128)(2,1)} %get-tuple-element.95.rest_0_.g_ref, bf16[1024,3200]{1,0:T(8,128)(2,1)} %get-tuple-element.106.w_ref, bf16[2048,1024]{1,0:T(8,128)(2,1)} %tok_ref.7, f32[1,1024]{1,0:T(1,128)} %get-tuple-element.170.gain_ref, f32[2048,1024]{1,0:T(8,128)} %get-tuple-element.107.gres_ref, ...), custom_call_target="tpu_custom_call" | custom-call | flops 49999998976 | bytes 1 | tf_op jit(solution)/shard_map/mixer_dx/pallas_call | solution.py:289
  432.2 1.7 copy-done
  434.0 5.2 spread.1
  439.2 1.4 collective-permute-done.26.refs_2_
  440.6 7.6 %line.1.rest_0_ = bf16[9472,128]{1,0:T(8,128)(2,1)} custom-call(bf16[8,1184,128]{2,1,0:T(8,128)(2,1)} %get-tuple-element.90.rest_0_.refs_0_, bf16[8,1184,128]{2,1,0:T(8,128)(2,1)} %collective-permute-done.25.refs_1_, bf16[8,1184,128]{2,1,0:T(8,128)(2,1)} %collective-permute-done.26.refs_2_, bf16[8,1184,128]{2,1,0:T(8,128)(2,1)} %collective-permute-done.27.refs_3_, ...), custom_call_target="tpu_custom_call" | custom-call | flops 1 | bytes 1 | tf_op jit(solution)/shard_map/line/pallas_call | solution.py:467
  448.9 1.5 collective-permute-start.23
  450.4 1.4 collective-permute-start.24
  451.8 14.1 %mixer_dx.3.rest_0_ = f32[2048,1024]{1,0:T(8,128)} custom-call(bf16[2048,3328]{1,0:T(8,128)(2,1)} %get-tuple-element.95.rest_0_.g_ref, bf16[1024,3200]{1,0:T(8,128)(2,1)} %get-tuple-element.106.w_ref, bf16[2048,1024]{1,0:T(8,128)(2,1)} %tok_ref.7, f32[1,1024]{1,0:T(1,128)} %get-tuple-element.170.gain_ref, ...), custom_call_target="tpu_custom_call", output_to_operand_aliasing={{}: (6, {})} | custom-call | flops 1 | bytes 1 | tf_op jit(solution)/shard_map/mixer_dx/pallas_call | solution.py:289
  465.9 12.7 %mlp_down.2.refs_4_.rest_1_ = bf16[2048,1024]{1,0:T(8,128)(2,1)} custom-call(f32[2048,1024]{1,0:T(8,128)} %get-tuple-element.67.res_ref, bf16[2048,2816]{1,0:T(8,128)(2,1)} %get-tuple-element.68.rest_0_.hid_ref, bf16[8,4,2112,128]{3,2,1,0:T(8,128)(2,1)} %bitcast.60, f32[2048,1024]{1,0:T(8,128)} %mixer_dx.3.rest_0_), custom_call_target="tpu_custom_call" | custom-call | flops 1 | bytes 1 | tf_op jit(solution)/shard_map/mlp_down/pallas_call | solution.py:361
  478.6 9.3 %collective-permute-done.23 = bf16[1,128,3328]{2,1,0:T(8,128)(2,1)S(1)} collective-permute-done((bf16[1,128,3328]{2,1,0:T(8,128)(2,1)}, bf16[1,128,3328]{2,1,0:T(8,128)(2,1)S(1)}, u32[]{:S(2)}, u32[]{:S(2)}) %collective-permute-start.23) | collective-permute-done | bytes 852000 | tf_op jit(solution)/shard_map/ppermute | solution.py:534
  489.1 3.4 stack.1
  492.5 3.5 all-to-all-start
  496.3 12.4 %mlp_down.3 = bf16[2048,1024]{1,0:T(8,128)(2,1)} custom-call(f32[2048,1024]{1,0:T(8,128)} %get-tuple-element.67.res_ref, bf16[2048,2816]{1,0:T(8,128)(2,1)} %get-tuple-element.68.rest_0_.hid_ref, bf16[8,4,2112,128]{3,2,1,0:T(8,128)(2,1)} %bitcast.61, bf16[4,32,3712]{2,1,0:T(8,128)(2,1)} %bitcast.63, ...), custom_call_target="tpu_custom_call", output_to_operand_aliasing={{}: (4, {})} | custom-call | flops 1 | bytes 1 | tf_op jit(solution)/shard_map/mlp_down/pallas_call | solution.py:361
  508.7 10.2 %all-to-all-done = bf16[4,32,3712]{2,1,0:T(8,128)(2,1)S(1)} async-done(((bf16[4,32,3712]{2,1,0:T(8,128)(2,1)}), bf16[4,32,3712]{2,1,0:T(8,128)(2,1)S(1)}, u32[]{:S(2)}, u32[]{:S(2)}) %all-to-all-start) | async-done | bytes 950304 | tf_op jit(solution)/shard_map/all_to_all | solution.py:672
  524.2 1.1 slice.149
  525.3 1.0 fusion.3
  (147 shorter events, 19.4 us)
Async XLA Ops:
  7.2 39.5 %copy-start.19 = (bf16[32,512]{1,0:T(8,128)(2,1)S(1)}, bf16[32,512]{1,0:T(8,128)(2,1)}, u32[]{:S(2)}) copy-start(bf16[32,512]{1,0:T(8,128)(2,1)} %param.21) | copy-start | bytes 98308
  7.2 39.5 %copy-start.21 = (bf16[32,512]{1,0:T(8,128)(2,1)S(1)}, bf16[32,512]{1,0:T(8,128)(2,1)}, u32[]{:S(2)}) copy-start(bf16[32,512]{1,0:T(8,128)(2,1)} %param.22) | copy-start | bytes 98308
  7.2 39.5 %copy-start.9 = (bf16[32,1024]{1,0:T(8,128)(2,1)S(1)}, bf16[32,1024]{1,0:T(8,128)(2,1)}, u32[]{:S(2)}) copy-start(bf16[32,1024]{1,0:T(8,128)(2,1)} %param.23) | copy-start | bytes 196612
  7.2 154.1 %all-gather.3.cloned.1.call-start = ((), (), s32[]{:S(2)}) async-start(), calls=%async_computation.3 | async-start | bytes 17842176 | tf_op jit(solution)/shard_map/all_gather | solution.py:591
  9.2 91.5 %copy-start.31 = (bf16[16,512]{1,0:T(8,128)(2,1)S(1)}, bf16[16,512]{1,0:T(8,128)(2,1)}, u32[]{:S(2)}) copy-start(bf16[16,512]{1,0:T(8,128)(2,1)} %param.26) | copy-start | bytes 49156
  9.2 92.2 %copy-start.35 = (bf16[256]{0:T(256)(128)(2,1)S(1)}, bf16[256]{0:T(256)(128)(2,1)}, u32[]{:S(2)}) copy-start(bf16[256]{0:T(256)(128)(2,1)} %param.28) | copy-start | bytes 1540
  9.2 92.7 %copy-start.34 = (s32[2,4]{1,0:T(2,128)S(1)}, s32[2,4]{1,0:T(2,128)}, u32[]{:S(2)}) copy-start(s32[2,4]{1,0:T(2,128)} %param.18) | copy-start | bytes 100
  9.2 93.3 %copy-start.32 = (bf16[512]{0:T(512)(128)(2,1)S(1)}, bf16[512]{0:T(512)(128)(2,1)}, u32[]{:S(2)}) copy-start(bf16[512]{0:T(512)(128)(2,1)} %param.27) | copy-start | bytes 3076
  9.2 514.9 %reduce-scatter.2.cloned.1.call-start = ((), (), s32[]{:S(2)}) async-start(), calls=%async_computation.2 | async-start | bytes 3031040 | tf_op jit(solution)/shard_map/reduce_scatter | solution.py:662
  10.1 34.6 %copy-start.23 = (bf16[32,16]{1,0:T(8,128)(2,1)}, bf16[32,16]{1,0:T(8,128)(2,1)S(1)}, u32[]{:S(2)}) copy-start(bf16[32,16]{1,0:T(8,128)(2,1)S(1)} %copy.59) | copy-start | bytes 3076
  10.8 33.8 %copy-start.25 = (bf16[32,1]{1,0:T(8,128)(2,1)}, bf16[32,1]{1,0:T(8,128)(2,1)S(1)}, u32[]{:S(2)}) copy-start(bf16[32,1]{1,0:T(8,128)(2,1)S(1)} %copy.60) | copy-start | bytes 196
  11.6 33.1 %copy-start.27 = (bf16[32,1]{1,0:T(8,128)(2,1)}, bf16[32,1]{1,0:T(8,128)(2,1)S(1)}, u32[]{:S(2)}) copy-start(bf16[32,1]{1,0:T(8,128)(2,1)S(1)} %copy.61) | copy-start | bytes 196
  11.6 33.1 %copy-start.29 = (bf16[32,110]{1,0:T(8,128)(2,1)}, bf16[32,110]{1,0:T(8,128)(2,1)S(1)}, u32[]{:S(2)}) copy-start(bf16[32,110]{1,0:T(8,128)(2,1)S(1)} %broadcast_in_dim.35) | copy-start | bytes 21124
  12.6 12.5 %collective-permute-start = (bf16[32,4224]{1,0:T(8,128)(2,1)S(1)}, bf16[32,4224]{1,0:T(8,128)(2,1)S(1)}, u32[]{:S(2)}, u32[]{:S(2)}) collective-permute-start(bf16[32,4224]{1,0:T(8,128)(2,1)S(1)} %concatenate.30), channel_id=1, source_target_pairs={{0,1},{1,2},{2,3},{3,0},{4,5},{5,6},{6,7},{7,4},{8,9},{9,10},{10,1... | collective-permute-start | bytes 811016 | tf_op jit(solution)/shard_map/ppermute | solution.py:546
  15.7 28.9 %collective-permute-start.1 = (bf16[32,4224]{1,0:T(8,128)(2,1)S(1)}, bf16[32,4224]{1,0:T(8,128)(2,1)S(1)}, u32[]{:S(2)}, u32[]{:S(2)}) collective-permute-start(bf16[32,4224]{1,0:T(8,128)(2,1)S(1)} %concatenate.30), channel_id=1, source_target_pairs={{0,2},{1,3},{2,0},{3,1},{4,6},{5,7},{6,4},{7,5},{8,10},{9,11},{10,... | collective-permute-start | bytes 811016 | tf_op jit(solution)/shard_map/ppermute | solution.py:546
  18.3 26.3 %collective-permute-start.2 = (bf16[32,4224]{1,0:T(8,128)(2,1)S(1)}, bf16[32,4224]{1,0:T(8,128)(2,1)S(1)}, u32[]{:S(2)}, u32[]{:S(2)}) collective-permute-start(bf16[32,4224]{1,0:T(8,128)(2,1)S(1)} %concatenate.30), channel_id=1, source_target_pairs={{0,3},{1,0},{2,1},{3,2},{4,7},{5,4},{6,5},{7,6},{8,11},{9,8},{10,9... | collective-permute-start | bytes 811016 | tf_op jit(solution)/shard_map/ppermute | solution.py:546
  44.8 59.0 %copy-start.2 = (bf16[128,2176]{1,0:T(8,128)(2,1)}, bf16[128,2176]{1,0:T(8,128)(2,1)S(1)}, u32[]{:S(2)}) copy-start(bf16[128,2176]{1,0:T(8,128)(2,1)S(1)} %pad_maximum_fusion.rest_8_) | copy-start | bytes 1671172
  44.8 18.8 %collective-permute-start.10 = (bf16[128,2176]{1,0:T(8,128)(2,1)S(1)}, bf16[128,2176]{1,0:T(8,128)(2,1)S(1)}, u32[]{:S(2)}, u32[]{:S(2)}) collective-permute-start(bf16[128,2176]{1,0:T(8,128)(2,1)S(1)} %pad_maximum_fusion.rest_8_), channel_id=1, source_target_pairs={{0,16},{4,20},{8,24},{12,28},{16,0},{20,4},{24,8},{28,12},{1,17},{... | collective-permute-start | bytes 1671176 | tf_op jit(solution)/shard_map/ppermute | solution.py:514
  46.7 57.0 %copy-start.3 = (bf16[128,2048]{1,0:T(8,128)(2,1)}, bf16[128,2048]{1,0:T(8,128)(2,1)S(1)}, u32[]{:S(2)}) copy-start(bf16[128,2048]{1,0:T(8,128)(2,1)S(1)} %pad_maximum_fusion.2.rest_0_) | copy-start | bytes 1572868
  46.7 16.8 %collective-permute-start.3 = (bf16[128,2048]{1,0:T(8,128)(2,1)S(1)}, bf16[128,2048]{1,0:T(8,128)(2,1)S(1)}, u32[]{:S(2)}, u32[]{:S(2)}) collective-permute-start(bf16[128,2048]{1,0:T(8,128)(2,1)S(1)} %pad_maximum_fusion.2.rest_0_), channel_id=1, source_target_pairs={{0,8},{4,12},{8,0},{12,4},{16,24},{20,28},{24,16},{28,20},{1,9},{5... | collective-permute-start | bytes 1572872 | tf_op jit(solution)/shard_map/ppermute | solution.py:514
  48.3 30.0 %collective-permute-start.4 = (bf16[128,2048]{1,0:T(8,128)(2,1)S(1)}, bf16[128,2048]{1,0:T(8,128)(2,1)}, u32[]{:S(2)}, u32[]{:S(2)}) collective-permute-start(bf16[128,2048]{1,0:T(8,128)(2,1)S(1)} %pad_maximum_fusion.2.rest_0_), channel_id=1, source_target_pairs={{0,16},{4,20},{8,24},{12,28},{16,0},{20,4},{24,8},{28,12},{1,17},{... | collective-permute-start | bytes 1572872 | tf_op jit(solution)/shard_map/ppermute | solution.py:514
  48.8 31.1 %collective-permute-start.6 = (bf16[128,2048]{1,0:T(8,128)(2,1)S(1)}, bf16[128,2048]{1,0:T(8,128)(2,1)S(1)}, u32[]{:S(2)}, u32[]{:S(2)}) collective-permute-start(bf16[128,2048]{1,0:T(8,128)(2,1)S(1)} %pad_maximum_fusion.2.rest_0_), channel_id=1, source_target_pairs={{0,4},{4,0},{8,12},{12,8},{16,20},{20,16},{24,28},{28,24},{1,5},{5... | collective-permute-start | bytes 1572872 | tf_op jit(solution)/shard_map/ppermute | solution.py:514
  48.8 38.6 %collective-permute-start.11 = (bf16[128,2176]{1,0:T(8,128)(2,1)S(1)}, bf16[128,2176]{1,0:T(8,128)(2,1)S(1)}, u32[]{:S(2)}, u32[]{:S(2)}) collective-permute-start(bf16[128,2176]{1,0:T(8,128)(2,1)S(1)} %pad_maximum_fusion.rest_8_), channel_id=1, source_target_pairs={{0,8},{4,12},{8,0},{12,4},{16,24},{20,28},{24,16},{28,20},{1,9},{5... | collective-permute-start | bytes 1671176 | tf_op jit(solution)/shard_map/ppermute | solution.py:514
  63.5 35.9 %copy-start.16 = (bf16[128,2048]{1,0:T(8,128)(2,1)}, bf16[128,2048]{1,0:T(8,128)(2,1)S(1)}, u32[]{:S(2)}) copy-start(bf16[128,2048]{1,0:T(8,128)(2,1)S(1)} %collective-permute-done.3.rest_1_) | copy-start | bytes 1572868
  63.5 23.9 %collective-permute-start.13 = (bf16[128,2176]{1,0:T(8,128)(2,1)S(1)}, bf16[128,2176]{1,0:T(8,128)(2,1)S(1)}, u32[]{:S(2)}, u32[]{:S(2)}) collective-permute-start(bf16[128,2176]{1,0:T(8,128)(2,1)S(1)} %pad_maximum_fusion.rest_8_), channel_id=1, source_target_pairs={{0,4},{4,0},{8,12},{12,8},{16,20},{20,16},{24,28},{28,24},{1,5},{5... | collective-permute-start | bytes 1671176 | tf_op jit(solution)/shard_map/ppermute | solution.py:514
  63.5 40.2 %copy-start.12 = (bf16[128,2176]{1,0:T(8,128)(2,1)}, bf16[128,2176]{1,0:T(8,128)(2,1)S(1)}, u32[]{:S(2)}) copy-start(bf16[128,2176]{1,0:T(8,128)(2,1)S(1)} %collective-permute-done.10.rest_9_) | copy-start | bytes 1671172
  63.5 35.9 %collective-permute-start.12 = (bf16[128,2176]{1,0:T(8,128)(2,1)S(1)}, bf16[128,2176]{1,0:T(8,128)(2,1)S(1)}, u32[]{:S(2)}, u32[]{:S(2)}) collective-permute-start(bf16[128,2176]{1,0:T(8,128)(2,1)S(1)} %collective-permute-done.10.rest_9_), channel_id=1, source_target_pairs={{0,8},{4,12},{8,0},{12,4},{16,24},{20,28},{24,16},{28,20},{1,9},{5... | collective-permute-start | bytes 1671176 | tf_op jit(solution)/shard_map/ppermute | solution.py:514
  78.4 21.0 %collective-permute-start.5 = (bf16[128,2048]{1,0:T(8,128)(2,1)S(1)}, bf16[128,2048]{1,0:T(8,128)(2,1)}, u32[]{:S(2)}, u32[]{:S(2)}) collective-permute-start(bf16[128,2048]{1,0:T(8,128)(2,1)S(1)} %collective-permute-done.3.rest_1_), channel_id=1, source_target_pairs={{0,16},{4,20},{8,24},{12,28},{16,0},{20,4},{24,8},{28,12},{1,17},{... | collective-permute-start | bytes 1572872 | tf_op jit(solution)/shard_map/ppermute | solution.py:514
  79.9 20.0 %copy-start.17 = (bf16[128,2048]{1,0:T(8,128)(2,1)}, bf16[128,2048]{1,0:T(8,128)(2,1)S(1)}, u32[]{:S(2)}) copy-start(bf16[128,2048]{1,0:T(8,128)(2,1)S(1)} %collective-permute-done.6.rest_4_) | copy-start | bytes 1572868
  79.9 20.0 %collective-permute-start.7 = (bf16[128,2048]{1,0:T(8,128)(2,1)S(1)}, bf16[128,2048]{1,0:T(8,128)(2,1)S(1)}, u32[]{:S(2)}, u32[]{:S(2)}) collective-permute-start(bf16[128,2048]{1,0:T(8,128)(2,1)S(1)} %collective-permute-done.3.rest_1_), channel_id=1, source_target_pairs={{0,4},{4,0},{8,12},{12,8},{16,20},{20,16},{24,28},{28,24},{1,5},{5... | collective-permute-start | bytes 1572872 | tf_op jit(solution)/shard_map/ppermute | solution.py:514
  87.4 16.3 %collective-permute-start.14 = (bf16[128,2176]{1,0:T(8,128)(2,1)S(1)}, bf16[128,2176]{1,0:T(8,128)(2,1)}, u32[]{:S(2)}, u32[]{:S(2)}) collective-permute-start(bf16[128,2176]{1,0:T(8,128)(2,1)S(1)} %collective-permute-done.10.rest_9_), channel_id=1, source_target_pairs={{0,4},{4,0},{8,12},{12,8},{16,20},{20,16},{24,28},{28,24},{1,5},{5... | collective-permute-start | bytes 1671176 | tf_op jit(solution)/shard_map/ppermute | solution.py:514
  87.4 16.3 %collective-permute-start.15 = (bf16[128,2176]{1,0:T(8,128)(2,1)S(1)}, bf16[128,2176]{1,0:T(8,128)(2,1)}, u32[]{:S(2)}, u32[]{:S(2)}) collective-permute-start(bf16[128,2176]{1,0:T(8,128)(2,1)S(1)} %collective-permute-done.11.rest_10_), channel_id=1, source_target_pairs={{0,4},{4,0},{8,12},{12,8},{16,20},{20,16},{24,28},{28,24},{1,5},{5... | collective-permute-start | bytes 1671176 | tf_op jit(solution)/shard_map/ppermute | solution.py:514
  99.4 4.4 collective-permute-start.16
  99.4 4.3 collective-permute-start.8
  99.9 3.8 collective-permute-start.9
  267.7 36.3 %collective-permute-start.19 = (bf16[4,2816,128]{2,1,0:T(8,128)(2,1)}, bf16[4,2816,128]{2,1,0:T(8,128)(2,1)S(1)}, u32[]{:S(2)}, u32[]{:S(2)}) collective-permute-start(bf16[4,2816,128]{2,1,0:T(8,128)(2,1)} %get-tuple-element.87), channel_id=1, source_target_pairs={{0,4},{4,0},{8,12},{12,8},{16,20},{20,16},{24,28},{28,24},{1,5},{5... | collective-permute-start | bytes 8650760 | tf_op jit(solution)/shard_map/ppermute | solution.py:514
  303.4 12.9 %collective-permute-start.17 = (bf16[4,2816,128]{2,1,0:T(8,128)(2,1)}, bf16[4,2816,128]{2,1,0:T(8,128)(2,1)}, u32[]{:S(2)}, u32[]{:S(2)}) collective-permute-start(bf16[4,2816,128]{2,1,0:T(8,128)(2,1)} %get-tuple-element.84), channel_id=1, source_target_pairs={{0,4},{4,0},{8,12},{12,8},{16,20},{20,16},{24,28},{28,24},{1,5},{5... | collective-permute-start | bytes 8650760 | tf_op jit(solution)/shard_map/ppermute | solution.py:514
  303.8 12.5 %collective-permute-start.18 = (bf16[4,2816,128]{2,1,0:T(8,128)(2,1)}, bf16[4,2816,128]{2,1,0:T(8,128)(2,1)}, u32[]{:S(2)}, u32[]{:S(2)}) collective-permute-start(bf16[4,2816,128]{2,1,0:T(8,128)(2,1)} %get-tuple-element.86), channel_id=1, source_target_pairs={{0,4},{4,0},{8,12},{12,8},{16,20},{20,16},{24,28},{28,24},{1,5},{5... | collective-permute-start | bytes 8650760 | tf_op jit(solution)/shard_map/ppermute | solution.py:514
  315.5 2.9 collective-permute-start.20
  332.3 106.9 %collective-permute-start.25 = (bf16[8,1184,128]{2,1,0:T(8,128)(2,1)}, bf16[8,1184,128]{2,1,0:T(8,128)(2,1)}, u32[]{:S(2)}, u32[]{:S(2)}) collective-permute-start(bf16[8,1184,128]{2,1,0:T(8,128)(2,1)} %get-tuple-element.91.rest_1_), channel_id=1, source_target_pairs={{0,8},{4,12},{8,0},{12,4},{16,24},{20,28},{24,16},{28,20},{1,9},{5... | collective-permute-start | bytes 7274504 | tf_op jit(solution)/shard_map/ppermute | solution.py:534
  333.8 106.8 %collective-permute-start.26 = (bf16[8,1184,128]{2,1,0:T(8,128)(2,1)}, bf16[8,1184,128]{2,1,0:T(8,128)(2,1)}, u32[]{:S(2)}, u32[]{:S(2)}) collective-permute-start(bf16[8,1184,128]{2,1,0:T(8,128)(2,1)} %get-tuple-element.92.rest_2_), channel_id=1, source_target_pairs={{0,16},{4,20},{8,24},{12,28},{16,0},{20,4},{24,8},{28,12},{1,17},{... | collective-permute-start | bytes 7274504 | tf_op jit(solution)/shard_map/ppermute | solution.py:534
  334.4 106.2 %collective-permute-start.27 = (bf16[8,1184,128]{2,1,0:T(8,128)(2,1)}, bf16[8,1184,128]{2,1,0:T(8,128)(2,1)}, u32[]{:S(2)}, u32[]{:S(2)}) collective-permute-start(bf16[8,1184,128]{2,1,0:T(8,128)(2,1)} %get-tuple-element.93.rest_3_), channel_id=1, source_target_pairs={{0,24},{4,28},{8,16},{12,20},{16,8},{20,12},{24,0},{28,4},{1,25},{... | collective-permute-start | bytes 7274504 | tf_op jit(solution)/shard_map/ppermute | solution.py:534
  418.4 13.8 %collective-permute-start.21 = (bf16[4,128,3328]{2,1,0:T(8,128)(2,1)}, bf16[4,128,3328]{2,1,0:T(8,128)(2,1)S(1)}, u32[]{:S(2)}, u32[]{:S(2)}) collective-permute-start(bf16[4,128,3328]{2,1,0:T(8,128)(2,1)} %get-tuple-element.105), channel_id=1, source_target_pairs={{0,4},{4,0},{8,12},{12,8},{16,20},{20,16},{24,28},{28,24},{1,5},{5... | collective-permute-start | bytes 10223624 | tf_op jit(solution)/shard_map/ppermute | solution.py:514
  448.2 30.3 %collective-permute-start.22 = (bf16[1,128,3328]{2,1,0:T(8,128)(2,1)}, bf16[1,128,3328]{2,1,0:T(8,128)(2,1)S(1)}, u32[]{:S(2)}, u32[]{:S(2)}) collective-permute-start(bf16[1,128,3328]{2,1,0:T(8,128)(2,1)} %get-tuple-element.109.refs_5_), channel_id=1, source_target_pairs={{0,8},{4,12},{8,0},{12,4},{16,24},{20,28},{24,16},{28,20},{1,9},{5... | collective-permute-start | bytes 2555912 | tf_op jit(solution)/shard_map/ppermute | solution.py:534
  448.9 39.0 %collective-permute-start.23 = (bf16[1,128,3328]{2,1,0:T(8,128)(2,1)}, bf16[1,128,3328]{2,1,0:T(8,128)(2,1)S(1)}, u32[]{:S(2)}, u32[]{:S(2)}) collective-permute-start(bf16[1,128,3328]{2,1,0:T(8,128)(2,1)} %get-tuple-element.110.refs_6_), channel_id=1, source_target_pairs={{0,16},{4,20},{8,24},{12,28},{16,0},{20,4},{24,8},{28,12},{1,17},{... | collective-permute-start | bytes 2555912 | tf_op jit(solution)/shard_map/ppermute | solution.py:534
  450.4 37.5 %collective-permute-start.24 = (bf16[1,128,3328]{2,1,0:T(8,128)(2,1)S(1)}, bf16[1,128,3328]{2,1,0:T(8,128)(2,1)S(1)}, u32[]{:S(2)}, u32[]{:S(2)}) collective-permute-start(bf16[1,128,3328]{2,1,0:T(8,128)(2,1)S(1)} %copy-done.8), channel_id=1, source_target_pairs={{0,24},{4,28},{8,16},{12,20},{16,8},{20,12},{24,0},{28,4},{1,25},{... | collective-permute-start | bytes 2555912 | tf_op jit(solution)/shard_map/ppermute | solution.py:534
  492.5 26.4 %all-to-all-start = ((bf16[4,32,3712]{2,1,0:T(8,128)(2,1)}), bf16[4,32,3712]{2,1,0:T(8,128)(2,1)S(1)}, u32[]{:S(2)}, u32[]{:S(2)}) async-start(bf16[4,32,3712]{2,1,0:T(8,128)(2,1)} %bitcast.62), calls=%async_computation | async-start | bytes 1900544 | tf_op jit(solution)/shard_map/all_to_all | solution.py:672
  496.2 25.5 %copy-start.33 = (bf16[32]{0:T(256)(128)(2,1)S(1)}, bf16[32]{0:T(256)(128)(2,1)}, u32[]{:S(2)}) copy-start(bf16[32]{0:T(256)(128)(2,1)} %param.20) | copy-start | bytes 196
  (19 other events, 119.5 us)
Sparse Core Ops, SparseCore 0:
  10.9 150.4 all-gather.2
  448.4 47.2 reduce-scatter.1

commit v7 on v6

--- a/solution.py
+++ b/solution.py
@@ -280,7 +280,7 @@
     gt_ref[...]=gres_ref[...]+r*sc-x*(r*r*r*inner)
 
 
-def dx_call(part,parts,begun,g,w,tok,gain,gres,deps,flops=1,T=256):
+def dx_call(part,parts,begun,g,w,tok,gain,gres,deps,flops=1,T=512):
     n,d=tok.shape; sd=jax.ShapeDtypeStruct; steps=n//T//parts; first=part*steps
     row=lambda a: pl.BlockSpec((T,a.shape[1]),lambda i:(first+i,0))
     const=lambda a: pl.BlockSpec(a.shape,lambda i:(0,0),pipeline_mode=pl.Buffered(1))

time: 541 us -> 542 us (level)
  no operation moved by 1% of the time
where the time goes in v7:
time: 542 us; the launch traced here: 536 us
  Pallas kernels  360 us (66%)
  waiting for transfers between devices  106 us (20%)
  starting transfers between devices  28.4 us (5%)
  local copies, waits for them, and re-layouts  21.5 us (4%)
  between operations  14.9 us (3%)
    pallas_call x4, Pallas kernels, dw_call(): pl.pallas_call(functools.partial(dw_kernel, count, wide, len(extra)), gri...  89.5 us
    pallas_call x1, Pallas kernels, mlp_call(): pl.pallas_call(functools.partial(mlp_kernel, chunk), grid=(n // T,), in_s...  86.5 us
    pallas_call x2, Pallas kernels, bwd_call(): pl.pallas_call(functools.partial(bwd_kernel, NT, seq), grid_spec=pltpu.Pr...  58.2 us
    ppermute x19, waiting for transfers between devices, swap(): return lax.ppermute(x, axis, [(i, i ^ 1 << bit) for i in range(count)])  47.8 us
    pallas_call x1, Pallas kernels, fwd_call(): pl.pallas_call(functools.partial(fwd_kernel, NT, cuts), grid_spec=pltpu.P...  42.1 us
    pallas_call x2, Pallas kernels, dx_call(): pl.pallas_call(dx_kernel, grid=(steps,), in_specs=[row(g), const(w), row(...  29.6 us
    pallas_call x2, Pallas kernels, down_call(): pl.pallas_call(down_kernel, grid=(steps,), in_specs=[row(d), row(ff), hbm...  24.9 us
    ppermute x3, waiting for transfers between devices, gather_pieces(): lax.ppermute(x, 'mlp', [(i, (i + step) % mlps) for i in range(mlps)])  24 us
  transfers between devices with their start and end apart: 31, of which 11 were waited for; matrix products, arithmetic and copies ran while one was open for 3% of the time, Pallas kernels for 43%

profile of v7, /device:TPU:0, one launch (start us, length us, event | category | flops | bytes accessed | tf_op | source)
XLA Modules:
  0.0 536.1 jit_solution(10162224245488410131)
XLA Ops:
  7.3 1.9 pad_maximum_fusion.1
  11.6 1.0 concatenate.30
  12.6 3.1 collective-permute-start
  15.7 2.6 collective-permute-start.1
  18.3 1.3 collective-permute-start.2
  19.6 1.0 concatenate.32
  20.6 4.6 collective-permute-done
  25.2 19.4 %collective-permute-done.1 = bf16[32,4224]{1,0:T(8,128)(2,1)S(1)} collective-permute-done((bf16[32,4224]{1,0:T(8,128)(2,1)S(1)}, bf16[32,4224]{1,0:T(8,128)(2,1)S(1)}, u32[]{:S(2)}, u32[]{:S(2)}) %collective-permute-start.1) | collective-permute-done | bytes 270368 | tf_op jit(solution)/shard_map/ppermute | solution.py:546
  44.8 1.8 collective-permute-start.10
  46.7 1.6 collective-permute-start.3
  49.1 14.4 %collective-permute-done.3.rest_1_ = bf16[128,2048]{1,0:T(8,128)(2,1)S(1)} collective-permute-done((bf16[128,2048]{1,0:T(8,128)(2,1)S(1)}, bf16[128,2048]{1,0:T(8,128)(2,1)S(1)}, u32[]{:S(2)}, u32[]{:S(2)}) %collective-permute-start.3) | collective-permute-done | bytes 524320 | tf_op jit(solution)/shard_map/ppermute | solution.py:514
  63.5 2.6 collective-permute-start.12
  66.1 12.3 %collective-permute-done.4.rest_2_ = bf16[128,2048]{1,0:T(8,128)(2,1)} collective-permute-done((bf16[128,2048]{1,0:T(8,128)(2,1)S(1)}, bf16[128,2048]{1,0:T(8,128)(2,1)}, u32[]{:S(2)}, u32[]{:S(2)}) %collective-permute-start.4) | collective-permute-done | bytes 524320 | tf_op jit(solution)/shard_map/ppermute | solution.py:514
  78.4 1.5 collective-permute-start.5
  79.9 7.5 %collective-permute-done.11.rest_10_ = bf16[128,2176]{1,0:T(8,128)(2,1)S(1)} collective-permute-done((bf16[128,2176]{1,0:T(8,128)(2,1)S(1)}, bf16[128,2176]{1,0:T(8,128)(2,1)S(1)}, u32[]{:S(2)}, u32[]{:S(2)}) %collective-permute-start.11) | collective-permute-done | bytes 557088 | tf_op jit(solution)/shard_map/ppermute | solution.py:514
  87.9 11.5 %collective-permute-done.12.rest_11_ = bf16[128,2176]{1,0:T(8,128)(2,1)S(1)} collective-permute-done((bf16[128,2176]{1,0:T(8,128)(2,1)S(1)}, bf16[128,2176]{1,0:T(8,128)(2,1)S(1)}, u32[]{:S(2)}, u32[]{:S(2)}) %collective-permute-start.12) | collective-permute-done | bytes 557088 | tf_op jit(solution)/shard_map/ppermute | solution.py:514
  103.8 42.1 %mixer_fwd.1 = (bf16[2048,1024]{1,0:T(8,128)(2,1)}, f32[2048,512]{1,0:T(8,128)}, f32[2048,512]{1,0:T(8,128)}, f32[2048,512]{1,0:T(8,128)}, f32[2048,512]{1,0:T(8...) custom-call(s32[8]{0:T(128)} %reshape.87.st_ref, ...), custom_call_target="tpu_custom_call" | custom-call | flops 1 | bytes 1 | tf_op jit(solution)/shard_map/mixer_fwd/pallas_call | solution.py:165
  145.9 1.4 fusion.5
  147.3 14.0 %all-gather.3.cloned.1.call-done = bf16[67584,128]{1,0:T(8,128)(2,1)} async-done(((bf16[2112,128]{1,0:T(8,128)(2,1)}), bf16[67584,128]{1,0:T(8,128)(2,1)}) %all-gather.3.cloned.1.call-update) | async-done | bytes 17301520 | tf_op jit(solution)/shard_map/all_gather | solution.py:591
  161.3 86.5 %mlp.1 = (f32[2048,1024]{1,0:T(8,128)}, bf16[2048,1024]{1,0:T(8,128)(2,1)}, bf16[2048,2816]{1,0:T(8,128)(2,1)}, bf16[2048,2816]{1,0:T(8,128)(2,1)}, bf16[2048,28...) custom-call(bf16[2048,1024]{1,0:T(8,128)(2,1)} %tok_ref.7, ...), custom_call_target="tpu_custom_call" | custom-call | flops 1 | bytes 1 | tf_op jit(solution)/shard_map/mlp/pallas_call | solution.py:341
  247.9 19.8 %grad_w.4 = (bf16[4,2816,128]{2,1,0:T(8,128)(2,1)}, bf16[4,2816,128]{2,1,0:T(8,128)(2,1)}) custom-call(s32[1]{0:T(128)} %bitcast.8.sel_ref, bf16[2048,2816]{1,0:T(8,128)(2,1)} %get-tuple-element.68.rest_0_.hid_ref, bf16[2048,1024]{1,0:T(8,128)(2,1)} %rest_1_.1, bf16[2048,1024]{1,0:T(8,128)(2,1)} %get-tuple-element.81.rest_2_), custom_call_target="tpu_custom_call" | custom-call | flops 99999997952 | bytes 1 | tf_op jit(solution)/shard_map/grad_w/pallas_call | solution.py:416
  268.0 35.4 %grad_w.5 = (bf16[4,2816,128]{2,1,0:T(8,128)(2,1)}, bf16[4,2816,128]{2,1,0:T(8,128)(2,1)}, bf16[4,2816,128]{2,1,0:T(8,128)(2,1)}, bf16[4,2816,128]{2,1,0:T(8,128)(2,1)}) custom-call(s32[1]{0:T(128)} %bitcast.8.sel_ref, bf16[2048,2816]{1,0:T(8,128)(2,1)} %get-tuple-element.79.rest_0_, bf16[2048,2816]{1,0:T(8,128)(2,1)} %get-tuple-element.80.rest_1_, ...), custom_call_target="tpu_custom_call" | custom-call | flops 99999997952 | bytes 1 | tf_op jit(solution)/shard_map/grad_w/pallas_call | solution.py:416
  304.0 1.6 copy-done.1
  305.6 9.9 %grad_w.6 = (bf16[4,1024,128]{2,1,0:T(8,128)(2,1)}, bf16[4,1024,128]{2,1,0:T(8,128)(2,1)}) custom-call(s32[1]{0:T(128)} %bitcast.8.sel_ref, bf16[2048,1024]{1,0:T(8,128)(2,1)} %get-tuple-element.64.mix_ref.rest_0_, bf16[2048,1024]{1,0:T(8,128)(2,1)} %get-tuple-element.69.rest_1_.gmix_ref, bf16[4,2816,128]{2,1,0:T(8,128)(2,1)} %get-tuple-element.83.rest_2_.rest_0_, ...), custom_call_target="tpu_custom_call" | custom-call | flops 99999997952 | bytes 1 | tf_op jit(solution)/shard_map/grad_w/pallas_call | solution.py:416
  316.3 2.1 collective-permute-done.20.rest_7_
  318.4 1.0 copy-done.4
  319.5 12.8 %plane.1 = (bf16[8,1184,128]{2,1,0:T(8,128)(2,1)}, bf16[8,1184,128]{2,1,0:T(8,128)(2,1)}, bf16[8,1184,128]{2,1,0:T(8,128)(2,1)}, bf16[8,1184,128]{2,1,0:T(8,128)(2,1)}) custom-call(s32[4]{0:T(128)} %iota_xor_fusion.at_ref, bf16[4,2816,128]{2,1,0:T(8,128)(2,1)} %get-tuple-element.83.rest_2_.rest_0_, bf16[4,2816,128]{2,1,0:T(8,128)(2,1)} %collective-permute-done.17.rest_1_, ...), custom_call_target="tpu_custom_call" | custom-call | flops 1 | bytes 1 | tf_op jit(solution)/shard_map/plane/pallas_call | solution.py:438
  332.3 1.5 collective-permute-start.25
  334.4 1.5 collective-permute-start.27
  335.8 29.2 %mixer_bwd.2 = (bf16[2048,3328]{1,0:T(8,128)(2,1)}, f32[128,512]{1,0:T(8,128)}, f32[8,512]{1,0:T(8,128)}, f32[8,256]{1,0:T(8,128)}) custom-call(s32[8]{0:T(128)} %reshape.87.st_ref, bf16[2048,1024]{1,0:T(8,128)(2,1)} %get-tuple-element.69.rest_1_.gmix_ref, bf16[1024,1024]{1,0:T(8,128)(2,1)} %get-tuple-element.66.wo_ref.w_ref, ...), custom_call_target="tpu_custom_call" | custom-call | flops 1 | bytes 1 | tf_op jit(solution)/shard_map/mixer_bwd/pallas_call | solution.py:263
  365.0 29.1 %mixer_bwd.3 = (bf16[2048,3328]{1,0:T(8,128)(2,1)}, f32[128,512]{1,0:T(8,128)}, f32[8,512]{1,0:T(8,128)}, f32[8,256]{1,0:T(8,128)}) custom-call(s32[8]{0:T(128)} %reshape.87.st_ref, bf16[2048,1024]{1,0:T(8,128)(2,1)} %get-tuple-element.69.rest_1_.gmix_ref, bf16[1024,1024]{1,0:T(8,128)(2,1)} %get-tuple-element.66.wo_ref.w_ref, ...), custom_call_target="tpu_custom_call", output_to_operand_aliasing={{0}: (14, {})} | custom-call | flops 1 | bytes 1 | tf_op jit(solution)/shard_map/mixer_bwd/pallas_call | solution.py:263
  394.1 24.4 %grad_w.7 = (bf16[4,128,3328]{2,1,0:T(8,128)(2,1)}, bf16[4,128,3328]{2,1,0:T(8,128)(2,1)}) custom-call(s32[1]{0:T(128)} %bitcast.8.sel_ref, bf16[2048,3328]{1,0:T(8,128)(2,1)} %get-tuple-element.95.rest_0_.g_ref, bf16[2048,1024]{1,0:T(8,128)(2,1)} %get-tuple-element.96.rest_1_, f32[128,512]{1,0:T(8,128)} %get-tuple-element.97.rest_2_, ...), custom_call_target="tpu_custom_call" | custom-call | flops 1 | bytes 1 | tf_op jit(solution)/shard_map/grad_w/pallas_call | solution.py:416
  418.5 14.5 %mixer_dx.2.rest_2_.rest_1_ = f32[2048,1024]{1,0:T(8,128)} custom-call(bf16[2048,3328]{1,0:T(8,128)(2,1)} %get-tuple-element.95.rest_0_.g_ref, bf16[1024,3200]{1,0:T(8,128)(2,1)} %get-tuple-element.106.w_ref, bf16[2048,1024]{1,0:T(8,128)(2,1)} %tok_ref.7, f32[1,1024]{1,0:T(1,128)} %get-tuple-element.170.gain_ref, f32[2048,1024]{1,0:T(8,128)} %get-tuple-element.107.gres_ref, ...), custom_call_target="tpu_custom_call" | custom-call | flops 49999998976 | bytes 1 | tf_op jit(solution)/shard_map/mixer_dx/pallas_call | solution.py:289
  433.1 1.7 copy-done
  434.8 5.2 spread.1
  440.6 7.6 %line.1.rest_0_ = bf16[9472,128]{1,0:T(8,128)(2,1)} custom-call(bf16[8,1184,128]{2,1,0:T(8,128)(2,1)} %get-tuple-element.90.rest_0_.refs_0_, bf16[8,1184,128]{2,1,0:T(8,128)(2,1)} %collective-permute-done.25.refs_1_, bf16[8,1184,128]{2,1,0:T(8,128)(2,1)} %collective-permute-done.26.refs_2_, bf16[8,1184,128]{2,1,0:T(8,128)(2,1)} %collective-permute-done.27.refs_3_, ...), custom_call_target="tpu_custom_call" | custom-call | flops 1 | bytes 1 | tf_op jit(solution)/shard_map/line/pallas_call | solution.py:467
  448.2 1.0 collective-permute-start.22
  449.2 1.2 collective-permute-start.23
  450.4 1.4 collective-permute-start.24
  451.8 15.0 %mixer_dx.3.rest_0_ = f32[2048,1024]{1,0:T(8,128)} custom-call(bf16[2048,3328]{1,0:T(8,128)(2,1)} %get-tuple-element.95.rest_0_.g_ref, bf16[1024,3200]{1,0:T(8,128)(2,1)} %get-tuple-element.106.w_ref, bf16[2048,1024]{1,0:T(8,128)(2,1)} %tok_ref.7, f32[1,1024]{1,0:T(1,128)} %get-tuple-element.170.gain_ref, ...), custom_call_target="tpu_custom_call", output_to_operand_aliasing={{}: (6, {})} | custom-call | flops 1 | bytes 1 | tf_op jit(solution)/shard_map/mixer_dx/pallas_call | solution.py:289
  466.8 12.5 %mlp_down.2.refs_4_.rest_1_ = bf16[2048,1024]{1,0:T(8,128)(2,1)} custom-call(f32[2048,1024]{1,0:T(8,128)} %get-tuple-element.67.res_ref, bf16[2048,2816]{1,0:T(8,128)(2,1)} %get-tuple-element.68.rest_0_.hid_ref, bf16[8,4,2112,128]{3,2,1,0:T(8,128)(2,1)} %bitcast.60, f32[2048,1024]{1,0:T(8,128)} %mixer_dx.3.rest_0_), custom_call_target="tpu_custom_call" | custom-call | flops 1 | bytes 1 | tf_op jit(solution)/shard_map/mlp_down/pallas_call | solution.py:361
  479.3 9.4 %collective-permute-done.23 = bf16[1,128,3328]{2,1,0:T(8,128)(2,1)S(1)} collective-permute-done((bf16[1,128,3328]{2,1,0:T(8,128)(2,1)}, bf16[1,128,3328]{2,1,0:T(8,128)(2,1)S(1)}, u32[]{:S(2)}, u32[]{:S(2)}) %collective-permute-start.23) | collective-permute-done | bytes 852000 | tf_op jit(solution)/shard_map/ppermute | solution.py:534
  490.0 3.4 stack.1
  493.4 3.5 all-to-all-start
  497.1 12.4 %mlp_down.3 = bf16[2048,1024]{1,0:T(8,128)(2,1)} custom-call(f32[2048,1024]{1,0:T(8,128)} %get-tuple-element.67.res_ref, bf16[2048,2816]{1,0:T(8,128)(2,1)} %get-tuple-element.68.rest_0_.hid_ref, bf16[8,4,2112,128]{3,2,1,0:T(8,128)(2,1)} %bitcast.61, bf16[4,32,3712]{2,1,0:T(8,128)(2,1)} %bitcast.63, ...), custom_call_target="tpu_custom_call", output_to_operand_aliasing={{}: (4, {})} | custom-call | flops 1 | bytes 1 | tf_op jit(solution)/shard_map/mlp_down/pallas_call | solution.py:361
  509.5 10.6 %all-to-all-done = bf16[4,32,3712]{2,1,0:T(8,128)(2,1)S(1)} async-done(((bf16[4,32,3712]{2,1,0:T(8,128)(2,1)}), bf16[4,32,3712]{2,1,0:T(8,128)(2,1)S(1)}, u32[]{:S(2)}, u32[]{:S(2)}) %all-to-all-start) | async-done | bytes 950304 | tf_op jit(solution)/shard_map/all_to_all | solution.py:672
  525.4 1.1 slice.149
  526.5 1.0 fusion.3
  (147 shorter events, 19.3 us)
Async XLA Ops:
  7.2 39.5 %copy-start.19 = (bf16[32,512]{1,0:T(8,128)(2,1)S(1)}, bf16[32,512]{1,0:T(8,128)(2,1)}, u32[]{:S(2)}) copy-start(bf16[32,512]{1,0:T(8,128)(2,1)} %param.21) | copy-start | bytes 98308
  7.2 39.5 %copy-start.21 = (bf16[32,512]{1,0:T(8,128)(2,1)S(1)}, bf16[32,512]{1,0:T(8,128)(2,1)}, u32[]{:S(2)}) copy-start(bf16[32,512]{1,0:T(8,128)(2,1)} %param.22) | copy-start | bytes 98308
  7.2 39.5 %copy-start.9 = (bf16[32,1024]{1,0:T(8,128)(2,1)S(1)}, bf16[32,1024]{1,0:T(8,128)(2,1)}, u32[]{:S(2)}) copy-start(bf16[32,1024]{1,0:T(8,128)(2,1)} %param.23) | copy-start | bytes 196612
  7.2 154.1 %all-gather.3.cloned.1.call-start = ((), (), s32[]{:S(2)}) async-start(), calls=%async_computation.3 | async-start | bytes 17842176 | tf_op jit(solution)/shard_map/all_gather | solution.py:591
  9.2 91.5 %copy-start.31 = (bf16[16,512]{1,0:T(8,128)(2,1)S(1)}, bf16[16,512]{1,0:T(8,128)(2,1)}, u32[]{:S(2)}) copy-start(bf16[16,512]{1,0:T(8,128)(2,1)} %param.26) | copy-start | bytes 49156
  9.2 92.2 %copy-start.35 = (bf16[256]{0:T(256)(128)(2,1)S(1)}, bf16[256]{0:T(256)(128)(2,1)}, u32[]{:S(2)}) copy-start(bf16[256]{0:T(256)(128)(2,1)} %param.28) | copy-start | bytes 1540
  9.2 92.7 %copy-start.34 = (s32[2,4]{1,0:T(2,128)S(1)}, s32[2,4]{1,0:T(2,128)}, u32[]{:S(2)}) copy-start(s32[2,4]{1,0:T(2,128)} %param.18) | copy-start | bytes 100
  9.2 93.3 %copy-start.32 = (bf16[512]{0:T(512)(128)(2,1)S(1)}, bf16[512]{0:T(512)(128)(2,1)}, u32[]{:S(2)}) copy-start(bf16[512]{0:T(512)(128)(2,1)} %param.27) | copy-start | bytes 3076
  9.2 516.2 %reduce-scatter.2.cloned.1.call-start = ((), (), s32[]{:S(2)}) async-start(), calls=%async_computation.2 | async-start | bytes 3031040 | tf_op jit(solution)/shard_map/reduce_scatter | solution.py:662
  10.1 34.6 %copy-start.23 = (bf16[32,16]{1,0:T(8,128)(2,1)}, bf16[32,16]{1,0:T(8,128)(2,1)S(1)}, u32[]{:S(2)}) copy-start(bf16[32,16]{1,0:T(8,128)(2,1)S(1)} %copy.59) | copy-start | bytes 3076
  10.8 33.8 %copy-start.25 = (bf16[32,1]{1,0:T(8,128)(2,1)}, bf16[32,1]{1,0:T(8,128)(2,1)S(1)}, u32[]{:S(2)}) copy-start(bf16[32,1]{1,0:T(8,128)(2,1)S(1)} %copy.60) | copy-start | bytes 196
  11.6 33.1 %copy-start.27 = (bf16[32,1]{1,0:T(8,128)(2,1)}, bf16[32,1]{1,0:T(8,128)(2,1)S(1)}, u32[]{:S(2)}) copy-start(bf16[32,1]{1,0:T(8,128)(2,1)S(1)} %copy.61) | copy-start | bytes 196
  11.6 33.1 %copy-start.29 = (bf16[32,110]{1,0:T(8,128)(2,1)}, bf16[32,110]{1,0:T(8,128)(2,1)S(1)}, u32[]{:S(2)}) copy-start(bf16[32,110]{1,0:T(8,128)(2,1)S(1)} %broadcast_in_dim.35) | copy-start | bytes 21124
  12.6 12.5 %collective-permute-start = (bf16[32,4224]{1,0:T(8,128)(2,1)S(1)}, bf16[32,4224]{1,0:T(8,128)(2,1)S(1)}, u32[]{:S(2)}, u32[]{:S(2)}) collective-permute-start(bf16[32,4224]{1,0:T(8,128)(2,1)S(1)} %concatenate.30), channel_id=1, source_target_pairs={{0,1},{1,2},{2,3},{3,0},{4,5},{5,6},{6,7},{7,4},{8,9},{9,10},{10,1... | collective-permute-start | bytes 811016 | tf_op jit(solution)/shard_map/ppermute | solution.py:546
  15.7 28.9 %collective-permute-start.1 = (bf16[32,4224]{1,0:T(8,128)(2,1)S(1)}, bf16[32,4224]{1,0:T(8,128)(2,1)S(1)}, u32[]{:S(2)}, u32[]{:S(2)}) collective-permute-start(bf16[32,4224]{1,0:T(8,128)(2,1)S(1)} %concatenate.30), channel_id=1, source_target_pairs={{0,2},{1,3},{2,0},{3,1},{4,6},{5,7},{6,4},{7,5},{8,10},{9,11},{10,... | collective-permute-start | bytes 811016 | tf_op jit(solution)/shard_map/ppermute | solution.py:546
  18.3 26.3 %collective-permute-start.2 = (bf16[32,4224]{1,0:T(8,128)(2,1)S(1)}, bf16[32,4224]{1,0:T(8,128)(2,1)S(1)}, u32[]{:S(2)}, u32[]{:S(2)}) collective-permute-start(bf16[32,4224]{1,0:T(8,128)(2,1)S(1)} %concatenate.30), channel_id=1, source_target_pairs={{0,3},{1,0},{2,1},{3,2},{4,7},{5,4},{6,5},{7,6},{8,11},{9,8},{10,9... | collective-permute-start | bytes 811016 | tf_op jit(solution)/shard_map/ppermute | solution.py:546
  44.8 59.0 %copy-start.2 = (bf16[128,2176]{1,0:T(8,128)(2,1)}, bf16[128,2176]{1,0:T(8,128)(2,1)S(1)}, u32[]{:S(2)}) copy-start(bf16[128,2176]{1,0:T(8,128)(2,1)S(1)} %pad_maximum_fusion.rest_8_) | copy-start | bytes 1671172
  44.8 18.8 %collective-permute-start.10 = (bf16[128,2176]{1,0:T(8,128)(2,1)S(1)}, bf16[128,2176]{1,0:T(8,128)(2,1)S(1)}, u32[]{:S(2)}, u32[]{:S(2)}) collective-permute-start(bf16[128,2176]{1,0:T(8,128)(2,1)S(1)} %pad_maximum_fusion.rest_8_), channel_id=1, source_target_pairs={{0,16},{4,20},{8,24},{12,28},{16,0},{20,4},{24,8},{28,12},{1,17},{... | collective-permute-start | bytes 1671176 | tf_op jit(solution)/shard_map/ppermute | solution.py:514
  46.7 57.0 %copy-start.3 = (bf16[128,2048]{1,0:T(8,128)(2,1)}, bf16[128,2048]{1,0:T(8,128)(2,1)S(1)}, u32[]{:S(2)}) copy-start(bf16[128,2048]{1,0:T(8,128)(2,1)S(1)} %pad_maximum_fusion.2.rest_0_) | copy-start | bytes 1572868
  46.7 16.8 %collective-permute-start.3 = (bf16[128,2048]{1,0:T(8,128)(2,1)S(1)}, bf16[128,2048]{1,0:T(8,128)(2,1)S(1)}, u32[]{:S(2)}, u32[]{:S(2)}) collective-permute-start(bf16[128,2048]{1,0:T(8,128)(2,1)S(1)} %pad_maximum_fusion.2.rest_0_), channel_id=1, source_target_pairs={{0,8},{4,12},{8,0},{12,4},{16,24},{20,28},{24,16},{28,20},{1,9},{5... | collective-permute-start | bytes 1572872 | tf_op jit(solution)/shard_map/ppermute | solution.py:514
  48.3 30.0 %collective-permute-start.4 = (bf16[128,2048]{1,0:T(8,128)(2,1)S(1)}, bf16[128,2048]{1,0:T(8,128)(2,1)}, u32[]{:S(2)}, u32[]{:S(2)}) collective-permute-start(bf16[128,2048]{1,0:T(8,128)(2,1)S(1)} %pad_maximum_fusion.2.rest_0_), channel_id=1, source_target_pairs={{0,16},{4,20},{8,24},{12,28},{16,0},{20,4},{24,8},{28,12},{1,17},{... | collective-permute-start | bytes 1572872 | tf_op jit(solution)/shard_map/ppermute | solution.py:514
  48.8 31.1 %collective-permute-start.6 = (bf16[128,2048]{1,0:T(8,128)(2,1)S(1)}, bf16[128,2048]{1,0:T(8,128)(2,1)S(1)}, u32[]{:S(2)}, u32[]{:S(2)}) collective-permute-start(bf16[128,2048]{1,0:T(8,128)(2,1)S(1)} %pad_maximum_fusion.2.rest_0_), channel_id=1, source_target_pairs={{0,4},{4,0},{8,12},{12,8},{16,20},{20,16},{24,28},{28,24},{1,5},{5... | collective-permute-start | bytes 1572872 | tf_op jit(solution)/shard_map/ppermute | solution.py:514
  48.8 38.6 %collective-permute-start.11 = (bf16[128,2176]{1,0:T(8,128)(2,1)S(1)}, bf16[128,2176]{1,0:T(8,128)(2,1)S(1)}, u32[]{:S(2)}, u32[]{:S(2)}) collective-permute-start(bf16[128,2176]{1,0:T(8,128)(2,1)S(1)} %pad_maximum_fusion.rest_8_), channel_id=1, source_target_pairs={{0,8},{4,12},{8,0},{12,4},{16,24},{20,28},{24,16},{28,20},{1,9},{5... | collective-permute-start | bytes 1671176 | tf_op jit(solution)/shard_map/ppermute | solution.py:514
  63.5 35.9 %copy-start.16 = (bf16[128,2048]{1,0:T(8,128)(2,1)}, bf16[128,2048]{1,0:T(8,128)(2,1)S(1)}, u32[]{:S(2)}) copy-start(bf16[128,2048]{1,0:T(8,128)(2,1)S(1)} %collective-permute-done.3.rest_1_) | copy-start | bytes 1572868
  63.5 23.9 %collective-permute-start.13 = (bf16[128,2176]{1,0:T(8,128)(2,1)S(1)}, bf16[128,2176]{1,0:T(8,128)(2,1)S(1)}, u32[]{:S(2)}, u32[]{:S(2)}) collective-permute-start(bf16[128,2176]{1,0:T(8,128)(2,1)S(1)} %pad_maximum_fusion.rest_8_), channel_id=1, source_target_pairs={{0,4},{4,0},{8,12},{12,8},{16,20},{20,16},{24,28},{28,24},{1,5},{5... | collective-permute-start | bytes 1671176 | tf_op jit(solution)/shard_map/ppermute | solution.py:514
  63.5 40.2 %copy-start.12 = (bf16[128,2176]{1,0:T(8,128)(2,1)}, bf16[128,2176]{1,0:T(8,128)(2,1)S(1)}, u32[]{:S(2)}) copy-start(bf16[128,2176]{1,0:T(8,128)(2,1)S(1)} %collective-permute-done.10.rest_9_) | copy-start | bytes 1671172
  63.5 35.9 %collective-permute-start.12 = (bf16[128,2176]{1,0:T(8,128)(2,1)S(1)}, bf16[128,2176]{1,0:T(8,128)(2,1)S(1)}, u32[]{:S(2)}, u32[]{:S(2)}) collective-permute-start(bf16[128,2176]{1,0:T(8,128)(2,1)S(1)} %collective-permute-done.10.rest_9_), channel_id=1, source_target_pairs={{0,8},{4,12},{8,0},{12,4},{16,24},{20,28},{24,16},{28,20},{1,9},{5... | collective-permute-start | bytes 1671176 | tf_op jit(solution)/shard_map/ppermute | solution.py:514
  78.4 21.0 %collective-permute-start.5 = (bf16[128,2048]{1,0:T(8,128)(2,1)S(1)}, bf16[128,2048]{1,0:T(8,128)(2,1)}, u32[]{:S(2)}, u32[]{:S(2)}) collective-permute-start(bf16[128,2048]{1,0:T(8,128)(2,1)S(1)} %collective-permute-done.3.rest_1_), channel_id=1, source_target_pairs={{0,16},{4,20},{8,24},{12,28},{16,0},{20,4},{24,8},{28,12},{1,17},{... | collective-permute-start | bytes 1572872 | tf_op jit(solution)/shard_map/ppermute | solution.py:514
  79.9 20.0 %copy-start.17 = (bf16[128,2048]{1,0:T(8,128)(2,1)}, bf16[128,2048]{1,0:T(8,128)(2,1)S(1)}, u32[]{:S(2)}) copy-start(bf16[128,2048]{1,0:T(8,128)(2,1)S(1)} %collective-permute-done.6.rest_4_) | copy-start | bytes 1572868
  79.9 20.0 %collective-permute-start.7 = (bf16[128,2048]{1,0:T(8,128)(2,1)S(1)}, bf16[128,2048]{1,0:T(8,128)(2,1)S(1)}, u32[]{:S(2)}, u32[]{:S(2)}) collective-permute-start(bf16[128,2048]{1,0:T(8,128)(2,1)S(1)} %collective-permute-done.3.rest_1_), channel_id=1, source_target_pairs={{0,4},{4,0},{8,12},{12,8},{16,20},{20,16},{24,28},{28,24},{1,5},{5... | collective-permute-start | bytes 1572872 | tf_op jit(solution)/shard_map/ppermute | solution.py:514
  87.4 16.3 %collective-permute-start.14 = (bf16[128,2176]{1,0:T(8,128)(2,1)S(1)}, bf16[128,2176]{1,0:T(8,128)(2,1)}, u32[]{:S(2)}, u32[]{:S(2)}) collective-permute-start(bf16[128,2176]{1,0:T(8,128)(2,1)S(1)} %collective-permute-done.10.rest_9_), channel_id=1, source_target_pairs={{0,4},{4,0},{8,12},{12,8},{16,20},{20,16},{24,28},{28,24},{1,5},{5... | collective-permute-start | bytes 1671176 | tf_op jit(solution)/shard_map/ppermute | solution.py:514
  87.4 16.3 %collective-permute-start.15 = (bf16[128,2176]{1,0:T(8,128)(2,1)S(1)}, bf16[128,2176]{1,0:T(8,128)(2,1)}, u32[]{:S(2)}, u32[]{:S(2)}) collective-permute-start(bf16[128,2176]{1,0:T(8,128)(2,1)S(1)} %collective-permute-done.11.rest_10_), channel_id=1, source_target_pairs={{0,4},{4,0},{8,12},{12,8},{16,20},{20,16},{24,28},{28,24},{1,5},{5... | collective-permute-start | bytes 1671176 | tf_op jit(solution)/shard_map/ppermute | solution.py:514
  99.4 4.4 collective-permute-start.16
  99.4 4.3 collective-permute-start.8
  99.9 3.8 collective-permute-start.9
  267.7 36.3 %collective-permute-start.19 = (bf16[4,2816,128]{2,1,0:T(8,128)(2,1)}, bf16[4,2816,128]{2,1,0:T(8,128)(2,1)S(1)}, u32[]{:S(2)}, u32[]{:S(2)}) collective-permute-start(bf16[4,2816,128]{2,1,0:T(8,128)(2,1)} %get-tuple-element.87), channel_id=1, source_target_pairs={{0,4},{4,0},{8,12},{12,8},{16,20},{20,16},{24,28},{28,24},{1,5},{5... | collective-permute-start | bytes 8650760 | tf_op jit(solution)/shard_map/ppermute | solution.py:514
  303.4 12.9 %collective-permute-start.17 = (bf16[4,2816,128]{2,1,0:T(8,128)(2,1)}, bf16[4,2816,128]{2,1,0:T(8,128)(2,1)}, u32[]{:S(2)}, u32[]{:S(2)}) collective-permute-start(bf16[4,2816,128]{2,1,0:T(8,128)(2,1)} %get-tuple-element.84), channel_id=1, source_target_pairs={{0,4},{4,0},{8,12},{12,8},{16,20},{20,16},{24,28},{28,24},{1,5},{5... | collective-permute-start | bytes 8650760 | tf_op jit(solution)/shard_map/ppermute | solution.py:514
  303.8 12.5 %collective-permute-start.18 = (bf16[4,2816,128]{2,1,0:T(8,128)(2,1)}, bf16[4,2816,128]{2,1,0:T(8,128)(2,1)}, u32[]{:S(2)}, u32[]{:S(2)}) collective-permute-start(bf16[4,2816,128]{2,1,0:T(8,128)(2,1)} %get-tuple-element.86), channel_id=1, source_target_pairs={{0,4},{4,0},{8,12},{12,8},{16,20},{20,16},{24,28},{28,24},{1,5},{5... | collective-permute-start | bytes 8650760 | tf_op jit(solution)/shard_map/ppermute | solution.py:514
  315.5 2.9 collective-permute-start.20
  332.3 107.8 %collective-permute-start.25 = (bf16[8,1184,128]{2,1,0:T(8,128)(2,1)}, bf16[8,1184,128]{2,1,0:T(8,128)(2,1)}, u32[]{:S(2)}, u32[]{:S(2)}) collective-permute-start(bf16[8,1184,128]{2,1,0:T(8,128)(2,1)} %get-tuple-element.91.rest_1_), channel_id=1, source_target_pairs={{0,8},{4,12},{8,0},{12,4},{16,24},{20,28},{24,16},{28,20},{1,9},{5... | collective-permute-start | bytes 7274504 | tf_op jit(solution)/shard_map/ppermute | solution.py:534
  333.8 106.8 %collective-permute-start.26 = (bf16[8,1184,128]{2,1,0:T(8,128)(2,1)}, bf16[8,1184,128]{2,1,0:T(8,128)(2,1)}, u32[]{:S(2)}, u32[]{:S(2)}) collective-permute-start(bf16[8,1184,128]{2,1,0:T(8,128)(2,1)} %get-tuple-element.92.rest_2_), channel_id=1, source_target_pairs={{0,16},{4,20},{8,24},{12,28},{16,0},{20,4},{24,8},{28,12},{1,17},{... | collective-permute-start | bytes 7274504 | tf_op jit(solution)/shard_map/ppermute | solution.py:534
  334.4 106.2 %collective-permute-start.27 = (bf16[8,1184,128]{2,1,0:T(8,128)(2,1)}, bf16[8,1184,128]{2,1,0:T(8,128)(2,1)}, u32[]{:S(2)}, u32[]{:S(2)}) collective-permute-start(bf16[8,1184,128]{2,1,0:T(8,128)(2,1)} %get-tuple-element.93.rest_3_), channel_id=1, source_target_pairs={{0,24},{4,28},{8,16},{12,20},{16,8},{20,12},{24,0},{28,4},{1,25},{... | collective-permute-start | bytes 7274504 | tf_op jit(solution)/shard_map/ppermute | solution.py:534
  418.4 14.6 %collective-permute-start.21 = (bf16[4,128,3328]{2,1,0:T(8,128)(2,1)}, bf16[4,128,3328]{2,1,0:T(8,128)(2,1)S(1)}, u32[]{:S(2)}, u32[]{:S(2)}) collective-permute-start(bf16[4,128,3328]{2,1,0:T(8,128)(2,1)} %get-tuple-element.105), channel_id=1, source_target_pairs={{0,4},{4,0},{8,12},{12,8},{16,20},{20,16},{24,28},{28,24},{1,5},{5... | collective-permute-start | bytes 10223624 | tf_op jit(solution)/shard_map/ppermute | solution.py:514
  448.2 31.1 %collective-permute-start.22 = (bf16[1,128,3328]{2,1,0:T(8,128)(2,1)}, bf16[1,128,3328]{2,1,0:T(8,128)(2,1)S(1)}, u32[]{:S(2)}, u32[]{:S(2)}) collective-permute-start(bf16[1,128,3328]{2,1,0:T(8,128)(2,1)} %get-tuple-element.109.refs_5_), channel_id=1, source_target_pairs={{0,8},{4,12},{8,0},{12,4},{16,24},{20,28},{24,16},{28,20},{1,9},{5... | collective-permute-start | bytes 2555912 | tf_op jit(solution)/shard_map/ppermute | solution.py:534
  449.2 39.5 %collective-permute-start.23 = (bf16[1,128,3328]{2,1,0:T(8,128)(2,1)}, bf16[1,128,3328]{2,1,0:T(8,128)(2,1)S(1)}, u32[]{:S(2)}, u32[]{:S(2)}) collective-permute-start(bf16[1,128,3328]{2,1,0:T(8,128)(2,1)} %get-tuple-element.110.refs_6_), channel_id=1, source_target_pairs={{0,16},{4,20},{8,24},{12,28},{16,0},{20,4},{24,8},{28,12},{1,17},{... | collective-permute-start | bytes 2555912 | tf_op jit(solution)/shard_map/ppermute | solution.py:534
  450.4 38.4 %collective-permute-start.24 = (bf16[1,128,3328]{2,1,0:T(8,128)(2,1)S(1)}, bf16[1,128,3328]{2,1,0:T(8,128)(2,1)S(1)}, u32[]{:S(2)}, u32[]{:S(2)}) collective-permute-start(bf16[1,128,3328]{2,1,0:T(8,128)(2,1)S(1)} %copy-done.8), channel_id=1, source_target_pairs={{0,24},{4,28},{8,16},{12,20},{16,8},{20,12},{24,0},{28,4},{1,25},{... | collective-permute-start | bytes 2555912 | tf_op jit(solution)/shard_map/ppermute | solution.py:534
  493.4 26.8 %all-to-all-start = ((bf16[4,32,3712]{2,1,0:T(8,128)(2,1)}), bf16[4,32,3712]{2,1,0:T(8,128)(2,1)S(1)}, u32[]{:S(2)}, u32[]{:S(2)}) async-start(bf16[4,32,3712]{2,1,0:T(8,128)(2,1)} %bitcast.62), calls=%async_computation | async-start | bytes 1900544 | tf_op jit(solution)/shard_map/all_to_all | solution.py:672
  497.1 25.9 %copy-start.33 = (bf16[32]{0:T(256)(128)(2,1)S(1)}, bf16[32]{0:T(256)(128)(2,1)}, u32[]{:S(2)}) copy-start(bf16[32]{0:T(256)(128)(2,1)} %param.20) | copy-start | bytes 196
  (19 other events, 119.7 us)
Sparse Core Ops, SparseCore 0:
  10.9 150.4 all-gather.2
  448.4 47.2 reduce-scatter.1
